TPU v7x, 32 devices: a whole 2x2x4 slice. The times are simulated.
32 devices in a mesh: pb: 8 (over z, x), sa: 4 (over y, core).
Axes of the slice: x: 2, y: 2, z: 4, core: 2. Of those that a mesh axis runs over, the one named last changes fastest.
Arguments:
- question_states: bfloat16 [8, 4, 256, 768], P('pb', 'sa'), may hold values from -16 to 16
- question_ids: int32 [8, 4, 256], P('pb'), may hold values from 0 to 30521, as said below
- q_inner_weight: bfloat16 [768, 3072], P(None, 'sa'), may hold values from -0.21875 to 0.21875
- q_outer_weight: bfloat16 [3072, 768], P('sa'), may hold values from -0.109375 to 0.109375
- q_norm_gain: float32 [768], replicated, may hold values from 0.1 to 1.9
- sql_states: bfloat16 [4, 8, 256, 768], P('sa', 'pb'), may hold values from -16 to 16
- sql_ids: int32 [4, 8, 256], P('sa'), may hold values from 0 to 32099, as said below
- s_inner_weight: bfloat16 [768, 3072], P(None, 'pb'), may hold values from -0.21875 to 0.21875
- s_outer_weight: bfloat16 [3072, 768], P('pb'), may hold values from -0.109375 to 0.109375
- s_norm_gain: float32 [768], replicated, may hold values from 0.1 to 1.9
- positive_column: int32 [32], P('pb'), may hold values from 0 to 31, each once
Outputs:
- loss: float32 [], replicated
- q_inner_grad: float32 [768, 3072], P(None, 'sa')
- q_outer_grad: float32 [3072, 768], P('sa')
- q_gain_grad: float32 [768], replicated
- s_inner_grad: float32 [768, 3072], P(None, 'pb')
- s_outer_grad: float32 [3072, 768], P('pb')
- s_gain_grad: float32 [768], replicated
Inputs may be any that keep to these rules, and one draw needn't show every extreme that they name: `question_ids`: each sequence is a run of nonzero ids followed by padding zeros, the run 3 * 64 long or longer. `sql_ids`: each sequence is a run of nonzero ids followed by padding zeros, the run 3 * 64 long or longer.
All inputs are finite; a program needn't handle non-finite values.
Results may differ from a plain program's by a relative error of at most 0.0051.
Values may be sent and summed in bfloat16 or wider, within the bound.
No kernel may reach another device: no remote copies, remote signals or barrier semaphores. Data moves between devices by JAX's collectives and lax.ppermute only.
A program may use at most 128 MiB of HBM per device.

v0:
```python
import math

import jax
import jax.numpy as jnp
from jax import lax
from jax.sharding import PartitionSpec as P

D = 768


HIGH = lax.Precision.HIGHEST


def apply_rms_norm(input_float, norm_gain_vector, root_mean_square):
    if root_mean_square:
        input_normalized = input_float * lax.rsqrt(
            jnp.mean(input_float * input_float, axis=-1, keepdims=True) + 1e-06
        )
    else:
        mean_removed = input_float - jnp.mean(input_float, axis=-1, keepdims=True)
        input_normalized = mean_removed * lax.rsqrt(
            jnp.mean(mean_removed * mean_removed, axis=-1, keepdims=True) + 1e-05
        )
    return (input_normalized, (input_normalized * norm_gain_vector).astype(jnp.bfloat16))


def gelu_value(v):
    return 0.5 * v * (1.0 + lax.erf(v / math.sqrt(2.0)))


def gelu_slope(v):
    return 0.5 * (1.0 + lax.erf(v / math.sqrt(2.0))) + v * jnp.exp(-0.5 * v * v) / math.sqrt(
        2.0 * math.pi
    )


def pool_weights(ids):
    mask = (ids > 0).astype(jnp.float32)
    return mask / jnp.sum(mask, axis=-1, keepdims=True)


def forward_block(states, ids, inner, norm_gain_vector, root_mean_square):
    count, length, width = states.shape
    input_float = states.astype(jnp.float32).reshape(count * length, width)
    input_normalized, normalized_rows = apply_rms_norm(
        input_float, norm_gain_vector, root_mean_square
    )
    pre = jnp.dot(normalized_rows, inner, preferred_element_type=jnp.float32)
    hidden = gelu_value(pre).reshape(count, length, -1)
    return jnp.einsum("nt,ntf->nf", pool_weights(ids), hidden, precision=HIGH)


def residual_pool(states, ids):
    return jnp.einsum("nt,ntd->nd", pool_weights(ids), states.astype(jnp.float32), precision=HIGH)


def backward_block(states, ids, inner, norm_gain_vector, root_mean_square, hidden_grad):
    count, length, width = states.shape
    input_float = states.astype(jnp.float32).reshape(count * length, width)
    input_normalized, normalized_rows = apply_rms_norm(
        input_float, norm_gain_vector, root_mean_square
    )
    pre = jnp.dot(normalized_rows, inner, preferred_element_type=jnp.float32)
    weights = pool_weights(ids)
    slope = gelu_slope(pre).reshape(count, length, -1)
    dpre = (
        (weights[:, :, None] * hidden_grad[:, None, :] * slope)
        .reshape(count * length, -1)
        .astype(jnp.bfloat16)
    )
    inner_layer_grad = lax.dot_general(
        normalized_rows, dpre, (((0,), (0,)), ((), ())), preferred_element_type=jnp.float32
    )
    normalized_grad = lax.dot_general(
        dpre, inner, (((1,), (1,)), ((), ())), preferred_element_type=jnp.float32
    )
    return (inner_layer_grad, jnp.sum(input_normalized * normalized_grad, axis=0))


def per_device(
    question_states,
    question_ids,
    q_inner_weight,
    q_outer_weight,
    q_norm_gain,
    sql_states,
    sql_ids,
    s_inner_weight,
    s_outer_weight,
    s_norm_gain,
    positive_column,
):
    scale = 1.0 / math.sqrt(D)
    q_table = question_ids[0]
    s_table = sql_ids[0]
    q_rows = q_table.shape[0]
    s_rows = s_table.shape[0]
    own_count = question_states.shape[1]
    q_place = lax.axis_index("sa")
    s_place = lax.axis_index("pb")

    def s_forward(piece):
        pooled = forward_block(piece[0], s_table, s_inner_weight, s_norm_gain, True)
        return pooled

    ids = q_table
    pooled = forward_block(
        lax.all_gather(question_states, "sa", axis=1, tiled=True)[0],
        ids,
        q_inner_weight,
        q_norm_gain,
        False,
    )
    s_pooled = s_forward(lax.all_gather(sql_states, "pb", axis=1, tiled=True))
    q_first = q_place * own_count
    s_first = s_place * own_count
    q_own = residual_pool(
        question_states[0], lax.dynamic_slice_in_dim(q_table, q_first, own_count, 0)
    )
    s_own = residual_pool(sql_states[0], lax.dynamic_slice_in_dim(s_table, s_first, own_count, 0))
    q_resid = lax.dynamic_update_slice_in_dim(
        jnp.zeros((q_rows, D), jnp.float32), q_own, q_first, 0
    )
    s_resid = lax.dynamic_update_slice_in_dim(
        jnp.zeros((s_rows, D), jnp.float32), s_own, s_first, 0
    )
    q_outer_f = q_outer_weight.astype(jnp.float32)
    s_outer_f = s_outer_weight.astype(jnp.float32)
    q_embed = lax.psum(jnp.dot(pooled, q_outer_f, precision=HIGH) + q_resid, "sa")
    s_embed = lax.psum(jnp.dot(s_pooled, s_outer_f, precision=HIGH) + s_resid, "pb")
    tile = scale * lax.dot_general(q_embed, s_embed, (((1,), (1,)), ((), ())), precision=HIGH)
    columns = q_place * s_rows + jnp.arange(s_rows, dtype=jnp.int32)
    match = (positive_column[:, None] == columns[None, :]).astype(jnp.float32)
    row_top = lax.pmax(jnp.max(tile, axis=1), "sa")
    row_total, row_pos = lax.psum(
        (jnp.sum(jnp.exp(tile - row_top[:, None]), axis=1), jnp.sum(match * tile, axis=1)), "sa"
    )
    col_top = lax.pmax(jnp.max(tile, axis=0), "pb")
    col_total, col_pos = lax.psum(
        (jnp.sum(jnp.exp(tile - col_top[None, :]), axis=0), jnp.sum(match * tile, axis=0)), "pb"
    )
    row_lse = row_top + jnp.log(row_total)
    col_lse = col_top + jnp.log(col_total)
    pairs = q_rows * lax.axis_size("pb")
    row_part = jnp.where(q_place == 0, jnp.sum(row_lse - row_pos), 0.0)
    col_part = jnp.where(s_place == 0, jnp.sum(col_lse - col_pos), 0.0)
    loss_part = (row_part + col_part) / (2.0 * pairs)
    dscore = 0.5 * (
        jnp.exp(tile - row_lse[:, None]) + jnp.exp(tile - col_lse[None, :]) - 2.0 * match
    )
    q_grad = lax.psum(scale * jnp.dot(dscore, s_embed, precision=HIGH), "sa")
    s_grad = lax.psum(
        scale * lax.dot_general(dscore, q_embed, (((0,), (0,)), ((), ())), precision=HIGH), "pb"
    )
    q_outer_part = lax.dot_general(pooled, q_grad, (((0,), (0,)), ((), ())), precision=HIGH)
    s_outer_part = lax.dot_general(s_pooled, s_grad, (((0,), (0,)), ((), ())), precision=HIGH)
    q_hidden_grad = lax.dot_general(q_grad, q_outer_f, (((1,), (1,)), ((), ())), precision=HIGH)
    s_hidden_grad = lax.dot_general(s_grad, s_outer_f, (((1,), (1,)), ((), ())), precision=HIGH)

    def s_backward(piece):
        inner_layer_grad, gain_grad = backward_block(
            piece[0], s_table, s_inner_weight, s_norm_gain, True, s_hidden_grad
        )
        return (inner_layer_grad, gain_grad)

    ids = q_table
    inner_layer_grad, gain_grad = backward_block(
        lax.all_gather(question_states, "sa", axis=1, tiled=True)[0],
        ids,
        q_inner_weight,
        q_norm_gain,
        False,
        q_hidden_grad,
    )
    s_inner_part, s_gain_part = s_backward(lax.all_gather(sql_states, "pb", axis=1, tiled=True))
    q_inner_grad, q_outer_grad = lax.psum((inner_layer_grad, q_outer_part), "pb")
    s_inner_grad, s_outer_grad = lax.psum((s_inner_part, s_outer_part), "sa")
    q_gain_grad, s_gain_grad, loss = lax.psum((gain_grad, s_gain_part, loss_part), ("pb", "sa"))
    return (loss, q_inner_grad, q_outer_grad, q_gain_grad, s_inner_grad, s_outer_grad, s_gain_grad)


def solution(mesh):
    placed = (
        P("pb", "sa", None, None),
        P("pb", None, None),
        P(None, "sa"),
        P("sa", None),
        P(),
        P("sa", "pb", None, None),
        P("sa", None, None),
        P(None, "pb"),
        P("pb", None),
        P(),
        P("pb"),
    )
    return jax.shard_map(
        per_device,
        mesh=mesh,
        in_specs=placed,
        out_specs=(P(), P(None, "sa"), P("sa", None), P(), P(None, "pb"), P("pb", None), P()),
        check_vma=False,
    )
```

profile of v0, /device:TPU:0, one launch (start us, length us, event | category | flops | bytes accessed | tf_op | source)
XLA Modules:
  0.0 473.1 jit_solution(4002629526718179287)
XLA Ops:
  7.2 0.0 all-gather.3.cloned.1.call-start
  7.2 0.7 all-gather.3.cloned.1.call-update
  7.9 0.0 all-gather.5.cloned.1.call-start
  8.0 0.7 all-gather.5.cloned.1.call-update
  8.7 0.0 all-reduce.10.cloned.1.call-start
  8.7 1.3 fusion.39
  11.4 0.7 convert_bitcast_fusion
  12.2 0.1 convert_reduce_fusion.1
  12.3 0.1 broadcast_bitcast_fusion
  12.4 0.7 convert_bitcast_fusion.2
  13.1 0.1 convert_reduce_fusion.2
  13.2 0.1 broadcast_bitcast_fusion.1
  13.3 18.7 %all-gather.3.cloned.1.call-done = bf16[1,4,256,768]{3,2,0,1:T(8,128)(2,1)} async-done(((bf16[1,1,256,768]{3,2,0,1:T(8,128)(2,1)}), bf16[1,4,256,768]{3,2,0,1:T(8,128)(2,1)}) %all-gather.3.cloned.1.call-update) | async-done | bytes 1572880 | tf_op jit(solution)/shard_map/all_gather | solution.py:108
  32.0 1.8 convert_reduce_fusion
  33.8 2.0 multiply_reduce_fusion.3
  35.8 0.5 multiply_convert_fusion.1
  36.4 2.8 multiply_multiply_fusion.3
  39.2 1.6 fusion.33
  40.8 0.6 fusion.21
  41.4 1.0 convolution_add_fusion.1
  42.4 0.1 add.105
  42.4 11.0 %psum.105 = f32[4,768]{1,0:T(4,128)S(1)} all-reduce(f32[4,768]{1,0:T(4,128)S(1)} %add.105), channel_id=1, replica_groups=mesh['pb'=8,'sa'=4] {'sa'}, use_global_device_ids=true, to_apply=%region_4.0 | all-reduce | flops 3072 | bytes 24576 | tf_op jit(solution)/shard_map/psum | solution.py:129
  53.4 41.2 %all-gather.5.cloned.1.call-done = bf16[1,8,256,768]{3,2,0,1:T(8,128)(2,1)} async-done(((bf16[1,1,256,768]{3,2,0,1:T(8,128)(2,1)}), bf16[1,8,256,768]{3,2,0,1:T(8,128)(2,1)}) %all-gather.5.cloned.1.call-update) | async-done | bytes 3145744 | tf_op jit(solution)/shard_map/all_gather | solution.py:114
  94.6 2.7 multiply_reduce_fusion.1
  97.4 0.1 copy-done.4
  97.5 0.8 multiply_convert_fusion
  98.3 0.3 copy-done.18
  98.5 3.1 multiply_multiply_fusion.2
  101.7 1.6 fusion.29
  103.2 0.4 fusion.17
  103.6 1.0 convolution_add_fusion
  104.6 0.1 add.109
  104.7 34.8 %psum.106 = f32[8,768]{1,0:T(8,128)S(1)} all-reduce(f32[8,768]{1,0:T(8,128)S(1)} %add.109), channel_id=1, replica_groups=mesh['pb'=8,'sa'=4] {'pb'}, use_global_device_ids=true, to_apply=%region_8.0 | all-reduce | flops 6144 | bytes 49152 | tf_op jit(solution)/shard_map/psum | solution.py:130
  139.5 0.3 fusion.56
  139.7 17.1 %pmax.15 = f32[8]{0:T(128)S(1)} all-reduce(f32[8]{0:T(128)S(1)} %get-tuple-element.11), channel_id=1, replica_groups=mesh['pb'=8,'sa'=4] {'pb'}, use_global_device_ids=true, to_apply=%region_17.0 | all-reduce | flops 8 | bytes 64 | tf_op jit(solution)/shard_map/pmax | solution.py:138
  156.9 5.6 %pmax.14 = f32[4]{0:T(128)S(1)} all-reduce(f32[4]{0:T(128)S(1)} %get-tuple-element.12), channel_id=1, replica_groups=mesh['pb'=8,'sa'=4] {'sa'}, use_global_device_ids=true, to_apply=%region_10.0 | all-reduce | flops 4 | bytes 32 | tf_op jit(solution)/shard_map/pmax | solution.py:134
  162.5 0.2 fusion.37
  162.7 19.1 %psum.109 = f32[8]{0:T(128)S(1)} all-reduce(f32[8]{0:T(128)S(1)} %get-tuple-element.9), channel_id=1, replica_groups=mesh['pb'=8,'sa'=4] {'pb'}, use_global_device_ids=true, to_apply=%region_19.0 | all-reduce | flops 8 | bytes 64 | tf_op jit(solution)/shard_map/psum | solution.py:139
  181.9 5.7 %psum.107 = f32[4]{0:T(128)S(1)} all-reduce(f32[4]{0:T(128)S(1)} %get-tuple-element.10), channel_id=1, replica_groups=mesh['pb'=8,'sa'=4] {'sa'}, use_global_device_ids=true, to_apply=%region_12.0 | all-reduce | flops 4 | bytes 32 | tf_op jit(solution)/shard_map/psum | solution.py:135
  187.5 0.3 convolution_multiply_fusion
  187.8 33.2 %all-reduce.1 = (f32[8]{0:T(128)S(1)}, f32[8,768]{1,0:T(8,128)S(1)}) all-reduce(f32[8]{0:T(128)S(1)} %get-tuple-element.7, f32[8,768]{1,0:T(8,128)S(1)} %convolution_multiply_fusion), channel_id=1, replica_groups=mesh['pb'=8,'sa'=4] {'pb'}, use_global_device_ids=true, to_apply=%region_21.0 | all-reduce | flops 6152 | bytes 49216 | tf_op jit(solution)/shard_map/psum | solution.py:139
  221.1 0.6 fusion.61
  221.7 2.1 fusion.15
  223.8 2.8 fusion.11
  226.7 1.2 copy-done.6
  227.8 2.8 fusion.62
  230.7 0.0 all-reduce.8.cloned.1.call-start
  230.8 0.2 convolution_multiply_fusion.1
  231.0 10.7 %all-reduce.3 = (f32[4]{0:T(128)S(1)}, f32[4,768]{1,0:T(4,128)S(1)}) all-reduce(f32[4]{0:T(128)S(1)} %get-tuple-element.8, f32[4,768]{1,0:T(4,128)S(1)} %convolution_multiply_fusion.1), channel_id=1, replica_groups=mesh['pb'=8,'sa'=4] {'sa'}, use_global_device_ids=true, to_apply=%region_14.0 | all-reduce | flops 3076 | bytes 24608 | tf_op jit(solution)/shard_map/psum | solution.py:135
  241.7 2.3 fusion.59
  244.0 3.2 fusion.5
  247.3 3.5 fusion.19
  250.8 2.9 fusion.60
  253.6 0.6 subtract_reduce_fusion.1
  254.9 0.6 subtract_reduce_fusion
  256.2 3.0 multiply_reduce_fusion.2
  259.2 1.9 multiply_reduce_fusion
  261.2 37.4 %all-reduce = (f32[]{:T(128)}, f32[768]{0:T(1024)}, f32[768]{0:T(1024)}) all-reduce(f32[]{:T(128)S(6)} %div.113, f32[768]{0:T(1024)S(1)} %multiply_reduce_fusion.2, f32[768]{0:T(1024)S(1)} %multiply_reduce_fusion), channel_id=1, replica_groups=mesh['pb'=8,'sa'=4] {'pb','sa'}, use_global_device_ids=true, to_apply=%region_23.24 | all-reduce | flops 1537 | bytes 12296 | tf_op jit(solution)/shard_map/psum | solution.py:178
  298.6 160.4 %all-reduce.8.cloned.1.call-done = (f32[768,768]{1,0:T(8,128)}, f32[768,768]{1,0:T(8,128)}) async-done(((f32[768,768]{1,0:T(8,128)}, f32[768,768]{1,0:T(8,128)}), (f32[768,768]{1,0:T(8,128)}, f32[768,768]{1,0:T(8,128)})) %all-reduce.8.cloned.1.call-update) | async-done | bytes 4718608 | tf_op jit(solution)/shard_map/psum | solution.py:176
  459.0 3.4 copy.57
  462.4 1.4 copy.58
  463.8 0.7 copy-done.17
  464.5 1.0 copy.59
  465.5 1.0 copy.60
  (60 shorter events, 0.2 us)
Async XLA Ops:
  7.2 29.2 %copy-start = (bf16[768,768]{1,0:T(8,128)(2,1)S(1)}, bf16[768,768]{1,0:T(8,128)(2,1)}, u32[]{:S(2)}) copy-start(bf16[768,768]{1,0:T(8,128)(2,1)} %param.13) | copy-start | bytes 3538948
  7.2 28.6 %copy-start.20 = (f32[768]{0:T(1024)S(1)}, f32[768]{0:T(1024)}, u32[]{:S(2)}) copy-start(f32[768]{0:T(1024)} %param.15) | copy-start | bytes 9220
  7.2 24.8 %all-gather.3.cloned.1.call-start = ((), (), s32[]{:S(2)}) async-start(), calls=%async_computation | async-start | bytes 1966080 | tf_op jit(solution)/shard_map/all_gather | solution.py:108
  7.9 86.7 %all-gather.5.cloned.1.call-start = ((), (), s32[]{:S(2)}) async-start(), calls=%async_computation.1 | async-start | bytes 3538944 | tf_op jit(solution)/shard_map/all_gather | solution.py:114
  8.7 289.9 %all-reduce.10.cloned.1.call-start = ((), (), s32[]{:S(2)}) async-start(), calls=%async_computation.3 | async-start | bytes 4718592 | tf_op jit(solution)/shard_map/psum | solution.py:177
  32.0 3.9 copy-start.3
  36.4 2.8 copy-start.11
  39.2 1.6 copy-start.8
  39.2 2.2 copy-start.13
  40.8 56.6 %copy-start.21 = (f32[768]{0:T(1024)S(1)}, f32[768]{0:T(1024)}, u32[]{:S(2)}) copy-start(f32[768]{0:T(1024)} %param.20) | copy-start | bytes 9220
  94.6 2.8 copy-start.4
  97.5 1.1 copy-start.18
  98.5 3.1 copy-start.1
  101.6 1.6 copy-start.10
  101.6 2.0 copy-start.14
  101.6 60.9 %copy-start.22 = (s32[4]{0:T(128)S(1)}, s32[4]{0:T(128)}, u32[]{:S(2)}) copy-start(s32[4]{0:T(128)} %param.21) | copy-start | bytes 52
  221.1 6.8 %copy-start.2 = (bf16[2048,768]{1,0:T(8,128)(2,1)S(1)}, bf16[2048,768]{1,0:T(8,128)(2,1)}, u32[]{:S(2)}) copy-start(bf16[2048,768]{1,0:T(8,128)(2,1)} %copy-done.1) | copy-start | bytes 9437188
  226.7 1.2 copy-start.6
  230.7 228.3 %all-reduce.8.cloned.1.call-start = ((), (), s32[]{:S(2)}) async-start(), calls=%async_computation.2 | async-start | bytes 9437184 | tf_op jit(solution)/shard_map/psum | solution.py:176
  244.0 6.7 %copy-start.12 = (bf16[1024,768]{1,0:T(8,128)(2,1)S(1)}, bf16[1024,768]{1,0:T(8,128)(2,1)}, u32[]{:S(2)}) copy-start(bf16[1024,768]{1,0:T(8,128)(2,1)} %copy-done.11) | copy-start | bytes 4718596
  247.3 3.5 copy-start.15
  256.2 3.0 copy-start.5
  256.2 3.0 copy-start.7
  256.2 3.0 copy-start.19
  459.0 3.4 copy-start.9
  462.4 2.1 copy-start.17
  462.4 3.1 copy-start.16
Sparse Core Ops, SparseCore 0:
  9.6 22.3 all-gather.2
  34.2 60.4 all-gather.4
  230.8 54.2 all-reduce.9
  289.1 169.8 all-reduce.7
where the time goes:
time: 474 us; the launch traced here: 473 us
  waiting for transfers between devices  222 us (47%)
  blocking collectives  175 us (37%)
  matrix products  31.9 us (7%)
  other arithmetic  18.5 us (4%)
  between operations  16.8 us (4%)
  local copies, waits for them, and re-layouts  9.25 us (2%)
    psum x1, waiting for transfers between devices, per_device(): lax.psum((inner_layer_grad, q_outer_part), 'pb')  160 us
    psum x2, blocking collectives, per_device(): lax.psum((jnp.sum(jnp.exp(tile - col_top[None, :]), axis=0), jnp.sum(matc...  52.4 us
    all_gather x1, waiting for transfers between devices, per_device(): s_pooled = s_forward(lax.all_gather(sql_states, 'pb', axis=1, tiled=True))  41.2 us
    psum x1, blocking collectives, per_device(): lax.psum((gain_grad, s_gain_part, loss_part), ('pb', 'sa'))  37.4 us
    psum x1, blocking collectives, per_device(): lax.psum(jnp.dot(s_pooled, s_outer_f, precision=HIGH) + s_resid, 'pb')  34.8 us
    all_gather x1, waiting for transfers between devices, per_device(): lax.all_gather(question_states, 'sa', axis=1, tiled=True)[0]  18.7 us
    pmax x1, blocking collectives, per_device(): col_top = lax.pmax(jnp.max(tile, axis=0), 'pb')  17.1 us
    psum x2, blocking collectives, per_device(): lax.psum((jnp.sum(jnp.exp(tile - row_top[:, None]), axis=1), jnp.sum(matc...  16.3 us
  transfers between devices with their start and end apart: 4, of which 3 were waited for; matrix products, arithmetic and copies ran while one was open for 7% of the time, Pallas kernels for 0%

commit v1 on v0

v1 whole, which is shorter than its diff:
```python
import math

import jax
import jax.numpy as jnp
from jax import lax
from jax.sharding import PartitionSpec as P

HIGH = lax.Precision.HIGHEST
F32 = jnp.float32
BF16 = jnp.bfloat16


def normalize(x, gain, root_mean_square):
    x = x.astype(F32)
    if root_mean_square:
        xhat = x * lax.rsqrt(jnp.mean(x * x, axis=-1, keepdims=True) + 1e-06)
    else:
        centered = x - jnp.mean(x, axis=-1, keepdims=True)
        xhat = centered * lax.rsqrt(jnp.mean(centered * centered, axis=-1, keepdims=True) + 1e-05)
    return (xhat * gain).astype(BF16)


def gelu_value(v):
    return 0.5 * v * (1.0 + lax.erf(v / math.sqrt(2.0)))


def gelu_slope(v):
    return 0.5 * (1.0 + lax.erf(v / math.sqrt(2.0))) + v * jnp.exp(-0.5 * v * v) / math.sqrt(
        2.0 * math.pi
    )


def pool_weights(ids):
    mask = (ids > 0).astype(F32)
    return mask / jnp.sum(mask, axis=-1, keepdims=True)


def swap(x, axis, step):
    size = lax.axis_size(axis)
    return lax.ppermute(x, axis, [(i, i ^ step) for i in range(size)])


def ordered(mine, other, bit, axis=0):
    return jnp.where(
        bit == 0,
        jnp.concatenate([mine, other], axis),
        jnp.concatenate([other, mine], axis),
    )


def bits_of(size):
    return [1 << i for i in range(size.bit_length() - 1)]


def bit_at(place, step):
    return jnp.where((place & step) != 0, 1, 0)


def pick_rows(table, place, count):
    return jnp.stack(
        [lax.dynamic_index_in_dim(table, place ^ k, 0, keepdims=False) for k in range(count)]
    )


def canonical(rows, place):
    count = rows.shape[0]
    for step in bits_of(count):
        shape = rows.shape
        parts = rows.reshape((count // (2 * step), 2, step) + shape[1:])
        rows = jnp.where((place & step) != 0, parts[:, ::-1], parts).reshape(shape)
    return rows


def cut(x, index, size, axis=0):
    return lax.dynamic_slice_in_dim(x, index * size, size, axis)


def per_device(
    question_states,
    question_ids,
    q_inner_weight,
    q_outer_weight,
    q_norm_gain,
    sql_states,
    sql_ids,
    s_inner_weight,
    s_outer_weight,
    s_norm_gain,
    positive_column,
):
    n_pb, n_sa = lax.axis_size("pb"), lax.axis_size("sa")
    p, a = lax.axis_index("pb"), lax.axis_index("sa")
    width = question_states.shape[-1]
    length = question_states.shape[-2]
    scale = 1.0 / math.sqrt(width)
    group = 4
    q_pool = pool_weights(question_ids[0])
    s_pool = pool_weights(sql_ids[0])
    pair_bit = bit_at(p, 1)

    own_q = question_states[0, 0]
    own_s = sql_states[0, 0]
    s_tokens = [own_s] + [swap(own_s, "pb", k) for k in range(1, group)]
    core = bit_at(a, 1)

    def fetch(weight, step):
        half = weight.shape[0] // 2
        mine = swap(cut(weight, core, half), "pb", step)
        return ordered(mine, swap(mine, "sa", 1), core)

    q_tokens = [own_q] + [None] * (n_sa - 1)
    for step in reversed(bits_of(n_sa)):
        for k in range(0, n_sa, 2 * step):
            q_tokens[k + step] = swap(q_tokens[k], "sa", step)
    far = range(group, n_pb, group)
    s_inners = [s_inner_weight] + [fetch(s_inner_weight, k) for k in far]
    s_outers = [s_outer_weight] + [fetch(s_outer_weight, k) for k in far]
    s_inner_all = jnp.concatenate(s_inners, 1)
    s_outer_all = jnp.concatenate(s_outers, 0)
    positive = lax.all_gather(positive_column, "pb", axis=0, tiled=True)

    q_pool_own = pick_rows(q_pool, a, n_sa)
    q_normed = [normalize(t, q_norm_gain, False) for t in q_tokens]
    q_rows = jnp.concatenate(q_normed, 0)
    q_pre = jnp.dot(q_rows, q_inner_weight, preferred_element_type=F32)
    q_pooled = jnp.sum(
        gelu_value(q_pre).reshape(n_sa, length, -1) * q_pool_own[:, :, None], axis=1
    )
    q_pooled = canonical(q_pooled, a)
    s_pool_own = pick_rows(s_pool, p, group)
    s_rows = jnp.concatenate([normalize(t, s_norm_gain, True) for t in s_tokens], 0)
    s_pre = jnp.dot(s_rows, s_inner_all, preferred_element_type=F32).reshape(group, length, -1)
    s_pooled = jnp.sum(gelu_value(s_pre) * s_pool_own[:, :, None], axis=1)
    s_pooled = canonical(s_pooled, p)
    q_self = jnp.sum(own_q.astype(F32) * q_pool_own[0][:, None], axis=0)
    s_self = jnp.sum(own_s.astype(F32) * s_pool_own[0][:, None], axis=0)

    q_outer_f = q_outer_weight.astype(F32)
    s_outer_f = s_outer_all.astype(F32)
    q_part = jnp.dot(q_pooled, q_outer_f, precision=HIGH)
    s_part = jnp.dot(s_pooled, s_outer_f, precision=HIGH)
    q_part = q_part + jnp.where(jnp.arange(n_sa)[:, None] == a, q_self[None], 0.0)
    s_part = s_part + jnp.where(jnp.arange(group)[:, None] == p % group, s_self[None], 0.0)

    q_pool_pair = swap(q_pool, "pb", 1)
    other_q = swap(own_q, "pb", 1)
    pair_tokens = [other_q] + [None] * (n_sa - 1)
    for step in reversed(bits_of(n_sa)):
        for k in range(0, n_sa, 2 * step):
            pair_tokens[k + step] = swap(pair_tokens[k], "sa", step)

    q_sum_steps = bits_of(n_sa)[1:]
    s_sum_steps = bits_of(group)
    for step in q_sum_steps:
        q_part = q_part + swap(q_part, "sa", step)
    for step in s_sum_steps:
        s_part = s_part + swap(s_part, "pb", step)
    for step in bits_of(n_pb):
        q_part = ordered(q_part, swap(q_part, "pb", step), bit_at(p, step))
    for step in bits_of(n_pb)[2:]:
        s_part = ordered(s_part, swap(s_part, "pb", step), bit_at(p, step))
    for step in reversed(bits_of(n_sa)):
        pass
    q_embed = q_part + swap(q_part, "sa", 1)
    s_embed = s_part
    for step in bits_of(n_sa):
        s_embed = ordered(s_embed, swap(s_embed, "sa", step), bit_at(a, step))

    q_pooled_all = lax.all_gather(q_pooled, "pb", axis=0, tiled=True)
    block = s_inner_weight.shape[1]
    s_pooled_own = [s_pooled[:, :block]] + [
        swap(s_pooled[:, (i + 1) * block : (i + 2) * block], "pb", k) for i, k in enumerate(far)
    ]
    s_pooled_own = canonical(jnp.stack(s_pooled_own), p // group).reshape(n_pb, block)
    s_pooled_all = lax.all_gather(s_pooled_own, "sa", axis=0, tiled=True)

    half = q_inner_weight.shape[1] // 2
    q_inner_half = cut(q_inner_weight, pair_bit, half, 1)
    q_outer_half = cut(q_outer_f, pair_bit, half, 0)
    q_all_rows = jnp.concatenate(
        [q_rows] + [normalize(t, q_norm_gain, False) for t in pair_tokens], 0
    )
    q_pool_all = jnp.concatenate([q_pool_own, pick_rows(q_pool_pair, a, n_sa)], 0)
    q_slope = gelu_slope(jnp.dot(q_all_rows, q_inner_half, preferred_element_type=F32))
    q_slope = q_slope.reshape(2 * n_sa, length, half) * q_pool_all[:, :, None]
    s_slope = gelu_slope(s_pre) * s_pool_own[:, :, None]

    score = scale * lax.dot_general(q_embed, s_embed, (((1,), (1,)), ((), ())), precision=HIGH)
    count = score.shape[0]
    match = (positive[:, None] == jnp.arange(count, dtype=jnp.int32)[None, :]).astype(F32)
    row_max = jnp.max(score, axis=1, keepdims=True)
    col_max = jnp.max(score, axis=0, keepdims=True)
    row_lse = row_max + jnp.log(jnp.sum(jnp.exp(score - row_max), axis=1, keepdims=True))
    col_lse = col_max + jnp.log(jnp.sum(jnp.exp(score - col_max), axis=0, keepdims=True))
    matched = jnp.sum(match * score)
    loss = (jnp.sum(row_lse) + jnp.sum(col_lse) - 2.0 * matched) / (2.0 * count)
    dscore = 0.5 * (jnp.exp(score - row_lse) + jnp.exp(score - col_lse) - 2.0 * match)
    q_grad = scale * jnp.dot(dscore, s_embed, precision=HIGH)
    s_grad = scale * lax.dot_general(dscore, q_embed, (((0,), (0,)), ((), ())), precision=HIGH)

    def hidden(grad, outer):
        return lax.dot_general(grad, outer, (((1,), (1,)), ((), ())), precision=HIGH)

    q_hidden = hidden(
        jnp.concatenate(
            [
                pick_rows(cut(q_grad, p, n_sa), a, n_sa),
                pick_rows(cut(q_grad, p ^ 1, n_sa), a, n_sa),
            ],
            0,
        ),
        q_outer_half,
    )
    s_hidden = hidden(pick_rows(cut(s_grad, a, n_pb), p, group), s_outer_f)
    q_dpre = (q_slope * q_hidden[:, None, :]).astype(BF16).reshape(-1, half)
    s_dpre = (s_slope * s_hidden[:, None, :]).astype(BF16).reshape(group * length, -1)
    contract = (((0,), (0,)), ((), ()))
    q_inner_part = lax.dot_general(q_all_rows, q_dpre, contract, preferred_element_type=F32)
    s_inner_part = lax.dot_general(s_rows, s_dpre, contract, preferred_element_type=F32)

    gains = jnp.stack(
        [
            jnp.sum(q_inner_part * q_inner_half.astype(F32), axis=1) / q_norm_gain,
            jnp.sum(s_inner_part * s_inner_all.astype(F32), axis=1) / s_norm_gain,
        ]
    )
    for step in bits_of(n_sa):
        gains = gains + swap(gains, "sa", step)
    for step in bits_of(n_pb):
        gains = gains + swap(gains, "pb", step)

    pairs = n_pb // 2
    q_chunk = width // pairs
    mine = p // 2
    q_total = cut(q_inner_part, mine, q_chunk)
    q_half_part = q_inner_part.astype(BF16)
    for k in range(1, pairs):
        q_total = q_total + swap(cut(q_half_part, mine ^ k, q_chunk), "pb", 2 * k).astype(F32)
    q_total = q_total.astype(BF16)
    chunks = [q_total] + [swap(q_total, "pb", 2 * k) for k in range(1, pairs)]
    others = [swap(c, "pb", 1) for c in chunks]
    q_inner_grad = jnp.zeros((width, 2 * half), F32)
    for k in range(pairs):
        rows = ordered(chunks[k], others[k], pair_bit, 1).astype(F32)
        q_inner_grad = lax.dynamic_update_slice_in_dim(q_inner_grad, rows, (mine ^ k) * q_chunk, 0)

    s_total = s_inner_part
    for step in bits_of(n_sa):
        size = s_total.shape[0] // 2
        bit = bit_at(a, step)
        keep = cut(s_total, bit, size)
        s_total = keep + swap(cut(s_total, 1 - bit, size).astype(BF16), "sa", step).astype(F32)
    s_sum = s_total[:, :block]
    for i, k in enumerate(far):
        piece = s_total[:, (i + 1) * block : (i + 2) * block].astype(BF16)
        s_sum = s_sum + swap(piece, "pb", k).astype(F32)
    s_sum = s_sum.astype(BF16)
    for step in reversed(bits_of(n_sa)):
        s_sum = ordered(s_sum, swap(s_sum, "sa", step), bit_at(a, step))
    s_inner_grad = s_sum.astype(F32)

    q_outer_grad = lax.dot_general(q_pooled_all, q_grad, contract, precision=HIGH)
    s_outer_grad = lax.dot_general(s_pooled_all, s_grad, contract, precision=HIGH)
    return (loss, q_inner_grad, q_outer_grad, gains[0], s_inner_grad, s_outer_grad, gains[1])


def solution(mesh):
    placed = (
        P("pb", "sa", None, None),
        P("pb", None, None),
        P(None, "sa"),
        P("sa", None),
        P(),
        P("sa", "pb", None, None),
        P("sa", None, None),
        P(None, "pb"),
        P("pb", None),
        P(),
        P("pb"),
    )
    return jax.shard_map(
        per_device,
        mesh=mesh,
        in_specs=placed,
        out_specs=(P(), P(None, "sa"), P("sa", None), P(), P(None, "pb"), P("pb", None), P()),
        check_vma=False,
    )
```

time: 474 us -> 241 us (0.51)
  waiting for transfers between devices: 222 us -> 63 us
  blocking collectives: 175 us -> 49.7 us
  starting transfers between devices: 0.16 us -> 41.1 us
  other arithmetic: 18.5 us -> 35.7 us
  between operations: 16.8 us -> 5.47 us
    psum x2 -> x0, waiting for transfers between devices: 160 us -> none  [the longest x1 160 us: per_device(): lax.psum((inner_layer_grad, q_outer_part), 'pb')]
    psum x7 -> x0, blocking collectives: 152 us -> none  [the longest x2 52.4 us: per_device(): lax.psum((jnp.sum(jnp.exp(tile - col_top[None, :]), axis=0), jnp.sum(matc...]
    ppermute x0 -> x46, waiting for transfers between devices: none -> 63 us  [swap(): return lax.ppermute(x, axis, [(i, i ^ step) for i in range(size)])]
    all_gather x2 -> x0, waiting for transfers between devices: 59.9 us -> none  [the longest x1 41.2 us: per_device(): s_pooled = s_forward(lax.all_gather(sql_states, 'pb', axis=1, tiled=True))]
    ppermute x0 -> x46, starting transfers between devices: none -> 41.1 us  [swap(): return lax.ppermute(x, axis, [(i, i ^ step) for i in range(size)])]
    all_gather x0 -> x2, blocking collectives: none -> 37.6 us  [the longest x1 30.8 us: per_device(): q_pooled_all = lax.all_gather(q_pooled, 'pb', axis=0, tiled=True)]
    pmax x2 -> x0, blocking collectives: 22.8 us -> none  [the longest x1 17.1 us: per_device(): col_top = lax.pmax(jnp.max(tile, axis=0), 'pb')]
    unnamed x0 -> x1, blocking collectives: none -> 12.1 us
  transfers between devices with their start and end apart: 4 -> 46, of which waited for: 3 -> 17; matrix products, arithmetic and copies ran while one was open for 7% -> 28% of each run, Pallas kernels for 0% -> 0%
where the time goes in v1:
time: 241 us; the launch traced here: 240 us
  waiting for transfers between devices  63 us (26%)
  blocking collectives  49.7 us (21%)
  starting transfers between devices  41.1 us (17%)
  other arithmetic  35.7 us (15%)
  matrix products  32.4 us (13%)
  local copies, waits for them, and re-layouts  12.9 us (5%)
  between operations  5.47 us (2%)
    ppermute x46, waiting for transfers between devices, swap(): return lax.ppermute(x, axis, [(i, i ^ step) for i in range(size)])  63 us
    ppermute x46, starting transfers between devices, swap(): return lax.ppermute(x, axis, [(i, i ^ step) for i in range(size)])  41.1 us
    all_gather x1, blocking collectives, per_device(): q_pooled_all = lax.all_gather(q_pooled, 'pb', axis=0, tiled=True)  30.8 us
    unnamed x1, blocking collectives  12.1 us
    unnamed x8, other arithmetic  8.52 us
    all_gather x1, blocking collectives, per_device(): s_pooled_all = lax.all_gather(s_pooled_own, 'sa', axis=0, tiled=True)  6.83 us
    dot_general x1, matrix products, per_device(): lax.dot_general(q_all_rows, q_dpre, contract, preferred_element_type=F32)  4.92 us
  transfers between devices with their start and end apart: 46, of which 17 were waited for; matrix products, arithmetic and copies ran while one was open for 28% of the time, Pallas kernels for 0%

profile of v1, /device:TPU:0, one launch (start us, length us, event | category | flops | bytes accessed | tf_op | source)
XLA Modules:
  0.0 240.2 jit_solution(9731250159718862819)
XLA Ops:
  0.7 4.0 %collective-permute-start.10 = (bf16[256,768]{1,0:T(8,128)(2,1)}, bf16[256,768]{1,0:T(8,128)(2,1)S(1)}, u32[]{:S(2)}, u32[]{:S(2)}) collective-permute-start(bf16[256,768]{1,0:T(8,128)(2,1)} %bitcast.59), channel_id=1, source_target_pairs={{0,12},{4,8},{8,4},{12,0},{16,28},{20,24},{24,20},{28,16},{1,13},{... | collective-permute-start | bytes 1179656 | tf_op jit(solution)/shard_map/ppermute | solution.py:40
  6.2 1.8 collective-permute-start.24
  9.5 1.8 fusion.77
  11.9 1.8 fusion.73
  13.7 1.2 fusion.40
  14.9 1.7 constant_dynamic-slice_fusion.24
  16.6 1.7 constant_dynamic-slice_fusion.19
  20.1 1.1 constant_dynamic-update-slice_fusion.3
  23.4 12.1 %all-reduce = s32[32]{0:T(128)} all-reduce(s32[32]{0:T(128)S(1)} %dynamic-update-slice), channel_id=1, replica_groups=mesh['pb'=8,'sa'=4] {'pb'}, use_global_device_ids=true, to_apply=%add | all-reduce | flops 32 | bytes 256
  35.5 1.6 collective-permute-start.1
  37.1 1.4 constant_dynamic-slice_fusion.15
  40.5 2.6 %collective-permute-start.13 = (bf16[192,768]{1,0:T(8,128)(2,1)}, bf16[192,768]{1,0:T(8,128)(2,1)}, u32[]{:S(2)}, u32[]{:S(2)}) collective-permute-start(bf16[192,768]{1,0:T(8,128)(2,1)} %constant_dynamic-slice_fusion.19), channel_id=1, source_target_pairs={{0,16},{4,20},{8,24},{12,28},{16,0},{20,4},{24,8},{28,12},{1,17},{... | collective-permute-start | bytes 884744 | tf_op jit(solution)/shard_map/ppermute | solution.py:40
  43.3 16.3 %collective-permute-done.11 = bf16[384,384]{1,0:T(8,128)(2,1)S(1)} collective-permute-done((bf16[384,384]{1,0:T(8,128)(2,1)}, bf16[384,384]{1,0:T(8,128)(2,1)S(1)}, u32[]{:S(2)}, u32[]{:S(2)}) %collective-permute-start.11) | collective-permute-done | bytes 294944 | tf_op jit(solution)/shard_map/ppermute | solution.py:40
  60.2 5.8 %collective-permute-done.13 = bf16[192,768]{1,0:T(8,128)(2,1)} collective-permute-done((bf16[192,768]{1,0:T(8,128)(2,1)}, bf16[192,768]{1,0:T(8,128)(2,1)}, u32[]{:S(2)}, u32[]{:S(2)}) %collective-permute-start.13) | collective-permute-done | bytes 294944 | tf_op jit(solution)/shard_map/ppermute | solution.py:40
  68.1 2.5 %collective-permute-done.20 = bf16[256,768]{1,0:T(8,128)(2,1)S(1)} collective-permute-done((bf16[256,768]{1,0:T(8,128)(2,1)S(1)}, bf16[256,768]{1,0:T(8,128)(2,1)S(1)}, u32[]{:S(2)}, u32[]{:S(2)}) %collective-permute-start.20) | collective-permute-done | bytes 393248 | tf_op jit(solution)/shard_map/ppermute | solution.py:40
  72.6 1.1 constant_dynamic-update-slice_fusion.2
  73.8 1.6 fusion.76
  75.7 3.2 %multiply_reduce_fusion = (f32[4,768]{1,0:T(4,128)S(1)}, f32[1024,768]{1,0:T(8,128)}) fusion(f32[4,256]{1,0:T(4,128)S(1)} %copy-done.31, bf16[768,384]{1,0:T(8,128)(2,1)S(1)} %maximum_select_fusion, bf16[768,384]{1,0:T(8,128)(2,1)S(1)} %copy-done.19, bf16[256,768]{1,0:T(8,128)(2,1)S(1)} %get-tuple-element.66, bf16[256,768]{1,0:T(8,128)(2,1)S(1)} %get-tuple-element.65, ...), kind=kOutput, calls=%fused_computation.16 | convolution fusion | flops 1221325824 | bytes 5914624 | tf_op jit(solution)/shard_map/dot_general | solution.py:132
  79.2 1.4 maximum_select_fusion.1
  80.7 1.9 convolution_add_fusion
  83.1 3.2 %collective-permute-done.15 = f32[4,768]{1,0:T(4,128)S(1)} collective-permute-done((f32[4,768]{1,0:T(4,128)S(1)}, f32[4,768]{1,0:T(4,128)S(1)}, u32[]{:S(2)}, u32[]{:S(2)}) %collective-permute-start.15) | collective-permute-done | bytes 12320 | tf_op jit(solution)/shard_map/ppermute | solution.py:40
  86.3 1.8 constant_dynamic-update-slice_fusion.1
  88.1 1.9 collective-permute-done.16
  90.0 4.6 %collective-permute-done.17 = f32[4,768]{1,0:T(4,128)S(1)} collective-permute-done((f32[4,768]{1,0:T(4,128)S(1)}, f32[4,768]{1,0:T(4,128)S(1)}, u32[]{:S(2)}, u32[]{:S(2)}) %collective-permute-start.17) | collective-permute-done | bytes 12320 | tf_op jit(solution)/shard_map/ppermute | solution.py:40
  95.8 6.8 %all_gather.11 = f32[32,384]{1,0:T(8,128)} all-gather(f32[8,384]{1,0:T(8,128)} %reshape_reshape.11), channel_id=1, replica_groups=mesh['pb'=8,'sa'=4] {'sa'}, dimensions={0}, use_global_device_ids=true | all-gather | bytes 61440 | tf_op jit(solution)/shard_map/all_gather | solution.py:175
  102.6 1.4 maximum_select_fusion.13
  106.2 3.2 %multiply_reduce_fusion.1 = f32[4,768]{1,0:T(4,128)S(1)} fusion(f32[4,256]{1,0:T(4,128)} %pad_maximum_fusion.10, bf16[768,768]{1,0:T(8,128)(2,1)} %param.13, bf16[256,768]{1,0:T(8,128)(2,1)S(1)} %get-tuple-element.19, bf16[256,768]{1,0:T(8,128)(2,1)} %get-tuple-element.21, bf16[256,768]{1,0:T(8,128)(2,1)} %get-tuple-element.23, ...), kind=kOutput, calls=%fused_computation.19 | convolution fusion | flops 1218966528 | bytes 2768896 | tf_op jit(solution)/shard_map/dot_general | solution.py:125
  110.4 1.3 collective-permute-start.3
  112.5 1.6 collective-permute-done.3
  114.7 3.1 %collective-permute-done.4 = f32[4,768]{1,0:T(4,128)S(1)} collective-permute-done((f32[4,768]{1,0:T(4,128)S(1)}, f32[4,768]{1,0:T(4,128)S(1)}, u32[]{:S(2)}, u32[]{:S(2)}) %collective-permute-start.4) | collective-permute-done | bytes 12320 | tf_op jit(solution)/shard_map/ppermute | solution.py:40
  118.1 1.0 fusion.85
  119.1 2.6 %collective-permute-done.5 = f32[8,768]{1,0:T(8,128)S(1)} collective-permute-done((f32[8,768]{1,0:T(8,128)S(1)}, f32[8,768]{1,0:T(8,128)S(1)}, u32[]{:S(2)}, u32[]{:S(2)}) %collective-permute-start.5) | collective-permute-done | bytes 24608 | tf_op jit(solution)/shard_map/ppermute | solution.py:40
  121.7 1.0 fusion.86
  122.7 4.4 %collective-permute-done.6 = f32[16,768]{1,0:T(8,128)S(1)} collective-permute-done((f32[16,768]{1,0:T(8,128)S(1)}, f32[16,768]{1,0:T(8,128)S(1)}, u32[]{:S(2)}, u32[]{:S(2)}) %collective-permute-start.6) | collective-permute-done | bytes 49184 | tf_op jit(solution)/shard_map/ppermute | solution.py:40
  127.2 1.0 fusion.87
  128.5 1.3 fusion.114
  131.5 2.3 fusion.79
  133.9 1.8 fusion.13
  135.8 2.9 %multiply_reduce_fusion.2 = (f32[768]{0:T(1024)S(1)}, f32[768,768]{1,0:T(8,128)}) fusion(bf16[768,384]{1,0:T(8,128)(2,1)S(1)} %copy-done.4, bf16[768,384]{1,0:T(8,128)(2,1)S(1)} %copy-done.20, bf16[1024,768]{1,0:T(8,128)(2,1)S(1)} %fusion.13, bf16[256,768]{1,0:T(8,128)(2,1)S(1)} %copy-done.13, bf16[256,768]{1,0:T(8,128)(2,1)S(1)} %copy-done.11, ...), kind=kOutput, calls=%fused_computation.21 | convolution fusion | flops 1217789184 | bytes 6687744 | tf_op jit(solution)/shard_map/dot_general | solution.py:219
  138.7 1.3 convolution_multiply_fusion.1
  141.2 1.0 fusion.88
  142.2 4.3 %fusion.6 = bf16[2048,384]{1,0:T(8,128)(2,1)S(1)} fusion(f32[8,384]{1,0:T(8,128)S(1)} %fusion.81, f32[2048]{0:T(1024)S(1)} %bitcast.62, bf16[2048,768]{1,0:T(8,128)(2,1)} %fusion.88, bf16[768,768]{1,0:T(8,128)(2,1)S(1)} %copy-done.24, s32[]{:T(128)S(6)} %select_n.325), kind=kOutput, calls=%fused_computation.8 | convolution fusion | flops 1216610304 | bytes 5328900 | tf_op jit(solution)/shard_map/dot_general | solution.py:184
  146.4 4.9 %multiply_reduce_fusion.3 = (f32[768]{0:T(1024)S(1)}, bf16[768,384]{1,0:T(8,128)(2,1)}, f32[768,384]{1,0:T(8,128)}) fusion(bf16[768,768]{1,0:T(8,128)(2,1)S(1)} %copy-done.24, s32[]{:T(128)S(6)} %select_n.325, bf16[2048,768]{1,0:T(8,128)(2,1)} %fusion.88, bf16[2048,384]{1,0:T(8,128)(2,1)S(1)} %fusion.6), kind=kOutput, calls=%fused_computation.41 | convolution fusion | flops 1209138432 | bytes 7080964 | tf_op jit(solution)/shard_map/dot_general | solution.py:218
  151.7 1.3 dynamic-slice_convert_fusion
  153.4 1.3 collective-permute-start.36
  154.7 30.8 %all-gather = f32[8,4,768]{2,1,0:T(4,128)S(1)} all-gather(f32[1,4,768]{2,1,0:T(4,128)S(1)} %reshape.236), channel_id=1, replica_groups=mesh['pb'=8,'sa'=4] {'pb'}, dimensions={0}, use_global_device_ids=true | all-gather | bytes 110592 | tf_op jit(solution)/shard_map/all_gather | solution.py:169
  185.6 3.5 %fusion.121 = f32[768,768]{1,0:T(8,128)} fusion(f32[32,768]{1,0:T(8,128)S(1)} %reshape.237, f32[32,768]{1,0:T(8,128)S(1)} %convolution_multiply_fusion.1), kind=kOutput, calls=%fused_computation.263 | convolution fusion | flops 226492416 | bytes 2555904 | tf_op jit(solution)/shard_map/dot_general | solution.py:262
  189.3 1.6 convert_add_fusion
  191.7 2.1 fusion.122
  195.8 1.4 collective-permute-start.39
  197.2 1.1 constant_dynamic-slice_fusion.6
  199.1 2.9 %collective-permute-start.26 = (bf16[192,384]{1,0:T(8,128)(2,1)S(1)}, bf16[192,384]{1,0:T(8,128)(2,1)S(1)}, u32[]{:S(2)}, u32[]{:S(2)}) collective-permute-start(bf16[192,384]{1,0:T(8,128)(2,1)S(1)} %get-tuple-element.38), channel_id=1, source_target_pairs={{0,16},{4,20},{8,24},{12,28},{16,0},{20,4},{24,8},{28,12},{1,17},{... | collective-permute-start | bytes 442376 | tf_op jit(solution)/shard_map/ppermute | solution.py:40
  203.7 1.1 collective-permute-done.25
  204.9 6.7 %collective-permute-done.26 = bf16[192,384]{1,0:T(8,128)(2,1)S(1)} collective-permute-done((bf16[192,384]{1,0:T(8,128)(2,1)S(1)}, bf16[192,384]{1,0:T(8,128)(2,1)S(1)}, u32[]{:S(2)}, u32[]{:S(2)}) %collective-permute-start.26) | collective-permute-done | bytes 147488 | tf_op jit(solution)/shard_map/ppermute | solution.py:40
  211.6 1.0 add_convert_fusion
  213.0 8.3 %collective-permute-start.29 = (bf16[192,384]{1,0:T(8,128)(2,1)S(1)}, bf16[192,384]{1,0:T(8,128)(2,1)S(1)}, u32[]{:S(2)}, u32[]{:S(2)}) collective-permute-start(bf16[192,384]{1,0:T(8,128)(2,1)S(1)} %add_convert_fusion), channel_id=1, source_target_pairs={{0,8},{4,12},{8,0},{12,4},{16,24},{20,28},{24,16},{28,20},{1,9},{5... | collective-permute-start | bytes 442376 | tf_op jit(solution)/shard_map/ppermute | solution.py:40
  221.3 1.2 collective-permute-start.31
  222.5 1.5 collective-permute-start.33
  224.0 1.3 collective-permute-start.43
  226.0 4.5 %collective-permute-done.31 = bf16[192,384]{1,0:T(8,128)(2,1)S(1)} collective-permute-done((bf16[192,384]{1,0:T(8,128)(2,1)S(1)}, bf16[192,384]{1,0:T(8,128)(2,1)S(1)}, u32[]{:S(2)}, u32[]{:S(2)}) %collective-permute-start.31) | collective-permute-done | bytes 147488 | tf_op jit(solution)/shard_map/ppermute | solution.py:40
  230.8 1.7 collective-permute-start.34
  233.1 2.6 %collective-permute-done.32 = bf16[192,384]{1,0:T(8,128)(2,1)S(1)} collective-permute-done((bf16[192,384]{1,0:T(8,128)(2,1)S(1)}, bf16[192,384]{1,0:T(8,128)(2,1)S(1)}, u32[]{:S(2)}, u32[]{:S(2)}) %collective-permute-start.32) | collective-permute-done | bytes 147488 | tf_op jit(solution)/shard_map/ppermute | solution.py:40
  235.7 1.5 collective-permute-done.34
  237.3 1.3 fusion.80
  (260 shorter events, 30.5 us)
Async XLA Ops:
  0.6 109.1 %copy-start = (bf16[768,768]{1,0:T(8,128)(2,1)S(1)}, bf16[768,768]{1,0:T(8,128)(2,1)}, u32[]{:S(2)}) copy-start(bf16[768,768]{1,0:T(8,128)(2,1)} %param.14) | copy-start | bytes 3538948
  0.6 21.2 %copy-start.43 = (u32[32]{0:T(128)S(1)}, u32[32]{0:T(128)}, u32[]{:S(2)}) copy-start(u32[32]{0:T(128)} %constant.299) | copy-start | bytes 388
  0.7 19.5 %copy-start.2 = (bf16[1,1,256,768]{3,2,1,0:T(8,128)(2,1)S(1)}, bf16[1,1,256,768]{3,2,1,0:T(8,128)(2,1)}, u32[]{:S(2)}) copy-start(bf16[1,1,256,768]{3,2,1,0:T(8,128)(2,1)} %param.11) | copy-start | bytes 1179652
  0.7 19.5 %copy-start.23 = (f32[768]{0:T(1024)S(1)}, f32[768]{0:T(1024)}, u32[]{:S(2)}) copy-start(f32[768]{0:T(1024)} %param.15) | copy-start | bytes 9220
  0.7 22.5 %copy-start.42 = (s32[4]{0:T(128)S(1)}, s32[4]{0:T(128)}, u32[]{:S(2)}) copy-start(s32[4]{0:T(128)} %param.21) | copy-start | bytes 52
  0.7 39.2 %collective-permute-start.10 = (bf16[256,768]{1,0:T(8,128)(2,1)}, bf16[256,768]{1,0:T(8,128)(2,1)S(1)}, u32[]{:S(2)}, u32[]{:S(2)}) collective-permute-start(bf16[256,768]{1,0:T(8,128)(2,1)} %bitcast.59), channel_id=1, source_target_pairs={{0,12},{4,8},{8,4},{12,0},{16,28},{20,24},{24,20},{28,16},{1,13},{... | collective-permute-start | bytes 1179656 | tf_op jit(solution)/shard_map/ppermute | solution.py:40
  4.7 35.8 %collective-permute-start.9 = (bf16[256,768]{1,0:T(8,128)(2,1)}, bf16[256,768]{1,0:T(8,128)(2,1)S(1)}, u32[]{:S(2)}, u32[]{:S(2)}) collective-permute-start(bf16[256,768]{1,0:T(8,128)(2,1)} %bitcast.60), channel_id=1, source_target_pairs={{0,8},{4,12},{8,0},{12,4},{16,24},{20,28},{24,16},{28,20},{1,9},{5... | collective-permute-start | bytes 1179656 | tf_op jit(solution)/shard_map/ppermute | solution.py:40
  5.2 60.9 %collective-permute-start.8 = (bf16[256,768]{1,0:T(8,128)(2,1)}, bf16[256,768]{1,0:T(8,128)(2,1)S(1)}, u32[]{:S(2)}, u32[]{:S(2)}) collective-permute-start(bf16[256,768]{1,0:T(8,128)(2,1)} %bitcast.61), channel_id=1, source_target_pairs={{0,4},{4,0},{8,12},{12,8},{16,20},{20,16},{24,28},{28,24},{1,5},{5... | collective-permute-start | bytes 1179656 | tf_op jit(solution)/shard_map/ppermute | solution.py:40
  5.4 61.3 %collective-permute-start = (bf16[256,768]{1,0:T(8,128)(2,1)}, bf16[256,768]{1,0:T(8,128)(2,1)S(1)}, u32[]{:S(2)}, u32[]{:S(2)}) collective-permute-start(bf16[256,768]{1,0:T(8,128)(2,1)} %bitcast.56), channel_id=1, source_target_pairs={{0,1},{1,0},{2,3},{3,2},{4,5},{5,4},{6,7},{7,6},{8,9},{9,8},{10,11... | collective-permute-start | bytes 1179656 | tf_op jit(solution)/shard_map/ppermute | solution.py:40
  6.2 29.3 %collective-permute-start.24 = (f32[4,256]{1,0:T(4,128)S(1)}, f32[4,256]{1,0:T(4,128)}, u32[]{:S(2)}, u32[]{:S(2)}) collective-permute-start(f32[4,256]{1,0:T(4,128)S(1)} %fusion.103), channel_id=1, source_target_pairs={{0,4},{4,0},{8,12},{12,8},{16,20},{20,16},{24,28},{28,24},{1,5},{5... | collective-permute-start | bytes 12296 | tf_op jit(solution)/shard_map/ppermute | solution.py:40
  11.9 23.7 %copy-start.35 = (f32[1,256]{1,0:T(1,128)}, f32[1,256]{1,0:T(1,128)S(1)}, u32[]{:S(2)}) copy-start(f32[1,256]{1,0:T(1,128)S(1)} %get-tuple-element.68) | copy-start | bytes 3076
  11.9 23.7 %copy-start.36 = (f32[1,256]{1,0:T(1,128)}, f32[1,256]{1,0:T(1,128)S(1)}, u32[]{:S(2)}) copy-start(f32[1,256]{1,0:T(1,128)S(1)} %get-tuple-element.69) | copy-start | bytes 3076
  11.9 23.7 %copy-start.37 = (f32[1,256]{1,0:T(1,128)}, f32[1,256]{1,0:T(1,128)S(1)}, u32[]{:S(2)}) copy-start(f32[1,256]{1,0:T(1,128)S(1)} %get-tuple-element.70) | copy-start | bytes 3076
  35.5 31.6 %collective-permute-start.1 = (bf16[256,768]{1,0:T(8,128)(2,1)S(1)}, bf16[256,768]{1,0:T(8,128)(2,1)S(1)}, u32[]{:S(2)}, u32[]{:S(2)}) collective-permute-start(bf16[256,768]{1,0:T(8,128)(2,1)S(1)} %bitcast.57), channel_id=1, source_target_pairs={{0,2},{1,3},{2,0},{3,1},{4,6},{5,7},{6,4},{7,5},{8,10},{9,11},{10,... | collective-permute-start | bytes 1179656 | tf_op jit(solution)/shard_map/ppermute | solution.py:40
  39.9 33.9 %copy-start.14 = (bf16[1,1,256,768]{3,2,1,0:T(8,128)(2,1)S(1)}, bf16[1,1,256,768]{3,2,1,0:T(8,128)(2,1)}, u32[]{:S(2)}) copy-start(bf16[1,1,256,768]{3,2,1,0:T(8,128)(2,1)} %param.16) | copy-start | bytes 1179652
  39.9 33.9 %copy-start.28 = (f32[768]{0:T(1024)S(1)}, f32[768]{0:T(1024)}, u32[]{:S(2)}) copy-start(f32[768]{0:T(1024)} %param.20) | copy-start | bytes 9220
  39.9 33.9 %copy-start.38 = (f32[256]{0:T(256)S(1)}, f32[256]{0:T(256)}, u32[]{:S(2)}) copy-start(f32[256]{0:T(256)} %add_rsqrt_fusion.7) | copy-start | bytes 3076
  39.9 19.8 %collective-permute-start.11 = (bf16[384,384]{1,0:T(8,128)(2,1)}, bf16[384,384]{1,0:T(8,128)(2,1)S(1)}, u32[]{:S(2)}, u32[]{:S(2)}) collective-permute-start(bf16[384,384]{1,0:T(8,128)(2,1)} %constant_dynamic-slice_fusion.24), channel_id=1, source_target_pairs={{0,16},{4,20},{8,24},{12,28},{16,0},{20,4},{24,8},{28,12},{1,17},{... | collective-permute-start | bytes 884744 | tf_op jit(solution)/shard_map/ppermute | solution.py:40
  40.5 31.1 %copy-start.17 = (bf16[256,768]{1,0:T(8,128)(2,1)}, bf16[256,768]{1,0:T(8,128)(2,1)S(1)}, u32[]{:S(2)}) copy-start(bf16[256,768]{1,0:T(8,128)(2,1)S(1)} %collective-permute-done.9) | copy-start | bytes 1179652
  40.5 25.5 %collective-permute-start.13 = (bf16[192,768]{1,0:T(8,128)(2,1)}, bf16[192,768]{1,0:T(8,128)(2,1)}, u32[]{:S(2)}, u32[]{:S(2)}) collective-permute-start(bf16[192,768]{1,0:T(8,128)(2,1)} %constant_dynamic-slice_fusion.19), channel_id=1, source_target_pairs={{0,16},{4,20},{8,24},{12,28},{16,0},{20,4},{24,8},{28,12},{1,17},{... | collective-permute-start | bytes 884744 | tf_op jit(solution)/shard_map/ppermute | solution.py:40
  59.7 14.1 %copy-start.16 = (bf16[256,768]{1,0:T(8,128)(2,1)S(1)}, bf16[256,768]{1,0:T(8,128)(2,1)}, u32[]{:S(2)}) copy-start(bf16[256,768]{1,0:T(8,128)(2,1)} %copy-done.15) | copy-start | bytes 1179652
  59.7 10.9 %collective-permute-start.20 = (bf16[256,768]{1,0:T(8,128)(2,1)S(1)}, bf16[256,768]{1,0:T(8,128)(2,1)S(1)}, u32[]{:S(2)}, u32[]{:S(2)}) collective-permute-start(bf16[256,768]{1,0:T(8,128)(2,1)S(1)} %bitcast.58), channel_id=1, source_target_pairs={{0,4},{4,0},{8,12},{12,8},{16,20},{20,16},{24,28},{28,24},{1,5},{5... | collective-permute-start | bytes 1179656 | tf_op jit(solution)/shard_map/ppermute | solution.py:40
  66.0 9.4 %collective-permute-start.12 = (bf16[384,384]{1,0:T(8,128)(2,1)S(1)}, bf16[384,384]{1,0:T(8,128)(2,1)S(1)}, u32[]{:S(2)}, u32[]{:S(2)}) collective-permute-start(bf16[384,384]{1,0:T(8,128)(2,1)S(1)} %collective-permute-done.11), channel_id=1, source_target_pairs={{0,1},{1,0},{2,3},{3,2},{4,5},{5,4},{6,7},{7,6},{8,9},{9,8},{10,11... | collective-permute-start | bytes 884744 | tf_op jit(solution)/shard_map/ppermute | solution.py:40
  66.0 13.2 %collective-permute-start.14 = (bf16[192,768]{1,0:T(8,128)(2,1)}, bf16[192,768]{1,0:T(8,128)(2,1)}, u32[]{:S(2)}, u32[]{:S(2)}) collective-permute-start(bf16[192,768]{1,0:T(8,128)(2,1)} %collective-permute-done.13), channel_id=1, source_target_pairs={{0,1},{1,0},{2,3},{3,2},{4,5},{5,4},{6,7},{7,6},{8,9},{9,8},{10,11... | collective-permute-start | bytes 884744 | tf_op jit(solution)/shard_map/ppermute | solution.py:40
  71.6 33.2 %collective-permute-start.2 = (bf16[256,768]{1,0:T(8,128)(2,1)S(1)}, bf16[256,768]{1,0:T(8,128)(2,1)S(1)}, u32[]{:S(2)}, u32[]{:S(2)}) collective-permute-start(bf16[256,768]{1,0:T(8,128)(2,1)S(1)} %collective-permute-done.1), channel_id=1, source_target_pairs={{0,1},{1,0},{2,3},{3,2},{4,5},{5,4},{6,7},{7,6},{8,9},{9,8},{10,11... | collective-permute-start | bytes 1179656 | tf_op jit(solution)/shard_map/ppermute | solution.py:40
  71.6 40.1 %collective-permute-start.21 = (bf16[256,768]{1,0:T(8,128)(2,1)S(1)}, bf16[256,768]{1,0:T(8,128)(2,1)S(1)}, u32[]{:S(2)}, u32[]{:S(2)}) collective-permute-start(bf16[256,768]{1,0:T(8,128)(2,1)S(1)} %collective-permute-done.20), channel_id=1, source_target_pairs={{0,1},{1,0},{2,3},{3,2},{4,5},{5,4},{6,7},{7,6},{8,9},{9,8},{10,11... | collective-permute-start | bytes 1179656 | tf_op jit(solution)/shard_map/ppermute | solution.py:40
  72.1 40.0 %collective-permute-start.22 = (bf16[256,768]{1,0:T(8,128)(2,1)S(1)}, bf16[256,768]{1,0:T(8,128)(2,1)S(1)}, u32[]{:S(2)}, u32[]{:S(2)}) collective-permute-start(bf16[256,768]{1,0:T(8,128)(2,1)S(1)} %collective-permute-done.20), channel_id=1, source_target_pairs={{0,2},{1,3},{2,0},{3,1},{4,6},{5,7},{6,4},{7,5},{8,10},{9,11},{10,... | collective-permute-start | bytes 1179656 | tf_op jit(solution)/shard_map/ppermute | solution.py:40
  80.7 25.6 %copy-start.22 = (bf16[256,768]{1,0:T(8,128)(2,1)S(1)}, bf16[256,768]{1,0:T(8,128)(2,1)}, u32[]{:S(2)}) copy-start(bf16[256,768]{1,0:T(8,128)(2,1)} %get-tuple-element.25) | copy-start | bytes 1179652
  82.5 3.7 %collective-permute-start.15 = (f32[4,768]{1,0:T(4,128)S(1)}, f32[4,768]{1,0:T(4,128)S(1)}, u32[]{:S(2)}, u32[]{:S(2)}) collective-permute-start(f32[4,768]{1,0:T(4,128)S(1)} %convolution_add_fusion), channel_id=1, source_target_pairs={{0,4},{4,0},{8,12},{12,8},{16,20},{20,16},{24,28},{28,24},{1,5},{5... | collective-permute-start | bytes 36872 | tf_op jit(solution)/shard_map/ppermute | solution.py:40
  83.1 6.9 %collective-permute-start.45 = (f32[4,384]{1,0:T(4,128)S(1)}, f32[4,384]{1,0:T(4,128)S(1)}, u32[]{:S(2)}, u32[]{:S(2)}) collective-permute-start(f32[4,384]{1,0:T(4,128)S(1)} %get-tuple-element.52), channel_id=1, source_target_pairs={{0,16},{4,20},{8,24},{12,28},{16,0},{20,4},{24,8},{28,12},{1,17},{... | collective-permute-start | bytes 18440 | tf_op jit(solution)/shard_map/ppermute | solution.py:40
  86.3 3.7 %collective-permute-start.16 = (f32[4,768]{1,0:T(4,128)S(1)}, f32[4,768]{1,0:T(4,128)S(1)}, u32[]{:S(2)}, u32[]{:S(2)}) collective-permute-start(f32[4,768]{1,0:T(4,128)S(1)} %add.341), channel_id=1, source_target_pairs={{0,8},{4,12},{8,0},{12,4},{16,24},{20,28},{24,16},{28,20},{1,9},{5... | collective-permute-start | bytes 36872 | tf_op jit(solution)/shard_map/ppermute | solution.py:40
  90.0 4.6 %collective-permute-start.17 = (f32[4,768]{1,0:T(4,128)S(1)}, f32[4,768]{1,0:T(4,128)S(1)}, u32[]{:S(2)}, u32[]{:S(2)}) collective-permute-start(f32[4,768]{1,0:T(4,128)S(1)} %add.342), channel_id=1, source_target_pairs={{0,16},{4,20},{8,24},{12,28},{16,0},{20,4},{24,8},{28,12},{1,17},{... | collective-permute-start | bytes 36872 | tf_op jit(solution)/shard_map/ppermute | solution.py:40
  95.2 7.5 %collective-permute-start.18 = (f32[8,768]{1,0:T(8,128)}, f32[8,768]{1,0:T(8,128)}, u32[]{:S(2)}, u32[]{:S(2)}) collective-permute-start(f32[8,768]{1,0:T(8,128)} %maximum_select_fusion.15), channel_id=1, source_target_pairs={{0,1},{1,0},{2,3},{3,2},{4,5},{5,4},{6,7},{7,6},{8,9},{9,8},{10,11... | collective-permute-start | bytes 73736 | tf_op jit(solution)/shard_map/ppermute | solution.py:40
  104.1 24.4 %collective-permute-start.19 = (f32[16,768]{1,0:T(8,128)}, f32[16,768]{1,0:T(8,128)}, u32[]{:S(2)}, u32[]{:S(2)}) collective-permute-start(f32[16,768]{1,0:T(8,128)} %maximum_select_fusion.13), channel_id=1, source_target_pairs={{0,2},{1,3},{2,0},{3,1},{4,6},{5,7},{6,4},{7,5},{8,10},{9,11},{10,... | collective-permute-start | bytes 147464 | tf_op jit(solution)/shard_map/ppermute | solution.py:40
  109.4 8.6 %copy-start.33 = (f32[256]{0:T(256)S(1)}, f32[256]{0:T(256)}, u32[]{:S(2)}) copy-start(f32[256]{0:T(256)} %copy-done.32) | copy-start | bytes 3076
  110.3 19.4 %copy-start.40 = (s32[32]{0:T(128)S(1)}, s32[32]{0:T(128)}, u32[]{:S(2)}) copy-start(s32[32]{0:T(128)} %all-reduce) | copy-start | bytes 388
  110.4 3.7 %collective-permute-start.3 = (f32[4,768]{1,0:T(4,128)S(1)}, f32[4,768]{1,0:T(4,128)S(1)}, u32[]{:S(2)}, u32[]{:S(2)}) collective-permute-start(f32[4,768]{1,0:T(4,128)S(1)} %convolution_add_fusion.1), channel_id=1, source_target_pairs={{0,2},{1,3},{2,0},{3,1},{4,6},{5,7},{6,4},{7,5},{8,10},{9,11},{10,... | collective-permute-start | bytes 36872 | tf_op jit(solution)/shard_map/ppermute | solution.py:40
  114.1 3.7 %collective-permute-start.4 = (f32[4,768]{1,0:T(4,128)S(1)}, f32[4,768]{1,0:T(4,128)S(1)}, u32[]{:S(2)}, u32[]{:S(2)}) collective-permute-start(f32[4,768]{1,0:T(4,128)S(1)} %add.326), channel_id=1, source_target_pairs={{0,4},{4,0},{8,12},{12,8},{16,20},{20,16},{24,28},{28,24},{1,5},{5... | collective-permute-start | bytes 36872 | tf_op jit(solution)/shard_map/ppermute | solution.py:40
  114.7 26.1 %collective-permute-start.23 = (bf16[256,768]{1,0:T(8,128)(2,1)S(1)}, bf16[256,768]{1,0:T(8,128)(2,1)S(1)}, u32[]{:S(2)}, u32[]{:S(2)}) collective-permute-start(bf16[256,768]{1,0:T(8,128)(2,1)S(1)} %collective-permute-done.22), channel_id=1, source_target_pairs={{0,1},{1,0},{2,3},{3,2},{4,5},{5,4},{6,7},{7,6},{8,9},{9,8},{10,11... | collective-permute-start | bytes 1179656 | tf_op jit(solution)/shard_map/ppermute | solution.py:40
  117.8 3.9 %collective-permute-start.5 = (f32[8,768]{1,0:T(8,128)S(1)}, f32[8,768]{1,0:T(8,128)S(1)}, u32[]{:S(2)}, u32[]{:S(2)}) collective-permute-start(f32[8,768]{1,0:T(8,128)S(1)} %maximum_select_fusion.14), channel_id=1, source_target_pairs={{0,8},{4,12},{8,0},{12,4},{16,24},{20,28},{24,16},{28,20},{1,9},{5... | collective-permute-start | bytes 73736 | tf_op jit(solution)/shard_map/ppermute | solution.py:40
  119.0 14.7 %copy-start.1 = (f32[1024,768]{1,0:T(8,128)S(1)}, f32[1024,768]{1,0:T(8,128)}, u32[]{:S(2)}) copy-start(f32[1024,768]{1,0:T(8,128)} %get-tuple-element.72) | copy-start | bytes 9437188
  119.1 14.7 %copy-start.30 = (f32[1,2,4,128]{3,1,2,0:T(2,128)S(1)}, f32[1,2,4,128]{3,1,2,0:T(2,128)}, u32[]{:S(2)}) copy-start(f32[1,2,4,128]{3,1,2,0:T(2,128)} %copy.19) | copy-start | bytes 12292
  121.7 5.4 %collective-permute-start.6 = (f32[16,768]{1,0:T(8,128)S(1)}, f32[16,768]{1,0:T(8,128)S(1)}, u32[]{:S(2)}, u32[]{:S(2)}) collective-permute-start(f32[16,768]{1,0:T(8,128)S(1)} %maximum_select_fusion.12), channel_id=1, source_target_pairs={{0,16},{4,20},{8,24},{12,28},{16,0},{20,4},{24,8},{28,12},{1,17},{... | collective-permute-start | bytes 147464 | tf_op jit(solution)/shard_map/ppermute | solution.py:40
  127.1 1.4 collective-permute-start.7
  151.4 2.0 collective-permute-start.35
  153.0 36.3 %collective-permute-start.40 = (bf16[384,768]{1,0:T(8,128)(2,1)S(1)}, bf16[384,768]{1,0:T(8,128)(2,1)}, u32[]{:S(2)}, u32[]{:S(2)}) collective-permute-start(bf16[384,768]{1,0:T(8,128)(2,1)S(1)} %dynamic-slice_convert_fusion), channel_id=1, source_target_pairs={{0,1},{1,0},{2,3},{3,2},{4,5},{5,4},{6,7},{7,6},{8,9},{9,8},{10,11... | collective-permute-start | bytes 1769480 | tf_op jit(solution)/shard_map/ppermute | solution.py:40
  153.4 32.2 %collective-permute-start.36 = (f32[2,768]{1,0:T(2,128)S(1)}, f32[2,768]{1,0:T(2,128)S(1)}, u32[]{:S(2)}, u32[]{:S(2)}) collective-permute-start(f32[2,768]{1,0:T(2,128)S(1)} %fusion.113), channel_id=1, source_target_pairs={{0,2},{1,3},{2,0},{3,1},{4,6},{5,7},{6,4},{7,5},{8,10},{9,11},{10,... | collective-permute-start | bytes 18440 | tf_op jit(solution)/shard_map/ppermute | solution.py:40
  185.6 3.7 %collective-permute-start.37 = (f32[2,768]{1,0:T(2,128)S(1)}, f32[2,768]{1,0:T(2,128)S(1)}, u32[]{:S(2)}, u32[]{:S(2)}) collective-permute-start(f32[2,768]{1,0:T(2,128)S(1)} %fusion.138), channel_id=1, source_target_pairs={{0,4},{4,0},{8,12},{12,8},{16,20},{20,16},{24,28},{28,24},{1,5},{5... | collective-permute-start | bytes 18440 | tf_op jit(solution)/shard_map/ppermute | solution.py:40
  189.3 6.5 %collective-permute-start.38 = (f32[2,768]{1,0:T(2,128)S(1)}, f32[2,768]{1,0:T(2,128)S(1)}, u32[]{:S(2)}, u32[]{:S(2)}) collective-permute-start(f32[2,768]{1,0:T(2,128)S(1)} %add.368), channel_id=1, source_target_pairs={{0,8},{4,12},{8,0},{12,4},{16,24},{20,28},{24,16},{28,20},{1,9},{5... | collective-permute-start | bytes 18440 | tf_op jit(solution)/shard_map/ppermute | solution.py:40
  190.9 11.9 %collective-permute-start.41 = (bf16[192,768]{1,0:T(8,128)(2,1)S(1)}, bf16[192,768]{1,0:T(8,128)(2,1)S(1)}, u32[]{:S(2)}, u32[]{:S(2)}) collective-permute-start(bf16[192,768]{1,0:T(8,128)(2,1)S(1)} %dynamic-slice_convert_fusion.1), channel_id=1, source_target_pairs={{0,2},{1,3},{2,0},{3,1},{4,6},{5,7},{6,4},{7,5},{8,10},{9,11},{10,... | collective-permute-start | bytes 884744 | tf_op jit(solution)/shard_map/ppermute | solution.py:40
  195.8 6.9 %collective-permute-start.39 = (f32[2,768]{1,0:T(2,128)S(1)}, f32[2,768]{1,0:T(2,128)S(1)}, u32[]{:S(2)}, u32[]{:S(2)}) collective-permute-start(f32[2,768]{1,0:T(2,128)S(1)} %add.369), channel_id=1, source_target_pairs={{0,16},{4,20},{8,24},{12,28},{16,0},{20,4},{24,8},{28,12},{1,17},{... | collective-permute-start | bytes 18440 | tf_op jit(solution)/shard_map/ppermute | solution.py:40
  198.3 6.5 %collective-permute-start.25 = (bf16[192,384]{1,0:T(8,128)(2,1)S(1)}, bf16[192,384]{1,0:T(8,128)(2,1)S(1)}, u32[]{:S(2)}, u32[]{:S(2)}) collective-permute-start(bf16[192,384]{1,0:T(8,128)(2,1)S(1)} %get-tuple-element.36), channel_id=1, source_target_pairs={{0,8},{4,12},{8,0},{12,4},{16,24},{20,28},{24,16},{28,20},{1,9},{5... | collective-permute-start | bytes 442376 | tf_op jit(solution)/shard_map/ppermute | solution.py:40
  199.1 12.5 %collective-permute-start.26 = (bf16[192,384]{1,0:T(8,128)(2,1)S(1)}, bf16[192,384]{1,0:T(8,128)(2,1)S(1)}, u32[]{:S(2)}, u32[]{:S(2)}) collective-permute-start(bf16[192,384]{1,0:T(8,128)(2,1)S(1)} %get-tuple-element.38), channel_id=1, source_target_pairs={{0,16},{4,20},{8,24},{12,28},{16,0},{20,4},{24,8},{28,12},{1,17},{... | collective-permute-start | bytes 442376 | tf_op jit(solution)/shard_map/ppermute | solution.py:40
  202.0 9.6 %collective-permute-start.27 = (bf16[192,384]{1,0:T(8,128)(2,1)S(1)}, bf16[192,384]{1,0:T(8,128)(2,1)S(1)}, u32[]{:S(2)}, u32[]{:S(2)}) collective-permute-start(bf16[192,384]{1,0:T(8,128)(2,1)S(1)} %get-tuple-element.37), channel_id=1, source_target_pairs={{0,24},{4,28},{8,16},{12,20},{16,8},{20,12},{24,0},{28,4},{1,25},{... | collective-permute-start | bytes 442376 | tf_op jit(solution)/shard_map/ppermute | solution.py:40
  202.9 21.1 %collective-permute-start.42 = (bf16[192,384]{1,0:T(8,128)(2,1)S(1)}, bf16[192,384]{1,0:T(8,128)(2,1)S(1)}, u32[]{:S(2)}, u32[]{:S(2)}) collective-permute-start(bf16[192,384]{1,0:T(8,128)(2,1)S(1)} %slice.38), channel_id=1, source_target_pairs={{0,16},{4,20},{8,24},{12,28},{16,0},{20,4},{24,8},{28,12},{1,17},{... | collective-permute-start | bytes 442376 | tf_op jit(solution)/shard_map/ppermute | solution.py:40
  212.6 19.9 %collective-permute-start.28 = (bf16[192,384]{1,0:T(8,128)(2,1)S(1)}, bf16[192,384]{1,0:T(8,128)(2,1)S(1)}, u32[]{:S(2)}, u32[]{:S(2)}) collective-permute-start(bf16[192,384]{1,0:T(8,128)(2,1)S(1)} %add_convert_fusion), channel_id=1, source_target_pairs={{0,4},{4,0},{8,12},{12,8},{16,20},{20,16},{24,28},{28,24},{1,5},{5... | collective-permute-start | bytes 442376 | tf_op jit(solution)/shard_map/ppermute | solution.py:40
  213.0 12.9 %collective-permute-start.29 = (bf16[192,384]{1,0:T(8,128)(2,1)S(1)}, bf16[192,384]{1,0:T(8,128)(2,1)S(1)}, u32[]{:S(2)}, u32[]{:S(2)}) collective-permute-start(bf16[192,384]{1,0:T(8,128)(2,1)S(1)} %add_convert_fusion), channel_id=1, source_target_pairs={{0,8},{4,12},{8,0},{12,4},{16,24},{20,28},{24,16},{28,20},{1,9},{5... | collective-permute-start | bytes 442376 | tf_op jit(solution)/shard_map/ppermute | solution.py:40
  221.3 9.2 %collective-permute-start.31 = (bf16[192,384]{1,0:T(8,128)(2,1)S(1)}, bf16[192,384]{1,0:T(8,128)(2,1)S(1)}, u32[]{:S(2)}, u32[]{:S(2)}) collective-permute-start(bf16[192,384]{1,0:T(8,128)(2,1)S(1)} %add_convert_fusion), channel_id=1, source_target_pairs={{0,16},{4,20},{8,24},{12,28},{16,0},{20,4},{24,8},{28,12},{1,17},{... | collective-permute-start | bytes 442376 | tf_op jit(solution)/shard_map/ppermute | solution.py:40
  222.5 8.3 %collective-permute-start.33 = (bf16[192,384]{1,0:T(8,128)(2,1)S(1)}, bf16[192,384]{1,0:T(8,128)(2,1)S(1)}, u32[]{:S(2)}, u32[]{:S(2)}) collective-permute-start(bf16[192,384]{1,0:T(8,128)(2,1)S(1)} %add_convert_fusion), channel_id=1, source_target_pairs={{0,24},{4,28},{8,16},{12,20},{16,8},{20,12},{24,0},{28,4},{1,25},{... | collective-permute-start | bytes 442376 | tf_op jit(solution)/shard_map/ppermute | solution.py:40
  224.0 8.8 %collective-permute-start.43 = (bf16[192,384]{1,0:T(8,128)(2,1)S(1)}, bf16[192,384]{1,0:T(8,128)(2,1)S(1)}, u32[]{:S(2)}, u32[]{:S(2)}) collective-permute-start(bf16[192,384]{1,0:T(8,128)(2,1)S(1)} %fusion.89), channel_id=1, source_target_pairs={{0,2},{1,3},{2,0},{3,1},{4,6},{5,7},{6,4},{7,5},{8,10},{9,11},{10,... | collective-permute-start | bytes 442376 | tf_op jit(solution)/shard_map/ppermute | solution.py:40
  225.9 7.0 %collective-permute-start.30 = (bf16[192,384]{1,0:T(8,128)(2,1)S(1)}, bf16[192,384]{1,0:T(8,128)(2,1)S(1)}, u32[]{:S(2)}, u32[]{:S(2)}) collective-permute-start(bf16[192,384]{1,0:T(8,128)(2,1)S(1)} %collective-permute-done.29), channel_id=1, source_target_pairs={{0,4},{4,0},{8,12},{12,8},{16,20},{20,16},{24,28},{28,24},{1,5},{5... | collective-permute-start | bytes 442376 | tf_op jit(solution)/shard_map/ppermute | solution.py:40
  230.5 5.1 %collective-permute-start.32 = (bf16[192,384]{1,0:T(8,128)(2,1)S(1)}, bf16[192,384]{1,0:T(8,128)(2,1)S(1)}, u32[]{:S(2)}, u32[]{:S(2)}) collective-permute-start(bf16[192,384]{1,0:T(8,128)(2,1)S(1)} %collective-permute-done.31), channel_id=1, source_target_pairs={{0,4},{4,0},{8,12},{12,8},{16,20},{20,16},{24,28},{28,24},{1,5},{5... | collective-permute-start | bytes 442376 | tf_op jit(solution)/shard_map/ppermute | solution.py:40
  230.8 6.4 %collective-permute-start.34 = (bf16[192,384]{1,0:T(8,128)(2,1)S(1)}, bf16[192,384]{1,0:T(8,128)(2,1)S(1)}, u32[]{:S(2)}, u32[]{:S(2)}) collective-permute-start(bf16[192,384]{1,0:T(8,128)(2,1)S(1)} %collective-permute-done.33), channel_id=1, source_target_pairs={{0,4},{4,0},{8,12},{12,8},{16,20},{20,16},{24,28},{28,24},{1,5},{5... | collective-permute-start | bytes 442376 | tf_op jit(solution)/shard_map/ppermute | solution.py:40
  232.9 4.4 %collective-permute-start.44 = (bf16[384,384]{1,0:T(8,128)(2,1)S(1)}, bf16[384,384]{1,0:T(8,128)(2,1)S(1)}, u32[]{:S(2)}, u32[]{:S(2)}) collective-permute-start(bf16[384,384]{1,0:T(8,128)(2,1)S(1)} %maximum_select_fusion.7), channel_id=1, source_target_pairs={{0,1},{1,0},{2,3},{3,2},{4,5},{5,4},{6,7},{7,6},{8,9},{9,8},{10,11... | collective-permute-start | bytes 884744 | tf_op jit(solution)/shard_map/ppermute | solution.py:40
  (26 other events, 85.4 us)

commit v2 on v1

v2 whole, which is shorter than its diff:
```python
import functools
import math

import jax
import jax.numpy as jnp
from jax import lax
from jax.experimental import pallas as pl
from jax.experimental.pallas import tpu as pltpu
from jax.sharding import PartitionSpec as P

HIGH = lax.Precision.HIGHEST
F32 = jnp.float32
BF16 = jnp.bfloat16
CONTRACT_FIRST = (((0,), (0,)), ((), ()))
CONTRACT_LAST = (((1,), (1,)), ((), ()))
GROUP = 4
VMEM_LIMIT = 48 * 1024 * 1024


def gelu_value(v):
    return 0.5 * v * (1.0 + lax.erf(v / math.sqrt(2.0)))


def gelu_slope(v):
    return 0.5 * (1.0 + lax.erf(v / math.sqrt(2.0))) + v * jnp.exp(-0.5 * v * v) / math.sqrt(
        2.0 * math.pi
    )


def swap(x, axis, step):
    size = lax.axis_size(axis)
    return lax.ppermute(x, axis, [(i, i ^ step) for i in range(size)])


def ordered(mine, other, bit, axis=0):
    return jnp.where(
        bit == 0,
        jnp.concatenate([mine, other], axis),
        jnp.concatenate([other, mine], axis),
    )


def bits_of(size):
    return [1 << i for i in range(size.bit_length() - 1)]


def bit_at(place, step):
    return jnp.where((place & step) != 0, 1, 0)


def canonical(rows, place):
    count = rows.shape[0]
    for step in bits_of(count):
        shape = rows.shape
        parts = rows.reshape((count // (2 * step), 2, step) + shape[1:])
        rows = jnp.where((place & step) != 0, parts[:, ::-1], parts).reshape(shape)
    return rows


def cut(x, index, size, axis=0):
    return lax.dynamic_slice_in_dim(x, index * size, size, axis)


def rounded(x):
    return lax.reduce_precision(x, 8, 7)


def split_rows(x):
    high = rounded(x)
    rest = x - high
    middle = rounded(rest)
    return jnp.concatenate([high, middle, rest - middle], 0).astype(BF16)


def exact_dot(x, weight, dims=(((1,), (0,)), ((), ()))):
    rows = x.shape[0]
    out = lax.dot_general(split_rows(x), weight, dims, preferred_element_type=F32)
    return out[:rows] + (out[rows : 2 * rows] + out[2 * rows :])


def two_parts(x):
    high = rounded(x)
    return jnp.concatenate([high, x - high], 0).astype(BF16)


def norm_kernel(q_ref, s_ref, q_gain, s_gain, q_out, s_out):
    x = s_ref[...].astype(F32)
    xhat = x * lax.rsqrt(jnp.mean(x * x, axis=-1, keepdims=True) + 1e-06)
    s_out[...] = (xhat * s_gain[...]).astype(BF16)
    x = q_ref[...].astype(F32)
    x = x - jnp.mean(x, axis=-1, keepdims=True)
    xhat = x * lax.rsqrt(jnp.mean(x * x, axis=-1, keepdims=True) + 1e-05)
    q_out[...] = (xhat * q_gain[...]).astype(BF16)


def normalize(own_q, own_s, q_gain, s_gain):
    return pl.pallas_call(
        norm_kernel,
        out_shape=(
            jax.ShapeDtypeStruct(own_q.shape, BF16),
            jax.ShapeDtypeStruct(own_s.shape, BF16),
        ),
        compiler_params=pltpu.CompilerParams(vmem_limit_bytes=VMEM_LIMIT),
    )(own_q, own_s, q_gain[None], s_gain[None])


def score_kernel(
    n_sa,
    n_pb,
    place,
    q_ref,
    s_ref,
    positive_ref,
    q_outer,
    s_outer,
    loss_ref,
    q_grad_ref,
    s_grad_ref,
    q_hidden,
    s_hidden,
):
    p, a = place[0], place[1]
    q, s = q_ref[...], s_ref[...]
    count, width = q.shape
    scale = 1.0 / math.sqrt(width)
    score = scale * lax.dot_general(q, s, CONTRACT_LAST, precision=HIGH, preferred_element_type=F32)
    columns = lax.broadcasted_iota(jnp.int32, (count, count), 1)
    match = (positive_ref[...] == columns).astype(F32)
    row_max = jnp.max(score, axis=1, keepdims=True)
    col_max = jnp.max(score, axis=0, keepdims=True)
    row_lse = row_max + jnp.log(jnp.sum(jnp.exp(score - row_max), axis=1, keepdims=True))
    col_lse = col_max + jnp.log(jnp.sum(jnp.exp(score - col_max), axis=0, keepdims=True))
    matched = jnp.sum(match * score, axis=1, keepdims=True)
    row_part = jnp.sum(row_lse - matched, axis=0, keepdims=True)
    col_part = jnp.sum(col_lse, axis=1, keepdims=True) - jnp.sum(matched, axis=0, keepdims=True)
    loss_ref[...] = (row_part + col_part) / (2.0 * count)
    dscore = 0.5 * (jnp.exp(score - row_lse) + jnp.exp(score - col_lse) - 2.0 * match)
    q_grad = scale * jnp.dot(dscore, s, precision=HIGH, preferred_element_type=F32)
    s_grad = scale * lax.dot_general(
        dscore, q, CONTRACT_FIRST, precision=HIGH, preferred_element_type=F32
    )
    q_grad_ref[...] = q_grad
    s_grad_ref[...] = s_grad

    def hidden(grad, places, outer):
        rows = places.shape[0]
        chosen = lax.broadcasted_iota(jnp.int32, (rows, count), 1) == places
        picked = jnp.dot(chosen.astype(F32), grad, precision=HIGH, preferred_element_type=F32)
        high = picked.astype(BF16)
        low = (picked - high.astype(F32)).astype(BF16)
        return lax.dot_general(
            high, outer, CONTRACT_LAST, preferred_element_type=F32
        ) + lax.dot_general(low, outer, CONTRACT_LAST, preferred_element_type=F32)

    index = lax.broadcasted_iota(jnp.int32, (2 * n_sa, 1), 0)
    pair = (index >= n_sa).astype(jnp.int32)
    q_hidden[...] = hidden(
        q_grad, (p ^ pair) * n_sa + (a ^ (index - pair * n_sa)), q_outer[...]
    )
    index = lax.broadcasted_iota(jnp.int32, (8, 1), 0)
    s_hidden[...] = hidden(s_grad, a * n_pb + (p ^ index), s_outer[...])


def scores(place, q_embed, s_embed, positive, q_outer, s_outer, n_sa, n_pb):
    shape = q_embed.shape
    whole = pl.BlockSpec(memory_space=pltpu.VMEM)
    return pl.pallas_call(
        functools.partial(score_kernel, n_sa, n_pb),
        in_specs=[pl.BlockSpec(memory_space=pltpu.SMEM)] + [whole] * 5,
        out_shape=(
            jax.ShapeDtypeStruct((1, 1), F32),
            jax.ShapeDtypeStruct(shape, F32),
            jax.ShapeDtypeStruct(shape, F32),
            jax.ShapeDtypeStruct((2 * n_sa, q_outer.shape[0]), F32),
            jax.ShapeDtypeStruct((8, s_outer.shape[0]), F32),
        ),
        compiler_params=pltpu.CompilerParams(vmem_limit_bytes=VMEM_LIMIT),
    )(place, q_embed, s_embed, positive, q_outer, s_outer)


def per_device(
    question_states,
    question_ids,
    q_inner_weight,
    q_outer_weight,
    q_norm_gain,
    sql_states,
    sql_ids,
    s_inner_weight,
    s_outer_weight,
    s_norm_gain,
    positive_column,
):
    n_pb, n_sa = lax.axis_size("pb"), lax.axis_size("sa")
    p, a = lax.axis_index("pb"), lax.axis_index("sa")
    width = question_states.shape[-1]
    length = question_states.shape[-2]
    block = s_inner_weight.shape[1]
    half = q_inner_weight.shape[1] // 2
    pair_bit = bit_at(p, 1)
    far = range(GROUP, n_pb, GROUP)

    piece_index = sum(bit_at(a, n_sa >> (i + 1)) << i for i in range(n_sa.bit_length() - 1))
    fold = width // block
    thin = width // n_sa // fold
    inner_piece = cut(s_inner_weight, piece_index, width // n_sa)
    inner_piece = jnp.concatenate([inner_piece[i * thin : (i + 1) * thin] for i in range(fold)], 1)
    piece = jnp.concatenate([inner_piece, cut(s_outer_weight, piece_index, block // n_sa)], 0)
    pieces = [swap(piece, "pb", k)[None] for k in far]

    own_q, own_s = question_states[0, 0], sql_states[0, 0]
    q_normed, s_normed = normalize(own_q, own_s, q_norm_gain, s_norm_gain)
    s_tokens = [s_normed] + [swap(s_normed, "pb", k) for k in range(1, GROUP)]
    q_tokens = [q_normed] + [None] * (n_sa - 1)
    for step in reversed(bits_of(n_sa)):
        for k in range(0, n_sa, 2 * step):
            q_tokens[k + step] = swap(q_tokens[k], "sa", step)
    for step in reversed(bits_of(n_sa)):
        pieces = [ordered(x, swap(x, "sa", step), bit_at(a, step)) for x in pieces]
    s_inners, s_outers = [s_inner_weight], [s_outer_weight]
    for x in pieces:
        inner = x[:, :thin].reshape(n_sa, thin, fold, block).transpose(0, 2, 1, 3)
        s_inners.append(inner.reshape(width, block))
        s_outers.append(x[:, thin:].reshape(block, width))
    s_inner_all = jnp.concatenate(s_inners, 1)
    s_outer_all = jnp.concatenate(s_outers, 0)

    q_lengths = jnp.sum((question_ids[0] > 0).astype(F32), axis=-1, keepdims=True)
    s_lengths = jnp.sum((sql_ids[0] > 0).astype(F32), axis=-1, keepdims=True)
    position = jnp.arange(length, dtype=jnp.int32).astype(F32)[None, :]

    def pool(lengths):
        return (position < lengths).astype(F32) / lengths

    q_pool = pool(canonical(q_lengths, a))
    s_pool = pool(canonical(s_lengths, p)[:GROUP])

    q_rows = jnp.concatenate(q_tokens, 0)
    q_pre = jnp.dot(q_rows, q_inner_weight, preferred_element_type=F32)
    q_pooled = jnp.sum(gelu_value(q_pre).reshape(n_sa, length, -1) * q_pool[:, :, None], axis=1)
    q_pooled = canonical(q_pooled, a)
    q_self = jnp.sum(own_q.astype(F32) * q_pool[0][:, None], axis=0)
    q_part = exact_dot(q_pooled, q_outer_weight)
    q_part = q_part + jnp.where(jnp.arange(n_sa)[:, None] == a, q_self[None], 0.0)
    for step in reversed(bits_of(n_sa)):
        q_part = q_part + swap(q_part, "sa", step)
    meta = jnp.concatenate(
        [positive_column.astype(F32)[:, None], q_lengths, jnp.zeros((n_sa, 126), F32)], 1
    )
    q_all = jnp.concatenate([q_part, q_pooled, meta], 1)
    pair_meta = None
    for step in bits_of(n_pb):
        other = swap(q_all, "pb", step)
        if step == 1:
            pair_meta = other
        q_all = ordered(q_all, other, bit_at(p, step))
    q_embed = q_all[:, :width]
    q_pooled_all = q_all[:, width : width + 2 * half]
    positive = q_all[:, width + 2 * half : width + 2 * half + 1].astype(jnp.int32)
    pair_lengths = pair_meta[:, width + 2 * half + 1 : width + 2 * half + 2]

    s_rows = jnp.concatenate(s_tokens, 0)
    s_pre = jnp.dot(s_rows, s_inner_all, preferred_element_type=F32).reshape(GROUP, length, -1)
    s_pooled = canonical(jnp.sum(gelu_value(s_pre) * s_pool[:, :, None], axis=1), p)
    s_self = jnp.sum(own_s.astype(F32) * s_pool[0][:, None], axis=0)
    s_part = exact_dot(s_pooled, s_outer_all)
    s_part = s_part + jnp.where(jnp.arange(GROUP)[:, None] == p % GROUP, s_self[None], 0.0)
    s_others = [swap(s_part, "pb", k) for k in range(1, GROUP)]
    s_part = (s_part + s_others[0]) + (s_others[1] + s_others[2])
    rows = [jnp.concatenate([s_part, s_pooled[:, :block]], 1)]
    for i, k in enumerate(far):
        pooled_far = s_pooled[:, (i + 1) * block : (i + 2) * block]
        rows.append(swap(jnp.concatenate([s_part, pooled_far], 1), "pb", k))
    s_all = canonical(jnp.stack(rows), p // GROUP).reshape(n_pb, width + block)
    s_all = s_all[None]
    for step in bits_of(n_sa):
        s_all = ordered(s_all, swap(s_all, "sa", step), bit_at(a, step))
    s_all = s_all.reshape(n_sa * n_pb, width + block)
    s_embed = s_all[:, :width]
    s_pooled_all = s_all[:, width:]

    pair_tokens = [swap(q_normed, "pb", 1)] + [None] * (n_sa - 1)
    for step in reversed(bits_of(n_sa)):
        for k in range(0, n_sa, 2 * step):
            pair_tokens[k + step] = swap(pair_tokens[k], "sa", step)
    q_inner_half = cut(q_inner_weight, pair_bit, half, 1)
    q_outer_half = cut(q_outer_weight, pair_bit, half, 0)
    q_both = jnp.concatenate([q_rows] + pair_tokens, 0)
    q_pool_both = jnp.concatenate([q_pool, pool(canonical(pair_lengths, a))], 0)

    place = jnp.stack([p, a]).astype(jnp.int32)
    loss, q_grad, s_grad, q_hidden, s_hidden = scores(
        place, q_embed, s_embed, positive, q_outer_half, s_outer_all, n_sa, n_pb
    )
    s_hidden = s_hidden[:GROUP]

    q_slope = gelu_slope(jnp.dot(q_both, q_inner_half, preferred_element_type=F32))
    q_slope = q_slope.reshape(2 * n_sa, length, half) * q_pool_both[:, :, None]
    s_slope = gelu_slope(s_pre) * s_pool[:, :, None]
    q_dpre = (q_slope * q_hidden[:, None, :]).astype(BF16).reshape(-1, half)
    s_dpre = (s_slope * s_hidden[:, None, :]).astype(BF16).reshape(GROUP * length, -1)
    q_inner_part = lax.dot_general(q_both, q_dpre, CONTRACT_FIRST, preferred_element_type=F32)
    s_inner_part = lax.dot_general(s_rows, s_dpre, CONTRACT_FIRST, preferred_element_type=F32)

    gains = jnp.stack(
        [
            jnp.sum(q_inner_part * q_inner_half.astype(F32), axis=1) / q_norm_gain,
            jnp.sum(s_inner_part * s_inner_all.astype(F32), axis=1) / s_norm_gain,
        ]
    )

    def pack(gains, columns):
        parts = two_parts(gains).reshape(-1, columns)
        return jnp.concatenate([parts, jnp.zeros((-parts.shape[0] % 16, columns), BF16)], 0)

    def unpack(rows):
        parts = rows[: 4 * width // rows.shape[1]].reshape(4, width).astype(F32)
        return parts[:2] + parts[2:]

    pairs = n_pb // 2
    q_chunk = width // pairs
    mine = p // 2
    q_half_part = q_inner_part.astype(BF16)
    packed = pack(gains, half)
    q_sent = []
    for k in range(1, pairs):
        chunk = cut(q_half_part, mine ^ k, q_chunk)
        q_sent.append(swap(jnp.concatenate([chunk, packed], 0), "pb", 2 * k))
    q_total = cut(q_inner_part, mine, q_chunk)
    sums = [unpack(packed)]
    for arrived in q_sent:
        q_total = q_total + arrived[:q_chunk].astype(F32)
        sums.append(unpack(arrived[q_chunk:]))
    while len(sums) > 1:
        sums = [sums[i] + sums[i + 1] for i in range(0, len(sums), 2)]
    gains = sums[0]
    q_total = q_total.astype(BF16)
    chunks = [q_total] + [swap(q_total, "pb", 2 * k) for k in range(1, pairs)]
    packed = pack(gains, half)
    first = swap(jnp.concatenate([q_total, packed], 0), "pb", 1)
    gains = unpack(packed) + unpack(first[q_chunk:])
    others = [first[:q_chunk]] + [swap(c, "pb", 1) for c in chunks[1:]]
    q_inner_grad = jnp.zeros((width, 2 * half), F32)
    for k in range(pairs):
        full = ordered(chunks[k], others[k], pair_bit, 1).astype(F32)
        q_inner_grad = lax.dynamic_update_slice_in_dim(q_inner_grad, full, (mine ^ k) * q_chunk, 0)

    s_total = s_inner_part
    for step in bits_of(n_sa):
        size = s_total.shape[0] // 2
        bit = bit_at(a, step)
        keep = cut(s_total, bit, size)
        s_total = keep + swap(cut(s_total, 1 - bit, size).astype(BF16), "sa", step).astype(F32)
    s_sum = s_total[:, :block]
    for i, k in enumerate(far):
        far_part = s_total[:, (i + 1) * block : (i + 2) * block].astype(BF16)
        s_sum = s_sum + swap(far_part, "pb", k).astype(F32)
    s_sum = s_sum.astype(BF16)
    for step in reversed(bits_of(n_sa)):
        size = s_sum.shape[0]
        packed = pack(gains, block)
        arrived = swap(jnp.concatenate([s_sum, packed], 0), "sa", step)
        gains = unpack(packed) + unpack(arrived[size:])
        s_sum = ordered(s_sum, arrived[:size], bit_at(a, step))
    s_inner_grad = s_sum.astype(F32)

    q_outer_grad = lax.dot_general(q_pooled_all, q_grad, CONTRACT_FIRST, precision=HIGH)
    s_outer_grad = lax.dot_general(s_pooled_all, s_grad, CONTRACT_FIRST, precision=HIGH)
    return (
        loss[0, 0],
        q_inner_grad,
        q_outer_grad,
        gains[0],
        s_inner_grad,
        s_outer_grad,
        gains[1],
    )


def solution(mesh):
    placed = (
        P("pb", "sa", None, None),
        P("pb", None, None),
        P(None, "sa"),
        P("sa", None),
        P(),
        P("sa", "pb", None, None),
        P("sa", None, None),
        P(None, "pb"),
        P("pb", None),
        P(),
        P("pb"),
    )
    return jax.shard_map(
        per_device,
        mesh=mesh,
        in_specs=placed,
        out_specs=(P(), P(None, "sa"), P("sa", None), P(), P(None, "pb"), P("pb", None), P()),
        check_vma=False,
    )
```

time: 241 us -> 176 us (0.73)
  blocking collectives: 49.7 us -> 0 us
  local copies, waits for them, and re-layouts: 12.9 us -> 32.9 us
  other arithmetic: 35.7 us -> 20.2 us
  waiting for transfers between devices: 63 us -> 50.3 us
  matrix products: 32.4 us -> 21.4 us
  starting transfers between devices: 41.1 us -> 46.3 us
  between operations: 5.47 us -> 1.49 us
  Pallas kernels: 0 us -> 2.86 us
    all_gather x2 -> x0, blocking collectives: 37.6 us -> none  [the longest x1 30.8 us: per_device(): q_pooled_all = lax.all_gather(q_pooled, 'pb', axis=0, tiled=True)]
    unnamed x95 -> x67, local copies, waits for them, and re-layouts: 2.85 us -> 19.9 us
    ppermute x46 -> x39, waiting for transfers between devices: 63 us -> 50.3 us  [swap(): return lax.ppermute(x, axis, [(i, i ^ step) for i in range(size)])]
    unnamed x1 -> x0, blocking collectives: 12.1 us -> none
    dot_general x12 -> x7, matrix products: 25.9 us -> 14.9 us  [the longest x1 3.46 us: per_device(): lax.dot_general(q_pooled_all, q_grad, CONTRACT_FIRST, precision=HIGH)]
    reduce_sum x24 -> x4, other arithmetic: 10.8 us -> 0.53 us  [the longest x1 0.15 us: per_device(): q_self = jnp.sum(own_q.astype(F32) * q_pool[0][:, None], axis=0)]
    unnamed x8 -> x1, other arithmetic: 8.52 us -> 0.01 us
    dynamic_update_slice x4, other arithmetic: 0.29 us -> 5.67 us  [per_device(): lax.dynamic_update_slice_in_dim(q_inner_grad, full, (mine ^ k) * q_chunk, 0)]
  transfers between devices with their start and end apart: 46 -> 39, of which waited for: 17 -> 17; matrix products, arithmetic and copies ran while one was open for 28% -> 35% of each run, Pallas kernels for 0% -> 0%
where the time goes in v2:
time: 176 us; the launch traced here: 175 us
  waiting for transfers between devices  50.3 us (29%)
  starting transfers between devices  46.3 us (26%)
  local copies, waits for them, and re-layouts  32.9 us (19%)
  matrix products  21.4 us (12%)
  other arithmetic  20.2 us (11%)
  Pallas kernels  2.86 us (2%)
    ppermute x39, waiting for transfers between devices, swap(): return lax.ppermute(x, axis, [(i, i ^ step) for i in range(size)])  50.3 us
    ppermute x39, starting transfers between devices, swap(): return lax.ppermute(x, axis, [(i, i ^ step) for i in range(size)])  46.3 us
    unnamed x67, local copies, waits for them, and re-layouts  19.9 us
    dynamic_update_slice x4, other arithmetic, per_device(): lax.dynamic_update_slice_in_dim(q_inner_grad, full, (mine ^ k) * q_chunk, 0)  5.67 us
  transfers between devices with their start and end apart: 39, of which 17 were waited for; matrix products, arithmetic and copies ran while one was open for 35% of the time, Pallas kernels for 0%

profile of v2, /device:TPU:0, one launch (start us, length us, event | category | flops | bytes accessed | tf_op | source)
XLA Modules:
  0.0 175.4 jit_solution(4323322247221770498)
XLA Ops:
  4.6 3.0 %collective-permute-start.1 = (bf16[256,768]{1,0:T(8,128)(2,1)S(1)}, bf16[256,768]{1,0:T(8,128)(2,1)S(1)}, u32[]{:S(2)}, u32[]{:S(2)}) collective-permute-start(bf16[256,768]{1,0:T(8,128)(2,1)S(1)} %get-tuple-element.14), channel_id=1, source_target_pairs={{0,2},{1,3},{2,0},{3,1},{4,6},{5,7},{6,4},{7,5},{8,10},{9,11},{10,... | collective-permute-start | bytes 1179656 | tf_op jit(solution)/shard_map/ppermute | solution.py:32
  7.6 1.5 collective-permute-start.20
  11.7 2.6 %collective-permute-start.11 = (bf16[192,768]{1,0:T(8,128)(2,1)}, bf16[192,768]{1,0:T(8,128)(2,1)}, u32[]{:S(2)}, u32[]{:S(2)}) collective-permute-start(bf16[192,768]{1,0:T(8,128)(2,1)} %pad_maximum_fusion.9), channel_id=1, source_target_pairs={{0,16},{4,20},{8,24},{12,28},{16,0},{20,4},{24,8},{28,12},{1,17},{... | collective-permute-start | bytes 884744 | tf_op jit(solution)/shard_map/ppermute | solution.py:32
  18.9 9.5 %collective-permute-done.11 = bf16[192,768]{1,0:T(8,128)(2,1)} collective-permute-done((bf16[192,768]{1,0:T(8,128)(2,1)}, bf16[192,768]{1,0:T(8,128)(2,1)}, u32[]{:S(2)}, u32[]{:S(2)}) %collective-permute-start.11) | collective-permute-done | bytes 294944 | tf_op jit(solution)/shard_map/ppermute | solution.py:32
  30.4 1.3 collective-permute-start.10
  31.8 1.8 %constant_dynamic-update-slice_fusion.10 = bf16[2048,768]{1,0:T(8,128)(2,1)} fusion(bf16[2048,768]{1,0:T(8,128)(2,1)} %get-tuple-element.70, bf16[256,768]{1,0:T(8,128)(2,1)} %collective-permute-done), kind=kLoop, calls=%fused_computation.92 | loop fusion | bytes 786432
  35.3 1.8 %constant_dynamic-update-slice_fusion.2 = bf16[1024,768]{1,0:T(8,128)(2,1)} fusion(bf16[1024,768]{1,0:T(8,128)(2,1)} %get-tuple-element.69, bf16[256,768]{1,0:T(8,128)(2,1)} %collective-permute-done.8), kind=kLoop, calls=%fused_computation.84 | loop fusion | bytes 786432
  37.1 3.4 %collective-permute-done.9 = bf16[256,768]{1,0:T(8,128)(2,1)} collective-permute-done((bf16[256,768]{1,0:T(8,128)(2,1)S(1)}, bf16[256,768]{1,0:T(8,128)(2,1)}, u32[]{:S(2)}, u32[]{:S(2)}) %collective-permute-start.9) | collective-permute-done | bytes 393248 | tf_op jit(solution)/shard_map/ppermute | solution.py:32
  41.0 1.8 %constant_dynamic-update-slice_fusion.1 = bf16[1024,768]{1,0:T(8,128)(2,1)} fusion(bf16[1024,768]{1,0:T(8,128)(2,1)} %constant_dynamic-update-slice_fusion.2, bf16[256,768]{1,0:T(8,128)(2,1)} %collective-permute-done.9), kind=kLoop, calls=%fused_computation.83 | loop fusion | bytes 786432
  42.8 4.4 %collective-permute-done.10 = bf16[256,768]{1,0:T(8,128)(2,1)S(1)} collective-permute-done((bf16[256,768]{1,0:T(8,128)(2,1)S(1)}, bf16[256,768]{1,0:T(8,128)(2,1)S(1)}, u32[]{:S(2)}, u32[]{:S(2)}) %collective-permute-start.10) | collective-permute-done | bytes 393248 | tf_op jit(solution)/shard_map/ppermute | solution.py:32
  48.0 1.1 maximum_select_fusion.1
  50.0 3.3 %multiply_reduce_fusion.1 = f32[4,768]{1,0:T(4,128)} fusion(f32[4,256]{1,0:T(4,128)S(1)} %convert_divide_fusion.3, bf16[768,768]{1,0:T(8,128)(2,1)S(1)} %copy-done.14, bf16[256,768]{1,0:T(8,128)(2,1)S(1)} %collective-permute-done.2, bf16[256,768]{1,0:T(8,128)(2,1)S(1)} %collective-permute-done.1, bf16[256,768]{1,0:T(8,128)(2,1)} %collective-permute-done, ...), kind=kOutput, calls=%fused_computation.19 | convolution fusion | flops 1218966528 | bytes 2768896 | tf_op jit(solution)/shard_map/dot_general | solution.py:239
  56.3 1.8 %constant_dynamic-update-slice_fusion.8 = bf16[2048,768]{1,0:T(8,128)(2,1)} fusion(bf16[2048,768]{1,0:T(8,128)(2,1)} %constant_dynamic-update-slice_fusion.9, bf16[256,768]{1,0:T(8,128)(2,1)} %copy-done.13), kind=kLoop, calls=%fused_computation.90 | loop fusion | bytes 786432
  59.5 1.8 %constant_dynamic-update-slice_fusion.6 = bf16[2048,768]{1,0:T(8,128)(2,1)} fusion(bf16[2048,768]{1,0:T(8,128)(2,1)} %constant_dynamic-update-slice_fusion.7, bf16[256,768]{1,0:T(8,128)(2,1)} %collective-permute-done.21), kind=kLoop, calls=%fused_computation.88 | loop fusion | bytes 786432
  61.4 1.4 collective-permute-start.5
  62.7 1.8 %constant_dynamic-update-slice_fusion.5 = bf16[2048,768]{1,0:T(8,128)(2,1)} fusion(bf16[2048,768]{1,0:T(8,128)(2,1)} %constant_dynamic-update-slice_fusion.6, bf16[256,768]{1,0:T(8,128)(2,1)} %collective-permute-done.22), kind=kLoop, calls=%fused_computation.87 | loop fusion | bytes 786432
  65.8 1.2 collective-permute-start.6
  67.1 2.8 %collective-permute-done.6 = f32[8,1664]{1,0:T(8,128)S(1)} collective-permute-done((f32[8,1664]{1,0:T(8,128)S(1)}, f32[8,1664]{1,0:T(8,128)S(1)}, u32[]{:S(2)}, u32[]{:S(2)}) %collective-permute-start.6) | collective-permute-done | bytes 53280 | tf_op jit(solution)/shard_map/ppermute | solution.py:32
  70.0 2.9 %collective-permute-start.7 = (f32[16,1664]{1,0:T(8,128)S(1)}, f32[16,1664]{1,0:T(8,128)S(1)}, u32[]{:S(2)}, u32[]{:S(2)}) collective-permute-start(f32[16,1664]{1,0:T(8,128)S(1)} %maximum_select_fusion.10), channel_id=1, source_target_pairs={{0,16},{4,20},{8,24},{12,28},{16,0},{20,4},{24,8},{28,12},{1,17},{... | collective-permute-start | bytes 319496 | tf_op jit(solution)/shard_map/ppermute | solution.py:32
  73.0 2.7 %collective-permute-done.7 = f32[16,1664]{1,0:T(8,128)S(1)} collective-permute-done((f32[16,1664]{1,0:T(8,128)S(1)}, f32[16,1664]{1,0:T(8,128)S(1)}, u32[]{:S(2)}, u32[]{:S(2)}) %collective-permute-start.7) | collective-permute-done | bytes 106528 | tf_op jit(solution)/shard_map/ppermute | solution.py:32
  75.7 1.4 maximum_select_fusion
  77.3 1.2 copy-done.7
  78.7 3.2 %multiply_reduce_fusion = (f32[4,768]{1,0:T(4,128)S(1)}, f32[1024,768]{1,0:T(8,128)}) fusion(f32[4,256]{1,0:T(4,128)S(1)} %get-tuple-element.62, bf16[1024,768]{1,0:T(8,128)(2,1)S(1)} %copy-done.7, bf16[768,384]{1,0:T(8,128)(2,1)S(1)} %bitcast.70, bf16[768,384]{1,0:T(8,128)(2,1)S(1)} %copy-done.11), kind=kOutput, calls=%fused_computation.16 | convolution fusion | flops 1215034368 | bytes 5914624 | tf_op jit(solution)/shard_map/dot_general | solution.py:263
  82.2 1.3 fusion.40
  83.6 1.4 collective-permute-start.14
  85.0 2.1 %collective-permute-start.15 = (f32[4,768]{1,0:T(4,128)S(1)}, f32[4,768]{1,0:T(4,128)S(1)}, u32[]{:S(2)}, u32[]{:S(2)}) collective-permute-start(f32[4,768]{1,0:T(4,128)S(1)} %fusion.50), channel_id=1, source_target_pairs={{0,8},{4,12},{8,0},{12,4},{16,24},{20,28},{24,16},{28,20},{1,9},{5... | collective-permute-start | bytes 36872 | tf_op jit(solution)/shard_map/ppermute | solution.py:32
  87.3 1.5 collective-permute-done.15
  88.8 2.9 %collective-permute-done.16 = f32[4,768]{1,0:T(4,128)S(1)} collective-permute-done((f32[4,768]{1,0:T(4,128)S(1)}, f32[4,768]{1,0:T(4,128)S(1)}, u32[]{:S(2)}, u32[]{:S(2)}) %collective-permute-start.16) | collective-permute-done | bytes 12320 | tf_op jit(solution)/shard_map/ppermute | solution.py:32
  91.8 3.4 %collective-permute-start.17 = (f32[4,1152]{1,0:T(4,128)S(1)}, f32[4,1152]{1,0:T(4,128)S(1)}, u32[]{:S(2)}, u32[]{:S(2)}) collective-permute-start(f32[4,1152]{1,0:T(4,128)S(1)} %get-tuple-element.50), channel_id=1, source_target_pairs={{0,16},{4,20},{8,24},{12,28},{16,0},{20,4},{24,8},{28,12},{1,17},{... | collective-permute-start | bytes 55304 | tf_op jit(solution)/shard_map/ppermute | solution.py:32
  95.3 1.7 collective-permute-done.17
  97.1 1.3 pad_maximum_fusion.1.s_outer
  98.5 1.5 collective-permute-start.19
  99.9 1.8 %constant_dynamic-update-slice_fusion.4 = bf16[2048,768]{1,0:T(8,128)(2,1)} fusion(bf16[2048,768]{1,0:T(8,128)(2,1)} %constant_dynamic-update-slice_fusion.5, bf16[256,768]{1,0:T(8,128)(2,1)} %collective-permute-done.23), kind=kLoop, calls=%fused_computation.86 | loop fusion | bytes 786432 | tf_op jit(solution)/shard_map/concatenate | solution.py:288
  101.7 1.3 collective-permute-done.19
  103.1 2.5 %shard_map.163 = (f32[1,1]{1,0:T(1,128)}, f32[32,768]{1,0:T(8,128)S(1)}, f32[32,768]{1,0:T(8,128)S(1)}, f32[8,384]{1,0:T(8,128)S(1)}, f32[8,768]{1,0:T(8,128)S(1)}) custom-call(s32[2]{0:T(128)S(1)} %pad_add_fusion.place, f32[32,768]{1,0:T(8,128)S(1)} %slice.262.q_ref, f32[32,768]{1,0:T(8,128)S(1)} %slice.271.s_ref, ...), custom_call_target="tpu_custom_call" | custom-call | tf_op jit(solution)/shard_map/pallas_call | solution.py:167
  105.6 1.8 %fusion.13 = bf16[1024,768]{1,0:T(8,128)(2,1)S(1)} fusion(f32[1024,768]{1,0:T(8,128)S(1)} %copy-done.5, f32[4,768]{1,0:T(4,128)S(1)} %slice.219, f32[1024]{0:T(1024)S(1)} %convert_divide_fusion), kind=kLoop, calls=%fused_computation.15 | loop fusion | flops 8650752 | bytes 4734976 | tf_op jit(solution)/shard_map/convert_element_type | solution.py:301
  107.5 1.6 multiply_reduce_fusion.2
  109.7 3.1 %fusion.6 = bf16[2048,384]{1,0:T(8,128)(2,1)S(1)} fusion(f32[8,384]{1,0:T(8,128)S(1)} %get-tuple-element.17, f32[2048]{0:T(1024)S(1)} %bitcast.75, bf16[2048,768]{1,0:T(8,128)(2,1)S(1)} %copy-done.6, bf16[768,768]{1,0:T(8,128)(2,1)S(1)} %copy-done.15, s32[]{:T(128)S(6)} %select_n.311), kind=kOutput, calls=%fused_computation.8 | convolution fusion | flops 1216610304 | bytes 5328900 | tf_op jit(solution)/shard_map/dot_general | solution.py:297
  112.8 3.0 %fusion.74 = (bf16[768,384]{1,0:T(8,128)(2,1)}, f32[768]{0:T(1024)S(1)}, f32[768,384]{1,0:T(8,128)}) fusion(bf16[768,768]{1,0:T(8,128)(2,1)S(1)} %copy-done.15, s32[]{:T(128)S(6)} %select_n.311, bf16[2048,768]{1,0:T(8,128)(2,1)S(1)} %copy-done.6, bf16[2048,384]{1,0:T(8,128)(2,1)S(1)} %fusion.6), kind=kOutput, calls=%fused_computation.206 | convolution fusion | flops 1209138432 | bytes 7080964 | tf_op jit(solution)/shard_map/dot_general | solution.py:302
  115.9 1.1 constant_dynamic-slice_fusion.3
  117.2 3.0 %collective-permute-start.25 = (bf16[208,384]{1,0:T(8,128)(2,1)S(1)}, bf16[208,384]{1,0:T(8,128)(2,1)S(1)}, u32[]{:S(2)}, u32[]{:S(2)}) collective-permute-start(bf16[208,384]{1,0:T(8,128)(2,1)S(1)} %get-tuple-element.47), channel_id=1, source_target_pairs={{0,16},{4,20},{8,24},{12,28},{16,0},{20,4},{24,8},{28,12},{1,17},{... | collective-permute-start | bytes 479240 | tf_op jit(solution)/shard_map/ppermute | solution.py:32
  120.2 1.4 collective-permute-start.26
  121.6 3.5 %fusion.30 = f32[768,768]{1,0:T(8,128)} fusion(f32[32,768]{1,0:T(8,128)S(1)} %get-tuple-element.19, f32[32,1664]{1,0:T(8,128)S(1)} %maximum_select_fusion.8), kind=kOutput, calls=%fused_computation.74 | convolution fusion | flops 226492416 | bytes 2555904 | tf_op jit(solution)/shard_map/dot_general | solution.py:367
  125.0 1.6 collective-permute-done.24
  126.7 5.9 %collective-permute-done.26 = bf16[208,384]{1,0:T(8,128)(2,1)S(1)} collective-permute-done((bf16[208,384]{1,0:T(8,128)(2,1)S(1)}, bf16[208,384]{1,0:T(8,128)(2,1)S(1)}, u32[]{:S(2)}, u32[]{:S(2)}) %collective-permute-start.26) | collective-permute-done | bytes 159776 | tf_op jit(solution)/shard_map/ppermute | solution.py:32
  132.5 1.0 add_convert_fusion
  133.6 3.2 %collective-permute-start.28 = (bf16[192,384]{1,0:T(8,128)(2,1)S(1)}, bf16[192,384]{1,0:T(8,128)(2,1)}, u32[]{:S(2)}, u32[]{:S(2)}) collective-permute-start(bf16[192,384]{1,0:T(8,128)(2,1)S(1)} %add_convert_fusion), channel_id=1, source_target_pairs={{0,8},{4,12},{8,0},{12,4},{16,24},{20,28},{24,16},{28,20},{1,9},{5... | collective-permute-start | bytes 442376 | tf_op jit(solution)/shard_map/ppermute | solution.py:32
  136.8 2.0 %collective-permute-start.30 = (bf16[192,384]{1,0:T(8,128)(2,1)S(1)}, bf16[192,384]{1,0:T(8,128)(2,1)}, u32[]{:S(2)}, u32[]{:S(2)}) collective-permute-start(bf16[192,384]{1,0:T(8,128)(2,1)S(1)} %add_convert_fusion), channel_id=1, source_target_pairs={{0,16},{4,20},{8,24},{12,28},{16,0},{20,4},{24,8},{28,12},{1,17},{... | collective-permute-start | bytes 442376 | tf_op jit(solution)/shard_map/ppermute | solution.py:32
  138.7 1.4 collective-permute-start.32
  140.9 1.4 convert_add_fusion
  142.3 1.5 collective-permute-start.35
  143.8 1.9 %collective-permute-done.27 = bf16[208,384]{1,0:T(8,128)(2,1)S(1)} collective-permute-done((bf16[208,384]{1,0:T(8,128)(2,1)S(1)}, bf16[208,384]{1,0:T(8,128)(2,1)S(1)}, u32[]{:S(2)}, u32[]{:S(2)}) %collective-permute-start.27) | collective-permute-done | bytes 159776 | tf_op jit(solution)/shard_map/ppermute | solution.py:32
  146.3 3.7 %collective-permute-done.35 = bf16[192,768]{1,0:T(8,128)(2,1)} collective-permute-done((bf16[192,768]{1,0:T(8,128)(2,1)S(1)}, bf16[192,768]{1,0:T(8,128)(2,1)}, u32[]{:S(2)}, u32[]{:S(2)}) %collective-permute-start.35) | collective-permute-done | bytes 294944 | tf_op jit(solution)/shard_map/ppermute | solution.py:32
  151.1 1.8 %collective-permute-start.36 = (bf16[192,384]{1,0:T(8,128)(2,1)S(1)}, bf16[192,384]{1,0:T(8,128)(2,1)S(1)}, u32[]{:S(2)}, u32[]{:S(2)}) collective-permute-start(bf16[192,384]{1,0:T(8,128)(2,1)S(1)} %slice.398), channel_id=1, source_target_pairs={{0,16},{4,20},{8,24},{12,28},{16,0},{20,4},{24,8},{28,12},{1,17},{... | collective-permute-start | bytes 442376 | tf_op jit(solution)/shard_map/ppermute | solution.py:32
  152.9 5.8 %collective-permute-done.36 = bf16[192,384]{1,0:T(8,128)(2,1)S(1)} collective-permute-done((bf16[192,384]{1,0:T(8,128)(2,1)S(1)}, bf16[192,384]{1,0:T(8,128)(2,1)S(1)}, u32[]{:S(2)}, u32[]{:S(2)}) %collective-permute-start.36) | collective-permute-done | bytes 147488 | tf_op jit(solution)/shard_map/ppermute | solution.py:32
  158.8 1.5 collective-permute-start.37
  160.3 2.1 %fusion.32 = f32[384,768]{1,0:T(8,128)} fusion(f32[32,768]{1,0:T(8,128)S(1)} %get-tuple-element.20, f32[32,1152]{1,0:T(8,128)S(1)} %fusion.29), kind=kOutput, calls=%fused_computation.79 | convolution fusion | flops 113246208 | bytes 1327104 | tf_op jit(solution)/shard_map/dot_general | solution.py:368
  162.5 1.5 collective-permute-start.29
  164.5 1.5 collective-permute-start.33
  166.3 1.4 copy-done.9
  168.0 1.9 %convert_dynamic-update-slice_fusion.2 = f32[768,768]{1,0:T(8,128)} fusion(f32[768,768]{1,0:T(8,128)} %copy-done.9, s32[]{:T(128)S(6)} %select_n.317, bf16[192,384]{1,0:T(8,128)(2,1)S(1)} %collective-permute-done.29, bf16[192,384]{1,0:T(8,128)(2,1)} %collective-permute-done.28, pred[]{:T(512)S(6)} %eq.49), kind=kLoop, calls=%fused_computation.47 | loop fusion | flops 1474560 | bytes 884741 | tf_op jit(solution)/shard_map/dynamic_update_slice | solution.py:346
  169.9 1.9 %convert_dynamic-update-slice_fusion.1 = f32[768,768]{1,0:T(8,128)} fusion(f32[768,768]{1,0:T(8,128)} %convert_dynamic-update-slice_fusion.2, s32[]{:T(128)S(6)} %select_n.318, bf16[192,384]{1,0:T(8,128)(2,1)S(1)} %collective-permute-done.31, bf16[192,384]{1,0:T(8,128)(2,1)} %collective-permute-done.30, pred[]{:T(512)S(6)} %eq.49), kind=kLoop, calls=%fused_computation.46 | loop fusion | flops 1474560 | bytes 884741 | tf_op jit(solution)/shard_map/dynamic_update_slice | solution.py:346
  171.7 1.9 %convert_dynamic-update-slice_fusion = f32[768,768]{1,0:T(8,128)} fusion(f32[768,768]{1,0:T(8,128)} %convert_dynamic-update-slice_fusion.1, s32[]{:T(128)S(6)} %select_n.319, bf16[192,384]{1,0:T(8,128)(2,1)S(1)} %collective-permute-done.33, bf16[192,384]{1,0:T(8,128)(2,1)} %collective-permute-done.32, pred[]{:T(512)S(6)} %eq.49), kind=kLoop, calls=%fused_computation.45 | loop fusion | flops 1474560 | bytes 884741 | tf_op jit(solution)/shard_map/dynamic_update_slice | solution.py:346
  173.6 1.1 fusion.25
  (239 shorter events, 29.2 us)
Async XLA Ops:
  0.6 17.1 %copy-start = (bf16[768,768]{1,0:T(8,128)(2,1)S(1)}, bf16[768,768]{1,0:T(8,128)(2,1)}, u32[]{:S(2)}) copy-start(bf16[768,768]{1,0:T(8,128)(2,1)} %param.14) | copy-start | bytes 3538948
  0.6 15.1 %copy-start.23 = (s32[1,4,256]{2,1,0:T(4,128)S(1)}, s32[1,4,256]{2,1,0:T(4,128)}, u32[]{:S(2)}) copy-start(s32[1,4,256]{2,1,0:T(4,128)} %param.12) | copy-start | bytes 12292
  0.7 15.8 %copy-start.27 = (s32[4]{0:T(128)S(1)}, s32[4]{0:T(128)}, u32[]{:S(2)}) copy-start(s32[4]{0:T(128)} %param.21) | copy-start | bytes 52
  0.7 15.8 %copy-start.22 = (s32[1,8,256]{2,1,0:T(8,128)S(1)}, s32[1,8,256]{2,1,0:T(8,128)}, u32[]{:S(2)}) copy-start(s32[1,8,256]{2,1,0:T(8,128)} %param.17) | copy-start | bytes 24580
  2.1 1.0 copy-start.1
  4.1 12.1 %copy-start.2 = (bf16[1,1,256,768]{3,2,1,0:T(8,128)(2,1)S(1)}, bf16[1,1,256,768]{3,2,1,0:T(8,128)(2,1)}, u32[]{:S(2)}) copy-start(bf16[1,1,256,768]{3,2,1,0:T(8,128)(2,1)} %param.11) | copy-start | bytes 1179652
  4.6 29.0 %collective-permute-start.1 = (bf16[256,768]{1,0:T(8,128)(2,1)S(1)}, bf16[256,768]{1,0:T(8,128)(2,1)S(1)}, u32[]{:S(2)}, u32[]{:S(2)}) collective-permute-start(bf16[256,768]{1,0:T(8,128)(2,1)S(1)} %get-tuple-element.14), channel_id=1, source_target_pairs={{0,2},{1,3},{2,0},{3,1},{4,6},{5,7},{6,4},{7,5},{8,10},{9,11},{10,... | collective-permute-start | bytes 1179656 | tf_op jit(solution)/shard_map/ppermute | solution.py:32
  7.6 22.9 %collective-permute-start = (bf16[256,768]{1,0:T(8,128)(2,1)S(1)}, bf16[256,768]{1,0:T(8,128)(2,1)}, u32[]{:S(2)}, u32[]{:S(2)}) collective-permute-start(bf16[256,768]{1,0:T(8,128)(2,1)S(1)} %get-tuple-element.14), channel_id=1, source_target_pairs={{0,1},{1,0},{2,3},{3,2},{4,5},{5,4},{6,7},{7,6},{8,9},{9,8},{10,11... | collective-permute-start | bytes 1179656 | tf_op jit(solution)/shard_map/ppermute | solution.py:32
  7.6 27.2 %collective-permute-start.20 = (bf16[256,768]{1,0:T(8,128)(2,1)S(1)}, bf16[256,768]{1,0:T(8,128)(2,1)S(1)}, u32[]{:S(2)}, u32[]{:S(2)}) collective-permute-start(bf16[256,768]{1,0:T(8,128)(2,1)S(1)} %get-tuple-element.14), channel_id=1, source_target_pairs={{0,4},{4,0},{8,12},{12,8},{16,20},{20,16},{24,28},{28,24},{1,5},{5... | collective-permute-start | bytes 1179656 | tf_op jit(solution)/shard_map/ppermute | solution.py:32
  11.7 16.7 %collective-permute-start.11 = (bf16[192,768]{1,0:T(8,128)(2,1)}, bf16[192,768]{1,0:T(8,128)(2,1)}, u32[]{:S(2)}, u32[]{:S(2)}) collective-permute-start(bf16[192,768]{1,0:T(8,128)(2,1)} %pad_maximum_fusion.9), channel_id=1, source_target_pairs={{0,16},{4,20},{8,24},{12,28},{16,0},{20,4},{24,8},{28,12},{1,17},{... | collective-permute-start | bytes 884744 | tf_op jit(solution)/shard_map/ppermute | solution.py:32
  14.3 20.5 %collective-permute-start.8 = (bf16[256,768]{1,0:T(8,128)(2,1)S(1)}, bf16[256,768]{1,0:T(8,128)(2,1)}, u32[]{:S(2)}, u32[]{:S(2)}) collective-permute-start(bf16[256,768]{1,0:T(8,128)(2,1)S(1)} %get-tuple-element.15), channel_id=1, source_target_pairs={{0,4},{4,0},{8,12},{12,8},{16,20},{20,16},{24,28},{28,24},{1,5},{5... | collective-permute-start | bytes 1179656 | tf_op jit(solution)/shard_map/ppermute | solution.py:32
  28.4 12.2 %collective-permute-start.9 = (bf16[256,768]{1,0:T(8,128)(2,1)S(1)}, bf16[256,768]{1,0:T(8,128)(2,1)}, u32[]{:S(2)}, u32[]{:S(2)}) collective-permute-start(bf16[256,768]{1,0:T(8,128)(2,1)S(1)} %get-tuple-element.15), channel_id=1, source_target_pairs={{0,8},{4,12},{8,0},{12,4},{16,24},{20,28},{24,16},{28,20},{1,9},{5... | collective-permute-start | bytes 1179656 | tf_op jit(solution)/shard_map/ppermute | solution.py:32
  30.4 16.7 %collective-permute-start.10 = (bf16[256,768]{1,0:T(8,128)(2,1)S(1)}, bf16[256,768]{1,0:T(8,128)(2,1)S(1)}, u32[]{:S(2)}, u32[]{:S(2)}) collective-permute-start(bf16[256,768]{1,0:T(8,128)(2,1)S(1)} %get-tuple-element.15), channel_id=1, source_target_pairs={{0,12},{4,8},{8,4},{12,0},{16,28},{20,24},{24,20},{28,16},{1,13},{... | collective-permute-start | bytes 1179656 | tf_op jit(solution)/shard_map/ppermute | solution.py:32
  33.5 16.4 %copy-start.14 = (bf16[768,768]{1,0:T(8,128)(2,1)S(1)}, bf16[768,768]{1,0:T(8,128)(2,1)}, u32[]{:S(2)}) copy-start(bf16[768,768]{1,0:T(8,128)(2,1)} %param.13) | copy-start | bytes 3538948
  33.6 14.4 %collective-permute-start.12 = (bf16[1,192,768]{2,1,0:T(8,128)(2,1)}, bf16[1,192,768]{2,1,0:T(8,128)(2,1)S(1)}, u32[]{:S(2)}, u32[]{:S(2)}) collective-permute-start(bf16[1,192,768]{2,1,0:T(8,128)(2,1)} %bitcast.10), channel_id=1, source_target_pairs={{0,2},{1,3},{2,0},{3,1},{4,6},{5,7},{6,4},{7,5},{8,10},{9,11},{10,... | collective-permute-start | bytes 884744 | tf_op jit(solution)/shard_map/ppermute | solution.py:32
  34.8 14.4 %collective-permute-start.2 = (bf16[256,768]{1,0:T(8,128)(2,1)S(1)}, bf16[256,768]{1,0:T(8,128)(2,1)S(1)}, u32[]{:S(2)}, u32[]{:S(2)}) collective-permute-start(bf16[256,768]{1,0:T(8,128)(2,1)S(1)} %collective-permute-done.1), channel_id=1, source_target_pairs={{0,1},{1,0},{2,3},{3,2},{4,5},{5,4},{6,7},{7,6},{8,9},{9,8},{10,11... | collective-permute-start | bytes 1179656 | tf_op jit(solution)/shard_map/ppermute | solution.py:32
  34.8 24.6 %collective-permute-start.21 = (bf16[256,768]{1,0:T(8,128)(2,1)S(1)}, bf16[256,768]{1,0:T(8,128)(2,1)}, u32[]{:S(2)}, u32[]{:S(2)}) collective-permute-start(bf16[256,768]{1,0:T(8,128)(2,1)S(1)} %collective-permute-done.20), channel_id=1, source_target_pairs={{0,1},{1,0},{2,3},{3,2},{4,5},{5,4},{6,7},{7,6},{8,9},{9,8},{10,11... | collective-permute-start | bytes 1179656 | tf_op jit(solution)/shard_map/ppermute | solution.py:32
  40.5 18.3 %collective-permute-start.22 = (bf16[256,768]{1,0:T(8,128)(2,1)S(1)}, bf16[256,768]{1,0:T(8,128)(2,1)}, u32[]{:S(2)}, u32[]{:S(2)}) collective-permute-start(bf16[256,768]{1,0:T(8,128)(2,1)S(1)} %collective-permute-done.20), channel_id=1, source_target_pairs={{0,2},{1,3},{2,0},{3,1},{4,6},{5,7},{6,4},{7,5},{8,10},{9,11},{10,... | collective-permute-start | bytes 1179656 | tf_op jit(solution)/shard_map/ppermute | solution.py:32
  49.1 26.6 %collective-permute-start.13 = (bf16[2,192,768]{2,1,0:T(8,128)(2,1)S(1)}, bf16[2,192,768]{2,1,0:T(8,128)(2,1)}, u32[]{:S(2)}, u32[]{:S(2)}) collective-permute-start(bf16[2,192,768]{2,1,0:T(8,128)(2,1)S(1)} %maximum_select_fusion.1), channel_id=1, source_target_pairs={{0,1},{1,0},{2,3},{3,2},{4,5},{5,4},{6,7},{7,6},{8,9},{9,8},{10,11... | collective-permute-start | bytes 1769480 | tf_op jit(solution)/shard_map/ppermute | solution.py:32
  53.2 6.0 %copy-start.25 = (pred[4]{0:T(512)(128)(4,1)S(1)}, pred[4]{0:T(512)(128)(4,1)}, u32[]{:S(2)}) copy-start(pred[4]{0:T(512)(128)(4,1)} %iota_compare_fusion.1) | copy-start | bytes 16
  53.2 8.0 %copy-start.20 = (f32[4,1]{1,0:T(4,128)S(1)}, f32[4,1]{1,0:T(4,128)}, u32[]{:S(2)}) copy-start(f32[4,1]{1,0:T(4,128)} %copy.24) | copy-start | bytes 52
  53.2 8.0 %copy-start.21 = (f32[4,1]{1,0:T(4,128)S(1)}, f32[4,1]{1,0:T(4,128)}, u32[]{:S(2)}) copy-start(f32[4,1]{1,0:T(4,128)} %copy.23) | copy-start | bytes 52
  54.5 12.5 %copy-start.26 = (f32[4]{0:T(128)S(1)}, f32[4]{0:T(128)}, u32[]{:S(2)}) copy-start(f32[4]{0:T(128)} %slice_bitcast_fusion) | copy-start | bytes 52
  54.5 18.4 %copy-start.4 = (bf16[1,1,256,768]{3,2,1,0:T(8,128)(2,1)S(1)}, bf16[1,1,256,768]{3,2,1,0:T(8,128)(2,1)}, u32[]{:S(2)}) copy-start(bf16[1,1,256,768]{3,2,1,0:T(8,128)(2,1)} %param.16) | copy-start | bytes 1179652
  55.5 3.7 %collective-permute-start.3 = (f32[4,768]{1,0:T(4,128)S(1)}, f32[4,768]{1,0:T(4,128)S(1)}, u32[]{:S(2)}, u32[]{:S(2)}) collective-permute-start(f32[4,768]{1,0:T(4,128)S(1)} %fusion.52), channel_id=1, source_target_pairs={{0,2},{1,3},{2,0},{3,1},{4,6},{5,7},{6,4},{7,5},{8,10},{9,11},{10,... | collective-permute-start | bytes 36872 | tf_op jit(solution)/shard_map/ppermute | solution.py:32
  58.9 41.1 %collective-permute-start.23 = (bf16[256,768]{1,0:T(8,128)(2,1)}, bf16[256,768]{1,0:T(8,128)(2,1)}, u32[]{:S(2)}, u32[]{:S(2)}) collective-permute-start(bf16[256,768]{1,0:T(8,128)(2,1)} %collective-permute-done.22), channel_id=1, source_target_pairs={{0,1},{1,0},{2,3},{3,2},{4,5},{5,4},{6,7},{7,6},{8,9},{9,8},{10,11... | collective-permute-start | bytes 1179656 | tf_op jit(solution)/shard_map/ppermute | solution.py:32
  59.3 1.9 %collective-permute-start.4 = (f32[4,768]{1,0:T(4,128)S(1)}, f32[4,768]{1,0:T(4,128)S(1)}, u32[]{:S(2)}, u32[]{:S(2)}) collective-permute-start(f32[4,768]{1,0:T(4,128)S(1)} %fusion.87), channel_id=1, source_target_pairs={{0,1},{1,0},{2,3},{3,2},{4,5},{5,4},{6,7},{7,6},{8,9},{9,8},{10,11... | collective-permute-start | bytes 36872 | tf_op jit(solution)/shard_map/ppermute | solution.py:32
  61.4 3.9 %collective-permute-start.5 = (f32[4,1664]{1,0:T(4,128)S(1)}, f32[4,1664]{1,0:T(4,128)S(1)}, u32[]{:S(2)}, u32[]{:S(2)}) collective-permute-start(f32[4,1664]{1,0:T(4,128)S(1)} %concatenate.156), channel_id=1, source_target_pairs={{0,4},{4,0},{8,12},{12,8},{16,20},{20,16},{24,28},{28,24},{1,5},{5... | collective-permute-start | bytes 79880 | tf_op jit(solution)/shard_map/ppermute | solution.py:32
  65.8 4.2 %collective-permute-start.6 = (f32[8,1664]{1,0:T(8,128)S(1)}, f32[8,1664]{1,0:T(8,128)S(1)}, u32[]{:S(2)}, u32[]{:S(2)}) collective-permute-start(f32[8,1664]{1,0:T(8,128)S(1)} %maximum_select_fusion.12), channel_id=1, source_target_pairs={{0,8},{4,12},{8,0},{12,4},{16,24},{20,28},{24,16},{28,20},{1,9},{5... | collective-permute-start | bytes 159752 | tf_op jit(solution)/shard_map/ppermute | solution.py:32
  70.0 5.7 %collective-permute-start.7 = (f32[16,1664]{1,0:T(8,128)S(1)}, f32[16,1664]{1,0:T(8,128)S(1)}, u32[]{:S(2)}, u32[]{:S(2)}) collective-permute-start(f32[16,1664]{1,0:T(8,128)S(1)} %maximum_select_fusion.10), channel_id=1, source_target_pairs={{0,16},{4,20},{8,24},{12,28},{16,0},{20,4},{24,8},{28,12},{1,17},{... | collective-permute-start | bytes 319496 | tf_op jit(solution)/shard_map/ppermute | solution.py:32
  77.1 1.4 copy-start.7
  77.1 1.5 copy-start.11
  78.7 4.9 %copy-start.24 = (pred[4]{0:T(512)(128)(4,1)S(1)}, pred[4]{0:T(512)(128)(4,1)}, u32[]{:S(2)}) copy-start(pred[4]{0:T(512)(128)(4,1)} %iota_compare_fusion) | copy-start | bytes 16
  83.6 3.7 %collective-permute-start.14 = (f32[4,768]{1,0:T(4,128)S(1)}, f32[4,768]{1,0:T(4,128)S(1)}, u32[]{:S(2)}, u32[]{:S(2)}) collective-permute-start(f32[4,768]{1,0:T(4,128)S(1)} %fusion.50), channel_id=1, source_target_pairs={{0,4},{4,0},{8,12},{12,8},{16,20},{20,16},{24,28},{28,24},{1,5},{5... | collective-permute-start | bytes 36872 | tf_op jit(solution)/shard_map/ppermute | solution.py:32
  85.0 3.8 %collective-permute-start.15 = (f32[4,768]{1,0:T(4,128)S(1)}, f32[4,768]{1,0:T(4,128)S(1)}, u32[]{:S(2)}, u32[]{:S(2)}) collective-permute-start(f32[4,768]{1,0:T(4,128)S(1)} %fusion.50), channel_id=1, source_target_pairs={{0,8},{4,12},{8,0},{12,4},{16,24},{20,28},{24,16},{28,20},{1,9},{5... | collective-permute-start | bytes 36872 | tf_op jit(solution)/shard_map/ppermute | solution.py:32
  87.1 4.6 %collective-permute-start.16 = (f32[4,768]{1,0:T(4,128)S(1)}, f32[4,768]{1,0:T(4,128)S(1)}, u32[]{:S(2)}, u32[]{:S(2)}) collective-permute-start(f32[4,768]{1,0:T(4,128)S(1)} %fusion.50), channel_id=1, source_target_pairs={{0,12},{4,8},{8,4},{12,0},{16,28},{20,24},{24,20},{28,16},{1,13},{... | collective-permute-start | bytes 36872 | tf_op jit(solution)/shard_map/ppermute | solution.py:32
  91.8 5.2 %collective-permute-start.17 = (f32[4,1152]{1,0:T(4,128)S(1)}, f32[4,1152]{1,0:T(4,128)S(1)}, u32[]{:S(2)}, u32[]{:S(2)}) collective-permute-start(f32[4,1152]{1,0:T(4,128)S(1)} %get-tuple-element.50), channel_id=1, source_target_pairs={{0,16},{4,20},{8,24},{12,28},{16,0},{20,4},{24,8},{28,12},{1,17},{... | collective-permute-start | bytes 55304 | tf_op jit(solution)/shard_map/ppermute | solution.py:32
  97.0 8.5 %copy-start.5 = (f32[1024,768]{1,0:T(8,128)S(1)}, f32[1024,768]{1,0:T(8,128)}, u32[]{:S(2)}) copy-start(f32[1024,768]{1,0:T(8,128)} %get-tuple-element.65) | copy-start | bytes 9437188
  97.1 1.4 collective-permute-start.18
  98.5 4.6 %collective-permute-start.19 = (f32[2,8,1152]{2,1,0:T(8,128)S(1)}, f32[2,8,1152]{2,1,0:T(8,128)S(1)}, u32[]{:S(2)}, u32[]{:S(2)}) collective-permute-start(f32[2,8,1152]{2,1,0:T(8,128)S(1)} %maximum_select_fusion.11), channel_id=1, source_target_pairs={{0,2},{1,3},{2,0},{3,1},{4,6},{5,7},{6,4},{7,5},{8,10},{9,11},{10,... | collective-permute-start | bytes 221192 | tf_op jit(solution)/shard_map/ppermute | solution.py:32
  105.6 1.9 %copy-start.8 = (bf16[1024,768]{1,0:T(8,128)(2,1)S(1)}, bf16[1024,768]{1,0:T(8,128)(2,1)}, u32[]{:S(2)}) copy-start(bf16[1024,768]{1,0:T(8,128)(2,1)} %constant_dynamic-update-slice_fusion) | copy-start | bytes 4718596
  105.6 1.9 %copy-start.12 = (bf16[768,384]{1,0:T(8,128)(2,1)S(1)}, bf16[768,384]{1,0:T(8,128)(2,1)}, u32[]{:S(2)}) copy-start(bf16[768,384]{1,0:T(8,128)(2,1)} %param.18) | copy-start | bytes 1769476
  107.5 1.9 %copy-start.6 = (bf16[2048,768]{1,0:T(8,128)(2,1)S(1)}, bf16[2048,768]{1,0:T(8,128)(2,1)}, u32[]{:S(2)}) copy-start(bf16[2048,768]{1,0:T(8,128)(2,1)} %constant_dynamic-update-slice_fusion.4) | copy-start | bytes 9437188
  107.5 2.2 %copy-start.15 = (bf16[768,768]{1,0:T(8,128)(2,1)S(1)}, bf16[768,768]{1,0:T(8,128)(2,1)}, u32[]{:S(2)}) copy-start(bf16[768,768]{1,0:T(8,128)(2,1)} %param.13) | copy-start | bytes 3538948
  109.1 3.7 %copy-start.10 = (f32[768,768]{1,0:T(8,128)}, f32[768,768]{1,0:T(8,128)S(1)}, u32[]{:S(2)}) copy-start(f32[768,768]{1,0:T(8,128)S(1)} %get-tuple-element.67) | copy-start | bytes 7077892
  109.1 31.7 %collective-permute-start.34 = (bf16[384,768]{1,0:T(8,128)(2,1)S(1)}, bf16[384,768]{1,0:T(8,128)(2,1)S(1)}, u32[]{:S(2)}, u32[]{:S(2)}) collective-permute-start(bf16[384,768]{1,0:T(8,128)(2,1)S(1)} %dynamic-slice_convert_fusion), channel_id=1, source_target_pairs={{0,1},{1,0},{2,3},{3,2},{4,5},{5,4},{6,7},{7,6},{8,9},{9,8},{10,11... | collective-permute-start | bytes 1769480 | tf_op jit(solution)/shard_map/ppermute | solution.py:32
  112.8 3.1 %copy-start.18 = (f32[768]{0:T(1024)S(1)}, f32[768]{0:T(1024)}, u32[]{:S(2)}) copy-start(f32[768]{0:T(1024)} %param.15) | copy-start | bytes 9220
  112.8 3.1 %copy-start.19 = (f32[768]{0:T(1024)S(1)}, f32[768]{0:T(1024)}, u32[]{:S(2)}) copy-start(f32[768]{0:T(1024)} %param.20) | copy-start | bytes 9220
  117.1 9.6 %collective-permute-start.24 = (bf16[208,384]{1,0:T(8,128)(2,1)S(1)}, bf16[208,384]{1,0:T(8,128)(2,1)S(1)}, u32[]{:S(2)}, u32[]{:S(2)}) collective-permute-start(bf16[208,384]{1,0:T(8,128)(2,1)S(1)} %get-tuple-element.46), channel_id=1, source_target_pairs={{0,8},{4,12},{8,0},{12,4},{16,24},{20,28},{24,16},{28,20},{1,9},{5... | collective-permute-start | bytes 479240 | tf_op jit(solution)/shard_map/ppermute | solution.py:32
  117.2 9.5 %collective-permute-start.25 = (bf16[208,384]{1,0:T(8,128)(2,1)S(1)}, bf16[208,384]{1,0:T(8,128)(2,1)S(1)}, u32[]{:S(2)}, u32[]{:S(2)}) collective-permute-start(bf16[208,384]{1,0:T(8,128)(2,1)S(1)} %get-tuple-element.47), channel_id=1, source_target_pairs={{0,16},{4,20},{8,24},{12,28},{16,0},{20,4},{24,8},{28,12},{1,17},{... | collective-permute-start | bytes 479240 | tf_op jit(solution)/shard_map/ppermute | solution.py:32
  120.2 12.4 %collective-permute-start.26 = (bf16[208,384]{1,0:T(8,128)(2,1)S(1)}, bf16[208,384]{1,0:T(8,128)(2,1)S(1)}, u32[]{:S(2)}, u32[]{:S(2)}) collective-permute-start(bf16[208,384]{1,0:T(8,128)(2,1)S(1)} %get-tuple-element.48), channel_id=1, source_target_pairs={{0,24},{4,28},{8,16},{12,20},{16,8},{20,12},{24,0},{28,4},{1,25},{... | collective-permute-start | bytes 479240 | tf_op jit(solution)/shard_map/ppermute | solution.py:32
  133.6 28.9 %collective-permute-start.28 = (bf16[192,384]{1,0:T(8,128)(2,1)S(1)}, bf16[192,384]{1,0:T(8,128)(2,1)}, u32[]{:S(2)}, u32[]{:S(2)}) collective-permute-start(bf16[192,384]{1,0:T(8,128)(2,1)S(1)} %add_convert_fusion), channel_id=1, source_target_pairs={{0,8},{4,12},{8,0},{12,4},{16,24},{20,28},{24,16},{28,20},{1,9},{5... | collective-permute-start | bytes 442376 | tf_op jit(solution)/shard_map/ppermute | solution.py:32
  136.8 27.2 %collective-permute-start.30 = (bf16[192,384]{1,0:T(8,128)(2,1)S(1)}, bf16[192,384]{1,0:T(8,128)(2,1)}, u32[]{:S(2)}, u32[]{:S(2)}) collective-permute-start(bf16[192,384]{1,0:T(8,128)(2,1)S(1)} %add_convert_fusion), channel_id=1, source_target_pairs={{0,16},{4,20},{8,24},{12,28},{16,0},{20,4},{24,8},{28,12},{1,17},{... | collective-permute-start | bytes 442376 | tf_op jit(solution)/shard_map/ppermute | solution.py:32
  138.7 25.8 %collective-permute-start.32 = (bf16[192,384]{1,0:T(8,128)(2,1)S(1)}, bf16[192,384]{1,0:T(8,128)(2,1)}, u32[]{:S(2)}, u32[]{:S(2)}) collective-permute-start(bf16[192,384]{1,0:T(8,128)(2,1)S(1)} %add_convert_fusion), channel_id=1, source_target_pairs={{0,24},{4,28},{8,16},{12,20},{16,8},{20,12},{24,0},{28,4},{1,25},{... | collective-permute-start | bytes 442376 | tf_op jit(solution)/shard_map/ppermute | solution.py:32
  140.3 5.3 %collective-permute-start.27 = (bf16[208,384]{1,0:T(8,128)(2,1)S(1)}, bf16[208,384]{1,0:T(8,128)(2,1)S(1)}, u32[]{:S(2)}, u32[]{:S(2)}) collective-permute-start(bf16[208,384]{1,0:T(8,128)(2,1)S(1)} %pad_maximum_fusion.4), channel_id=1, source_target_pairs={{0,4},{4,0},{8,12},{12,8},{16,20},{20,16},{24,28},{28,24},{1,5},{5... | collective-permute-start | bytes 479240 | tf_op jit(solution)/shard_map/ppermute | solution.py:32
  142.3 7.7 %collective-permute-start.35 = (bf16[192,768]{1,0:T(8,128)(2,1)S(1)}, bf16[192,768]{1,0:T(8,128)(2,1)}, u32[]{:S(2)}, u32[]{:S(2)}) collective-permute-start(bf16[192,768]{1,0:T(8,128)(2,1)S(1)} %dynamic-slice_convert_fusion.1), channel_id=1, source_target_pairs={{0,2},{1,3},{2,0},{3,1},{4,6},{5,7},{6,4},{7,5},{8,10},{9,11},{10,... | collective-permute-start | bytes 884744 | tf_op jit(solution)/shard_map/ppermute | solution.py:32
  151.1 14.9 %copy-start.17 = (bf16[208,384]{1,0:T(8,128)(2,1)S(1)}, bf16[208,384]{1,0:T(8,128)(2,1)}, u32[]{:S(2)}) copy-start(bf16[208,384]{1,0:T(8,128)(2,1)} %copy-done.16) | copy-start | bytes 479236
  151.1 7.7 %collective-permute-start.36 = (bf16[192,384]{1,0:T(8,128)(2,1)S(1)}, bf16[192,384]{1,0:T(8,128)(2,1)S(1)}, u32[]{:S(2)}, u32[]{:S(2)}) collective-permute-start(bf16[192,384]{1,0:T(8,128)(2,1)S(1)} %slice.398), channel_id=1, source_target_pairs={{0,16},{4,20},{8,24},{12,28},{16,0},{20,4},{24,8},{28,12},{1,17},{... | collective-permute-start | bytes 442376 | tf_op jit(solution)/shard_map/ppermute | solution.py:32
  158.8 7.4 %collective-permute-start.37 = (bf16[208,384]{1,0:T(8,128)(2,1)S(1)}, bf16[208,384]{1,0:T(8,128)(2,1)S(1)}, u32[]{:S(2)}, u32[]{:S(2)}) collective-permute-start(bf16[208,384]{1,0:T(8,128)(2,1)S(1)} %pad_maximum_fusion.3), channel_id=1, source_target_pairs={{0,2},{1,3},{2,0},{3,1},{4,6},{5,7},{6,4},{7,5},{8,10},{9,11},{10,... | collective-permute-start | bytes 479240 | tf_op jit(solution)/shard_map/ppermute | solution.py:32
  162.5 5.5 %collective-permute-start.29 = (bf16[192,384]{1,0:T(8,128)(2,1)}, bf16[192,384]{1,0:T(8,128)(2,1)S(1)}, u32[]{:S(2)}, u32[]{:S(2)}) collective-permute-start(bf16[192,384]{1,0:T(8,128)(2,1)} %collective-permute-done.28), channel_id=1, source_target_pairs={{0,4},{4,0},{8,12},{12,8},{16,20},{20,16},{24,28},{28,24},{1,5},{5... | collective-permute-start | bytes 442376 | tf_op jit(solution)/shard_map/ppermute | solution.py:32
  164.0 5.9 %collective-permute-start.31 = (bf16[192,384]{1,0:T(8,128)(2,1)}, bf16[192,384]{1,0:T(8,128)(2,1)S(1)}, u32[]{:S(2)}, u32[]{:S(2)}) collective-permute-start(bf16[192,384]{1,0:T(8,128)(2,1)} %collective-permute-done.30), channel_id=1, source_target_pairs={{0,4},{4,0},{8,12},{12,8},{16,20},{20,16},{24,28},{28,24},{1,5},{5... | collective-permute-start | bytes 442376 | tf_op jit(solution)/shard_map/ppermute | solution.py:32
  164.5 7.2 %collective-permute-start.33 = (bf16[192,384]{1,0:T(8,128)(2,1)}, bf16[192,384]{1,0:T(8,128)(2,1)S(1)}, u32[]{:S(2)}, u32[]{:S(2)}) collective-permute-start(bf16[192,384]{1,0:T(8,128)(2,1)} %collective-permute-done.32), channel_id=1, source_target_pairs={{0,4},{4,0},{8,12},{12,8},{16,20},{20,16},{24,28},{28,24},{1,5},{5... | collective-permute-start | bytes 442376 | tf_op jit(solution)/shard_map/ppermute | solution.py:32
  166.3 1.4 copy-start.9
  167.9 5.7 %collective-permute-start.38 = (bf16[400,384]{1,0:T(8,128)(2,1)S(1)}, bf16[400,384]{1,0:T(8,128)(2,1)S(1)}, u32[]{:S(2)}, u32[]{:S(2)}) collective-permute-start(bf16[400,384]{1,0:T(8,128)(2,1)S(1)} %pad_maximum_fusion.8), channel_id=1, source_target_pairs={{0,1},{1,0},{2,3},{3,2},{4,5},{5,4},{6,7},{7,6},{8,9},{9,8},{10,11... | collective-permute-start | bytes 921608 | tf_op jit(solution)/shard_map/ppermute | solution.py:32
  (3 other events, 2.4 us)

commit v3 on v2

v3 whole, which is shorter than its diff:
```python
import functools
import math

import jax
import jax.numpy as jnp
from jax import lax
from jax.experimental import pallas as pl
from jax.experimental.pallas import tpu as pltpu
from jax.sharding import PartitionSpec as P

HIGH = lax.Precision.HIGHEST
F32 = jnp.float32
BF16 = jnp.bfloat16
CONTRACT_FIRST = (((0,), (0,)), ((), ()))
CONTRACT_LAST = (((1,), (1,)), ((), ()))
GROUP = 4
PARTS = 4
GAIN_ROWS = 16
ROOT_HALF = 1.0 / math.sqrt(2.0)
VMEM = pl.BlockSpec(memory_space=pltpu.VMEM)
SMEM = pl.BlockSpec(memory_space=pltpu.SMEM)
HBM = pl.BlockSpec(memory_space=pltpu.HBM)
LOAD = "load"


def call(body, in_specs, out_shape, scratch=(), limit=16, flops=0, bytes_accessed=0):
    loads = [i for i, spec in enumerate(in_specs) if spec is LOAD]
    n_in, n_own = len(in_specs), len(out_shape) + len(scratch)

    def kernel(*refs):
        ins, rest = list(refs[:n_in]), refs[n_in:]
        copies = []
        for j, i in enumerate(loads):
            buffer = rest[n_own + j]
            copies.append(pltpu.make_async_copy(ins[i], buffer, rest[-1].at[j]))
            ins[i] = buffer
        for copy in copies:
            copy.start()
        for copy in copies:
            copy.wait()
        body(*ins, *rest[:n_own])

    def run(*args):
        buffers = [pltpu.VMEM(args[i].shape, args[i].dtype) for i in loads]
        if loads:
            buffers.append(pltpu.SemaphoreType.DMA((len(loads),)))
        return pl.pallas_call(
            kernel,
            in_specs=[HBM if spec is LOAD else spec for spec in in_specs],
            out_shape=tuple(jax.ShapeDtypeStruct(s, t) for s, t in out_shape),
            out_specs=tuple(VMEM for _ in out_shape),
            scratch_shapes=list(scratch) + buffers,
            cost_estimate=pl.CostEstimate(
                flops=flops, bytes_accessed=bytes_accessed, transcendentals=0
            ),
            compiler_params=pltpu.CompilerParams(vmem_limit_bytes=limit * 1024 * 1024),
        )(*args)

    return run


def gelu_value(v):
    return 0.5 * v * (1.0 + lax.erf(v * ROOT_HALF))


def gelu_slope(v):
    return 0.5 * (1.0 + lax.erf(v * ROOT_HALF)) + v * jnp.exp(-0.5 * v * v) * (
        1.0 / math.sqrt(2.0 * math.pi)
    )


def swap(x, axis, step):
    size = lax.axis_size(axis)
    return lax.ppermute(x, axis, [(i, i ^ step) for i in range(size)])


def ordered(mine, other, bit, axis=0):
    return jnp.where(
        bit == 0,
        jnp.concatenate([mine, other], axis),
        jnp.concatenate([other, mine], axis),
    )


def bits_of(size):
    return [1 << i for i in range(size.bit_length() - 1)]


def bit_at(place, step):
    return jnp.where((place & step) != 0, 1, 0)


def canonical(rows, place):
    rows = list(rows)
    for step in bits_of(len(rows)):
        odd = (place & step) != 0
        for k in range(len(rows)):
            if not k & step:
                first, second = rows[k], rows[k + step]
                rows[k] = jnp.where(odd, second, first)
                rows[k + step] = jnp.where(odd, first, second)
    return jnp.concatenate(rows, 0)


def together(*values):
    return lax.optimization_barrier(values)


def pack(gains, columns):
    high = lax.reduce_precision(gains, 8, 7)
    parts = jnp.concatenate([high, gains - high], 0).astype(BF16).reshape(-1, columns)
    return jnp.concatenate([parts, jnp.zeros((-parts.shape[0] % 16, columns), BF16)], 0)


def unpack(rows, width):
    parts = rows[: 4 * width // rows.shape[1]].reshape(4, width).astype(F32)
    return parts[:2] + parts[2:]


def column_tiles(size):
    tile = 256 if size % 256 == 0 else size
    return [slice(c, c + tile) for c in range(0, size, tile)]


def run_mask(rows, offset, length):
    return lax.broadcasted_iota(jnp.int32, (rows, 1), 0) + offset < length


def product(x, weight):
    return jnp.dot(x, weight, preferred_element_type=F32)


def rms_rows(x_ref, gain, out):
    x = x_ref[...].astype(F32)
    xhat = x * lax.rsqrt(jnp.mean(x * x, axis=-1, keepdims=True) + 1e-06)
    out[...] = (xhat * gain[...][None, :]).astype(BF16)


def prepare_kernel(
    fold,
    place,
    q_hbm,
    s_hbm,
    q_gain,
    s_gain,
    inner,
    outer,
    q_out,
    s_out,
    piece,
    q_ref,
    s_ref,
    sems,
):
    thin = inner.shape[0] // PARTS // fold
    block = inner.shape[1]
    rows = outer.shape[0] // PARTS
    index = place[2]
    tokens = [
        pltpu.make_async_copy(s_hbm, s_ref, sems.at[0]),
        pltpu.make_async_copy(q_hbm, q_ref, sems.at[1]),
    ]
    copies = []
    for i in range(fold):
        first = pl.multiple_of(index * (thin * fold) + i * thin, 16)
        copies.append(
            pltpu.make_async_copy(
                inner.at[pl.ds(first, thin), :],
                piece.at[pl.ds(0, thin), pl.ds(i * block, block)],
                sems.at[2 + i],
            )
        )
    copies.append(
        pltpu.make_async_copy(
            outer.at[pl.ds(pl.multiple_of(index * rows, 16), rows), :],
            piece.at[pl.ds(thin, rows), :],
            sems.at[2 + fold],
        )
    )
    for copy in tokens + copies:
        copy.start()
    tokens[0].wait()
    rms_rows(s_ref, s_gain, s_out)
    tokens[1].wait()
    x = q_ref[...].astype(F32)
    x = x - jnp.mean(x, axis=-1, keepdims=True)
    xhat = x * lax.rsqrt(jnp.mean(x * x, axis=-1, keepdims=True) + 1e-05)
    q_out[...] = (xhat * q_gain[...][None, :]).astype(BF16)
    for copy in copies:
        copy.wait()


def norm_only_kernel(q_ref, s_ref, q_gain, s_gain, q_out, s_out):
    rms_rows(s_ref, s_gain, s_out)
    x = q_ref[...].astype(F32)
    x = x - jnp.mean(x, axis=-1, keepdims=True)
    xhat = x * lax.rsqrt(jnp.mean(x * x, axis=-1, keepdims=True) + 1e-05)
    q_out[...] = (xhat * q_gain[...][None, :]).astype(BF16)


def prepare(place, own_q, own_s, q_gain, s_gain, inner, outer):
    width, block = inner.shape
    fold = width // block
    thin = width // PARTS // fold
    rows = block // PARTS
    if block % 128 == 0:
        return call(
            functools.partial(prepare_kernel, fold),
            [SMEM] + [HBM] * 2 + [LOAD] * 2 + [HBM] * 2,
            [(own_q.shape, BF16), (own_s.shape, BF16), ((thin + rows, width), BF16)],
            [
                pltpu.VMEM(own_q.shape, BF16),
                pltpu.VMEM(own_s.shape, BF16),
                pltpu.SemaphoreType.DMA((fold + 3,)),
            ],
        )(place, own_q, own_s, q_gain, s_gain, inner, outer)
    piece = lax.dynamic_slice_in_dim(inner, place[2] * (thin * fold), thin * fold, 0)
    piece = jnp.concatenate([piece[i * thin : (i + 1) * thin] for i in range(fold)], 1)
    other = lax.dynamic_slice_in_dim(outer, place[2] * rows, rows, 0)
    normed = call(norm_only_kernel, [VMEM] * 4, [(own_q.shape, BF16), (own_s.shape, BF16)])(
        own_q, own_s, q_gain, s_gain
    )
    return *normed, jnp.concatenate([piece, other], 0)


def gather_rows(token_refs, rows, sems):
    copies = []
    first = 0
    for i, token in enumerate(token_refs):
        count = token.shape[0]
        copies.append(pltpu.make_async_copy(token, rows.at[pl.ds(first, count), :], sems.at[i]))
        first += count
    for copy in copies:
        copy.start()
    for copy in copies:
        copy.wait()


def forward_kernel(n, far, axis, *refs):
    place, lengths, own = refs[:3]
    token_refs, refs = refs[3 : 3 + n], refs[3 + n :]
    inners, outers = [refs[0]], [refs[1]]
    pieces = refs[2 : 2 + PARTS * far]
    refs = refs[2 + PARTS * far :]
    pooled, part, rows = refs[:3]
    gather_rows(token_refs, rows, refs[-1])
    me = place[axis]
    y, core = place[3], place[4]
    places = (
        core * 2 + y,
        core * 2 + (1 - y),
        (1 - core) * 2 + y,
        (1 - core) * 2 + (1 - y),
    )
    for f in range(far):
        inner, outer = refs[3 + 2 * f : 5 + 2 * f]
        block = inner.shape[1]
        fold = inner.shape[0] // block
        thin = inner.shape[0] // PARTS // fold
        deep = block // PARTS
        for j in range(PARTS):
            piece = pieces[PARTS * f + j]
            for i in range(fold):
                first = pl.multiple_of(places[j] * (thin * fold) + i * thin, 16)
                inner[pl.ds(first, thin), :] = piece[:thin, i * block : (i + 1) * block]
            first = pl.multiple_of(places[j] * deep, 16)
            outer[pl.ds(first, deep), :] = piece[thin:, :]
        inners.append(inner)
        outers.append(outer)
    total = part.shape[0]
    span = own.shape[0]
    index = lax.broadcasted_iota(jnp.int32, (total, 1), 0)
    base = 0
    for inner in inners:
        for columns in column_tiles(inner.shape[1]):
            weight = inner[:, columns]
            tile = jnp.zeros((total, weight.shape[1]), F32)
            for k in range(total):
                length = lengths[me ^ k]
                value = gelu_value(product(rows[k * span : (k + 1) * span, :], weight))
                value = jnp.where(run_mask(span, 0, length), value, 0.0)
                row = jnp.sum(value, axis=0, keepdims=True) / length.astype(F32)
                tile = jnp.where(index == ((me ^ k) & (total - 1)), row, tile)
            pooled[:, base + columns.start : base + columns.stop] = tile
        base += inner.shape[1]
    x = own[...].astype(F32)
    length = lengths[me]
    x = jnp.where(run_mask(span, 0, length), x, 0.0)
    own_row = jnp.sum(x, axis=0, keepdims=True) / length.astype(F32)
    result = jnp.where(index == (me & (total - 1)), own_row, 0.0)
    base = 0
    for outer in outers:
        units = pooled[:, base : base + outer.shape[0]]
        high = units.astype(BF16)
        rest = units - high.astype(F32)
        middle = rest.astype(BF16)
        low = (rest - middle.astype(F32)).astype(BF16)
        weight = outer[...]
        result = result + (
            product(high, weight) + (product(middle, weight) + product(low, weight))
        )
        base += outer.shape[0]
    part[...] = result


def forward(place, lengths, own, tokens, inner, outer, pieces, axis):
    width, units = inner.shape
    far = len(pieces) // PARTS
    rows = sum(t.shape[0] for t in tokens)
    count = rows // own.shape[0]
    return call(
        functools.partial(forward_kernel, len(tokens), far, axis),
        [SMEM] * 2 + [LOAD] + [HBM] * len(tokens) + [LOAD] * (2 + len(pieces)),
        [((count, units * (1 + far)), F32), ((count, width), F32), ((rows, width), BF16)]
        + [((width, units), BF16), ((units, width), BF16)] * far,
        [pltpu.SemaphoreType.DMA((len(tokens),))],
        flops=3 * 10**9,
        bytes_accessed=3 * 10**6,
    )(place, lengths, own, *tokens, inner, outer, *pieces)


def slope_kernel(n, axis, span, gathered, place, lengths, *refs):
    token_refs = refs[:n]
    if gathered:
        weights, out, rows = refs[n:-3], refs[-3], refs[-2]
        gather_rows(token_refs, rows, refs[-1])
    else:
        weights, out, rows = refs[n:-1], refs[-1], token_refs[0]
    me = place[axis] & (lengths.shape[0] - 1)
    base = 0
    for weight in weights:
        for columns in column_tiles(weight.shape[1]):
            w = weight[:, columns]
            for k in range(out.shape[0] // span):
                length = lengths[me ^ k]
                part = slice(k * span, (k + 1) * span)
                value = gelu_slope(product(rows[part, :], w)) * (1.0 / length.astype(F32))
                value = jnp.where(run_mask(span, 0, length), value, 0.0)
                out[part, base + columns.start : base + columns.stop] = value
        base += weight.shape[1]


def slopes(place, lengths, tokens, weights, axis, span):
    gathered = len(tokens) > 1
    rows = sum(t.shape[0] for t in tokens)
    width, units = weights[0].shape[0], sum(w.shape[1] for w in weights)
    return call(
        functools.partial(slope_kernel, len(tokens), axis, span, gathered),
        [SMEM] * 2 + [HBM if gathered else VMEM] * len(tokens) + [VMEM] * len(weights),
        [((rows, units), F32)] + [((rows, width), BF16)] * gathered,
        [pltpu.SemaphoreType.DMA((len(tokens),))] * gathered,
        flops=3 * rows * units * width,
        bytes_accessed=3 * 10**6,
    )(place, lengths, *tokens, *weights)


def inner_gradient(row_refs, slope_refs, hidden, weights, gain, total, span):
    base = 0
    gains = jnp.zeros((total.shape[0], 128), F32)
    for weight in weights:
        for columns in column_tiles(weight.shape[1]):
            part = slice(base + columns.start, base + columns.stop)
            result = 0.0
            k = 0
            for rows, slope in zip(row_refs, slope_refs):
                for first in range(0, rows.shape[0], span):
                    dpre = slope[first : first + span, part] * hidden[k : k + 1, part]
                    result = result + lax.dot_general(
                        rows[first : first + span, :],
                        dpre.astype(BF16),
                        CONTRACT_FIRST,
                        preferred_element_type=F32,
                    )
                    k += 1
            total[:, part] = result
            shares = result * weight[:, columns].astype(F32)
            lanes = shares.shape[1]
            if lanes % 128:
                shares = jnp.concatenate(
                    [shares, jnp.zeros((shares.shape[0], -lanes % 128), F32)], 1
                )
            for c in range(0, shares.shape[1], 128):
                gains = gains + shares[:, c : c + 128]
        base += weight.shape[1]
    return jnp.sum(gains.T, axis=0, keepdims=True) / gain[...][None, :]


def q_backward_kernel(pairs, span, place, *refs):
    rows, pair_rows, own_slope, pair_slope, hidden, weight, gain = refs[:7]
    sends, (keep, gains, total) = refs[7 : 6 + pairs], refs[6 + pairs :]
    gains[...] = inner_gradient(
        [rows, pair_rows], [own_slope, pair_slope], hidden, [weight], gain, total, span
    )
    mine = place[0] // 2
    size = keep.shape[0]
    keep[...] = total[pl.ds(pl.multiple_of(mine * size, 16), size), :]
    for k in range(1, pairs):
        first = pl.multiple_of((mine ^ k) * size, 16)
        sends[k - 1][...] = total[pl.ds(first, size), :].astype(BF16)


def q_backward(place, rows, slope, pair_rows, pair_slope, hidden, weight, gain, pairs, span):
    width, units = weight.shape
    size = width // pairs
    return call(
        functools.partial(q_backward_kernel, pairs, span),
        [SMEM] + [VMEM] * 6 + [LOAD],
        [((size, units), BF16)] * (pairs - 1) + [((size, units), F32), ((1, width), F32)],
        [pltpu.VMEM((width, units), F32)],
        flops=4 * 10**9,
        bytes_accessed=3 * 10**6,
    )(place, rows, pair_rows, slope, pair_slope, hidden, weight, gain)


def s_backward_kernel(span, axis, place, lengths, *refs):
    rows, hidden = refs[:2]
    weights = refs[2:-7]
    gain, q_gains, send, keep, gains, total, slope = refs[-7:]
    slope_kernel(1, axis, span, False, place, lengths, rows, *weights, slope)
    s_gains = inner_gradient([rows], [slope], hidden, weights, gain, total, span)
    core = place[4]
    size = keep.shape[0]
    keep[...] = total[pl.ds(pl.multiple_of(core * size, 16), size), :]
    first = pl.multiple_of((1 - core) * size, 16)
    send[...] = total[pl.ds(first, size), :].astype(BF16)
    index = lax.broadcasted_iota(jnp.int32, (GAIN_ROWS, 1), 0)
    packed = jnp.zeros((GAIN_ROWS, total.shape[0]), F32)
    for i, row in enumerate((q_gains[...], s_gains)):
        high = row.astype(BF16).astype(F32)
        packed = jnp.where(index == i, high, packed)
        packed = jnp.where(index == i + 2, row - high, packed)
    gains[...] = packed.astype(BF16)


def s_backward(place, lengths, rows, hidden, weights, gain, q_gains, axis, span):
    width = weights[0].shape[0]
    units = sum(w.shape[1] for w in weights)
    return call(
        functools.partial(s_backward_kernel, span, axis),
        [SMEM] * 2 + [VMEM] * 2 + [LOAD] + [VMEM] * (len(weights) - 1) + [LOAD, VMEM],
        [
            ((width // 2, units), BF16),
            ((width // 2, units), F32),
            ((GAIN_ROWS, width), BF16),
        ],
        [pltpu.VMEM((width, units), F32), pltpu.VMEM((rows.shape[0], units), F32)],
        flops=6 * 10**9,
        bytes_accessed=3 * 10**6,
    )(place, lengths, rows, hidden, *weights, gain, q_gains)


def score_kernel(
    n_sa, n_pb, width, place, q_ref, s_ref, q_outer, *refs
):
    s_outers = refs[:-5]
    loss_ref, q_grad_ref, s_grad_ref, q_hidden, s_hidden = refs[-5:]
    p, a = place[0], place[1]
    q, s = q_ref[:, :width], s_ref[:, :width]
    positive = q_ref[:, q_ref.shape[1] - 128 : q_ref.shape[1] - 127].astype(jnp.int32)
    count = q.shape[0]
    scale = 1.0 / math.sqrt(width)
    score = scale * lax.dot_general(q, s, CONTRACT_LAST, precision=HIGH, preferred_element_type=F32)
    columns = lax.broadcasted_iota(jnp.int32, (count, count), 1)
    match = (positive == columns).astype(F32)
    row_max = jnp.max(score, axis=1, keepdims=True)
    col_max = jnp.max(score, axis=0, keepdims=True)
    row_lse = row_max + jnp.log(jnp.sum(jnp.exp(score - row_max), axis=1, keepdims=True))
    col_lse = col_max + jnp.log(jnp.sum(jnp.exp(score - col_max), axis=0, keepdims=True))
    matched = jnp.sum(match * score, axis=1, keepdims=True)
    row_part = jnp.sum(row_lse - matched, axis=0, keepdims=True)
    col_part = jnp.sum(col_lse, axis=1, keepdims=True) - jnp.sum(matched, axis=0, keepdims=True)
    loss_ref[...] = (row_part + col_part) / (2.0 * count)
    dscore = 0.5 * (jnp.exp(score - row_lse) + jnp.exp(score - col_lse) - 2.0 * match)
    q_grad = scale * jnp.dot(dscore, s, precision=HIGH, preferred_element_type=F32)
    s_grad = scale * lax.dot_general(
        dscore, q, CONTRACT_FIRST, precision=HIGH, preferred_element_type=F32
    )
    q_grad_ref[...] = q_grad
    s_grad_ref[...] = s_grad

    def hidden(grad, places, outers, out):
        rows = places.shape[0]
        chosen = lax.broadcasted_iota(jnp.int32, (rows, count), 1) == places
        picked = jnp.dot(chosen.astype(F32), grad, precision=HIGH, preferred_element_type=F32)
        high = picked.astype(BF16)
        low = (picked - high.astype(F32)).astype(BF16)
        base = 0
        for outer in outers:
            weight = outer[...]
            result = lax.dot_general(high, weight, CONTRACT_LAST, preferred_element_type=F32)
            result += lax.dot_general(low, weight, CONTRACT_LAST, preferred_element_type=F32)
            out[:, base : base + weight.shape[0]] = result
            base += weight.shape[0]

    index = lax.broadcasted_iota(jnp.int32, (2 * n_sa, 1), 0)
    pair = (index >= n_sa).astype(jnp.int32)
    hidden(q_grad, (p ^ pair) * n_sa + (a ^ (index - pair * n_sa)), [q_outer], q_hidden)
    index = lax.broadcasted_iota(jnp.int32, (8, 1), 0)
    hidden(s_grad, a * n_pb + (p ^ index), s_outers, s_hidden)


def scores(place, q_all, s_all, q_outer, s_outers, n_sa, n_pb, width):
    shape = (q_all.shape[0], width)
    units = sum(w.shape[0] for w in s_outers)
    return call(
        functools.partial(score_kernel, n_sa, n_pb, width),
        [SMEM] + [VMEM] * 3 + [LOAD] + [VMEM] * (len(s_outers) - 1),
        [
            ((1, 1), F32),
            (shape, F32),
            (shape, F32),
            ((2 * n_sa, q_outer.shape[0]), F32),
            ((8, units), F32),
        ],
    )(place, q_all, s_all, q_outer, *s_outers)


def assemble_kernel(pairs, place, *refs):
    out = refs[-1]
    chunks, (own_other, first, rest) = refs[:pairs], refs[pairs:-1]
    rows, half = own_other.shape
    mine = place[0] // 2
    even = place[0] % 2 == 0
    for k in range(pairs):
        a = chunks[k][:rows, :].astype(F32)
        b = own_other if k == 0 else first if k == 1 else rest.at[pl.ds((k - 2) * rows, rows), :]
        b = b[...].astype(F32)
        where = pl.ds(pl.multiple_of((mine ^ k) * rows, 8), rows)
        out[where, :half] = jnp.where(even, a, b)
        out[where, half:] = jnp.where(even, b, a)


def assemble(place, chunks, own_other, first, rest):
    rows, half = own_other.shape
    pairs = len(chunks)
    return call(
        functools.partial(assemble_kernel, pairs),
        [SMEM] + [LOAD] * (pairs + 3),
        [((rows * pairs, 2 * half), F32)],
    )(place, *chunks, own_other, first, rest)[0]


def per_device(
    question_states,
    question_ids,
    q_inner_weight,
    q_outer_weight,
    q_norm_gain,
    sql_states,
    sql_ids,
    s_inner_weight,
    s_outer_weight,
    s_norm_gain,
    positive_column,
):
    n_pb, n_sa = lax.axis_size("pb"), lax.axis_size("sa")
    p, a = lax.axis_index("pb"), lax.axis_index("sa")
    width, length = question_states.shape[-1], question_states.shape[-2]
    block = s_inner_weight.shape[1]
    units = q_inner_weight.shape[1]
    half = units // 2
    pairs = n_pb // 2
    far = range(GROUP, n_pb, GROUP)
    y, core = bit_at(a, 2), bit_at(a, 1)
    place = jnp.stack([p, a, core * 2 + y, y, core]).astype(jnp.int32)

    own_q, own_s = question_states[0, 0], sql_states[0, 0]
    q_normed, s_normed, piece = prepare(
        place, own_q, own_s, q_norm_gain, s_norm_gain, s_inner_weight, s_outer_weight
    )
    top = n_sa // 2
    mine = [swap(piece, "pb", k) for k in far]
    beside = [swap(piece, "sa", 1) for piece in mine]
    from_x, from_z = swap(s_normed, "pb", 1), swap(s_normed, "pb", 2)
    pair_token = swap(q_normed, "pb", 1)
    q_far = swap(q_normed, "sa", top)
    pair_bit = bit_at(p, 1)
    q_inner_half = lax.dynamic_slice_in_dim(q_inner_weight, pair_bit * half, half, 1)
    q_outer_half = lax.dynamic_slice_in_dim(q_outer_weight, pair_bit * half, half, 0)
    q_lengths = jnp.sum((question_ids[0] > 0).astype(jnp.int32), axis=-1)
    s_lengths = jnp.sum((sql_ids[0] > 0).astype(jnp.int32), axis=-1)
    (
        from_x,
        from_z,
        mine,
        beside,
        q_far,
        pair_token,
        s_late,
        q_inner_half,
        q_outer_half,
        q_lengths,
        s_lengths,
    ) = together(
        from_x,
        from_z,
        mine,
        beside,
        q_far,
        pair_token,
        s_normed,
        q_inner_half,
        q_outer_half,
        q_lengths,
        s_lengths,
    )

    across = [swap(piece, "sa", 2) for piece in mine]
    from_xz = swap(s_late, "pb", 3)
    q_tokens = [q_normed] + [None] * (n_sa - 1)
    q_tokens[top] = q_far
    for step in reversed(bits_of(n_sa)):
        for k in range(0, n_sa, 2 * step):
            if q_tokens[k + step] is None:
                q_tokens[k + step] = swap(q_tokens[k], "sa", step)

    q_pooled, q_part, q_rows = forward(
        place, q_lengths, own_q, q_tokens, q_inner_weight, q_outer_weight, [], 1
    )
    (own_slope,) = slopes(place, q_lengths, [q_rows], [q_inner_half], 1, length)
    q_steps = list(reversed(bits_of(n_sa)))
    for step in q_steps[:-1]:
        q_part = q_part + swap(q_part, "sa", step)
    from_xz, across, q_part, own_slope, pair_late = together(
        from_xz, across, q_part, own_slope, pair_token
    )
    pair_far = swap(pair_late, "sa", top)

    pieces = []
    for one, two, three in zip(mine, across, beside):
        pieces += [one, two, three, swap(two, "sa", 1)]
    s_tokens = [s_normed, from_x, from_z, from_xz]
    q_part = q_part + swap(q_part, "sa", q_steps[-1])
    meta = jnp.stack([positive_column, q_lengths], 1).astype(F32)
    meta = jnp.concatenate([meta, jnp.zeros((n_sa, 126), F32)], 1)
    q_all = jnp.concatenate([q_part, q_pooled, meta], 1)
    s_pooled, s_part, s_rows, *far_weights = forward(
        place, s_lengths, own_s, s_tokens, s_inner_weight, s_outer_weight, pieces, 0
    )
    s_inners = [s_inner_weight] + far_weights[0::2]
    s_outers = [s_outer_weight] + far_weights[1::2]
    s_part, q_all = together(s_part, q_all)

    s_others = [swap(s_part, "pb", k) for k in range(1, GROUP)]
    pair_meta = swap(q_all, "pb", 1)
    q_all = ordered(q_all, pair_meta, pair_bit)
    pair_lengths = pair_meta[:, width + units + 1].astype(jnp.int32)
    s_part = (s_part + s_others[0]) + (s_others[1] + s_others[2])
    s_part, q_all = together(s_part, q_all)

    s_sent = [jnp.concatenate([s_part, s_pooled[:, :block]], 1)]
    for i, k in enumerate(far):
        pooled_far = s_pooled[:, (i + 1) * block : (i + 2) * block]
        s_sent.append(swap(jnp.concatenate([s_part, pooled_far], 1), "pb", k))
    q_all = ordered(q_all, swap(q_all, "pb", 2), bit_at(p, 2))
    s_all = canonical(s_sent, p // GROUP)[None]
    s_all, q_all = together(s_all, q_all)
    pair_tokens = [pair_token] + [None] * (n_sa - 1)
    pair_tokens[top] = pair_far
    for step in reversed(bits_of(n_sa)):
        for k in range(0, n_sa, 2 * step):
            if pair_tokens[k + step] is None:
                pair_tokens[k + step] = swap(pair_tokens[k], "sa", step)
    for step in bits_of(n_pb)[2:]:
        q_all = ordered(q_all, swap(q_all, "pb", step), bit_at(p, step))
    for step in reversed(bits_of(n_sa)):
        s_all = ordered(s_all, swap(s_all, "sa", step), bit_at(a, step))
    order = [
        sum(((i >> b) & 1) << (n_sa.bit_length() - 2 - b) for b in range(n_sa.bit_length() - 1))
        for i in range(n_sa)
    ]
    s_all = jnp.concatenate([s_all[order[i]] for i in range(n_sa)], 0)
    pair_slope, pair_rows = slopes(place, pair_lengths, pair_tokens, [q_inner_half], 1, length)
    q_all, s_all, pair_slope = together(q_all, s_all, pair_slope)

    loss, q_grad, s_grad, q_hidden, s_hidden = scores(
        place, q_all, s_all, q_outer_half, s_outers, n_sa, n_pb, width
    )

    *q_sends, q_keep, q_gains = q_backward(
        place,
        q_rows,
        own_slope,
        pair_rows,
        pair_slope,
        q_hidden,
        q_inner_half,
        q_norm_gain,
        pairs,
        length,
    )
    q_arrived = [swap(x, "pb", 2 * k) for k, x in enumerate(q_sends, 1)]
    s_hidden, q_gains = together(s_hidden, q_gains)
    s_send, s_keep, packed = s_backward(
        place, s_lengths, s_rows, s_hidden, s_inners, s_norm_gain, q_gains, 0, length
    )

    def outer_gradient(pooled, grad):
        high = lax.reduce_precision(pooled, 8, 7)
        top = lax.reduce_precision(grad, 8, 7)
        left = jnp.concatenate([high, pooled - high, high], 0).astype(BF16)
        right = jnp.concatenate([top, top, grad - top], 0).astype(BF16)
        return lax.dot_general(left, right, CONTRACT_FIRST, preferred_element_type=F32)

    q_outer_grad = outer_gradient(q_all[:, width : width + units], q_grad)
    s_outer_grad = outer_gradient(s_all[:, width:], s_grad)
    q_arrived, s_send, s_keep, packed, q_outer_grad, s_outer_grad = together(
        q_arrived, s_send, s_keep, packed, q_outer_grad, s_outer_grad
    )
    s_beside = swap(s_send, "sa", 1)

    q_total = q_keep
    for x in q_arrived:
        q_total = q_total + x.astype(F32)
    q_total = q_total.astype(BF16)
    rows = q_total.shape[0]
    packed = jnp.concatenate(jnp.split(packed, width // half, 1), 0)
    sent = jnp.concatenate([q_total, packed], 0)
    arrivals = [swap(sent, "pb", 2 * k) for k in range(1, pairs)]
    own_other = swap(q_total, "pb", 1)
    size = width // 2
    s_total = s_keep + s_beside.astype(F32)
    for step in bits_of(n_sa)[1:]:
        size = size // 2
        bit = bit_at(a, step)
        away = lax.dynamic_slice_in_dim(s_total, (1 - bit) * size, size, 0).astype(BF16)
        arrived = swap(away, "sa", step)
        s_total = lax.dynamic_slice_in_dim(s_total, bit * size, size, 0)
        s_total = s_total + arrived.astype(F32)
    first = swap(arrivals[0][:rows], "pb", 1)
    arrivals, own_other, first, s_total = together(arrivals, own_other, first, s_total)

    chunks = [q_total] + list(arrivals)

    def gain_sums(tail):
        tail = jnp.concatenate(jnp.split(tail, width // half, 0), 1)
        return tail[:2].astype(F32) + tail[2:4].astype(F32)

    sums = [gain_sums(packed)] + [gain_sums(x[rows:]) for x in arrivals]
    while len(sums) > 1:
        sums = [sums[i] + sums[i + 1] for i in range(0, len(sums), 2)]
    gains = sums[0]
    packed = pack(gains, half)
    rest = swap(jnp.concatenate([x[:rows] for x in chunks[2:]] + [packed], 0), "pb", 1)
    s_sum = s_total[:, :block]
    for i, k in enumerate(far):
        far_part = s_total[:, (i + 1) * block : (i + 2) * block].astype(BF16)
        s_sum = s_sum + swap(far_part, "pb", k).astype(F32)
    rest, s_sum = together(rest, s_sum)
    gains = unpack(packed, width) + unpack(rest[(pairs - 2) * rows :], width)
    q_inner_grad = assemble(place, chunks, own_other, first, rest)

    s_sum = s_sum.astype(BF16)
    for step in reversed(bits_of(n_sa)):
        size = s_sum.shape[0]
        packed = pack(gains, block)
        if step == 1:
            s_sum, q_inner_grad = together(s_sum, q_inner_grad)
        arrived = swap(jnp.concatenate([s_sum, packed], 0), "sa", step)
        gains = unpack(packed, width) + unpack(arrived[size:], width)
        s_sum = ordered(s_sum, arrived[:size], bit_at(a, step))
    s_inner_grad = s_sum.astype(F32)

    return (
        loss[0, 0],
        q_inner_grad,
        q_outer_grad,
        gains[0],
        s_inner_grad,
        s_outer_grad,
        gains[1],
    )


def solution(mesh):
    placed = (
        P("pb", "sa", None, None),
        P("pb", None, None),
        P(None, "sa"),
        P("sa", None),
        P(),
        P("sa", "pb", None, None),
        P("sa", None, None),
        P(None, "pb"),
        P("pb", None),
        P(),
        P("pb"),
    )
    return jax.shard_map(
        per_device,
        mesh=mesh,
        in_specs=placed,
        out_specs=(P(), P(None, "sa"), P("sa", None), P(), P(None, "pb"), P("pb", None), P()),
        check_vma=False,
    )
```

time: 176 us -> 153 us (0.87)
  Pallas kernels: 2.86 us -> 31.1 us
  matrix products: 21.4 us -> 3.25 us
  other arithmetic: 20.2 us -> 4.28 us
  local copies, waits for them, and re-layouts: 32.9 us -> 18.6 us
  waiting for transfers between devices: 50.3 us -> 48.3 us
    pallas_call x2 -> x9, Pallas kernels: 2.86 us -> 31.1 us  [run(): pl.pallas_call(kernel, in_specs=[HBM if spec is LOAD else spec for spec i...]
    dot_general x9 -> x2, matrix products: 21.4 us -> 3.25 us  [outer_gradient(): lax.dot_general(left, right, CONTRACT_FIRST, preferred_element_type=F32)]
    dynamic_update_slice x4 -> x0, other arithmetic: 5.67 us -> none  [per_device(): lax.dynamic_update_slice_in_dim(q_inner_grad, full, (mine ^ k) * q_chunk, 0)]
    unnamed x67 -> x70, local copies, waits for them, and re-layouts: 19.9 us -> 16.3 us
    broadcast_in_dim x6 -> x1, local copies, waits for them, and re-layouts: 2.95 us -> 0.01 us  [per_device(): meta = jnp.concatenate([meta, jnp.zeros((n_sa, 126), F32)], 1)]
    select_n x8 -> x6, other arithmetic: 2.74 us -> 0.16 us  [ordered(): jnp.where(bit == 0, jnp.concatenate([mine, other], axis), jnp.concatenate...]
    concatenate x2 -> x0, local copies, waits for them, and re-layouts: 2.55 us -> none  [the longest x1 1.78 us: per_device(): q_both = jnp.concatenate([q_rows] + pair_tokens, 0)]
    concatenate x4, other arithmetic: 2.1 us -> 0.07 us  [the longest x1 0.03 us: per_device(): jnp.concatenate([x[:rows] for x in chunks[2:]] + [packed], 0)]
  transfers between devices with their start and end apart: 39 -> 39, of which waited for: 17 -> 23; matrix products, arithmetic and copies ran while one was open for 35% -> 4% of each run, Pallas kernels for 0% -> 10%
where the time goes in v3:
time: 153 us; the launch traced here: 152 us
  waiting for transfers between devices  48.3 us (32%)
  starting transfers between devices  45.4 us (30%)
  Pallas kernels  31.1 us (20%)
  local copies, waits for them, and re-layouts  18.6 us (12%)
  other arithmetic  4.28 us (3%)
  matrix products  3.25 us (2%)
    ppermute x39, waiting for transfers between devices, swap(): return lax.ppermute(x, axis, [(i, i ^ step) for i in range(size)])  48.3 us
    ppermute x39, starting transfers between devices, swap(): return lax.ppermute(x, axis, [(i, i ^ step) for i in range(size)])  45.4 us
    pallas_call x9, Pallas kernels, run(): pl.pallas_call(kernel, in_specs=[HBM if spec is LOAD else spec for spec i...  31.1 us
    unnamed x70, local copies, waits for them, and re-layouts  16.3 us
    dot_general x2, matrix products, outer_gradient(): lax.dot_general(left, right, CONTRACT_FIRST, preferred_element_type=F32)  3.25 us
  transfers between devices with their start and end apart: 39, of which 23 were waited for; matrix products, arithmetic and copies ran while one was open for 4% of the time, Pallas kernels for 10%

profile of v3, /device:TPU:0, one launch (start us, length us, event | category | flops | bytes accessed | tf_op | source)
XLA Modules:
  0.0 152.4 jit_solution(934074433158910673)
XLA Ops:
  0.8 1.1 copy-done
  1.8 1.1 copy-done.6
  2.9 1.0 copy-done.9
  3.9 1.0 copy-done.11
  6.3 2.5 %shard_map.162 = (bf16[256,768]{1,0:T(8,128)(2,1)}, bf16[256,768]{1,0:T(8,128)(2,1)}, bf16[192,768]{1,0:T(8,128)(2,1)S(1)}) custom-call(s32[5]{0:T(128)S(1)} %stack.32.refs_0_, bf16[256,768]{1,0:T(8,128)(2,1)S(1)} %bitcast.20, bf16[256,768]{1,0:T(8,128)(2,1)S(1)} %bitcast.22, f32[768]{0:T(1024)S(1)} %copy-done.19, f32[768]{0:T(1024)S(1)} %copy-done.21, ...), custom_call_target="tpu_custom_call" | custom-call | tf_op jit(solution)/shard_map/pallas_call | solution.py:47
  8.8 4.1 %collective-permute-start.2 = (bf16[192,768]{1,0:T(8,128)(2,1)S(1)}, bf16[192,768]{1,0:T(8,128)(2,1)}, u32[]{:S(2)}, u32[]{:S(2)}) collective-permute-start(bf16[192,768]{1,0:T(8,128)(2,1)S(1)} %get-tuple-element.79), channel_id=1, source_target_pairs={{0,16},{4,20},{8,24},{12,28},{16,0},{20,4},{24,8},{28,12},{1,17},{... | collective-permute-start | bytes 884744 | tf_op jit(solution)/shard_map/ppermute | solution.py:74
  12.9 1.5 collective-permute-start
  14.4 1.6 %collective-permute-start.1 = (bf16[256,768]{1,0:T(8,128)(2,1)}, bf16[256,768]{1,0:T(8,128)(2,1)}, u32[]{:S(2)}, u32[]{:S(2)}) collective-permute-start(bf16[256,768]{1,0:T(8,128)(2,1)} %get-tuple-element.84.refs_3_), channel_id=1, source_target_pairs={{0,8},{4,12},{8,0},{12,4},{16,24},{20,28},{24,16},{28,20},{1,9},{5... | collective-permute-start | bytes 1179656 | tf_op jit(solution)/shard_map/ppermute | solution.py:74
  16.0 1.5 collective-permute-start.4
  18.1 8.3 %collective-permute-done.2.refs_9_ = bf16[192,768]{1,0:T(8,128)(2,1)} collective-permute-done((bf16[192,768]{1,0:T(8,128)(2,1)S(1)}, bf16[192,768]{1,0:T(8,128)(2,1)}, u32[]{:S(2)}, u32[]{:S(2)}) %collective-permute-start.2) | collective-permute-done | bytes 294944 | tf_op jit(solution)/shard_map/ppermute | solution.py:74
  28.0 2.2 %collective-permute-done.1.refs_5_ = bf16[256,768]{1,0:T(8,128)(2,1)} collective-permute-done((bf16[256,768]{1,0:T(8,128)(2,1)}, bf16[256,768]{1,0:T(8,128)(2,1)}, u32[]{:S(2)}, u32[]{:S(2)}) %collective-permute-start.1) | collective-permute-done | bytes 393248 | tf_op jit(solution)/shard_map/ppermute | solution.py:74
  30.2 2.1 %collective-permute-done.5.refs_2_ = bf16[256,768]{1,0:T(8,128)(2,1)} collective-permute-done((bf16[256,768]{1,0:T(8,128)(2,1)}, bf16[256,768]{1,0:T(8,128)(2,1)}, u32[]{:S(2)}, u32[]{:S(2)}) %collective-permute-start.5) | collective-permute-done | bytes 393248 | tf_op jit(solution)/shard_map/ppermute | solution.py:74
  32.2 2.5 %collective-permute-start.6 = (bf16[256,768]{1,0:T(8,128)(2,1)}, bf16[256,768]{1,0:T(8,128)(2,1)S(1)}, u32[]{:S(2)}, u32[]{:S(2)}) collective-permute-start(bf16[256,768]{1,0:T(8,128)(2,1)} %get-tuple-element.84.refs_3_), channel_id=1, source_target_pairs={{0,12},{4,8},{8,4},{12,0},{16,28},{20,24},{24,20},{28,16},{1,13},{... | collective-permute-start | bytes 1179656 | tf_op jit(solution)/shard_map/ppermute | solution.py:74
  34.7 1.5 collective-permute-start.7
  36.3 1.3 copy-done.18
  37.5 4.5 %shard_map.163 = (f32[4,768]{1,0:T(4,128)S(1)}, f32[4,768]{1,0:T(4,128)S(1)}, bf16[1024,768]{1,0:T(8,128)(2,1)S(1)}) custom-call(s32[5]{0:T(128)S(1)} %stack.32.refs_0_, s32[4]{0:T(128)S(1)} %convert_reduce_fusion.1.refs_1_, bf16[256,768]{1,0:T(8,128)(2,1)S(1)} %bitcast.21, bf16[256,768]{1,0:T(8,128)(2,1)} %get-tuple-element.80.refs_3_, ...), custom_call_target="tpu_custom_call" | custom-call | flops 3000000000 | bytes 3000000 | tf_op jit(solution)/shard_map/pallas_call | solution.py:47
  42.7 1.8 %shard_map.164.refs_3_ = f32[1024,384]{1,0:T(8,128)S(1)} custom-call(s32[5]{0:T(128)S(1)} %stack.32.refs_0_, s32[4]{0:T(128)S(1)} %convert_reduce_fusion.1.refs_1_, bf16[1024,768]{1,0:T(8,128)(2,1)S(1)} %get-tuple-element.89.refs_2_.refs_1_, bf16[768,384]{1,0:T(8,128)(2,1)S(1)} %constant_dynamic-slice_fusion.1.refs_3_.refs_6_), custom_call_target="tpu_custom_call" | custom-call | flops 905969664 | bytes 3000000 | tf_op jit(solution)/shard_map/pallas_call | solution.py:47
  44.5 1.1 copy-done.2
  47.4 0.8 collective-permute-done.12
  48.6 1.1 copy-done.7
  49.6 1.0 copy-done.12
  50.6 1.0 copy-done.24
  51.6 1.0 copy-done.26
  52.6 6.0 %shard_map.165 = (f32[4,768]{1,0:T(4,128)S(1)}, f32[4,768]{1,0:T(4,128)S(1)}, bf16[1024,768]{1,0:T(8,128)(2,1)S(1)}, bf16[768,384]{1,0:T(8,128)(2,1)S(1)}, bf16[384,768]{1,0:T(8,128)(2,1)S(1)}) custom-call(s32[5]{0:T(128)S(1)} %stack.32.refs_0_, s32[8]{0:T(128)S(1)} %convert_reduce_fusion.refs_1_, bf16[256,768]{1,0:T(8,128)(2,1)S(1)} %bitcast.23, ...), custom_call_target="tpu_custom_call" | custom-call | flops 3000000000 | bytes 3000000 | tf_op jit(solution)/shard_map/pallas_call | solution.py:47
  59.4 1.1 copy-done.27
  61.9 1.4 collective-permute-start.15
  63.4 1.5 collective-permute-start.13
  65.4 1.1 collective-permute-done.15
  67.2 1.5 %collective-permute-done.16 = f32[4,1664]{1,0:T(4,128)S(1)} collective-permute-done((f32[4,1664]{1,0:T(4,128)S(1)}, f32[4,1664]{1,0:T(4,128)S(1)}, u32[]{:S(2)}, u32[]{:S(2)}) %collective-permute-start.16) | collective-permute-done | bytes 26656 | tf_op jit(solution)/shard_map/ppermute | solution.py:74
  69.2 1.3 collective-permute-start.23
  71.2 2.5 %collective-permute-done.17 = f32[4,1152]{1,0:T(4,128)S(1)} collective-permute-done((f32[4,1152]{1,0:T(4,128)S(1)}, f32[4,1152]{1,0:T(4,128)S(1)}, u32[]{:S(2)}, u32[]{:S(2)}) %collective-permute-start.17) | collective-permute-done | bytes 18464 | tf_op jit(solution)/shard_map/ppermute | solution.py:74
  73.8 0.9 collective-permute-done.18
  75.6 2.6 %collective-permute-start.19 = (f32[16,1664]{1,0:T(8,128)S(1)}, f32[16,1664]{1,0:T(8,128)S(1)}, u32[]{:S(2)}, u32[]{:S(2)}) collective-permute-start(f32[16,1664]{1,0:T(8,128)S(1)} %maximum_select_fusion.4), channel_id=1, source_target_pairs={{0,16},{4,20},{8,24},{12,28},{16,0},{20,4},{24,8},{28,12},{1,17},{... | collective-permute-start | bytes 319496 | tf_op jit(solution)/shard_map/ppermute | solution.py:74
  78.2 3.1 %collective-permute-done.23.refs_4_ = bf16[256,768]{1,0:T(8,128)(2,1)S(1)} collective-permute-done((bf16[256,768]{1,0:T(8,128)(2,1)}, bf16[256,768]{1,0:T(8,128)(2,1)S(1)}, u32[]{:S(2)}, u32[]{:S(2)}) %collective-permute-start.23) | collective-permute-done | bytes 393248 | tf_op jit(solution)/shard_map/ppermute | solution.py:74
  81.9 0.9 collective-permute-done.19
  83.2 2.9 %shard_map.166 = (f32[1024,384]{1,0:T(8,128)S(1)}, bf16[1024,768]{1,0:T(8,128)(2,1)S(1)}) custom-call(s32[5]{0:T(128)S(1)} %stack.32.refs_0_, s32[4]{0:T(128)S(1)} %fusion.32.refs_1_, bf16[256,768]{1,0:T(8,128)(2,1)} %collective-permute-done.5.refs_2_, bf16[256,768]{1,0:T(8,128)(2,1)S(1)} %collective-permute-done.22.refs_3_, ...), custom_call_target="tpu_custom_call" | custom-call | flops 905969664 | bytes 3000000 | tf_op jit(solution)/shard_map/pallas_call | solution.py:47
  86.2 2.8 %shard_map.167 = (f32[1,1]{1,0:T(1,128)}, f32[32,768]{1,0:T(8,128)S(1)}, f32[32,768]{1,0:T(8,128)S(1)}, f32[8,384]{1,0:T(8,128)S(1)}, f32[8,768]{1,0:T(8,128)S(1)}) custom-call(s32[5]{0:T(128)S(1)} %stack.32.refs_0_, f32[32,1664]{1,0:T(8,128)S(1)} %maximum_select_fusion.2.refs_1_, f32[32,1152]{1,0:T(8,128)S(1)} %pad_maximum_fusion.4.refs_2_, ...), custom_call_target="tpu_custom_call" | custom-call | tf_op jit(solution)/shard_map/pallas_call | solution.py:47
  89.0 2.5 %shard_map.168 = (bf16[192,384]{1,0:T(8,128)(2,1)S(1)}, bf16[192,384]{1,0:T(8,128)(2,1)S(1)}, bf16[192,384]{1,0:T(8,128)(2,1)S(1)}, f32[192,384]{1,0:T(8,128)S(1)}, f32[1,768]{1,0:T(1,128)S(1)}) custom-call(s32[5]{0:T(128)S(1)} %stack.32.refs_0_, bf16[1024,768]{1,0:T(8,128)(2,1)S(1)} %get-tuple-element.89.refs_2_.refs_1_, ...), custom_call_target="tpu_custom_call" | custom-call | flops 4000000000 | bytes 3000000 | tf_op jit(solution)/shard_map/pallas_call | solution.py:47
  92.1 2.6 %collective-permute-start.26 = (bf16[192,384]{1,0:T(8,128)(2,1)S(1)}, bf16[192,384]{1,0:T(8,128)(2,1)S(1)}, u32[]{:S(2)}, u32[]{:S(2)}) collective-permute-start(bf16[192,384]{1,0:T(8,128)(2,1)S(1)} %get-tuple-element.118), channel_id=1, source_target_pairs={{0,16},{4,20},{8,24},{12,28},{16,0},{20,4},{24,8},{28,12},{1,17},{... | collective-permute-start | bytes 442376 | tf_op jit(solution)/shard_map/ppermute | solution.py:74
  94.7 1.3 collective-permute-start.27
  96.0 4.6 %shard_map.169 = (bf16[384,768]{1,0:T(8,128)(2,1)S(1)}, f32[384,768]{1,0:T(8,128)S(1)}, bf16[16,768]{1,0:T(8,128)(2,1)S(1)}) custom-call(s32[5]{0:T(128)S(1)} %stack.32.refs_0_, s32[8]{0:T(128)S(1)} %convert_reduce_fusion.refs_1_, bf16[1024,768]{1,0:T(8,128)(2,1)S(1)} %copy-done.28, f32[8,768]{1,0:T(8,128)S(1)} %get-tuple-element.123.refs_3_, ...), custom_call_target="tpu_custom_call" | custom-call | flops 6000000000 | bytes 3000000 | tf_op jit(solution)/shard_map/pallas_call | solution.py:47
  100.6 1.9 %fusion.1 = f32[768,768]{1,0:T(8,128)} fusion(bf16[32,768]{1,0:T(8,128)(2,1)S(1)} %get-tuple-element.160, bf16[32,768]{1,0:T(8,128)(2,1)S(1)} %get-tuple-element.159, bf16[32,768]{1,0:T(8,128)(2,1)S(1)} %get-tuple-element.187, bf16[32,768]{1,0:T(8,128)(2,1)S(1)} %get-tuple-element.188), kind=kOutput, calls=%fused_computation.16 | convolution fusion | flops 114130944 | bytes 2555904 | tf_op jit(solution)/shard_map/dot_general | solution.py:703
  102.5 1.4 fusion.12
  103.9 2.0 %collective-permute-done.26 = bf16[192,384]{1,0:T(8,128)(2,1)S(1)} collective-permute-done((bf16[192,384]{1,0:T(8,128)(2,1)S(1)}, bf16[192,384]{1,0:T(8,128)(2,1)S(1)}, u32[]{:S(2)}, u32[]{:S(2)}) %collective-permute-start.26) | collective-permute-done | bytes 147488 | tf_op jit(solution)/shard_map/ppermute | solution.py:74
  106.0 2.0 %collective-permute-done.33 = bf16[384,768]{1,0:T(8,128)(2,1)} collective-permute-done((bf16[384,768]{1,0:T(8,128)(2,1)S(1)}, bf16[384,768]{1,0:T(8,128)(2,1)}, u32[]{:S(2)}, u32[]{:S(2)}) %collective-permute-start.33) | collective-permute-done | bytes 589856 | tf_op jit(solution)/shard_map/ppermute | solution.py:74
  108.0 1.2 convert_add_fusion
  109.3 1.8 %collective-permute-start.34 = (bf16[192,768]{1,0:T(8,128)(2,1)S(1)}, bf16[192,768]{1,0:T(8,128)(2,1)S(1)}, u32[]{:S(2)}, u32[]{:S(2)}) collective-permute-start(bf16[192,768]{1,0:T(8,128)(2,1)S(1)} %dynamic-slice_convert_fusion), channel_id=1, source_target_pairs={{0,2},{1,3},{2,0},{3,1},{4,6},{5,7},{6,4},{7,5},{8,10},{9,11},{10,... | collective-permute-start | bytes 884744 | tf_op jit(solution)/shard_map/ppermute | solution.py:74
  111.0 2.7 %collective-permute-start.28 = (bf16[224,384]{1,0:T(8,128)(2,1)S(1)}, bf16[224,384]{1,0:T(8,128)(2,1)S(1)}, u32[]{:S(2)}, u32[]{:S(2)}) collective-permute-start(bf16[224,384]{1,0:T(8,128)(2,1)S(1)} %pad_maximum_fusion.2), channel_id=1, source_target_pairs={{0,8},{4,12},{8,0},{12,4},{16,24},{20,28},{24,16},{28,20},{1,9},{5... | collective-permute-start | bytes 516104 | tf_op jit(solution)/shard_map/ppermute | solution.py:74
  113.8 1.8 %collective-permute-start.29 = (bf16[224,384]{1,0:T(8,128)(2,1)S(1)}, bf16[224,384]{1,0:T(8,128)(2,1)S(1)}, u32[]{:S(2)}, u32[]{:S(2)}) collective-permute-start(bf16[224,384]{1,0:T(8,128)(2,1)S(1)} %pad_maximum_fusion.2), channel_id=1, source_target_pairs={{0,16},{4,20},{8,24},{12,28},{16,0},{20,4},{24,8},{28,12},{1,17},{... | collective-permute-start | bytes 516104 | tf_op jit(solution)/shard_map/ppermute | solution.py:74
  115.6 1.4 collective-permute-start.30
  117.7 3.4 %collective-permute-done.28.refs_2_ = bf16[224,384]{1,0:T(8,128)(2,1)S(1)} collective-permute-done((bf16[224,384]{1,0:T(8,128)(2,1)S(1)}, bf16[224,384]{1,0:T(8,128)(2,1)S(1)}, u32[]{:S(2)}, u32[]{:S(2)}) %collective-permute-start.28) | collective-permute-done | bytes 172064 | tf_op jit(solution)/shard_map/ppermute | solution.py:74
  121.2 1.3 collective-permute-start.32
  122.5 0.9 convert_add_fusion.1
  123.3 6.0 %collective-permute-done.29.refs_3_ = bf16[224,384]{1,0:T(8,128)(2,1)S(1)} collective-permute-done((bf16[224,384]{1,0:T(8,128)(2,1)S(1)}, bf16[224,384]{1,0:T(8,128)(2,1)S(1)}, u32[]{:S(2)}, u32[]{:S(2)}) %collective-permute-start.29) | collective-permute-done | bytes 172064 | tf_op jit(solution)/shard_map/ppermute | solution.py:74
  129.5 1.0 slice.267
  130.5 4.6 %collective-permute-start.36 = (bf16[192,384]{1,0:T(8,128)(2,1)S(1)}, bf16[192,384]{1,0:T(8,128)(2,1)S(1)}, u32[]{:S(2)}, u32[]{:S(2)}) collective-permute-start(bf16[192,384]{1,0:T(8,128)(2,1)S(1)} %slice.267), channel_id=1, source_target_pairs={{0,16},{4,20},{8,24},{12,28},{16,0},{20,4},{24,8},{28,12},{1,17},{... | collective-permute-start | bytes 442376 | tf_op jit(solution)/shard_map/ppermute | solution.py:74
  135.2 0.8 collective-permute-start.35
  136.0 5.4 %collective-permute-done.36 = bf16[192,384]{1,0:T(8,128)(2,1)S(1)} collective-permute-done((bf16[192,384]{1,0:T(8,128)(2,1)S(1)}, bf16[192,384]{1,0:T(8,128)(2,1)S(1)}, u32[]{:S(2)}, u32[]{:S(2)}) %collective-permute-start.36) | collective-permute-done | bytes 147488 | tf_op jit(solution)/shard_map/ppermute | solution.py:74
  141.4 1.8 %collective-permute-done.35.refs_7_ = bf16[400,384]{1,0:T(8,128)(2,1)S(1)} collective-permute-done((bf16[400,384]{1,0:T(8,128)(2,1)S(1)}, bf16[400,384]{1,0:T(8,128)(2,1)S(1)}, u32[]{:S(2)}, u32[]{:S(2)}) %collective-permute-start.35) | collective-permute-done | bytes 307232 | tf_op jit(solution)/shard_map/ppermute | solution.py:74
  143.3 0.8 collective-permute-start.37
  144.2 3.6 %shard_map.170 = f32[768,768]{1,0:T(8,128)} custom-call(s32[5]{0:T(128)S(1)} %stack.32.refs_0_, bf16[192,384]{1,0:T(8,128)(2,1)S(1)} %add_convert_fusion.refs_1_, bf16[224,384]{1,0:T(8,128)(2,1)S(1)} %collective-permute-done.28.refs_2_, bf16[224,384]{1,0:T(8,128)(2,1)S(1)} %collective-permute-done.29.refs_3_, ...), custom_call_target="tpu_custom_call" | custom-call | tf_op jit(solution)/shard_map/pallas_call | solution.py:47
  147.8 0.9 collective-permute-done.37
  149.0 1.6 %collective-permute-done.38 = bf16[400,384]{1,0:T(8,128)(2,1)S(1)} collective-permute-done((bf16[400,384]{1,0:T(8,128)(2,1)S(1)}, bf16[400,384]{1,0:T(8,128)(2,1)S(1)}, u32[]{:S(2)}, u32[]{:S(2)}) %collective-permute-start.38) | collective-permute-done | bytes 307232 | tf_op jit(solution)/shard_map/ppermute | solution.py:74
  151.3 1.1 fusion
  (166 shorter events, 15.7 us)
Async XLA Ops:
  0.6 17.4 %copy-start.32 = (s32[1,8,256]{2,1,0:T(8,128)S(1)}, s32[1,8,256]{2,1,0:T(8,128)}, u32[]{:S(2)}) copy-start(s32[1,8,256]{2,1,0:T(8,128)} %param.17) | copy-start | bytes 24580
  0.6 25.8 %copy-start.33 = (s32[1,4,256]{2,1,0:T(4,128)S(1)}, s32[1,4,256]{2,1,0:T(4,128)}, u32[]{:S(2)}) copy-start(s32[1,4,256]{2,1,0:T(4,128)} %param.12) | copy-start | bytes 12292
  0.8 1.1 copy-start
  1.8 1.1 copy-start.6
  2.9 1.0 copy-start.9
  6.2 20.3 %copy-start.15 = (bf16[768,768]{1,0:T(8,128)(2,1)S(1)}, bf16[768,768]{1,0:T(8,128)(2,1)}, u32[]{:S(2)}) copy-start(bf16[768,768]{1,0:T(8,128)(2,1)} %refs_7_.3) | copy-start | bytes 3538948
  6.3 20.4 %copy-start.17 = (bf16[768,768]{1,0:T(8,128)(2,1)S(1)}, bf16[768,768]{1,0:T(8,128)(2,1)}, u32[]{:S(2)}) copy-start(bf16[768,768]{1,0:T(8,128)(2,1)} %refs_8_.2) | copy-start | bytes 3538948
  8.8 17.6 %collective-permute-start.2 = (bf16[192,768]{1,0:T(8,128)(2,1)S(1)}, bf16[192,768]{1,0:T(8,128)(2,1)}, u32[]{:S(2)}, u32[]{:S(2)}) collective-permute-start(bf16[192,768]{1,0:T(8,128)(2,1)S(1)} %get-tuple-element.79), channel_id=1, source_target_pairs={{0,16},{4,20},{8,24},{12,28},{16,0},{20,4},{24,8},{28,12},{1,17},{... | collective-permute-start | bytes 884744 | tf_op jit(solution)/shard_map/ppermute | solution.py:74
  12.9 13.8 %collective-permute-start = (bf16[256,768]{1,0:T(8,128)(2,1)}, bf16[256,768]{1,0:T(8,128)(2,1)S(1)}, u32[]{:S(2)}, u32[]{:S(2)}) collective-permute-start(bf16[256,768]{1,0:T(8,128)(2,1)} %get-tuple-element.84.refs_3_), channel_id=1, source_target_pairs={{0,4},{4,0},{8,12},{12,8},{16,20},{20,16},{24,28},{28,24},{1,5},{5... | collective-permute-start | bytes 1179656 | tf_op jit(solution)/shard_map/ppermute | solution.py:74
  14.4 15.8 %collective-permute-start.1 = (bf16[256,768]{1,0:T(8,128)(2,1)}, bf16[256,768]{1,0:T(8,128)(2,1)}, u32[]{:S(2)}, u32[]{:S(2)}) collective-permute-start(bf16[256,768]{1,0:T(8,128)(2,1)} %get-tuple-element.84.refs_3_), channel_id=1, source_target_pairs={{0,8},{4,12},{8,0},{12,4},{16,24},{20,28},{24,16},{28,20},{1,9},{5... | collective-permute-start | bytes 1179656 | tf_op jit(solution)/shard_map/ppermute | solution.py:74
  16.0 14.2 %collective-permute-start.4 = (bf16[256,768]{1,0:T(8,128)(2,1)}, bf16[256,768]{1,0:T(8,128)(2,1)}, u32[]{:S(2)}, u32[]{:S(2)}) collective-permute-start(bf16[256,768]{1,0:T(8,128)(2,1)} %get-tuple-element.80.refs_3_), channel_id=1, source_target_pairs={{0,2},{1,3},{2,0},{3,1},{4,6},{5,7},{6,4},{7,5},{8,10},{9,11},{10,... | collective-permute-start | bytes 1179656 | tf_op jit(solution)/shard_map/ppermute | solution.py:74
  17.5 14.7 %collective-permute-start.5 = (bf16[256,768]{1,0:T(8,128)(2,1)}, bf16[256,768]{1,0:T(8,128)(2,1)}, u32[]{:S(2)}, u32[]{:S(2)}) collective-permute-start(bf16[256,768]{1,0:T(8,128)(2,1)} %get-tuple-element.80.refs_3_), channel_id=1, source_target_pairs={{0,4},{4,0},{8,12},{12,8},{16,20},{20,16},{24,28},{28,24},{1,5},{5... | collective-permute-start | bytes 1179656 | tf_op jit(solution)/shard_map/ppermute | solution.py:74
  26.4 5.8 %collective-permute-start.3 = (bf16[192,768]{1,0:T(8,128)(2,1)}, bf16[192,768]{1,0:T(8,128)(2,1)}, u32[]{:S(2)}, u32[]{:S(2)}) collective-permute-start(bf16[192,768]{1,0:T(8,128)(2,1)} %collective-permute-done.2.refs_9_), channel_id=1, source_target_pairs={{0,1},{1,0},{2,3},{3,2},{4,5},{5,4},{6,7},{7,6},{8,9},{9,8},{10,11... | collective-permute-start | bytes 884744 | tf_op jit(solution)/shard_map/ppermute | solution.py:74
  26.6 9.7 %copy-start.10 = (bf16[1,1,256,768]{3,2,1,0:T(8,128)(2,1)S(1)}, bf16[1,1,256,768]{3,2,1,0:T(8,128)(2,1)}, u32[]{:S(2)}) copy-start(bf16[1,1,256,768]{3,2,1,0:T(8,128)(2,1)} %param.11) | copy-start | bytes 1179652
  26.6 9.7 %copy-start.16 = (bf16[768,768]{1,0:T(8,128)(2,1)S(1)}, bf16[768,768]{1,0:T(8,128)(2,1)}, u32[]{:S(2)}) copy-start(bf16[768,768]{1,0:T(8,128)(2,1)} %refs_7_.3) | copy-start | bytes 3538948
  27.5 8.8 %collective-permute-start.8 = (bf16[256,768]{1,0:T(8,128)(2,1)}, bf16[256,768]{1,0:T(8,128)(2,1)S(1)}, u32[]{:S(2)}, u32[]{:S(2)}) collective-permute-start(bf16[256,768]{1,0:T(8,128)(2,1)} %get-tuple-element.80.refs_3_), channel_id=1, source_target_pairs={{0,1},{1,0},{2,3},{3,2},{4,5},{5,4},{6,7},{7,6},{8,9},{9,8},{10,11... | collective-permute-start | bytes 1179656 | tf_op jit(solution)/shard_map/ppermute | solution.py:74
  32.2 4.0 %collective-permute-start.9 = (bf16[256,768]{1,0:T(8,128)(2,1)}, bf16[256,768]{1,0:T(8,128)(2,1)S(1)}, u32[]{:S(2)}, u32[]{:S(2)}) collective-permute-start(bf16[256,768]{1,0:T(8,128)(2,1)} %collective-permute-done.4.refs_5_), channel_id=1, source_target_pairs={{0,1},{1,0},{2,3},{3,2},{4,5},{5,4},{6,7},{7,6},{8,9},{9,8},{10,11... | collective-permute-start | bytes 1179656 | tf_op jit(solution)/shard_map/ppermute | solution.py:74
  32.2 13.7 %collective-permute-start.6 = (bf16[256,768]{1,0:T(8,128)(2,1)}, bf16[256,768]{1,0:T(8,128)(2,1)S(1)}, u32[]{:S(2)}, u32[]{:S(2)}) collective-permute-start(bf16[256,768]{1,0:T(8,128)(2,1)} %get-tuple-element.84.refs_3_), channel_id=1, source_target_pairs={{0,12},{4,8},{8,4},{12,0},{16,28},{20,24},{24,20},{28,16},{1,13},{... | collective-permute-start | bytes 1179656 | tf_op jit(solution)/shard_map/ppermute | solution.py:74
  34.7 11.1 %collective-permute-start.7 = (bf16[192,768]{1,0:T(8,128)(2,1)}, bf16[192,768]{1,0:T(8,128)(2,1)}, u32[]{:S(2)}, u32[]{:S(2)}) collective-permute-start(bf16[192,768]{1,0:T(8,128)(2,1)} %collective-permute-done.2.refs_9_), channel_id=1, source_target_pairs={{0,2},{1,3},{2,0},{3,1},{4,6},{5,7},{6,4},{7,5},{8,10},{9,11},{10,... | collective-permute-start | bytes 884744 | tf_op jit(solution)/shard_map/ppermute | solution.py:74
  36.3 1.3 copy-start.18
  42.1 3.8 %collective-permute-start.10 = (f32[4,768]{1,0:T(4,128)S(1)}, f32[4,768]{1,0:T(4,128)S(1)}, u32[]{:S(2)}, u32[]{:S(2)}) collective-permute-start(f32[4,768]{1,0:T(4,128)S(1)} %get-tuple-element.88), channel_id=1, source_target_pairs={{0,2},{1,3},{2,0},{3,1},{4,6},{5,7},{6,4},{7,5},{8,10},{9,11},{10,... | collective-permute-start | bytes 36872 | tf_op jit(solution)/shard_map/ppermute | solution.py:74
  42.7 4.0 %copy-start.34 = (s32[4]{0:T(128)S(1)}, s32[4]{0:T(128)}, u32[]{:S(2)}) copy-start(s32[4]{0:T(128)} %param.21) | copy-start | bytes 52
  42.7 5.9 %copy-start.1 = (bf16[384,768]{1,0:T(8,128)(2,1)S(1)}, bf16[384,768]{1,0:T(8,128)(2,1)}, u32[]{:S(2)}) copy-start(bf16[384,768]{1,0:T(8,128)(2,1)} %refs_4_.4) | copy-start | bytes 1769476
  44.5 1.1 copy-start.2
  46.6 1.9 %collective-permute-start.11 = (bf16[192,768]{1,0:T(8,128)(2,1)}, bf16[192,768]{1,0:T(8,128)(2,1)}, u32[]{:S(2)}, u32[]{:S(2)}) collective-permute-start(bf16[192,768]{1,0:T(8,128)(2,1)} %collective-permute-done.7.refs_10_), channel_id=1, source_target_pairs={{0,1},{1,0},{2,3},{3,2},{4,5},{5,4},{6,7},{7,6},{8,9},{9,8},{10,11... | collective-permute-start | bytes 884744 | tf_op jit(solution)/shard_map/ppermute | solution.py:74
  46.8 1.4 collective-permute-start.12
  48.6 1.1 copy-start.7
  59.4 1.1 copy-start.27
  61.4 4.0 %collective-permute-start.14 = (f32[4,768]{1,0:T(4,128)S(1)}, f32[4,768]{1,0:T(4,128)S(1)}, u32[]{:S(2)}, u32[]{:S(2)}) collective-permute-start(f32[4,768]{1,0:T(4,128)S(1)} %get-tuple-element.98), channel_id=1, source_target_pairs={{0,8},{4,12},{8,0},{12,4},{16,24},{20,28},{24,16},{28,20},{1,9},{5... | collective-permute-start | bytes 36872 | tf_op jit(solution)/shard_map/ppermute | solution.py:74
  61.9 4.6 %collective-permute-start.15 = (f32[4,768]{1,0:T(4,128)S(1)}, f32[4,768]{1,0:T(4,128)S(1)}, u32[]{:S(2)}, u32[]{:S(2)}) collective-permute-start(f32[4,768]{1,0:T(4,128)S(1)} %get-tuple-element.98), channel_id=1, source_target_pairs={{0,12},{4,8},{8,4},{12,0},{16,28},{20,24},{24,20},{28,16},{1,13},{... | collective-permute-start | bytes 36872 | tf_op jit(solution)/shard_map/ppermute | solution.py:74
  63.4 3.8 %collective-permute-start.13 = (f32[4,768]{1,0:T(4,128)S(1)}, f32[4,768]{1,0:T(4,128)S(1)}, u32[]{:S(2)}, u32[]{:S(2)}) collective-permute-start(f32[4,768]{1,0:T(4,128)S(1)} %get-tuple-element.98), channel_id=1, source_target_pairs={{0,4},{4,0},{8,12},{12,8},{16,20},{20,16},{24,28},{28,24},{1,5},{5... | collective-permute-start | bytes 36872 | tf_op jit(solution)/shard_map/ppermute | solution.py:74
  64.8 3.8 %collective-permute-start.16 = (f32[4,1664]{1,0:T(4,128)S(1)}, f32[4,1664]{1,0:T(4,128)S(1)}, u32[]{:S(2)}, u32[]{:S(2)}) collective-permute-start(f32[4,1664]{1,0:T(4,128)S(1)} %concatenate.104), channel_id=1, source_target_pairs={{0,4},{4,0},{8,12},{12,8},{16,20},{20,16},{24,28},{28,24},{1,5},{5... | collective-permute-start | bytes 79880 | tf_op jit(solution)/shard_map/ppermute | solution.py:74
  68.7 5.0 %collective-permute-start.17 = (f32[4,1152]{1,0:T(4,128)S(1)}, f32[4,1152]{1,0:T(4,128)S(1)}, u32[]{:S(2)}, u32[]{:S(2)}) collective-permute-start(f32[4,1152]{1,0:T(4,128)S(1)} %pad_maximum_fusion.6), channel_id=1, source_target_pairs={{0,16},{4,20},{8,24},{12,28},{16,0},{20,4},{24,8},{28,12},{1,17},{... | collective-permute-start | bytes 55304 | tf_op jit(solution)/shard_map/ppermute | solution.py:74
  69.2 14.0 %collective-permute-start.22 = (bf16[256,768]{1,0:T(8,128)(2,1)}, bf16[256,768]{1,0:T(8,128)(2,1)S(1)}, u32[]{:S(2)}, u32[]{:S(2)}) collective-permute-start(bf16[256,768]{1,0:T(8,128)(2,1)} %collective-permute-done.5.refs_2_), channel_id=1, source_target_pairs={{0,1},{1,0},{2,3},{3,2},{4,5},{5,4},{6,7},{7,6},{8,9},{9,8},{10,11... | collective-permute-start | bytes 1179656 | tf_op jit(solution)/shard_map/ppermute | solution.py:74
  69.2 12.1 %collective-permute-start.23 = (bf16[256,768]{1,0:T(8,128)(2,1)}, bf16[256,768]{1,0:T(8,128)(2,1)S(1)}, u32[]{:S(2)}, u32[]{:S(2)}) collective-permute-start(bf16[256,768]{1,0:T(8,128)(2,1)} %collective-permute-done.5.refs_2_), channel_id=1, source_target_pairs={{0,2},{1,3},{2,0},{3,1},{4,6},{5,7},{6,4},{7,5},{8,10},{9,11},{10,... | collective-permute-start | bytes 1179656 | tf_op jit(solution)/shard_map/ppermute | solution.py:74
  70.5 4.2 %collective-permute-start.18 = (f32[8,1664]{1,0:T(8,128)S(1)}, f32[8,1664]{1,0:T(8,128)S(1)}, u32[]{:S(2)}, u32[]{:S(2)}) collective-permute-start(f32[8,1664]{1,0:T(8,128)S(1)} %maximum_select_fusion.6), channel_id=1, source_target_pairs={{0,8},{4,12},{8,0},{12,4},{16,24},{20,28},{24,16},{28,20},{1,9},{5... | collective-permute-start | bytes 159752 | tf_op jit(solution)/shard_map/ppermute | solution.py:74
  74.7 7.0 %collective-permute-start.20 = (f32[1,8,1152]{2,1,0:T(8,128)S(1)}, f32[1,8,1152]{2,1,0:T(8,128)S(1)}, u32[]{:S(2)}, u32[]{:S(2)}) collective-permute-start(f32[1,8,1152]{2,1,0:T(8,128)S(1)} %maximum_bitcast_fusion), channel_id=1, source_target_pairs={{0,2},{1,3},{2,0},{3,1},{4,6},{5,7},{6,4},{7,5},{8,10},{9,11},{10,... | collective-permute-start | bytes 110600 | tf_op jit(solution)/shard_map/ppermute | solution.py:74
  75.6 7.2 %collective-permute-start.19 = (f32[16,1664]{1,0:T(8,128)S(1)}, f32[16,1664]{1,0:T(8,128)S(1)}, u32[]{:S(2)}, u32[]{:S(2)}) collective-permute-start(f32[16,1664]{1,0:T(8,128)S(1)} %maximum_select_fusion.4), channel_id=1, source_target_pairs={{0,16},{4,20},{8,24},{12,28},{16,0},{20,4},{24,8},{28,12},{1,17},{... | collective-permute-start | bytes 319496 | tf_op jit(solution)/shard_map/ppermute | solution.py:74
  81.3 1.9 %collective-permute-start.24 = (bf16[256,768]{1,0:T(8,128)(2,1)S(1)}, bf16[256,768]{1,0:T(8,128)(2,1)S(1)}, u32[]{:S(2)}, u32[]{:S(2)}) collective-permute-start(bf16[256,768]{1,0:T(8,128)(2,1)S(1)} %collective-permute-done.23.refs_4_), channel_id=1, source_target_pairs={{0,1},{1,0},{2,3},{3,2},{4,5},{5,4},{6,7},{7,6},{8,9},{9,8},{10,11... | collective-permute-start | bytes 1179656 | tf_op jit(solution)/shard_map/ppermute | solution.py:74
  81.7 1.4 collective-permute-start.21
  83.2 3.0 %copy-start.5 = (bf16[384,768]{1,0:T(8,128)(2,1)S(1)}, bf16[384,768]{1,0:T(8,128)(2,1)}, u32[]{:S(2)}) copy-start(bf16[384,768]{1,0:T(8,128)(2,1)} %copy-done.4) | copy-start | bytes 1769476
  86.1 2.8 %copy-start.3 = (f32[1024,384]{1,0:T(8,128)S(1)}, f32[1024,384]{1,0:T(8,128)}, u32[]{:S(2)}) copy-start(f32[1024,384]{1,0:T(8,128)} %copy-done.2) | copy-start | bytes 4718596
  86.1 2.8 %copy-start.20 = (f32[768]{0:T(1024)S(1)}, f32[768]{0:T(1024)}, u32[]{:S(2)}) copy-start(f32[768]{0:T(1024)} %refs_7_.5) | copy-start | bytes 9220
  89.0 7.0 %copy-start.8 = (bf16[768,384]{1,0:T(8,128)(2,1)S(1)}, bf16[768,384]{1,0:T(8,128)(2,1)}, u32[]{:S(2)}) copy-start(bf16[768,384]{1,0:T(8,128)(2,1)} %refs_4_.5) | copy-start | bytes 1769476
  89.0 7.0 %copy-start.22 = (f32[768]{0:T(1024)S(1)}, f32[768]{0:T(1024)}, u32[]{:S(2)}) copy-start(f32[768]{0:T(1024)} %refs_6_.3) | copy-start | bytes 9220
  89.0 7.0 %copy-start.28 = (bf16[1024,768]{1,0:T(8,128)(2,1)S(1)}, bf16[1024,768]{1,0:T(8,128)(2,1)}, u32[]{:S(2)}) copy-start(bf16[1024,768]{1,0:T(8,128)(2,1)} %copy-done.27) | copy-start | bytes 4718596
  89.0 7.0 %copy-start.30 = (bf16[768,384]{1,0:T(8,128)(2,1)S(1)}, bf16[768,384]{1,0:T(8,128)(2,1)}, u32[]{:S(2)}) copy-start(bf16[768,384]{1,0:T(8,128)(2,1)} %copy-done.29) | copy-start | bytes 1769476
  91.5 9.1 %copy-start.13 = (f32[192,384]{1,0:T(8,128)}, f32[192,384]{1,0:T(8,128)S(1)}, u32[]{:S(2)}) copy-start(f32[192,384]{1,0:T(8,128)S(1)} %get-tuple-element.116) | copy-start | bytes 884740
  91.5 12.4 %collective-permute-start.25 = (bf16[192,384]{1,0:T(8,128)(2,1)S(1)}, bf16[192,384]{1,0:T(8,128)(2,1)S(1)}, u32[]{:S(2)}, u32[]{:S(2)}) collective-permute-start(bf16[192,384]{1,0:T(8,128)(2,1)S(1)} %get-tuple-element.117), channel_id=1, source_target_pairs={{0,8},{4,12},{8,0},{12,4},{16,24},{20,28},{24,16},{28,20},{1,9},{5... | collective-permute-start | bytes 442376 | tf_op jit(solution)/shard_map/ppermute | solution.py:74
  92.1 13.8 %collective-permute-start.26 = (bf16[192,384]{1,0:T(8,128)(2,1)S(1)}, bf16[192,384]{1,0:T(8,128)(2,1)S(1)}, u32[]{:S(2)}, u32[]{:S(2)}) collective-permute-start(bf16[192,384]{1,0:T(8,128)(2,1)S(1)} %get-tuple-element.118), channel_id=1, source_target_pairs={{0,16},{4,20},{8,24},{12,28},{16,0},{20,4},{24,8},{28,12},{1,17},{... | collective-permute-start | bytes 442376 | tf_op jit(solution)/shard_map/ppermute | solution.py:74
  94.7 11.2 %collective-permute-start.27 = (bf16[192,384]{1,0:T(8,128)(2,1)S(1)}, bf16[192,384]{1,0:T(8,128)(2,1)S(1)}, u32[]{:S(2)}, u32[]{:S(2)}) collective-permute-start(bf16[192,384]{1,0:T(8,128)(2,1)S(1)} %get-tuple-element.119), channel_id=1, source_target_pairs={{0,24},{4,28},{8,16},{12,20},{16,8},{20,12},{24,0},{28,4},{1,25},{... | collective-permute-start | bytes 442376 | tf_op jit(solution)/shard_map/ppermute | solution.py:74
  102.5 3.4 %copy-start.14 = (f32[192,384]{1,0:T(8,128)S(1)}, f32[192,384]{1,0:T(8,128)}, u32[]{:S(2)}) copy-start(f32[192,384]{1,0:T(8,128)} %copy-done.13) | copy-start | bytes 884740
  105.9 2.1 %collective-permute-start.33 = (bf16[384,768]{1,0:T(8,128)(2,1)S(1)}, bf16[384,768]{1,0:T(8,128)(2,1)}, u32[]{:S(2)}, u32[]{:S(2)}) collective-permute-start(bf16[384,768]{1,0:T(8,128)(2,1)S(1)} %get-tuple-element.136), channel_id=1, source_target_pairs={{0,1},{1,0},{2,3},{3,2},{4,5},{5,4},{6,7},{7,6},{8,9},{9,8},{10,11... | collective-permute-start | bytes 1769480 | tf_op jit(solution)/shard_map/ppermute | solution.py:74
  109.3 13.2 %collective-permute-start.34 = (bf16[192,768]{1,0:T(8,128)(2,1)S(1)}, bf16[192,768]{1,0:T(8,128)(2,1)S(1)}, u32[]{:S(2)}, u32[]{:S(2)}) collective-permute-start(bf16[192,768]{1,0:T(8,128)(2,1)S(1)} %dynamic-slice_convert_fusion), channel_id=1, source_target_pairs={{0,2},{1,3},{2,0},{3,1},{4,6},{5,7},{6,4},{7,5},{8,10},{9,11},{10,... | collective-permute-start | bytes 884744 | tf_op jit(solution)/shard_map/ppermute | solution.py:74
  111.0 10.1 %collective-permute-start.28 = (bf16[224,384]{1,0:T(8,128)(2,1)S(1)}, bf16[224,384]{1,0:T(8,128)(2,1)S(1)}, u32[]{:S(2)}, u32[]{:S(2)}) collective-permute-start(bf16[224,384]{1,0:T(8,128)(2,1)S(1)} %pad_maximum_fusion.2), channel_id=1, source_target_pairs={{0,8},{4,12},{8,0},{12,4},{16,24},{20,28},{24,16},{28,20},{1,9},{5... | collective-permute-start | bytes 516104 | tf_op jit(solution)/shard_map/ppermute | solution.py:74
  113.8 15.6 %collective-permute-start.29 = (bf16[224,384]{1,0:T(8,128)(2,1)S(1)}, bf16[224,384]{1,0:T(8,128)(2,1)S(1)}, u32[]{:S(2)}, u32[]{:S(2)}) collective-permute-start(bf16[224,384]{1,0:T(8,128)(2,1)S(1)} %pad_maximum_fusion.2), channel_id=1, source_target_pairs={{0,16},{4,20},{8,24},{12,28},{16,0},{20,4},{24,8},{28,12},{1,17},{... | collective-permute-start | bytes 516104 | tf_op jit(solution)/shard_map/ppermute | solution.py:74
  115.6 13.7 %collective-permute-start.30 = (bf16[224,384]{1,0:T(8,128)(2,1)S(1)}, bf16[224,384]{1,0:T(8,128)(2,1)S(1)}, u32[]{:S(2)}, u32[]{:S(2)}) collective-permute-start(bf16[224,384]{1,0:T(8,128)(2,1)S(1)} %pad_maximum_fusion.2), channel_id=1, source_target_pairs={{0,24},{4,28},{8,16},{12,20},{16,8},{20,12},{24,0},{28,4},{1,25},{... | collective-permute-start | bytes 516104 | tf_op jit(solution)/shard_map/ppermute | solution.py:74
  117.0 6.3 %collective-permute-start.31 = (bf16[192,384]{1,0:T(8,128)(2,1)S(1)}, bf16[192,384]{1,0:T(8,128)(2,1)S(1)}, u32[]{:S(2)}, u32[]{:S(2)}) collective-permute-start(bf16[192,384]{1,0:T(8,128)(2,1)S(1)} %add_convert_fusion.refs_1_), channel_id=1, source_target_pairs={{0,4},{4,0},{8,12},{12,8},{16,20},{20,16},{24,28},{28,24},{1,5},{5... | collective-permute-start | bytes 442376 | tf_op jit(solution)/shard_map/ppermute | solution.py:74
  121.2 8.2 %collective-permute-start.32 = (bf16[192,384]{1,0:T(8,128)(2,1)S(1)}, bf16[192,384]{1,0:T(8,128)(2,1)S(1)}, u32[]{:S(2)}, u32[]{:S(2)}) collective-permute-start(bf16[192,384]{1,0:T(8,128)(2,1)S(1)} %slice.193), channel_id=1, source_target_pairs={{0,4},{4,0},{8,12},{12,8},{16,20},{20,16},{24,28},{28,24},{1,5},{5... | collective-permute-start | bytes 442376 | tf_op jit(solution)/shard_map/ppermute | solution.py:74
  123.3 18.1 %copy-start.31 = (f32[192,768]{1,0:T(8,128)S(1)}, f32[192,768]{1,0:T(8,128)}, u32[]{:S(2)}) copy-start(f32[192,768]{1,0:T(8,128)} %convert_add_fusion.1) | copy-start | bytes 1769476
  130.5 10.9 %collective-permute-start.36 = (bf16[192,384]{1,0:T(8,128)(2,1)S(1)}, bf16[192,384]{1,0:T(8,128)(2,1)S(1)}, u32[]{:S(2)}, u32[]{:S(2)}) collective-permute-start(bf16[192,384]{1,0:T(8,128)(2,1)S(1)} %slice.267), channel_id=1, source_target_pairs={{0,16},{4,20},{8,24},{12,28},{16,0},{20,4},{24,8},{28,12},{1,17},{... | collective-permute-start | bytes 442376 | tf_op jit(solution)/shard_map/ppermute | solution.py:74
  135.2 8.1 %collective-permute-start.35 = (bf16[400,384]{1,0:T(8,128)(2,1)S(1)}, bf16[400,384]{1,0:T(8,128)(2,1)S(1)}, u32[]{:S(2)}, u32[]{:S(2)}) collective-permute-start(bf16[400,384]{1,0:T(8,128)(2,1)S(1)} %pad_maximum_fusion.1), channel_id=1, source_target_pairs={{0,4},{4,0},{8,12},{12,8},{16,20},{20,16},{24,28},{28,24},{1,5},{5... | collective-permute-start | bytes 921608 | tf_op jit(solution)/shard_map/ppermute | solution.py:74
  143.3 5.3 %collective-permute-start.37 = (bf16[208,384]{1,0:T(8,128)(2,1)S(1)}, bf16[208,384]{1,0:T(8,128)(2,1)S(1)}, u32[]{:S(2)}, u32[]{:S(2)}) collective-permute-start(bf16[208,384]{1,0:T(8,128)(2,1)S(1)} %pad_maximum_fusion.3), channel_id=1, source_target_pairs={{0,2},{1,3},{2,0},{3,1},{4,6},{5,7},{6,4},{7,5},{8,10},{9,11},{10,... | collective-permute-start | bytes 479240 | tf_op jit(solution)/shard_map/ppermute | solution.py:74
  148.9 1.7 %collective-permute-start.38 = (bf16[400,384]{1,0:T(8,128)(2,1)S(1)}, bf16[400,384]{1,0:T(8,128)(2,1)S(1)}, u32[]{:S(2)}, u32[]{:S(2)}) collective-permute-start(bf16[400,384]{1,0:T(8,128)(2,1)S(1)} %pad_maximum_fusion), channel_id=1, source_target_pairs={{0,1},{1,0},{2,3},{3,2},{4,5},{5,4},{6,7},{7,6},{8,9},{9,8},{10,11... | collective-permute-start | bytes 921608 | tf_op jit(solution)/shard_map/ppermute | solution.py:74
  (10 other events, 8.5 us)

commit v4 on v3

--- a/solution.py
+++ b/solution.py
@@ -23,7 +23,7 @@
 LOAD = "load"
 
 
-def call(body, in_specs, out_shape, scratch=(), limit=16, flops=0, bytes_accessed=0):
+def call(body, in_specs, out_shape, scratch=(), limit=16, flops=0, bytes_accessed=0, outs=None):
     loads = [i for i, spec in enumerate(in_specs) if spec is LOAD]
     n_in, n_own = len(in_specs), len(out_shape) + len(scratch)
 
@@ -48,7 +48,7 @@
             kernel,
             in_specs=[HBM if spec is LOAD else spec for spec in in_specs],
             out_shape=tuple(jax.ShapeDtypeStruct(s, t) for s, t in out_shape),
-            out_specs=tuple(VMEM for _ in out_shape),
+            out_specs=tuple(outs or [VMEM] * len(out_shape)),
             scratch_shapes=list(scratch) + buffers,
             cost_estimate=pl.CostEstimate(
                 flops=flops, bytes_accessed=bytes_accessed, transcendentals=0
@@ -213,6 +213,7 @@
                 pltpu.VMEM(own_s.shape, BF16),
                 pltpu.SemaphoreType.DMA((fold + 3,)),
             ],
+            limit=60,
         )(place, own_q, own_s, q_gain, s_gain, inner, outer)
     piece = lax.dynamic_slice_in_dim(inner, place[2] * (thin * fold), thin * fold, 0)
     piece = jnp.concatenate([piece[i * thin : (i + 1) * thin] for i in range(fold)], 1)
@@ -242,8 +243,12 @@
     inners, outers = [refs[0]], [refs[1]]
     pieces = refs[2 : 2 + PARTS * far]
     refs = refs[2 + PARTS * far :]
-    pooled, part, rows = refs[:3]
-    gather_rows(token_refs, rows, refs[-1])
+    pooled, part = refs[:2]
+    results, (buffers, sems) = refs[2 : 3 + 2 * far], (refs[3 + 2 * far : -1], refs[-1])
+    rows = buffers[0]
+    gather_rows(token_refs, rows, sems)
+    leaving = [pltpu.make_async_copy(x, y, sems.at[i]) for i, (x, y) in enumerate(zip(buffers, results))]
+    leaving[0].start()
     me = place[axis]
     y, core = place[3], place[4]
     places = (
@@ -253,7 +258,7 @@
         (1 - core) * 2 + (1 - y),
     )
     for f in range(far):
-        inner, outer = refs[3 + 2 * f : 5 + 2 * f]
+        inner, outer = buffers[1 + 2 * f : 3 + 2 * f]
         block = inner.shape[1]
         fold = inner.shape[0] // block
         thin = inner.shape[0] // PARTS // fold
@@ -267,6 +272,8 @@
             outer[pl.ds(first, deep), :] = piece[thin:, :]
         inners.append(inner)
         outers.append(outer)
+    for copy in leaving[1:]:
+        copy.start()
     total = part.shape[0]
     span = own.shape[0]
     index = lax.broadcasted_iota(jnp.int32, (total, 1), 0)
@@ -301,6 +308,8 @@
         )
         base += outer.shape[0]
     part[...] = result
+    for copy in leaving:
+        copy.wait()
 
 
 def forward(place, lengths, own, tokens, inner, outer, pieces, axis):
@@ -308,14 +317,17 @@
     far = len(pieces) // PARTS
     rows = sum(t.shape[0] for t in tokens)
     count = rows // own.shape[0]
+    large = [(rows, width)] + [(width, units), (units, width)] * far
     return call(
         functools.partial(forward_kernel, len(tokens), far, axis),
         [SMEM] * 2 + [LOAD] + [HBM] * len(tokens) + [LOAD] * (2 + len(pieces)),
-        [((count, units * (1 + far)), F32), ((count, width), F32), ((rows, width), BF16)]
-        + [((width, units), BF16), ((units, width), BF16)] * far,
-        [pltpu.SemaphoreType.DMA((len(tokens),))],
+        [((count, units * (1 + far)), F32), ((count, width), F32)] + [(x, BF16) for x in large],
+        [pltpu.VMEM(x, BF16) for x in large]
+        + [pltpu.SemaphoreType.DMA((max(len(tokens), len(large)),))],
         flops=3 * 10**9,
         bytes_accessed=3 * 10**6,
+        limit=60 if far else 24,
+        outs=[VMEM] * 2 + [HBM] * len(large),
     )(place, lengths, own, *tokens, inner, outer, *pieces)
 
 
@@ -537,6 +549,8 @@
         functools.partial(assemble_kernel, pairs),
         [SMEM] + [LOAD] * (pairs + 3),
         [((rows * pairs, 2 * half), F32)],
+        flops=60 * 10**9,
+        bytes_accessed=6 * 10**6,
     )(place, *chunks, own_other, first, rest)[0]
 
 
@@ -646,7 +660,7 @@
     q_all = ordered(q_all, pair_meta, pair_bit)
     pair_lengths = pair_meta[:, width + units + 1].astype(jnp.int32)
     s_part = (s_part + s_others[0]) + (s_others[1] + s_others[2])
-    s_part, q_all = together(s_part, q_all)
+    s_part, q_all, pair_far = together(s_part, q_all, pair_far)
 
     s_sent = [jnp.concatenate([s_part, s_pooled[:, :block]], 1)]
     for i, k in enumerate(far):
@@ -654,25 +668,25 @@
         s_sent.append(swap(jnp.concatenate([s_part, pooled_far], 1), "pb", k))
     q_all = ordered(q_all, swap(q_all, "pb", 2), bit_at(p, 2))
     s_all = canonical(s_sent, p // GROUP)[None]
-    s_all, q_all = together(s_all, q_all)
     pair_tokens = [pair_token] + [None] * (n_sa - 1)
     pair_tokens[top] = pair_far
     for step in reversed(bits_of(n_sa)):
         for k in range(0, n_sa, 2 * step):
             if pair_tokens[k + step] is None:
                 pair_tokens[k + step] = swap(pair_tokens[k], "sa", step)
+    s_all, q_all, pair_tokens = together(s_all, q_all, pair_tokens)
     for step in bits_of(n_pb)[2:]:
         q_all = ordered(q_all, swap(q_all, "pb", step), bit_at(p, step))
+    pair_slope, pair_rows = slopes(place, pair_lengths, pair_tokens, [q_inner_half], 1, length)
     for step in reversed(bits_of(n_sa)):
+        if step == 1:
+            s_all, pair_slope = together(s_all, pair_slope)
         s_all = ordered(s_all, swap(s_all, "sa", step), bit_at(a, step))
     order = [
         sum(((i >> b) & 1) << (n_sa.bit_length() - 2 - b) for b in range(n_sa.bit_length() - 1))
         for i in range(n_sa)
     ]
     s_all = jnp.concatenate([s_all[order[i]] for i in range(n_sa)], 0)
-    pair_slope, pair_rows = slopes(place, pair_lengths, pair_tokens, [q_inner_half], 1, length)
-    q_all, s_all, pair_slope = together(q_all, s_all, pair_slope)
-
     loss, q_grad, s_grad, q_hidden, s_hidden = scores(
         place, q_all, s_all, q_outer_half, s_outers, n_sa, n_pb, width
     )
@@ -704,22 +718,33 @@
 
     q_outer_grad = outer_gradient(q_all[:, width : width + units], q_grad)
     s_outer_grad = outer_gradient(s_all[:, width:], s_grad)
-    q_arrived, s_send, s_keep, packed, q_outer_grad, s_outer_grad = together(
-        q_arrived, s_send, s_keep, packed, q_outer_grad, s_outer_grad
-    )
-    s_beside = swap(s_send, "sa", 1)
+    strips = 6
+    strip = s_send.shape[0] // strips
+    s_beside = [swap(s_send[i * strip : (i + 1) * strip], "sa", 1) for i in range(strips)]
+    s_total = s_keep + jnp.concatenate(s_beside, 0).astype(F32)
+    q_arrived, s_total, packed, q_outer_grad, s_outer_grad = together(
+        q_arrived, s_total, packed, q_outer_grad, s_outer_grad
+    )
 
     q_total = q_keep
     for x in q_arrived:
         q_total = q_total + x.astype(F32)
     q_total = q_total.astype(BF16)
     rows = q_total.shape[0]
-    packed = jnp.concatenate(jnp.split(packed, width // half, 1), 0)
-    sent = jnp.concatenate([q_total, packed], 0)
+
+    def with_gains(x, gains):
+        packed = pack(gains, x.shape[1])
+        return jnp.concatenate([x, packed], 0), unpack(packed, width)
+
+    def arrived_gains(x, rows):
+        return x[:rows], unpack(x[rows:], width)
+
+    gains = packed[:2].astype(F32) + packed[2:4].astype(F32)
+    sent, gains = with_gains(q_total, gains)
     arrivals = [swap(sent, "pb", 2 * k) for k in range(1, pairs)]
     own_other = swap(q_total, "pb", 1)
+    first = swap(arrivals[0][:rows], "pb", 1)
     size = width // 2
-    s_total = s_keep + s_beside.astype(F32)
     for step in bits_of(n_sa)[1:]:
         size = size // 2
         bit = bit_at(a, step)
@@ -727,38 +752,27 @@
         arrived = swap(away, "sa", step)
         s_total = lax.dynamic_slice_in_dim(s_total, bit * size, size, 0)
         s_total = s_total + arrived.astype(F32)
-    first = swap(arrivals[0][:rows], "pb", 1)
     arrivals, own_other, first, s_total = together(arrivals, own_other, first, s_total)
 
-    chunks = [q_total] + list(arrivals)
-
-    def gain_sums(tail):
-        tail = jnp.concatenate(jnp.split(tail, width // half, 0), 1)
-        return tail[:2].astype(F32) + tail[2:4].astype(F32)
-
-    sums = [gain_sums(packed)] + [gain_sums(x[rows:]) for x in arrivals]
+    sums = [gains] + [arrived_gains(x, rows)[1] for x in arrivals]
     while len(sums) > 1:
         sums = [sums[i] + sums[i + 1] for i in range(0, len(sums), 2)]
-    gains = sums[0]
-    packed = pack(gains, half)
-    rest = swap(jnp.concatenate([x[:rows] for x in chunks[2:]] + [packed], 0), "pb", 1)
+    gains = sums[0] + swap(sums[0], "pb", 1)
+    chunks = [q_total] + list(arrivals)
+    rest = swap(jnp.concatenate([x[:rows] for x in chunks[2:]], 0), "pb", 1)
+    q_inner_grad = assemble(place, chunks, own_other, first, rest)
     s_sum = s_total[:, :block]
     for i, k in enumerate(far):
         far_part = s_total[:, (i + 1) * block : (i + 2) * block].astype(BF16)
         s_sum = s_sum + swap(far_part, "pb", k).astype(F32)
-    rest, s_sum = together(rest, s_sum)
-    gains = unpack(packed, width) + unpack(rest[(pairs - 2) * rows :], width)
-    q_inner_grad = assemble(place, chunks, own_other, first, rest)
-
-    s_sum = s_sum.astype(BF16)
+    s_sum, gains = together(s_sum.astype(BF16), gains)
+
     for step in reversed(bits_of(n_sa)):
         size = s_sum.shape[0]
-        packed = pack(gains, block)
-        if step == 1:
-            s_sum, q_inner_grad = together(s_sum, q_inner_grad)
-        arrived = swap(jnp.concatenate([s_sum, packed], 0), "sa", step)
-        gains = unpack(packed, width) + unpack(arrived[size:], width)
-        s_sum = ordered(s_sum, arrived[:size], bit_at(a, step))
+        sent, gains = with_gains(s_sum, gains)
+        arrived, more = arrived_gains(swap(sent, "sa", step), size)
+        gains = gains + more
+        s_sum = ordered(s_sum, arrived, bit_at(a, step))
     s_inner_grad = s_sum.astype(F32)
 
     return (

time: 153 us -> 139 us (0.908)
  local copies, waits for them, and re-layouts: 18.6 us -> 7.91 us
  waiting for transfers between devices: 48.3 us -> 42.6 us
  Pallas kernels: 31.1 us -> 34.1 us
  starting transfers between devices: 45.4 us -> 43.3 us
    unnamed x70 -> x51, local copies, waits for them, and re-layouts: 16.3 us -> 3.35 us
    ppermute x39 -> x45, waiting for transfers between devices: 48.3 us -> 42.6 us  [swap(): return lax.ppermute(x, axis, [(i, i ^ step) for i in range(size)])]
    pallas_call x9, Pallas kernels: 31.1 us -> 34.1 us  [run(): pl.pallas_call(kernel, in_specs=[HBM if spec is LOAD else spec for spec i...]
    ppermute x39 -> x45, starting transfers between devices: 45.4 us -> 43.3 us  [swap(): return lax.ppermute(x, axis, [(i, i ^ step) for i in range(size)])]
  transfers between devices with their start and end apart: 39 -> 45, of which waited for: 23 -> 21; matrix products, arithmetic and copies ran while one was open for 4% -> 8% of each run, Pallas kernels for 10% -> 18%
where the time goes in v4:
time: 139 us; the launch traced here: 138 us
  starting transfers between devices  43.3 us (31%)
  waiting for transfers between devices  42.6 us (31%)
  Pallas kernels  34.1 us (25%)
  local copies, waits for them, and re-layouts  7.91 us (6%)
  other arithmetic  5.57 us (4%)
  matrix products  3.26 us (2%)
  between operations  1.44 us (1%)
    ppermute x45, starting transfers between devices, swap(): return lax.ppermute(x, axis, [(i, i ^ step) for i in range(size)])  43.3 us
    ppermute x45, waiting for transfers between devices, swap(): return lax.ppermute(x, axis, [(i, i ^ step) for i in range(size)])  42.6 us
    pallas_call x9, Pallas kernels, run(): pl.pallas_call(kernel, in_specs=[HBM if spec is LOAD else spec for spec i...  34.1 us
    unnamed x51, local copies, waits for them, and re-layouts  3.35 us
    dot_general x2, matrix products, outer_gradient(): lax.dot_general(left, right, CONTRACT_FIRST, preferred_element_type=F32)  3.26 us
  transfers between devices with their start and end apart: 45, of which 21 were waited for; matrix products, arithmetic and copies ran while one was open for 8% of the time, Pallas kernels for 18%

profile of v4, /device:TPU:0, one launch (start us, length us, event | category | flops | bytes accessed | tf_op | source)
XLA Modules:
  0.0 138.2 jit_solution(2002250009095217347)
XLA Ops:
  0.7 0.6 stack.32.refs_0_
  1.3 4.0 %shard_map.162 = (bf16[256,768]{1,0:T(8,128)(2,1)}, bf16[256,768]{1,0:T(8,128)(2,1)}, bf16[192,768]{1,0:T(8,128)(2,1)}) custom-call(s32[5]{0:T(128)} %stack.32.refs_0_, bf16[256,768]{1,0:T(8,128)(2,1)} %bitcast.20, bf16[256,768]{1,0:T(8,128)(2,1)} %bitcast.23, f32[768]{0:T(1024)} %refs_7_.5, f32[768]{0:T(1024)} %refs_6_.3, bf16[768,384]{1,0:T(8,128)(2,1)} %refs_4_.5, ...), custom_call_target="tpu_custom_call" | custom-call | tf_op jit(solution)/shard_map/pallas_call | solution.py:47
  5.3 4.1 %collective-permute-start.2 = (bf16[192,768]{1,0:T(8,128)(2,1)}, bf16[192,768]{1,0:T(8,128)(2,1)}, u32[]{:S(2)}, u32[]{:S(2)}) collective-permute-start(bf16[192,768]{1,0:T(8,128)(2,1)} %get-tuple-element.80), channel_id=1, source_target_pairs={{0,16},{4,20},{8,24},{12,28},{16,0},{20,4},{24,8},{28,12},{1,17},{... | collective-permute-start | bytes 884744 | tf_op jit(solution)/shard_map/ppermute | solution.py:74
  9.4 1.5 %collective-permute-start = (bf16[256,768]{1,0:T(8,128)(2,1)}, bf16[256,768]{1,0:T(8,128)(2,1)S(1)}, u32[]{:S(2)}, u32[]{:S(2)}) collective-permute-start(bf16[256,768]{1,0:T(8,128)(2,1)} %get-tuple-element.85.refs_3_), channel_id=1, source_target_pairs={{0,4},{4,0},{8,12},{12,8},{16,20},{20,16},{24,28},{28,24},{1,5},{5... | collective-permute-start | bytes 1179656 | tf_op jit(solution)/shard_map/ppermute | solution.py:74
  10.9 1.6 %collective-permute-start.1 = (bf16[256,768]{1,0:T(8,128)(2,1)}, bf16[256,768]{1,0:T(8,128)(2,1)}, u32[]{:S(2)}, u32[]{:S(2)}) collective-permute-start(bf16[256,768]{1,0:T(8,128)(2,1)} %get-tuple-element.85.refs_3_), channel_id=1, source_target_pairs={{0,8},{4,12},{8,0},{12,4},{16,24},{20,28},{24,16},{28,20},{1,9},{5... | collective-permute-start | bytes 1179656 | tf_op jit(solution)/shard_map/ppermute | solution.py:74
  12.5 1.5 %collective-permute-start.4 = (bf16[256,768]{1,0:T(8,128)(2,1)}, bf16[256,768]{1,0:T(8,128)(2,1)}, u32[]{:S(2)}, u32[]{:S(2)}) collective-permute-start(bf16[256,768]{1,0:T(8,128)(2,1)} %get-tuple-element.81.refs_3_), channel_id=1, source_target_pairs={{0,2},{1,3},{2,0},{3,1},{4,6},{5,7},{6,4},{7,5},{8,10},{9,11},{10,... | collective-permute-start | bytes 1179656 | tf_op jit(solution)/shard_map/ppermute | solution.py:74
  14.5 0.6 convert_reduce_fusion.refs_1_
  15.2 8.0 %collective-permute-done.2.refs_9_ = bf16[192,768]{1,0:T(8,128)(2,1)} collective-permute-done((bf16[192,768]{1,0:T(8,128)(2,1)}, bf16[192,768]{1,0:T(8,128)(2,1)}, u32[]{:S(2)}, u32[]{:S(2)}) %collective-permute-start.2) | collective-permute-done | bytes 294944 | tf_op jit(solution)/shard_map/ppermute | solution.py:74
  23.5 0.8 copy-done.15
  24.8 1.9 %collective-permute-done.1.refs_5_ = bf16[256,768]{1,0:T(8,128)(2,1)} collective-permute-done((bf16[256,768]{1,0:T(8,128)(2,1)}, bf16[256,768]{1,0:T(8,128)(2,1)}, u32[]{:S(2)}, u32[]{:S(2)}) %collective-permute-start.1) | collective-permute-done | bytes 393248 | tf_op jit(solution)/shard_map/ppermute | solution.py:74
  26.7 2.1 %collective-permute-done.5.refs_2_ = bf16[256,768]{1,0:T(8,128)(2,1)} collective-permute-done((bf16[256,768]{1,0:T(8,128)(2,1)}, bf16[256,768]{1,0:T(8,128)(2,1)}, u32[]{:S(2)}, u32[]{:S(2)}) %collective-permute-start.5) | collective-permute-done | bytes 393248 | tf_op jit(solution)/shard_map/ppermute | solution.py:74
  28.7 2.5 %collective-permute-start.6 = (bf16[256,768]{1,0:T(8,128)(2,1)}, bf16[256,768]{1,0:T(8,128)(2,1)}, u32[]{:S(2)}, u32[]{:S(2)}) collective-permute-start(bf16[256,768]{1,0:T(8,128)(2,1)} %get-tuple-element.85.refs_3_), channel_id=1, source_target_pairs={{0,12},{4,8},{8,4},{12,0},{16,28},{20,24},{24,20},{28,16},{1,13},{... | collective-permute-start | bytes 1179656 | tf_op jit(solution)/shard_map/ppermute | solution.py:74
  31.2 1.5 %collective-permute-start.7 = (bf16[192,768]{1,0:T(8,128)(2,1)}, bf16[192,768]{1,0:T(8,128)(2,1)}, u32[]{:S(2)}, u32[]{:S(2)}) collective-permute-start(bf16[192,768]{1,0:T(8,128)(2,1)} %collective-permute-done.2.refs_9_), channel_id=1, source_target_pairs={{0,2},{1,3},{2,0},{3,1},{4,6},{5,7},{6,4},{7,5},{8,10},{9,11},{10,... | collective-permute-start | bytes 884744 | tf_op jit(solution)/shard_map/ppermute | solution.py:74
  32.8 1.3 copy-done.9
  34.1 4.8 %shard_map.163 = (f32[4,768]{1,0:T(4,128)S(1)}, f32[4,768]{1,0:T(4,128)S(1)}, bf16[1024,768]{1,0:T(8,128)(2,1)S(1)}) custom-call(s32[5]{0:T(128)S(1)} %copy-done.10, s32[4]{0:T(128)S(1)} %convert_reduce_fusion.1.refs_1_, bf16[256,768]{1,0:T(8,128)(2,1)S(1)} %bitcast.21, bf16[256,768]{1,0:T(8,128)(2,1)S(1)} %copy-done.15, ...), custom_call_target="tpu_custom_call" | custom-call | flops 3000000000 | bytes 3000000 | tf_op jit(solution)/shard_map/pallas_call | solution.py:47
  38.9 0.6 collective-permute-start.10
  39.5 1.8 %shard_map.164.refs_3_ = f32[1024,384]{1,0:T(8,128)S(1)} custom-call(s32[5]{0:T(128)S(1)} %copy-done.10, s32[4]{0:T(128)S(1)} %convert_reduce_fusion.1.refs_1_, bf16[1024,768]{1,0:T(8,128)(2,1)S(1)} %get-tuple-element.90.refs_2_.refs_1_, bf16[768,384]{1,0:T(8,128)(2,1)S(1)} %constant_dynamic-slice_fusion.1.refs_3_.refs_6_), custom_call_target="tpu_custom_call" | custom-call | flops 905969664 | bytes 3000000 | tf_op jit(solution)/shard_map/pallas_call | solution.py:47
  41.3 1.1 copy-done.1
  42.7 0.6 add.108
  44.1 1.3 collective-permute-start.17
  45.6 1.3 add.109
  47.0 0.6 broadcast_in_dim.6
  47.5 1.4 %concatenate.97 = f32[4,1664]{1,0:T(4,128)} concatenate(f32[4,768]{1,0:T(4,128)} %add.109, f32[4,768]{1,0:T(4,128)S(1)} %get-tuple-element.98, f32[4,2]{1,0:T(4,128)S(1)} %add_convert_fusion.2, f32[4,126]{1,0:T(4,128)} %broadcast_in_dim.6), dimensions={1} | concatenate | bytes 53248 | tf_op jit(solution)/shard_map/concatenate | solution.py:650
  48.9 7.2 %shard_map.165 = (f32[4,768]{1,0:T(4,128)}, f32[4,768]{1,0:T(4,128)}, bf16[1024,768]{1,0:T(8,128)(2,1)}, bf16[768,384]{1,0:T(8,128)(2,1)}, bf16[384,768]{1,0:T(8,128)(2,1)}) custom-call(s32[5]{0:T(128)} %stack.32.refs_0_, s32[8]{0:T(128)} %convert_reduce_fusion.refs_1_, bf16[256,768]{1,0:T(8,128)(2,1)} %bitcast.24, ...), custom_call_target="tpu_custom_call" | custom-call | flops 3000000000 | bytes 3000000 | tf_op jit(solution)/shard_map/pallas_call | solution.py:47
  56.6 1.5 %collective-permute-start.15 = (f32[4,768]{1,0:T(4,128)}, f32[4,768]{1,0:T(4,128)S(1)}, u32[]{:S(2)}, u32[]{:S(2)}) collective-permute-start(f32[4,768]{1,0:T(4,128)} %get-tuple-element.99), channel_id=1, source_target_pairs={{0,12},{4,8},{8,4},{12,0},{16,28},{20,24},{24,20},{28,16},{1,13},{... | collective-permute-start | bytes 36872 | tf_op jit(solution)/shard_map/ppermute | solution.py:74
  58.2 1.5 %collective-permute-start.13 = (f32[4,768]{1,0:T(4,128)}, f32[4,768]{1,0:T(4,128)S(1)}, u32[]{:S(2)}, u32[]{:S(2)}) collective-permute-start(f32[4,768]{1,0:T(4,128)} %get-tuple-element.99), channel_id=1, source_target_pairs={{0,4},{4,0},{8,12},{12,8},{16,20},{20,16},{24,28},{28,24},{1,5},{5... | collective-permute-start | bytes 36872 | tf_op jit(solution)/shard_map/ppermute | solution.py:74
  59.7 0.7 fusion.44
  60.4 0.6 collective-permute-start.16
  61.4 0.6 collective-permute-done.13
  62.1 0.7 add_add_fusion
  62.8 1.5 %collective-permute-done.16 = f32[4,1664]{1,0:T(4,128)S(1)} collective-permute-done((f32[4,1664]{1,0:T(4,128)S(1)}, f32[4,1664]{1,0:T(4,128)S(1)}, u32[]{:S(2)}, u32[]{:S(2)}) %collective-permute-start.16) | collective-permute-done | bytes 26656 | tf_op jit(solution)/shard_map/ppermute | solution.py:74
  65.5 3.8 %collective-permute-done.18 = f32[4,1152]{1,0:T(4,128)S(1)} collective-permute-done((f32[4,1152]{1,0:T(4,128)S(1)}, f32[4,1152]{1,0:T(4,128)S(1)}, u32[]{:S(2)}, u32[]{:S(2)}) %collective-permute-start.18) | collective-permute-done | bytes 18464 | tf_op jit(solution)/shard_map/ppermute | solution.py:74
  69.4 2.4 %collective-permute-start.22 = (f32[16,1664]{1,0:T(8,128)S(1)}, f32[16,1664]{1,0:T(8,128)S(1)}, u32[]{:S(2)}, u32[]{:S(2)}) collective-permute-start(f32[16,1664]{1,0:T(8,128)S(1)} %maximum_select_fusion.4), channel_id=1, source_target_pairs={{0,16},{4,20},{8,24},{12,28},{16,0},{20,4},{24,8},{28,12},{1,17},{... | collective-permute-start | bytes 319496 | tf_op jit(solution)/shard_map/ppermute | solution.py:74
  71.8 1.3 collective-permute-start.23
  73.2 2.9 %shard_map.166 = (f32[1024,384]{1,0:T(8,128)S(1)}, bf16[1024,768]{1,0:T(8,128)(2,1)S(1)}) custom-call(s32[5]{0:T(128)S(1)} %copy-done.11, s32[4]{0:T(128)S(1)} %fusion.36.refs_1_, bf16[256,768]{1,0:T(8,128)(2,1)} %collective-permute-done.5.refs_2_, bf16[256,768]{1,0:T(8,128)(2,1)S(1)} %collective-permute-done.20.refs_3_, ...), custom_call_target="tpu_custom_call" | custom-call | flops 905969664 | bytes 3000000 | tf_op jit(solution)/shard_map/pallas_call | solution.py:47
  76.2 1.2 collective-permute-done.24
  77.6 2.6 %shard_map.167 = (f32[1,1]{1,0:T(1,128)}, f32[32,768]{1,0:T(8,128)S(1)}, f32[32,768]{1,0:T(8,128)S(1)}, f32[8,384]{1,0:T(8,128)S(1)}, f32[8,768]{1,0:T(8,128)S(1)}) custom-call(s32[5]{0:T(128)S(1)} %copy-done.11, f32[32,1664]{1,0:T(8,128)S(1)} %maximum_select_fusion.2.refs_1_, f32[32,1152]{1,0:T(8,128)S(1)} %pad_maximum_fusion.4.refs_2_, ...), custom_call_target="tpu_custom_call" | custom-call | tf_op jit(solution)/shard_map/pallas_call | solution.py:47
  80.2 2.5 %shard_map.168 = (bf16[192,384]{1,0:T(8,128)(2,1)S(1)}, bf16[192,384]{1,0:T(8,128)(2,1)S(1)}, bf16[192,384]{1,0:T(8,128)(2,1)S(1)}, f32[192,384]{1,0:T(8,128)S(1)}, f32[1,768]{1,0:T(1,128)S(1)}) custom-call(s32[5]{0:T(128)S(1)} %copy-done.11, bf16[1024,768]{1,0:T(8,128)(2,1)S(1)} %get-tuple-element.90.refs_2_.refs_1_, ...), custom_call_target="tpu_custom_call" | custom-call | flops 4000000000 | bytes 3000000 | tf_op jit(solution)/shard_map/pallas_call | solution.py:47
  83.2 1.6 %collective-permute-start.26 = (bf16[192,384]{1,0:T(8,128)(2,1)S(1)}, bf16[192,384]{1,0:T(8,128)(2,1)S(1)}, u32[]{:S(2)}, u32[]{:S(2)}) collective-permute-start(bf16[192,384]{1,0:T(8,128)(2,1)S(1)} %get-tuple-element.123), channel_id=1, source_target_pairs={{0,16},{4,20},{8,24},{12,28},{16,0},{20,4},{24,8},{28,12},{1,17},{... | collective-permute-start | bytes 442376 | tf_op jit(solution)/shard_map/ppermute | solution.py:74
  84.8 2.3 %collective-permute-start.27 = (bf16[192,384]{1,0:T(8,128)(2,1)S(1)}, bf16[192,384]{1,0:T(8,128)(2,1)S(1)}, u32[]{:S(2)}, u32[]{:S(2)}) collective-permute-start(bf16[192,384]{1,0:T(8,128)(2,1)S(1)} %get-tuple-element.124), channel_id=1, source_target_pairs={{0,24},{4,28},{8,16},{12,20},{16,8},{20,12},{24,0},{28,4},{1,25},{... | collective-permute-start | bytes 442376 | tf_op jit(solution)/shard_map/ppermute | solution.py:74
  87.2 4.8 %shard_map.169 = (bf16[384,768]{1,0:T(8,128)(2,1)S(1)}, f32[384,768]{1,0:T(8,128)S(1)}, bf16[16,768]{1,0:T(8,128)(2,1)S(1)}) custom-call(s32[5]{0:T(128)S(1)} %copy-done.11, s32[8]{0:T(128)S(1)} %copy-done.14, bf16[1024,768]{1,0:T(8,128)(2,1)S(1)} %copy-done.16, f32[8,768]{1,0:T(8,128)S(1)} %get-tuple-element.128.refs_3_, bf16[768,384]{1,0:T(8,128)(2,1)S(1)} %copy-done.4, ...), custom_call_target="tpu_custom_call" | custom-call | flops 6000000000 | bytes 3000000 | tf_op jit(solution)/shard_map/pallas_call | solution.py:47
  92.7 1.9 %fusion.1 = f32[768,768]{1,0:T(8,128)} fusion(bf16[32,768]{1,0:T(8,128)(2,1)S(1)} %get-tuple-element.166, bf16[32,768]{1,0:T(8,128)(2,1)S(1)} %get-tuple-element.165, bf16[32,768]{1,0:T(8,128)(2,1)S(1)} %get-tuple-element.187, bf16[32,768]{1,0:T(8,128)(2,1)S(1)} %get-tuple-element.188), kind=kOutput, calls=%fused_computation.16 | convolution fusion | flops 114130944 | bytes 2555904 | tf_op jit(solution)/shard_map/dot_general | solution.py:717
  94.6 1.4 fusion.12
  96.5 0.7 collective-permute-done.30
  97.8 0.7 collective-permute-done.32
  99.0 1.1 collective-permute-start.39
  100.3 0.9 collective-permute-start.34
  101.2 1.5 %collective-permute-start.35 = (bf16[208,384]{1,0:T(8,128)(2,1)S(1)}, bf16[208,384]{1,0:T(8,128)(2,1)S(1)}, u32[]{:S(2)}, u32[]{:S(2)}) collective-permute-start(bf16[208,384]{1,0:T(8,128)(2,1)S(1)} %pad_maximum_fusion.3), channel_id=1, source_target_pairs={{0,16},{4,20},{8,24},{12,28},{16,0},{20,4},{24,8},{28,12},{1,17},{... | collective-permute-start | bytes 479240 | tf_op jit(solution)/shard_map/ppermute | solution.py:74
  102.7 2.0 %collective-permute-start.36 = (bf16[208,384]{1,0:T(8,128)(2,1)S(1)}, bf16[208,384]{1,0:T(8,128)(2,1)S(1)}, u32[]{:S(2)}, u32[]{:S(2)}) collective-permute-start(bf16[208,384]{1,0:T(8,128)(2,1)S(1)} %pad_maximum_fusion.3), channel_id=1, source_target_pairs={{0,24},{4,28},{8,16},{12,20},{16,8},{20,12},{24,0},{28,4},{1,25},{... | collective-permute-start | bytes 479240 | tf_op jit(solution)/shard_map/ppermute | solution.py:74
  104.7 0.5 collective-permute-start.37
  105.3 3.4 %collective-permute-done.34.refs_2_ = bf16[208,384]{1,0:T(8,128)(2,1)S(1)} collective-permute-done((bf16[208,384]{1,0:T(8,128)(2,1)S(1)}, bf16[208,384]{1,0:T(8,128)(2,1)S(1)}, u32[]{:S(2)}, u32[]{:S(2)}) %collective-permute-start.34) | collective-permute-done | bytes 159776 | tf_op jit(solution)/shard_map/ppermute | solution.py:74
  109.2 0.6 collective-permute-done.37.refs_5_
  109.9 5.9 %collective-permute-done.35.refs_3_ = bf16[208,384]{1,0:T(8,128)(2,1)S(1)} collective-permute-done((bf16[208,384]{1,0:T(8,128)(2,1)S(1)}, bf16[208,384]{1,0:T(8,128)(2,1)S(1)}, u32[]{:S(2)}, u32[]{:S(2)}) %collective-permute-start.35) | collective-permute-done | bytes 159776 | tf_op jit(solution)/shard_map/ppermute | solution.py:74
  115.8 2.9 %collective-permute-start.41 = (bf16[192,384]{1,0:T(8,128)(2,1)S(1)}, bf16[192,384]{1,0:T(8,128)(2,1)S(1)}, u32[]{:S(2)}, u32[]{:S(2)}) collective-permute-start(bf16[192,384]{1,0:T(8,128)(2,1)S(1)} %slice.304), channel_id=1, source_target_pairs={{0,16},{4,20},{8,24},{12,28},{16,0},{20,4},{24,8},{28,12},{1,17},{... | collective-permute-start | bytes 442376 | tf_op jit(solution)/shard_map/ppermute | solution.py:74
  118.8 0.7 collective-permute-start.42
  119.5 3.0 %collective-permute-done.42 = f32[2,768]{1,0:T(2,128)S(1)} collective-permute-done((f32[2,768]{1,0:T(2,128)S(1)}, f32[2,768]{1,0:T(2,128)S(1)}, u32[]{:S(2)}, u32[]{:S(2)}) %collective-permute-start.42) | collective-permute-done | bytes 6176 | tf_op jit(solution)/shard_map/ppermute | solution.py:74
  122.5 2.2 %collective-permute-done.41 = bf16[192,384]{1,0:T(8,128)(2,1)S(1)} collective-permute-done((bf16[192,384]{1,0:T(8,128)(2,1)S(1)}, bf16[192,384]{1,0:T(8,128)(2,1)S(1)}, u32[]{:S(2)}, u32[]{:S(2)}) %collective-permute-start.41) | collective-permute-done | bytes 147488 | tf_op jit(solution)/shard_map/ppermute | solution.py:74
  124.8 1.1 collective-permute-start.43
  126.0 0.7 collective-permute-start.40
  126.7 3.4 %collective-permute-done.43 = bf16[208,384]{1,0:T(8,128)(2,1)S(1)} collective-permute-done((bf16[208,384]{1,0:T(8,128)(2,1)S(1)}, bf16[208,384]{1,0:T(8,128)(2,1)S(1)}, u32[]{:S(2)}, u32[]{:S(2)}) %collective-permute-start.43) | collective-permute-done | bytes 159776 | tf_op jit(solution)/shard_map/ppermute | solution.py:74
  130.4 2.4 %collective-permute-done.40.refs_7_ = bf16[384,384]{1,0:T(8,128)(2,1)S(1)} collective-permute-done((bf16[384,384]{1,0:T(8,128)(2,1)S(1)}, bf16[384,384]{1,0:T(8,128)(2,1)S(1)}, u32[]{:S(2)}, u32[]{:S(2)}) %collective-permute-start.40) | collective-permute-done | bytes 294944 | tf_op jit(solution)/shard_map/ppermute | solution.py:74
  132.8 3.5 %shard_map.170 = f32[768,768]{1,0:T(8,128)} custom-call(s32[5]{0:T(128)S(1)} %copy-done.11, bf16[192,384]{1,0:T(8,128)(2,1)S(1)} %add_convert_fusion.1.refs_1_, bf16[208,384]{1,0:T(8,128)(2,1)S(1)} %collective-permute-done.34.refs_2_, bf16[208,384]{1,0:T(8,128)(2,1)S(1)} %collective-permute-done.35.refs_3_, ...), custom_call_target="tpu_custom_call" | custom-call | flops 60000002048 | bytes 6000000 | tf_op jit(solution)/shard_map/pallas_call | solution.py:47
  136.4 0.6 slice_reduce_fusion
  137.0 1.1 fusion
  (162 shorter events, 9.1 us)
Async XLA Ops:
  0.6 13.9 %copy-start.19 = (s32[1,8,256]{2,1,0:T(8,128)S(1)}, s32[1,8,256]{2,1,0:T(8,128)}, u32[]{:S(2)}) copy-start(s32[1,8,256]{2,1,0:T(8,128)} %param.17) | copy-start | bytes 24580
  0.6 22.5 %copy-start.20 = (s32[1,4,256]{2,1,0:T(4,128)S(1)}, s32[1,4,256]{2,1,0:T(4,128)}, u32[]{:S(2)}) copy-start(s32[1,4,256]{2,1,0:T(4,128)} %param.12) | copy-start | bytes 12292
  0.7 22.6 %copy-start.6 = (bf16[768,768]{1,0:T(8,128)(2,1)S(1)}, bf16[768,768]{1,0:T(8,128)(2,1)}, u32[]{:S(2)}) copy-start(bf16[768,768]{1,0:T(8,128)(2,1)} %refs_7_.3) | copy-start | bytes 3538948
  1.3 22.1 %copy-start.8 = (bf16[768,768]{1,0:T(8,128)(2,1)S(1)}, bf16[768,768]{1,0:T(8,128)(2,1)}, u32[]{:S(2)}) copy-start(bf16[768,768]{1,0:T(8,128)(2,1)} %refs_8_.2) | copy-start | bytes 3538948
  5.3 17.9 %collective-permute-start.2 = (bf16[192,768]{1,0:T(8,128)(2,1)}, bf16[192,768]{1,0:T(8,128)(2,1)}, u32[]{:S(2)}, u32[]{:S(2)}) collective-permute-start(bf16[192,768]{1,0:T(8,128)(2,1)} %get-tuple-element.80), channel_id=1, source_target_pairs={{0,16},{4,20},{8,24},{12,28},{16,0},{20,4},{24,8},{28,12},{1,17},{... | collective-permute-start | bytes 884744 | tf_op jit(solution)/shard_map/ppermute | solution.py:74
  9.4 14.1 %collective-permute-start = (bf16[256,768]{1,0:T(8,128)(2,1)}, bf16[256,768]{1,0:T(8,128)(2,1)S(1)}, u32[]{:S(2)}, u32[]{:S(2)}) collective-permute-start(bf16[256,768]{1,0:T(8,128)(2,1)} %get-tuple-element.85.refs_3_), channel_id=1, source_target_pairs={{0,4},{4,0},{8,12},{12,8},{16,20},{20,16},{24,28},{28,24},{1,5},{5... | collective-permute-start | bytes 1179656 | tf_op jit(solution)/shard_map/ppermute | solution.py:74
  10.9 15.8 %collective-permute-start.1 = (bf16[256,768]{1,0:T(8,128)(2,1)}, bf16[256,768]{1,0:T(8,128)(2,1)}, u32[]{:S(2)}, u32[]{:S(2)}) collective-permute-start(bf16[256,768]{1,0:T(8,128)(2,1)} %get-tuple-element.85.refs_3_), channel_id=1, source_target_pairs={{0,8},{4,12},{8,0},{12,4},{16,24},{20,28},{24,16},{28,20},{1,9},{5... | collective-permute-start | bytes 1179656 | tf_op jit(solution)/shard_map/ppermute | solution.py:74
  12.5 14.2 %collective-permute-start.4 = (bf16[256,768]{1,0:T(8,128)(2,1)}, bf16[256,768]{1,0:T(8,128)(2,1)}, u32[]{:S(2)}, u32[]{:S(2)}) collective-permute-start(bf16[256,768]{1,0:T(8,128)(2,1)} %get-tuple-element.81.refs_3_), channel_id=1, source_target_pairs={{0,2},{1,3},{2,0},{3,1},{4,6},{5,7},{6,4},{7,5},{8,10},{9,11},{10,... | collective-permute-start | bytes 1179656 | tf_op jit(solution)/shard_map/ppermute | solution.py:74
  14.0 14.7 %collective-permute-start.5 = (bf16[256,768]{1,0:T(8,128)(2,1)}, bf16[256,768]{1,0:T(8,128)(2,1)}, u32[]{:S(2)}, u32[]{:S(2)}) collective-permute-start(bf16[256,768]{1,0:T(8,128)(2,1)} %get-tuple-element.81.refs_3_), channel_id=1, source_target_pairs={{0,4},{4,0},{8,12},{12,8},{16,20},{20,16},{24,28},{28,24},{1,5},{5... | collective-permute-start | bytes 1179656 | tf_op jit(solution)/shard_map/ppermute | solution.py:74
  23.2 5.6 %collective-permute-start.3 = (bf16[192,768]{1,0:T(8,128)(2,1)}, bf16[192,768]{1,0:T(8,128)(2,1)}, u32[]{:S(2)}, u32[]{:S(2)}) collective-permute-start(bf16[192,768]{1,0:T(8,128)(2,1)} %collective-permute-done.2.refs_9_), channel_id=1, source_target_pairs={{0,1},{1,0},{2,3},{3,2},{4,5},{5,4},{6,7},{7,6},{8,9},{9,8},{10,11... | collective-permute-start | bytes 884744 | tf_op jit(solution)/shard_map/ppermute | solution.py:74
  23.3 9.5 %copy-start.5 = (bf16[1,1,256,768]{3,2,1,0:T(8,128)(2,1)S(1)}, bf16[1,1,256,768]{3,2,1,0:T(8,128)(2,1)}, u32[]{:S(2)}) copy-start(bf16[1,1,256,768]{3,2,1,0:T(8,128)(2,1)} %param.11) | copy-start | bytes 1179652
  23.3 9.5 %copy-start.7 = (bf16[768,768]{1,0:T(8,128)(2,1)S(1)}, bf16[768,768]{1,0:T(8,128)(2,1)}, u32[]{:S(2)}) copy-start(bf16[768,768]{1,0:T(8,128)(2,1)} %refs_7_.3) | copy-start | bytes 3538948
  23.3 9.5 %copy-start.10 = (s32[5]{0:T(128)S(1)}, s32[5]{0:T(128)}, u32[]{:S(2)}) copy-start(s32[5]{0:T(128)} %stack.32.refs_0_) | copy-start | bytes 64
  24.3 14.6 %copy-start.22 = (bf16[256,768]{1,0:T(8,128)(2,1)}, bf16[256,768]{1,0:T(8,128)(2,1)S(1)}, u32[]{:S(2)}) copy-start(bf16[256,768]{1,0:T(8,128)(2,1)S(1)} %collective-permute-done.refs_4_) | copy-start | bytes 1179652
  24.3 8.5 %collective-permute-start.8 = (bf16[256,768]{1,0:T(8,128)(2,1)S(1)}, bf16[256,768]{1,0:T(8,128)(2,1)S(1)}, u32[]{:S(2)}, u32[]{:S(2)}) collective-permute-start(bf16[256,768]{1,0:T(8,128)(2,1)S(1)} %copy-done.15), channel_id=1, source_target_pairs={{0,1},{1,0},{2,3},{3,2},{4,5},{5,4},{6,7},{7,6},{8,9},{9,8},{10,11... | collective-permute-start | bytes 1179656 | tf_op jit(solution)/shard_map/ppermute | solution.py:74
  28.7 4.0 %collective-permute-start.9 = (bf16[256,768]{1,0:T(8,128)(2,1)}, bf16[256,768]{1,0:T(8,128)(2,1)S(1)}, u32[]{:S(2)}, u32[]{:S(2)}) collective-permute-start(bf16[256,768]{1,0:T(8,128)(2,1)} %collective-permute-done.4.refs_5_), channel_id=1, source_target_pairs={{0,1},{1,0},{2,3},{3,2},{4,5},{5,4},{6,7},{7,6},{8,9},{9,8},{10,11... | collective-permute-start | bytes 1179656 | tf_op jit(solution)/shard_map/ppermute | solution.py:74
  28.7 14.5 %collective-permute-start.6 = (bf16[256,768]{1,0:T(8,128)(2,1)}, bf16[256,768]{1,0:T(8,128)(2,1)}, u32[]{:S(2)}, u32[]{:S(2)}) collective-permute-start(bf16[256,768]{1,0:T(8,128)(2,1)} %get-tuple-element.85.refs_3_), channel_id=1, source_target_pairs={{0,12},{4,8},{8,4},{12,0},{16,28},{20,24},{24,20},{28,16},{1,13},{... | collective-permute-start | bytes 1179656 | tf_op jit(solution)/shard_map/ppermute | solution.py:74
  31.2 12.0 %collective-permute-start.7 = (bf16[192,768]{1,0:T(8,128)(2,1)}, bf16[192,768]{1,0:T(8,128)(2,1)}, u32[]{:S(2)}, u32[]{:S(2)}) collective-permute-start(bf16[192,768]{1,0:T(8,128)(2,1)} %collective-permute-done.2.refs_9_), channel_id=1, source_target_pairs={{0,2},{1,3},{2,0},{3,1},{4,6},{5,7},{6,4},{7,5},{8,10},{9,11},{10,... | collective-permute-start | bytes 884744 | tf_op jit(solution)/shard_map/ppermute | solution.py:74
  38.9 3.8 %collective-permute-start.10 = (f32[4,768]{1,0:T(4,128)S(1)}, f32[4,768]{1,0:T(4,128)S(1)}, u32[]{:S(2)}, u32[]{:S(2)}) collective-permute-start(f32[4,768]{1,0:T(4,128)S(1)} %get-tuple-element.89), channel_id=1, source_target_pairs={{0,2},{1,3},{2,0},{3,1},{4,6},{5,7},{6,4},{7,5},{8,10},{9,11},{10,... | collective-permute-start | bytes 36872 | tf_op jit(solution)/shard_map/ppermute | solution.py:74
  39.5 3.8 %copy-start.21 = (s32[4]{0:T(128)S(1)}, s32[4]{0:T(128)}, u32[]{:S(2)}) copy-start(s32[4]{0:T(128)} %param.21) | copy-start | bytes 52
  43.3 5.7 %collective-permute-start.11 = (bf16[192,768]{1,0:T(8,128)(2,1)}, bf16[192,768]{1,0:T(8,128)(2,1)}, u32[]{:S(2)}, u32[]{:S(2)}) collective-permute-start(bf16[192,768]{1,0:T(8,128)(2,1)} %collective-permute-done.7.refs_10_), channel_id=1, source_target_pairs={{0,1},{1,0},{2,3},{3,2},{4,5},{5,4},{6,7},{7,6},{8,9},{9,8},{10,11... | collective-permute-start | bytes 884744 | tf_op jit(solution)/shard_map/ppermute | solution.py:74
  43.4 26.0 %collective-permute-start.20 = (bf16[256,768]{1,0:T(8,128)(2,1)}, bf16[256,768]{1,0:T(8,128)(2,1)S(1)}, u32[]{:S(2)}, u32[]{:S(2)}) collective-permute-start(bf16[256,768]{1,0:T(8,128)(2,1)} %collective-permute-done.5.refs_2_), channel_id=1, source_target_pairs={{0,1},{1,0},{2,3},{3,2},{4,5},{5,4},{6,7},{7,6},{8,9},{9,8},{10,11... | collective-permute-start | bytes 1179656 | tf_op jit(solution)/shard_map/ppermute | solution.py:74
  44.0 1.7 %collective-permute-start.12 = (f32[4,768]{1,0:T(4,128)}, f32[4,768]{1,0:T(4,128)S(1)}, u32[]{:S(2)}, u32[]{:S(2)}) collective-permute-start(f32[4,768]{1,0:T(4,128)} %add.108), channel_id=1, source_target_pairs={{0,1},{1,0},{2,3},{3,2},{4,5},{5,4},{6,7},{7,6},{8,9},{9,8},{10,11... | collective-permute-start | bytes 36872 | tf_op jit(solution)/shard_map/ppermute | solution.py:74
  44.1 20.2 %collective-permute-start.17 = (bf16[256,768]{1,0:T(8,128)(2,1)}, bf16[256,768]{1,0:T(8,128)(2,1)S(1)}, u32[]{:S(2)}, u32[]{:S(2)}) collective-permute-start(bf16[256,768]{1,0:T(8,128)(2,1)} %collective-permute-done.5.refs_2_), channel_id=1, source_target_pairs={{0,2},{1,3},{2,0},{3,1},{4,6},{5,7},{6,4},{7,5},{8,10},{9,11},{10,... | collective-permute-start | bytes 1179656 | tf_op jit(solution)/shard_map/ppermute | solution.py:74
  48.9 11.5 %copy-start.18 = (f32[4,1664]{1,0:T(4,128)S(1)}, f32[4,1664]{1,0:T(4,128)}, u32[]{:S(2)}) copy-start(f32[4,1664]{1,0:T(4,128)} %concatenate.97) | copy-start | bytes 79876
  48.9 24.2 %copy-start.11 = (s32[5]{0:T(128)S(1)}, s32[5]{0:T(128)}, u32[]{:S(2)}) copy-start(s32[5]{0:T(128)} %stack.32.refs_0_) | copy-start | bytes 64
  56.1 4.3 %collective-permute-start.14 = (f32[4,768]{1,0:T(4,128)}, f32[4,768]{1,0:T(4,128)S(1)}, u32[]{:S(2)}, u32[]{:S(2)}) collective-permute-start(f32[4,768]{1,0:T(4,128)} %get-tuple-element.99), channel_id=1, source_target_pairs={{0,8},{4,12},{8,0},{12,4},{16,24},{20,28},{24,16},{28,20},{1,9},{5... | collective-permute-start | bytes 36872 | tf_op jit(solution)/shard_map/ppermute | solution.py:74
  56.6 4.8 %collective-permute-start.15 = (f32[4,768]{1,0:T(4,128)}, f32[4,768]{1,0:T(4,128)S(1)}, u32[]{:S(2)}, u32[]{:S(2)}) collective-permute-start(f32[4,768]{1,0:T(4,128)} %get-tuple-element.99), channel_id=1, source_target_pairs={{0,12},{4,8},{8,4},{12,0},{16,28},{20,24},{24,20},{28,16},{1,13},{... | collective-permute-start | bytes 36872 | tf_op jit(solution)/shard_map/ppermute | solution.py:74
  58.2 3.9 %collective-permute-start.13 = (f32[4,768]{1,0:T(4,128)}, f32[4,768]{1,0:T(4,128)S(1)}, u32[]{:S(2)}, u32[]{:S(2)}) collective-permute-start(f32[4,768]{1,0:T(4,128)} %get-tuple-element.99), channel_id=1, source_target_pairs={{0,4},{4,0},{8,12},{12,8},{16,20},{20,16},{24,28},{28,24},{1,5},{5... | collective-permute-start | bytes 36872 | tf_op jit(solution)/shard_map/ppermute | solution.py:74
  60.4 3.9 %collective-permute-start.16 = (f32[4,1664]{1,0:T(4,128)S(1)}, f32[4,1664]{1,0:T(4,128)S(1)}, u32[]{:S(2)}, u32[]{:S(2)}) collective-permute-start(f32[4,1664]{1,0:T(4,128)S(1)} %copy-done.18), channel_id=1, source_target_pairs={{0,4},{4,0},{8,12},{12,8},{16,20},{20,16},{24,28},{28,24},{1,5},{5... | collective-permute-start | bytes 79880 | tf_op jit(solution)/shard_map/ppermute | solution.py:74
  64.4 4.9 %collective-permute-start.18 = (f32[4,1152]{1,0:T(4,128)S(1)}, f32[4,1152]{1,0:T(4,128)S(1)}, u32[]{:S(2)}, u32[]{:S(2)}) collective-permute-start(f32[4,1152]{1,0:T(4,128)S(1)} %pad_maximum_fusion.6), channel_id=1, source_target_pairs={{0,16},{4,20},{8,24},{12,28},{16,0},{20,4},{24,8},{28,12},{1,17},{... | collective-permute-start | bytes 55304 | tf_op jit(solution)/shard_map/ppermute | solution.py:74
  65.0 4.4 %collective-permute-start.19 = (f32[8,1664]{1,0:T(8,128)S(1)}, f32[8,1664]{1,0:T(8,128)S(1)}, u32[]{:S(2)}, u32[]{:S(2)}) collective-permute-start(f32[8,1664]{1,0:T(8,128)S(1)} %maximum_select_fusion.6), channel_id=1, source_target_pairs={{0,8},{4,12},{8,0},{12,4},{16,24},{20,28},{24,16},{28,20},{1,9},{5... | collective-permute-start | bytes 159752 | tf_op jit(solution)/shard_map/ppermute | solution.py:74
  65.5 3.9 %collective-permute-start.21 = (bf16[256,768]{1,0:T(8,128)(2,1)S(1)}, bf16[256,768]{1,0:T(8,128)(2,1)S(1)}, u32[]{:S(2)}, u32[]{:S(2)}) collective-permute-start(bf16[256,768]{1,0:T(8,128)(2,1)S(1)} %collective-permute-done.17.refs_4_), channel_id=1, source_target_pairs={{0,1},{1,0},{2,3},{3,2},{4,5},{5,4},{6,7},{7,6},{8,9},{9,8},{10,11... | collective-permute-start | bytes 1179656 | tf_op jit(solution)/shard_map/ppermute | solution.py:74
  69.4 6.8 %collective-permute-start.22 = (f32[16,1664]{1,0:T(8,128)S(1)}, f32[16,1664]{1,0:T(8,128)S(1)}, u32[]{:S(2)}, u32[]{:S(2)}) collective-permute-start(f32[16,1664]{1,0:T(8,128)S(1)} %maximum_select_fusion.4), channel_id=1, source_target_pairs={{0,16},{4,20},{8,24},{12,28},{16,0},{20,4},{24,8},{28,12},{1,17},{... | collective-permute-start | bytes 319496 | tf_op jit(solution)/shard_map/ppermute | solution.py:74
  71.8 4.3 %collective-permute-start.23 = (f32[1,8,1152]{2,1,0:T(8,128)S(1)}, f32[1,8,1152]{2,1,0:T(8,128)S(1)}, u32[]{:S(2)}, u32[]{:S(2)}) collective-permute-start(f32[1,8,1152]{2,1,0:T(8,128)S(1)} %maximum_bitcast_fusion), channel_id=1, source_target_pairs={{0,2},{1,3},{2,0},{3,1},{4,6},{5,7},{6,4},{7,5},{8,10},{9,11},{10,... | collective-permute-start | bytes 110600 | tf_op jit(solution)/shard_map/ppermute | solution.py:74
  76.1 1.5 %copy-start = (bf16[384,768]{1,0:T(8,128)(2,1)S(1)}, bf16[384,768]{1,0:T(8,128)(2,1)}, u32[]{:S(2)}) copy-start(bf16[384,768]{1,0:T(8,128)(2,1)} %refs_4_.4) | copy-start | bytes 1769476
  76.1 1.3 collective-permute-start.24
  77.5 2.7 %copy-start.2 = (f32[1024,384]{1,0:T(8,128)S(1)}, f32[1024,384]{1,0:T(8,128)}, u32[]{:S(2)}) copy-start(f32[1024,384]{1,0:T(8,128)} %copy-done.1) | copy-start | bytes 4718596
  77.5 2.6 %copy-start.12 = (f32[768]{0:T(1024)S(1)}, f32[768]{0:T(1024)}, u32[]{:S(2)}) copy-start(f32[768]{0:T(1024)} %refs_7_.5) | copy-start | bytes 9220
  80.2 7.0 %copy-start.4 = (bf16[768,384]{1,0:T(8,128)(2,1)S(1)}, bf16[768,384]{1,0:T(8,128)(2,1)}, u32[]{:S(2)}) copy-start(bf16[768,384]{1,0:T(8,128)(2,1)} %refs_4_.5) | copy-start | bytes 1769476
  80.2 7.0 %copy-start.13 = (f32[768]{0:T(1024)S(1)}, f32[768]{0:T(1024)}, u32[]{:S(2)}) copy-start(f32[768]{0:T(1024)} %refs_6_.3) | copy-start | bytes 9220
  80.2 7.0 %copy-start.14 = (s32[8]{0:T(128)S(1)}, s32[8]{0:T(128)}, u32[]{:S(2)}) copy-start(s32[8]{0:T(128)} %convert_reduce_fusion.refs_1_) | copy-start | bytes 100
  80.2 7.0 %copy-start.16 = (bf16[1024,768]{1,0:T(8,128)(2,1)S(1)}, bf16[1024,768]{1,0:T(8,128)(2,1)}, u32[]{:S(2)}) copy-start(bf16[1024,768]{1,0:T(8,128)(2,1)} %get-tuple-element.125.refs_2_) | copy-start | bytes 4718596
  80.2 7.0 %copy-start.17 = (bf16[768,384]{1,0:T(8,128)(2,1)S(1)}, bf16[768,384]{1,0:T(8,128)(2,1)}, u32[]{:S(2)}) copy-start(bf16[768,384]{1,0:T(8,128)(2,1)} %get-tuple-element.129.refs_5_) | copy-start | bytes 1769476
  82.7 16.2 %collective-permute-start.25 = (bf16[192,384]{1,0:T(8,128)(2,1)S(1)}, bf16[192,384]{1,0:T(8,128)(2,1)S(1)}, u32[]{:S(2)}, u32[]{:S(2)}) collective-permute-start(bf16[192,384]{1,0:T(8,128)(2,1)S(1)} %get-tuple-element.122), channel_id=1, source_target_pairs={{0,8},{4,12},{8,0},{12,4},{16,24},{20,28},{24,16},{28,20},{1,9},{5... | collective-permute-start | bytes 442376 | tf_op jit(solution)/shard_map/ppermute | solution.py:74
  83.2 15.7 %collective-permute-start.26 = (bf16[192,384]{1,0:T(8,128)(2,1)S(1)}, bf16[192,384]{1,0:T(8,128)(2,1)S(1)}, u32[]{:S(2)}, u32[]{:S(2)}) collective-permute-start(bf16[192,384]{1,0:T(8,128)(2,1)S(1)} %get-tuple-element.123), channel_id=1, source_target_pairs={{0,16},{4,20},{8,24},{12,28},{16,0},{20,4},{24,8},{28,12},{1,17},{... | collective-permute-start | bytes 442376 | tf_op jit(solution)/shard_map/ppermute | solution.py:74
  84.8 14.1 %collective-permute-start.27 = (bf16[192,384]{1,0:T(8,128)(2,1)S(1)}, bf16[192,384]{1,0:T(8,128)(2,1)S(1)}, u32[]{:S(2)}, u32[]{:S(2)}) collective-permute-start(bf16[192,384]{1,0:T(8,128)(2,1)S(1)} %get-tuple-element.124), channel_id=1, source_target_pairs={{0,24},{4,28},{8,16},{12,20},{16,8},{20,12},{24,0},{28,4},{1,25},{... | collective-permute-start | bytes 442376 | tf_op jit(solution)/shard_map/ppermute | solution.py:74
  92.1 3.9 %collective-permute-start.28 = (bf16[64,768]{1,0:T(8,128)(2,1)S(1)}, bf16[64,768]{1,0:T(8,128)(2,1)S(1)}, u32[]{:S(2)}, u32[]{:S(2)}) collective-permute-start(bf16[64,768]{1,0:T(8,128)(2,1)S(1)} %get-tuple-element.164), channel_id=1, source_target_pairs={{0,1},{1,0},{2,3},{3,2},{4,5},{5,4},{6,7},{7,6},{8,9},{9,8},{10,11... | collective-permute-start | bytes 294920 | tf_op jit(solution)/shard_map/ppermute | solution.py:74
  92.2 3.9 %collective-permute-start.29 = (bf16[64,768]{1,0:T(8,128)(2,1)S(1)}, bf16[64,768]{1,0:T(8,128)(2,1)S(1)}, u32[]{:S(2)}, u32[]{:S(2)}) collective-permute-start(bf16[64,768]{1,0:T(8,128)(2,1)S(1)} %get-tuple-element.163), channel_id=1, source_target_pairs={{0,1},{1,0},{2,3},{3,2},{4,5},{5,4},{6,7},{7,6},{8,9},{9,8},{10,11... | collective-permute-start | bytes 294920 | tf_op jit(solution)/shard_map/ppermute | solution.py:74
  95.9 1.3 collective-permute-start.30
  96.0 1.4 %collective-permute-start.31 = (bf16[64,768]{1,0:T(8,128)(2,1)S(1)}, bf16[64,768]{1,0:T(8,128)(2,1)S(1)}, u32[]{:S(2)}, u32[]{:S(2)}) collective-permute-start(bf16[64,768]{1,0:T(8,128)(2,1)S(1)} %get-tuple-element.161), channel_id=1, source_target_pairs={{0,1},{1,0},{2,3},{3,2},{4,5},{5,4},{6,7},{7,6},{8,9},{9,8},{10,11... | collective-permute-start | bytes 294920 | tf_op jit(solution)/shard_map/ppermute | solution.py:74
  97.2 1.3 collective-permute-start.32
  97.5 1.3 collective-permute-start.33
  99.0 10.1 %collective-permute-start.39 = (bf16[192,768]{1,0:T(8,128)(2,1)S(1)}, bf16[192,768]{1,0:T(8,128)(2,1)S(1)}, u32[]{:S(2)}, u32[]{:S(2)}) collective-permute-start(bf16[192,768]{1,0:T(8,128)(2,1)S(1)} %dynamic-slice_convert_fusion), channel_id=1, source_target_pairs={{0,2},{1,3},{2,0},{3,1},{4,6},{5,7},{6,4},{7,5},{8,10},{9,11},{10,... | collective-permute-start | bytes 884744 | tf_op jit(solution)/shard_map/ppermute | solution.py:74
  100.3 8.4 %collective-permute-start.34 = (bf16[208,384]{1,0:T(8,128)(2,1)S(1)}, bf16[208,384]{1,0:T(8,128)(2,1)S(1)}, u32[]{:S(2)}, u32[]{:S(2)}) collective-permute-start(bf16[208,384]{1,0:T(8,128)(2,1)S(1)} %pad_maximum_fusion.3), channel_id=1, source_target_pairs={{0,8},{4,12},{8,0},{12,4},{16,24},{20,28},{24,16},{28,20},{1,9},{5... | collective-permute-start | bytes 479240 | tf_op jit(solution)/shard_map/ppermute | solution.py:74
  101.2 14.5 %collective-permute-start.35 = (bf16[208,384]{1,0:T(8,128)(2,1)S(1)}, bf16[208,384]{1,0:T(8,128)(2,1)S(1)}, u32[]{:S(2)}, u32[]{:S(2)}) collective-permute-start(bf16[208,384]{1,0:T(8,128)(2,1)S(1)} %pad_maximum_fusion.3), channel_id=1, source_target_pairs={{0,16},{4,20},{8,24},{12,28},{16,0},{20,4},{24,8},{28,12},{1,17},{... | collective-permute-start | bytes 479240 | tf_op jit(solution)/shard_map/ppermute | solution.py:74
  102.7 13.1 %collective-permute-start.36 = (bf16[208,384]{1,0:T(8,128)(2,1)S(1)}, bf16[208,384]{1,0:T(8,128)(2,1)S(1)}, u32[]{:S(2)}, u32[]{:S(2)}) collective-permute-start(bf16[208,384]{1,0:T(8,128)(2,1)S(1)} %pad_maximum_fusion.3), channel_id=1, source_target_pairs={{0,24},{4,28},{8,16},{12,20},{16,8},{20,12},{24,0},{28,4},{1,25},{... | collective-permute-start | bytes 479240 | tf_op jit(solution)/shard_map/ppermute | solution.py:74
  104.7 5.1 %collective-permute-start.37 = (bf16[192,384]{1,0:T(8,128)(2,1)S(1)}, bf16[192,384]{1,0:T(8,128)(2,1)S(1)}, u32[]{:S(2)}, u32[]{:S(2)}) collective-permute-start(bf16[192,384]{1,0:T(8,128)(2,1)S(1)} %add_convert_fusion.1.refs_1_), channel_id=1, source_target_pairs={{0,4},{4,0},{8,12},{12,8},{16,20},{20,16},{24,28},{28,24},{1,5},{5... | collective-permute-start | bytes 442376 | tf_op jit(solution)/shard_map/ppermute | solution.py:74
  108.7 7.1 %collective-permute-start.38 = (bf16[192,384]{1,0:T(8,128)(2,1)S(1)}, bf16[192,384]{1,0:T(8,128)(2,1)S(1)}, u32[]{:S(2)}, u32[]{:S(2)}) collective-permute-start(bf16[192,384]{1,0:T(8,128)(2,1)S(1)} %slice.216), channel_id=1, source_target_pairs={{0,4},{4,0},{8,12},{12,8},{16,20},{20,16},{24,28},{28,24},{1,5},{5... | collective-permute-start | bytes 442376 | tf_op jit(solution)/shard_map/ppermute | solution.py:74
  115.8 8.9 %collective-permute-start.41 = (bf16[192,384]{1,0:T(8,128)(2,1)S(1)}, bf16[192,384]{1,0:T(8,128)(2,1)S(1)}, u32[]{:S(2)}, u32[]{:S(2)}) collective-permute-start(bf16[192,384]{1,0:T(8,128)(2,1)S(1)} %slice.304), channel_id=1, source_target_pairs={{0,16},{4,20},{8,24},{12,28},{16,0},{20,4},{24,8},{28,12},{1,17},{... | collective-permute-start | bytes 442376 | tf_op jit(solution)/shard_map/ppermute | solution.py:74
  118.8 3.7 %collective-permute-start.42 = (f32[2,768]{1,0:T(2,128)S(1)}, f32[2,768]{1,0:T(2,128)S(1)}, u32[]{:S(2)}, u32[]{:S(2)}) collective-permute-start(f32[2,768]{1,0:T(2,128)S(1)} %fusion.33), channel_id=1, source_target_pairs={{0,4},{4,0},{8,12},{12,8},{16,20},{20,16},{24,28},{28,24},{1,5},{5... | collective-permute-start | bytes 18440 | tf_op jit(solution)/shard_map/ppermute | solution.py:74
  124.8 5.3 %collective-permute-start.43 = (bf16[208,384]{1,0:T(8,128)(2,1)S(1)}, bf16[208,384]{1,0:T(8,128)(2,1)S(1)}, u32[]{:S(2)}, u32[]{:S(2)}) collective-permute-start(bf16[208,384]{1,0:T(8,128)(2,1)S(1)} %pad_maximum_fusion.2), channel_id=1, source_target_pairs={{0,2},{1,3},{2,0},{3,1},{4,6},{5,7},{6,4},{7,5},{8,10},{9,11},{10,... | collective-permute-start | bytes 479240 | tf_op jit(solution)/shard_map/ppermute | solution.py:74
  126.0 6.8 %collective-permute-start.40 = (bf16[384,384]{1,0:T(8,128)(2,1)S(1)}, bf16[384,384]{1,0:T(8,128)(2,1)S(1)}, u32[]{:S(2)}, u32[]{:S(2)}) collective-permute-start(bf16[384,384]{1,0:T(8,128)(2,1)S(1)} %pad_maximum_fusion.1), channel_id=1, source_target_pairs={{0,4},{4,0},{8,12},{12,8},{16,20},{20,16},{24,28},{28,24},{1,5},{5... | collective-permute-start | bytes 884744 | tf_op jit(solution)/shard_map/ppermute | solution.py:74
  130.4 6.0 %collective-permute-start.44 = (bf16[400,384]{1,0:T(8,128)(2,1)S(1)}, bf16[400,384]{1,0:T(8,128)(2,1)S(1)}, u32[]{:S(2)}, u32[]{:S(2)}) collective-permute-start(bf16[400,384]{1,0:T(8,128)(2,1)S(1)} %pad_maximum_fusion), channel_id=1, source_target_pairs={{0,1},{1,0},{2,3},{3,2},{4,5},{5,4},{6,7},{7,6},{8,9},{9,8},{10,11... | collective-permute-start | bytes 921608 | tf_op jit(solution)/shard_map/ppermute | solution.py:74
  (4 other events, 4.9 us)

commit v5 on v4

--- a/solution.py
+++ b/solution.py
@@ -21,24 +21,35 @@
 SMEM = pl.BlockSpec(memory_space=pltpu.SMEM)
 HBM = pl.BlockSpec(memory_space=pltpu.HBM)
 LOAD = "load"
-
-
-def call(body, in_specs, out_shape, scratch=(), limit=16, flops=0, bytes_accessed=0, outs=None):
-    loads = [i for i, spec in enumerate(in_specs) if spec is LOAD]
+LATE = "late"
+
+
+def call(body, in_specs, out_shape, scratch=(), limit=16, flops=0, bytes_accessed=0, outs=None, aliases=None, staged=False):
+    loads = [i for i, spec in enumerate(in_specs) if spec in (LOAD, LATE)]
     n_in, n_own = len(in_specs), len(out_shape) + len(scratch)
 
     def kernel(*refs):
         ins, rest = list(refs[:n_in]), refs[n_in:]
-        copies = []
+        copies = {}
         for j, i in enumerate(loads):
             buffer = rest[n_own + j]
-            copies.append(pltpu.make_async_copy(ins[i], buffer, rest[-1].at[j]))
+            copies[i] = pltpu.make_async_copy(ins[i], buffer, rest[-1].at[j])
             ins[i] = buffer
-        for copy in copies:
-            copy.start()
-        for copy in copies:
-            copy.wait()
-        body(*ins, *rest[:n_own])
+        for wanted in (LOAD, LATE):
+            for i in loads:
+                if in_specs[i] is wanted:
+                    copies[i].start()
+
+        def arrive(wanted):
+            for i in loads:
+                if in_specs[i] is wanted:
+                    copies[i].wait()
+
+        if staged:
+            body(arrive, *ins, *rest[:n_own])
+        else:
+            arrive(LOAD)
+            body(*ins, *rest[:n_own])
 
     def run(*args):
         buffers = [pltpu.VMEM(args[i].shape, args[i].dtype) for i in loads]
@@ -46,10 +57,11 @@
             buffers.append(pltpu.SemaphoreType.DMA((len(loads),)))
         return pl.pallas_call(
             kernel,
-            in_specs=[HBM if spec is LOAD else spec for spec in in_specs],
+            in_specs=[HBM if spec in (LOAD, LATE) else spec for spec in in_specs],
             out_shape=tuple(jax.ShapeDtypeStruct(s, t) for s, t in out_shape),
             out_specs=tuple(outs or [VMEM] * len(out_shape)),
             scratch_shapes=list(scratch) + buffers,
+            input_output_aliases=aliases or {},
             cost_estimate=pl.CostEstimate(
                 flops=flops, bytes_accessed=bytes_accessed, transcendentals=0
             ),
@@ -233,23 +245,50 @@
         first += count
     for copy in copies:
         copy.start()
-    for copy in copies:
-        copy.wait()
-
-
-def forward_kernel(n, far, axis, *refs):
-    place, lengths, own = refs[:3]
-    token_refs, refs = refs[3 : 3 + n], refs[3 + n :]
+    return copies
+
+
+def forward_kernel(n, far, axis, arrive, place, lengths, positive, own, *refs):
+    token_refs, refs = refs[:n], refs[n:]
     inners, outers = [refs[0]], [refs[1]]
     pieces = refs[2 : 2 + PARTS * far]
     refs = refs[2 + PARTS * far :]
-    pooled, part = refs[:2]
-    results, (buffers, sems) = refs[2 : 3 + 2 * far], (refs[3 + 2 * far : -1], refs[-1])
+    width = own.shape[1]
+    if far:
+        part, *outs = refs[: 2 + far]
+        refs = refs[2 + far :]
+    else:
+        part, outs, refs = refs[0], [refs[0]], refs[1:]
+    start = 0 if far else width
+    results, buffers, sems = refs[: 1 + 2 * far], refs[1 + 2 * far : -1], refs[-1]
     rows = buffers[0]
-    gather_rows(token_refs, rows, sems)
-    leaving = [pltpu.make_async_copy(x, y, sems.at[i]) for i, (x, y) in enumerate(zip(buffers, results))]
+    gathered = gather_rows(token_refs, rows, sems)
+    leaving = [
+        pltpu.make_async_copy(x, y, sems.at[i]) for i, (x, y) in enumerate(zip(buffers, results))
+    ]
+    arrive(LOAD)
+    for copy in gathered:
+        copy.wait()
     leaving[0].start()
     me = place[axis]
+    span = own.shape[0]
+    total = rows.shape[0] // span
+    index = lax.broadcasted_iota(jnp.int32, (total, 1), 0)
+
+    def pool(inner, out):
+        for columns in column_tiles(inner.shape[1]):
+            weight = inner[:, columns]
+            tile = jnp.zeros((total, weight.shape[1]), F32)
+            for k in range(total):
+                length = lengths[me ^ k]
+                value = gelu_value(product(rows[k * span : (k + 1) * span, :], weight))
+                value = jnp.where(run_mask(span, 0, length), value, 0.0)
+                row = jnp.sum(value, axis=0, keepdims=True) / length.astype(F32)
+                tile = jnp.where(index == ((me ^ k) & (total - 1)), row, tile)
+            out[:, start + columns.start : start + columns.stop] = tile
+
+    pool(inners[0], outs[0])
+    arrive(LATE)
     y, core = place[3], place[4]
     places = (
         core * 2 + y,
@@ -274,30 +313,15 @@
         outers.append(outer)
     for copy in leaving[1:]:
         copy.start()
-    total = part.shape[0]
-    span = own.shape[0]
-    index = lax.broadcasted_iota(jnp.int32, (total, 1), 0)
-    base = 0
-    for inner in inners:
-        for columns in column_tiles(inner.shape[1]):
-            weight = inner[:, columns]
-            tile = jnp.zeros((total, weight.shape[1]), F32)
-            for k in range(total):
-                length = lengths[me ^ k]
-                value = gelu_value(product(rows[k * span : (k + 1) * span, :], weight))
-                value = jnp.where(run_mask(span, 0, length), value, 0.0)
-                row = jnp.sum(value, axis=0, keepdims=True) / length.astype(F32)
-                tile = jnp.where(index == ((me ^ k) & (total - 1)), row, tile)
-            pooled[:, base + columns.start : base + columns.stop] = tile
-        base += inner.shape[1]
+    for inner, out in zip(inners[1:], outs[1:]):
+        pool(inner, out)
     x = own[...].astype(F32)
     length = lengths[me]
     x = jnp.where(run_mask(span, 0, length), x, 0.0)
     own_row = jnp.sum(x, axis=0, keepdims=True) / length.astype(F32)
     result = jnp.where(index == (me & (total - 1)), own_row, 0.0)
-    base = 0
-    for outer in outers:
-        units = pooled[:, base : base + outer.shape[0]]
+    for outer, out in zip(outers, outs):
+        units = out[:, start : start + outer.shape[0]]
         high = units.astype(BF16)
         rest = units - high.astype(F32)
         middle = rest.astype(BF16)
@@ -306,36 +330,61 @@
         result = result + (
             product(high, weight) + (product(middle, weight) + product(low, weight))
         )
-        base += outer.shape[0]
-    part[...] = result
+    part[:, :width] = result
+    if positive is not None:
+        lane = lax.broadcasted_iota(jnp.int32, (total, 128), 1)
+        row = lax.broadcasted_iota(jnp.int32, (total, 128), 0)
+        meta = jnp.zeros((total, 128), F32)
+        for k in range(total):
+            pair = jnp.where(lane == 0, positive[k], jnp.where(lane == 1, lengths[k], 0))
+            meta = jnp.where(row == k, pair.astype(F32), meta)
+        part[:, part.shape[1] - 128 :] = meta
     for copy in leaving:
         copy.wait()
 
 
-def forward(place, lengths, own, tokens, inner, outer, pieces, axis):
+def forward(place, lengths, positive, own, tokens, inner, outer, pieces, axis):
     width, units = inner.shape
     far = len(pieces) // PARTS
     rows = sum(t.shape[0] for t in tokens)
     count = rows // own.shape[0]
     large = [(rows, width)] + [(width, units), (units, width)] * far
+    columns = width + units + 128
+    body = functools.partial(forward_kernel, len(tokens), far, axis)
+    if far:
+        return call(
+            lambda arrive, place, lengths, *refs: body(arrive, place, lengths, None, *refs),
+            [SMEM] * 2 + [LOAD] + [HBM] * len(tokens) + [LOAD] * 2 + [LATE] * len(pieces),
+            [((count, width), F32)]
+            + [((count, units), F32)] * (1 + far)
+            + [(x, BF16) for x in large],
+            [pltpu.VMEM(x, BF16) for x in large]
+            + [pltpu.SemaphoreType.DMA((max(len(tokens), len(large)),))],
+            flops=3 * 10**9,
+            bytes_accessed=3 * 10**6,
+            limit=62,
+            outs=[VMEM] * (2 + far) + [HBM] * len(large),
+            staged=True,
+        )(place, lengths, own, *tokens, inner, outer, *pieces)
     return call(
-        functools.partial(forward_kernel, len(tokens), far, axis),
-        [SMEM] * 2 + [LOAD] + [HBM] * len(tokens) + [LOAD] * (2 + len(pieces)),
-        [((count, units * (1 + far)), F32), ((count, width), F32)] + [(x, BF16) for x in large],
-        [pltpu.VMEM(x, BF16) for x in large]
-        + [pltpu.SemaphoreType.DMA((max(len(tokens), len(large)),))],
+        body,
+        [SMEM] * 3 + [LOAD] + [HBM] * len(tokens) + [LOAD] * 2,
+        [((count, columns), F32)] + [(x, BF16) for x in large],
+        [pltpu.VMEM(x, BF16) for x in large] + [pltpu.SemaphoreType.DMA((len(tokens),))],
         flops=3 * 10**9,
         bytes_accessed=3 * 10**6,
-        limit=60 if far else 24,
-        outs=[VMEM] * 2 + [HBM] * len(large),
-    )(place, lengths, own, *tokens, inner, outer, *pieces)
+        limit=24,
+        outs=[VMEM] + [HBM] * len(large),
+        staged=True,
+    )(place, lengths, positive, own, *tokens, inner, outer)
 
 
 def slope_kernel(n, axis, span, gathered, place, lengths, *refs):
     token_refs = refs[:n]
     if gathered:
         weights, out, rows = refs[n:-3], refs[-3], refs[-2]
-        gather_rows(token_refs, rows, refs[-1])
+        for copy in gather_rows(token_refs, rows, refs[-1]):
+            copy.wait()
     else:
         weights, out, rows = refs[n:-1], refs[-1], token_refs[0]
     me = place[axis] & (lengths.shape[0] - 1)
@@ -527,31 +576,45 @@
     )(place, q_all, s_all, q_outer, *s_outers)
 
 
-def assemble_kernel(pairs, place, *refs):
-    out = refs[-1]
-    chunks, (own_other, first, rest) = refs[:pairs], refs[pairs:-1]
-    rows, half = own_other.shape
+def assemble_kernel(first, own_rows, packed, continued, place, *refs):
+    out, buffer, sems = refs[-3:]
+    refs = refs[1:-3] if continued else refs[:-3]
+    count = len(refs) - 1 if packed else len(refs) // 2
+    chunks, others = refs[:count], refs[count:]
     mine = place[0] // 2
     even = place[0] % 2 == 0
-    for k in range(pairs):
-        a = chunks[k][:rows, :].astype(F32)
-        b = own_other if k == 0 else first if k == 1 else rest.at[pl.ds((k - 2) * rows, rows), :]
-        b = b[...].astype(F32)
-        where = pl.ds(pl.multiple_of((mine ^ k) * rows, 8), rows)
-        out[where, :half] = jnp.where(even, a, b)
-        out[where, half:] = jnp.where(even, b, a)
-
-
-def assemble(place, chunks, own_other, first, rest):
-    rows, half = own_other.shape
-    pairs = len(chunks)
+    copies = []
+    for k in range(count):
+        half = chunks[k].shape[1]
+        a = chunks[k][:own_rows, :].astype(F32)
+        b = others[0][k * own_rows : (k + 1) * own_rows, :] if packed else others[k][...]
+        b = b.astype(F32)
+        buffer[k, :, :half] = jnp.where(even, a, b)
+        buffer[k, :, half:] = jnp.where(even, b, a)
+        place_of = pl.multiple_of((mine ^ (first + k)) * own_rows, 8)
+        copies.append(
+            pltpu.make_async_copy(buffer.at[k], out.at[pl.ds(place_of, own_rows), :], sems.at[k])
+        )
+        copies[-1].start()
+    for copy in copies:
+        copy.wait()
+
+
+def assemble(place, chunks, others, first, rows, shape, packed=False, earlier=None):
+    before = [] if earlier is None else [earlier]
     return call(
-        functools.partial(assemble_kernel, pairs),
-        [SMEM] + [LOAD] * (pairs + 3),
-        [((rows * pairs, 2 * half), F32)],
-        flops=60 * 10**9,
-        bytes_accessed=6 * 10**6,
-    )(place, *chunks, own_other, first, rest)[0]
+        functools.partial(assemble_kernel, first, rows, packed, bool(before)),
+        [SMEM] + [HBM] * len(before) + [LOAD] * (len(chunks) + len(others)),
+        [(shape, F32)],
+        [
+            pltpu.VMEM((len(chunks), rows, shape[1]), F32),
+            pltpu.SemaphoreType.DMA((len(chunks),)),
+        ],
+        flops=2 * 10**9,
+        bytes_accessed=3 * 10**6,
+        outs=[HBM],
+        aliases={1: 0} if before else {},
+    )(place, *before, *chunks, *others)[0]
 
 
 def per_device(
@@ -586,7 +649,6 @@
     mine = [swap(piece, "pb", k) for k in far]
     beside = [swap(piece, "sa", 1) for piece in mine]
     from_x, from_z = swap(s_normed, "pb", 1), swap(s_normed, "pb", 2)
-    pair_token = swap(q_normed, "pb", 1)
     q_far = swap(q_normed, "sa", top)
     pair_bit = bit_at(p, 1)
     q_inner_half = lax.dynamic_slice_in_dim(q_inner_weight, pair_bit * half, half, 1)
@@ -599,8 +661,7 @@
         mine,
         beside,
         q_far,
-        pair_token,
-        s_late,
+        q_late,
         q_inner_half,
         q_outer_half,
         q_lengths,
@@ -611,8 +672,7 @@
         mine,
         beside,
         q_far,
-        pair_token,
-        s_normed,
+        q_normed,
         q_inner_half,
         q_outer_half,
         q_lengths,
@@ -620,7 +680,8 @@
     )
 
     across = [swap(piece, "sa", 2) for piece in mine]
-    from_xz = swap(s_late, "pb", 3)
+    from_xz = swap(from_x, "pb", 2)
+    pair_token = swap(q_late, "pb", 1)
     q_tokens = [q_normed] + [None] * (n_sa - 1)
     q_tokens[top] = q_far
     for step in reversed(bits_of(n_sa)):
@@ -628,28 +689,35 @@
             if q_tokens[k + step] is None:
                 q_tokens[k + step] = swap(q_tokens[k], "sa", step)
 
-    q_pooled, q_part, q_rows = forward(
-        place, q_lengths, own_q, q_tokens, q_inner_weight, q_outer_weight, [], 1
-    )
+    q_all, q_rows = forward(
+        place, q_lengths, positive_column, own_q, q_tokens, q_inner_weight, q_outer_weight, [], 1
+    )
+    in_part = jnp.arange(q_all.shape[1], dtype=jnp.int32)[None, :] < width
+
+    def add_part(x, step):
+        return jnp.where(in_part, x + swap(x, "sa", step), x)
+
     (own_slope,) = slopes(place, q_lengths, [q_rows], [q_inner_half], 1, length)
     q_steps = list(reversed(bits_of(n_sa)))
     for step in q_steps[:-1]:
-        q_part = q_part + swap(q_part, "sa", step)
-    from_xz, across, q_part, own_slope, pair_late = together(
-        from_xz, across, q_part, own_slope, pair_token
-    )
-    pair_far = swap(pair_late, "sa", top)
+        q_all = add_part(q_all, step)
+    from_xz, across, q_all, own_slope, pair_token = together(
+        from_xz, across, q_all, own_slope, pair_token
+    )
+    pair_far = swap(pair_token, "sa", top)
 
     pieces = []
     for one, two, three in zip(mine, across, beside):
         pieces += [one, two, three, swap(two, "sa", 1)]
     s_tokens = [s_normed, from_x, from_z, from_xz]
-    q_part = q_part + swap(q_part, "sa", q_steps[-1])
-    meta = jnp.stack([positive_column, q_lengths], 1).astype(F32)
-    meta = jnp.concatenate([meta, jnp.zeros((n_sa, 126), F32)], 1)
-    q_all = jnp.concatenate([q_part, q_pooled, meta], 1)
-    s_pooled, s_part, s_rows, *far_weights = forward(
-        place, s_lengths, own_s, s_tokens, s_inner_weight, s_outer_weight, pieces, 0
+    q_all = add_part(q_all, q_steps[-1])
+    s_part, *s_rest = forward(
+        place, s_lengths, None, own_s, s_tokens, s_inner_weight, s_outer_weight, pieces, 0
+    )
+    s_pooled, s_rows, far_weights = (
+        s_rest[: 1 + len(far)],
+        s_rest[1 + len(far)],
+        s_rest[2 + len(far) :],
     )
     s_inners = [s_inner_weight] + far_weights[0::2]
     s_outers = [s_outer_weight] + far_weights[1::2]
@@ -660,21 +728,25 @@
     q_all = ordered(q_all, pair_meta, pair_bit)
     pair_lengths = pair_meta[:, width + units + 1].astype(jnp.int32)
     s_part = (s_part + s_others[0]) + (s_others[1] + s_others[2])
-    s_part, q_all, pair_far = together(s_part, q_all, pair_far)
-
-    s_sent = [jnp.concatenate([s_part, s_pooled[:, :block]], 1)]
-    for i, k in enumerate(far):
-        pooled_far = s_pooled[:, (i + 1) * block : (i + 2) * block]
-        s_sent.append(swap(jnp.concatenate([s_part, pooled_far], 1), "pb", k))
+    s_part, q_all, pair_lengths = together(s_part, q_all, pair_lengths)
+
+    s_sent = [jnp.concatenate([s_part, s_pooled[0]], 1)]
+    for i, k in enumerate(far, 1):
+        s_sent.append(swap(jnp.concatenate([s_part, s_pooled[i]], 1), "pb", k))
     q_all = ordered(q_all, swap(q_all, "pb", 2), bit_at(p, 2))
     s_all = canonical(s_sent, p // GROUP)[None]
-    pair_tokens = [pair_token] + [None] * (n_sa - 1)
-    pair_tokens[top] = pair_far
+    pair_beside = swap(pair_token, "sa", 1)
+    s_all, q_all, pair_far, pair_beside = together(s_all, q_all, pair_far, pair_beside)
+    pair_tokens = [[pair_token], [pair_beside]] + [None] * (n_sa - 2)
+    pair_tokens[top] = [pair_far]
     for step in reversed(bits_of(n_sa)):
         for k in range(0, n_sa, 2 * step):
             if pair_tokens[k + step] is None:
-                pair_tokens[k + step] = swap(pair_tokens[k], "sa", step)
-    s_all, q_all, pair_tokens = together(s_all, q_all, pair_tokens)
+                cuts = 4 if step == 1 else 1
+                pair_tokens[k + step] = [
+                    swap(x, "sa", step) for x in jnp.split(pair_tokens[k][0], cuts, axis=0)
+                ]
+    pair_tokens = [x for parts in pair_tokens for x in parts]
     for step in bits_of(n_pb)[2:]:
         q_all = ordered(q_all, swap(q_all, "pb", step), bit_at(p, step))
     pair_slope, pair_rows = slopes(place, pair_lengths, pair_tokens, [q_inner_half], 1, length)
@@ -760,15 +832,19 @@
     gains = sums[0] + swap(sums[0], "pb", 1)
     chunks = [q_total] + list(arrivals)
     rest = swap(jnp.concatenate([x[:rows] for x in chunks[2:]], 0), "pb", 1)
-    q_inner_grad = assemble(place, chunks, own_other, first, rest)
+    shape = (width, 2 * half)
+    q_inner_grad = assemble(place, chunks[:2], [own_other, first], 0, rows, shape)
     s_sum = s_total[:, :block]
     for i, k in enumerate(far):
         far_part = s_total[:, (i + 1) * block : (i + 2) * block].astype(BF16)
         s_sum = s_sum + swap(far_part, "pb", k).astype(F32)
-    s_sum, gains = together(s_sum.astype(BF16), gains)
+    s_sum, gains, q_inner_grad, rest = together(s_sum.astype(BF16), gains, q_inner_grad, rest)
+    q_inner_grad = assemble(place, chunks[2:], [rest], 2, rows, shape, True, q_inner_grad)
 
     for step in reversed(bits_of(n_sa)):
         size = s_sum.shape[0]
+        if step == 1:
+            s_sum, q_inner_grad = together(s_sum, q_inner_grad)
         sent, gains = with_gains(s_sum, gains)
         arrived, more = arrived_gains(swap(sent, "sa", step), size)
         gains = gains + more

time: 139 us -> 135 us (0.971)
  waiting for transfers between devices: 42.6 us -> 39 us
  starting transfers between devices: 43.3 us -> 45.6 us
  local copies, waits for them, and re-layouts: 7.91 us -> 5.97 us
    ppermute x45 -> x48, waiting for transfers between devices: 42.6 us -> 39 us  [swap(): return lax.ppermute(x, axis, [(i, i ^ step) for i in range(size)])]
    ppermute x45 -> x48, starting transfers between devices: 43.3 us -> 45.6 us  [swap(): return lax.ppermute(x, axis, [(i, i ^ step) for i in range(size)])]
    add x2 -> x0, other arithmetic: 1.91 us -> none  [the longest x1 1.31 us: per_device(): q_part = q_part + swap(q_part, 'sa', q_steps[-1])]
    unnamed x51 -> x58, local copies, waits for them, and re-layouts: 3.35 us -> 2.34 us
    pallas_call x9 -> x10, Pallas kernels: 34.1 us -> 34.4 us  [run(): pl.pallas_call(kernel, in_specs=[HBM if spec in (LOAD, LATE) else spec fo...]
  transfers between devices with their start and end apart: 45 -> 48, of which waited for: 21 -> 24; matrix products, arithmetic and copies ran while one was open for 8% -> 6% of each run, Pallas kernels for 18% -> 14%
where the time goes in v5:
time: 135 us; the launch traced here: 134 us
  starting transfers between devices  45.6 us (34%)
  waiting for transfers between devices  39 us (29%)
  Pallas kernels  34.4 us (25%)
  local copies, waits for them, and re-layouts  5.97 us (4%)
  other arithmetic  4.27 us (3%)
  matrix products  3.26 us (2%)
  between operations  1.52 us (1%)
    ppermute x48, starting transfers between devices, swap(): return lax.ppermute(x, axis, [(i, i ^ step) for i in range(size)])  45.6 us
    ppermute x48, waiting for transfers between devices, swap(): return lax.ppermute(x, axis, [(i, i ^ step) for i in range(size)])  39 us
    pallas_call x10, Pallas kernels, run(): pl.pallas_call(kernel, in_specs=[HBM if spec in (LOAD, LATE) else spec fo...  34.4 us
    dot_general x2, matrix products, outer_gradient(): lax.dot_general(left, right, CONTRACT_FIRST, preferred_element_type=F32)  3.26 us
  transfers between devices with their start and end apart: 48, of which 24 were waited for; matrix products, arithmetic and copies ran while one was open for 6% of the time, Pallas kernels for 14%

profile of v5, /device:TPU:0, one launch (start us, length us, event | category | flops | bytes accessed | tf_op | source)
XLA Modules:
  0.0 134.1 jit_solution(381204719066136320)
XLA Ops:
  0.7 0.7 stack.23.refs_0_
  1.3 3.9 %shard_map.162 = (bf16[256,768]{1,0:T(8,128)(2,1)}, bf16[256,768]{1,0:T(8,128)(2,1)}, bf16[192,768]{1,0:T(8,128)(2,1)}) custom-call(s32[5]{0:T(128)} %stack.23.refs_0_, bf16[256,768]{1,0:T(8,128)(2,1)} %bitcast.18, bf16[256,768]{1,0:T(8,128)(2,1)} %bitcast.20, f32[768]{0:T(1024)} %refs_7_.3, f32[768]{0:T(1024)} %refs_6_.3, bf16[768,384]{1,0:T(8,128)(2,1)} %refs_4_.5, ...), custom_call_target="tpu_custom_call" | custom-call | tf_op jit(solution)/shard_map/pallas_call | solution.py:58
  5.2 4.1 %collective-permute-start.2 = (bf16[192,768]{1,0:T(8,128)(2,1)}, bf16[192,768]{1,0:T(8,128)(2,1)}, u32[]{:S(2)}, u32[]{:S(2)}) collective-permute-start(bf16[192,768]{1,0:T(8,128)(2,1)} %get-tuple-element.81), channel_id=1, source_target_pairs={{0,16},{4,20},{8,24},{12,28},{16,0},{20,4},{24,8},{28,12},{1,17},{... | collective-permute-start | bytes 884744 | tf_op jit(solution)/shard_map/ppermute | solution.py:86
  9.3 1.5 %collective-permute-start = (bf16[256,768]{1,0:T(8,128)(2,1)}, bf16[256,768]{1,0:T(8,128)(2,1)}, u32[]{:S(2)}, u32[]{:S(2)}) collective-permute-start(bf16[256,768]{1,0:T(8,128)(2,1)} %get-tuple-element.80.refs_3_), channel_id=1, source_target_pairs={{0,4},{4,0},{8,12},{12,8},{16,20},{20,16},{24,28},{28,24},{1,5},{5... | collective-permute-start | bytes 1179656 | tf_op jit(solution)/shard_map/ppermute | solution.py:86
  10.8 1.6 %collective-permute-start.1 = (bf16[256,768]{1,0:T(8,128)(2,1)}, bf16[256,768]{1,0:T(8,128)(2,1)S(1)}, u32[]{:S(2)}, u32[]{:S(2)}) collective-permute-start(bf16[256,768]{1,0:T(8,128)(2,1)} %get-tuple-element.80.refs_3_), channel_id=1, source_target_pairs={{0,8},{4,12},{8,0},{12,4},{16,24},{20,28},{24,16},{28,20},{1,9},{5... | collective-permute-start | bytes 1179656 | tf_op jit(solution)/shard_map/ppermute | solution.py:86
  12.4 1.5 %collective-permute-start.4 = (bf16[256,768]{1,0:T(8,128)(2,1)}, bf16[256,768]{1,0:T(8,128)(2,1)S(1)}, u32[]{:S(2)}, u32[]{:S(2)}) collective-permute-start(bf16[256,768]{1,0:T(8,128)(2,1)} %get-tuple-element.92.refs_4_), channel_id=1, source_target_pairs={{0,2},{1,3},{2,0},{3,1},{4,6},{5,7},{6,4},{7,5},{8,10},{9,11},{10,... | collective-permute-start | bytes 1179656 | tf_op jit(solution)/shard_map/ppermute | solution.py:86
  13.9 0.6 convert_reduce_fusion.refs_1_
  14.5 8.5 %collective-permute-done.2.refs_9_ = bf16[192,768]{1,0:T(8,128)(2,1)} collective-permute-done((bf16[192,768]{1,0:T(8,128)(2,1)}, bf16[192,768]{1,0:T(8,128)(2,1)}, u32[]{:S(2)}, u32[]{:S(2)}) %collective-permute-start.2) | collective-permute-done | bytes 294944 | tf_op jit(solution)/shard_map/ppermute | solution.py:86
  23.3 1.2 constant_dynamic-slice_fusion.refs_3_
  24.6 1.9 %collective-permute-done.1.refs_5_ = bf16[256,768]{1,0:T(8,128)(2,1)S(1)} collective-permute-done((bf16[256,768]{1,0:T(8,128)(2,1)}, bf16[256,768]{1,0:T(8,128)(2,1)S(1)}, u32[]{:S(2)}, u32[]{:S(2)}) %collective-permute-start.1) | collective-permute-done | bytes 393248 | tf_op jit(solution)/shard_map/ppermute | solution.py:86
  27.2 1.6 %collective-permute-start.6 = (bf16[192,768]{1,0:T(8,128)(2,1)}, bf16[192,768]{1,0:T(8,128)(2,1)S(1)}, u32[]{:S(2)}, u32[]{:S(2)}) collective-permute-start(bf16[192,768]{1,0:T(8,128)(2,1)} %collective-permute-done.2.refs_9_), channel_id=1, source_target_pairs={{0,2},{1,3},{2,0},{3,1},{4,6},{5,7},{6,4},{7,5},{8,10},{9,11},{10,... | collective-permute-start | bytes 884744 | tf_op jit(solution)/shard_map/ppermute | solution.py:86
  28.8 1.2 collective-permute-start.10
  30.0 4.6 %shard_map.163 = (f32[4,1664]{1,0:T(4,128)S(1)}, bf16[1024,768]{1,0:T(8,128)(2,1)S(1)}) custom-call(s32[5]{0:T(128)S(1)} %copy-done.10, s32[4]{0:T(128)S(1)} %convert_reduce_fusion.1.refs_1_, s32[4]{0:T(128)S(1)} %copy-done.16, bf16[256,768]{1,0:T(8,128)(2,1)S(1)} %bitcast.19, bf16[256,768]{1,0:T(8,128)(2,1)S(1)} %copy-done.15, ...), custom_call_target="tpu_custom_call" | custom-call | flops 3000000000 | bytes 3000000 | tf_op jit(solution)/shard_map/pallas_call | solution.py:58
  35.2 1.8 %shard_map.164.refs_3_ = f32[1024,384]{1,0:T(8,128)S(1)} custom-call(s32[5]{0:T(128)S(1)} %copy-done.10, s32[4]{0:T(128)S(1)} %convert_reduce_fusion.1.refs_1_, bf16[1024,768]{1,0:T(8,128)(2,1)S(1)} %get-tuple-element.90.refs_2_.refs_1_, bf16[768,384]{1,0:T(8,128)(2,1)S(1)} %constant_dynamic-slice_fusion.1.refs_3_.refs_9_.refs_6_), custom_call_target="tpu_custom_call" | custom-call | flops 905969664 | bytes 3000000 | tf_op jit(solution)/shard_map/pallas_call | solution.py:58
  37.1 1.2 copy-done.3
  38.6 0.8 collective-permute-done.10.refs_2_
  40.0 0.7 collective-permute-done.12
  41.2 0.7 copy-done.25
  41.9 6.6 %shard_map.165 = (f32[4,768]{1,0:T(4,128)}, f32[4,384]{1,0:T(4,128)}, f32[4,384]{1,0:T(4,128)}, bf16[1024,768]{1,0:T(8,128)(2,1)}, bf16[768,384]{1,0:T(8,128)(2,1)}, /*index=5*/bf16[384,768]{1,0:T(8,128)(2,1)}) custom-call(s32[5]{0:T(128)} %stack.23.refs_0_, s32[8]{0:T(128)} %convert_reduce_fusion.refs_1_, bf16[256,768]{1,0:T(8,128)(2,1)} %bitcast.21, ...), custom_call_target="tpu_custom_call" | custom-call | flops 3000000000 | bytes 3000000 | tf_op jit(solution)/shard_map/pallas_call | solution.py:58
  48.6 1.8 %collective-permute-start.14 = (f32[4,768]{1,0:T(4,128)}, f32[4,768]{1,0:T(4,128)S(1)}, u32[]{:S(2)}, u32[]{:S(2)}) collective-permute-start(f32[4,768]{1,0:T(4,128)} %get-tuple-element.98), channel_id=1, source_target_pairs={{0,8},{4,12},{8,0},{12,4},{16,24},{20,28},{24,16},{28,20},{1,9},{5... | collective-permute-start | bytes 36872 | tf_op jit(solution)/shard_map/ppermute | solution.py:86
  50.3 1.2 collective-permute-start.15
  51.5 0.6 collective-permute-start.13
  52.6 1.4 %collective-permute-start.16 = (f32[4,1664]{1,0:T(4,128)S(1)}, f32[4,1664]{1,0:T(4,128)S(1)}, u32[]{:S(2)}, u32[]{:S(2)}) collective-permute-start(f32[4,1664]{1,0:T(4,128)S(1)} %add_select_fusion), channel_id=1, source_target_pairs={{0,4},{4,0},{8,12},{12,8},{16,20},{20,16},{24,28},{28,24},{1,5},{5... | collective-permute-start | bytes 79880 | tf_op jit(solution)/shard_map/ppermute | solution.py:86
  54.0 1.1 collective-permute-done.15
  55.4 0.7 add_add_fusion
  56.7 0.7 pad_maximum_fusion.5
  57.4 2.7 %collective-permute-start.17 = (f32[4,1152]{1,0:T(4,128)S(1)}, f32[4,1152]{1,0:T(4,128)S(1)}, u32[]{:S(2)}, u32[]{:S(2)}) collective-permute-start(f32[4,1152]{1,0:T(4,128)S(1)} %pad_maximum_fusion.5), channel_id=1, source_target_pairs={{0,16},{4,20},{8,24},{12,28},{16,0},{20,4},{24,8},{28,12},{1,17},{... | collective-permute-start | bytes 55304 | tf_op jit(solution)/shard_map/ppermute | solution.py:86
  60.4 0.7 constant_dynamic-update-slice_fusion
  61.1 0.9 collective-permute-done.17
  62.1 2.2 %collective-permute-done.18 = f32[8,1664]{1,0:T(8,128)S(1)} collective-permute-done((f32[8,1664]{1,0:T(8,128)S(1)}, f32[8,1664]{1,0:T(8,128)S(1)}, u32[]{:S(2)}, u32[]{:S(2)}) %collective-permute-start.18) | collective-permute-done | bytes 53280 | tf_op jit(solution)/shard_map/ppermute | solution.py:86
  64.3 1.1 collective-permute-start.21
  65.4 1.1 collective-permute-start.22
  67.1 2.2 %collective-permute-done.22 = f32[1,8,1152]{2,1,0:T(8,128)S(1)} collective-permute-done((f32[1,8,1152]{2,1,0:T(8,128)S(1)}, f32[1,8,1152]{2,1,0:T(8,128)S(1)}, u32[]{:S(2)}, u32[]{:S(2)}) %collective-permute-start.22) | collective-permute-done | bytes 36896 | tf_op jit(solution)/shard_map/ppermute | solution.py:86
  69.4 1.3 collective-permute-done.26.refs_8_
  70.6 3.0 %shard_map.166 = (f32[1024,384]{1,0:T(8,128)S(1)}, bf16[1024,768]{1,0:T(8,128)(2,1)S(1)}) custom-call(s32[5]{0:T(128)S(1)} %copy-done.11, s32[4]{0:T(128)S(1)} %fusion.34.refs_1_, bf16[256,768]{1,0:T(8,128)(2,1)S(1)} %collective-permute-done.10.refs_2_, bf16[256,768]{1,0:T(8,128)(2,1)S(1)} %collective-permute-done.20.refs_3_, ...), custom_call_target="tpu_custom_call" | custom-call | flops 905969664 | bytes 3000000 | tf_op jit(solution)/shard_map/pallas_call | solution.py:58
  73.9 1.1 collective-permute-done.27
  75.1 2.6 %shard_map.167 = (f32[1,1]{1,0:T(1,128)}, f32[32,768]{1,0:T(8,128)S(1)}, f32[32,768]{1,0:T(8,128)S(1)}, f32[8,384]{1,0:T(8,128)S(1)}, f32[8,768]{1,0:T(8,128)S(1)}) custom-call(s32[5]{0:T(128)S(1)} %copy-done.11, f32[32,1664]{1,0:T(8,128)S(1)} %maximum_select_fusion.2.refs_1_, f32[32,1152]{1,0:T(8,128)S(1)} %pad_maximum_fusion.4.refs_2_, ...), custom_call_target="tpu_custom_call" | custom-call | tf_op jit(solution)/shard_map/pallas_call | solution.py:58
  77.8 2.5 %shard_map.168 = (bf16[192,384]{1,0:T(8,128)(2,1)S(1)}, bf16[192,384]{1,0:T(8,128)(2,1)S(1)}, bf16[192,384]{1,0:T(8,128)(2,1)S(1)}, f32[192,384]{1,0:T(8,128)S(1)}, f32[1,768]{1,0:T(1,128)S(1)}) custom-call(s32[5]{0:T(128)S(1)} %copy-done.11, bf16[1024,768]{1,0:T(8,128)(2,1)S(1)} %copy-done.2, bf16[1024,768]{1,0:T(8,128)(2,1)S(1)} %get-tuple-element.115.refs_2_, ...), custom_call_target="tpu_custom_call" | custom-call | flops 4000000000 | bytes 3000000 | tf_op jit(solution)/shard_map/pallas_call | solution.py:58
  80.3 0.9 collective-permute-start.28
  81.2 1.4 %collective-permute-start.29 = (bf16[192,384]{1,0:T(8,128)(2,1)S(1)}, bf16[192,384]{1,0:T(8,128)(2,1)S(1)}, u32[]{:S(2)}, u32[]{:S(2)}) collective-permute-start(bf16[192,384]{1,0:T(8,128)(2,1)S(1)} %get-tuple-element.121), channel_id=1, source_target_pairs={{0,16},{4,20},{8,24},{12,28},{16,0},{20,4},{24,8},{28,12},{1,17},{... | collective-permute-start | bytes 442376 | tf_op jit(solution)/shard_map/ppermute | solution.py:86
  82.6 2.1 %collective-permute-start.30 = (bf16[192,384]{1,0:T(8,128)(2,1)S(1)}, bf16[192,384]{1,0:T(8,128)(2,1)S(1)}, u32[]{:S(2)}, u32[]{:S(2)}) collective-permute-start(bf16[192,384]{1,0:T(8,128)(2,1)S(1)} %get-tuple-element.122), channel_id=1, source_target_pairs={{0,24},{4,28},{8,16},{12,20},{16,8},{20,12},{24,0},{28,4},{1,25},{... | collective-permute-start | bytes 442376 | tf_op jit(solution)/shard_map/ppermute | solution.py:86
  84.7 4.8 %shard_map.169 = (bf16[384,768]{1,0:T(8,128)(2,1)S(1)}, f32[384,768]{1,0:T(8,128)S(1)}, bf16[16,768]{1,0:T(8,128)(2,1)S(1)}) custom-call(s32[5]{0:T(128)S(1)} %copy-done.11, s32[8]{0:T(128)S(1)} %copy-done.14, bf16[1024,768]{1,0:T(8,128)(2,1)S(1)} %copy-done.17, f32[8,768]{1,0:T(8,128)S(1)} %get-tuple-element.126.refs_3_, bf16[768,384]{1,0:T(8,128)(2,1)S(1)} %copy-done.6, ...), custom_call_target="tpu_custom_call" | custom-call | flops 6000000000 | bytes 3000000 | tf_op jit(solution)/shard_map/pallas_call | solution.py:58
  90.2 1.9 %fusion.1 = f32[768,768]{1,0:T(8,128)} fusion(bf16[32,768]{1,0:T(8,128)(2,1)S(1)} %get-tuple-element.172, bf16[32,768]{1,0:T(8,128)(2,1)S(1)} %get-tuple-element.171, bf16[32,768]{1,0:T(8,128)(2,1)S(1)} %get-tuple-element.191, bf16[32,768]{1,0:T(8,128)(2,1)S(1)} %get-tuple-element.192), kind=kOutput, calls=%fused_computation.16 | convolution fusion | flops 114130944 | bytes 2555904 | tf_op jit(solution)/shard_map/dot_general | solution.py:789
  92.1 1.4 %fusion.12 = f32[384,768]{1,0:T(8,128)} fusion(bf16[32,768]{1,0:T(8,128)(2,1)S(1)} %get-tuple-element.180, bf16[32,768]{1,0:T(8,128)(2,1)S(1)} %get-tuple-element.179, bf16[32,384]{1,0:T(8,128)(2,1)S(1)} %get-tuple-element.174, bf16[32,384]{1,0:T(8,128)(2,1)S(1)} %get-tuple-element.173), kind=kOutput, calls=%fused_computation.27 | convolution fusion | flops 57286656 | bytes 1327104 | tf_op jit(solution)/shard_map/dot_general | solution.py:789
  94.1 0.7 collective-permute-done.33
  95.4 0.7 collective-permute-done.35
  96.6 1.2 collective-permute-start.42
  97.9 1.9 %collective-permute-start.37 = (bf16[208,384]{1,0:T(8,128)(2,1)S(1)}, bf16[208,384]{1,0:T(8,128)(2,1)S(1)}, u32[]{:S(2)}, u32[]{:S(2)}) collective-permute-start(bf16[208,384]{1,0:T(8,128)(2,1)S(1)} %pad_maximum_fusion.3), channel_id=1, source_target_pairs={{0,8},{4,12},{8,0},{12,4},{16,24},{20,28},{24,16},{28,20},{1,9},{5... | collective-permute-start | bytes 479240 | tf_op jit(solution)/shard_map/ppermute | solution.py:86
  99.7 1.1 collective-permute-start.38
  100.8 1.5 %collective-permute-start.39 = (bf16[208,384]{1,0:T(8,128)(2,1)S(1)}, bf16[208,384]{1,0:T(8,128)(2,1)S(1)}, u32[]{:S(2)}, u32[]{:S(2)}) collective-permute-start(bf16[208,384]{1,0:T(8,128)(2,1)S(1)} %pad_maximum_fusion.3), channel_id=1, source_target_pairs={{0,24},{4,28},{8,16},{12,20},{16,8},{20,12},{24,0},{28,4},{1,25},{... | collective-permute-start | bytes 479240 | tf_op jit(solution)/shard_map/ppermute | solution.py:86
  102.3 1.1 collective-permute-start.40
  103.4 2.8 %collective-permute-done.37.refs_2_ = bf16[208,384]{1,0:T(8,128)(2,1)S(1)} collective-permute-done((bf16[208,384]{1,0:T(8,128)(2,1)S(1)}, bf16[208,384]{1,0:T(8,128)(2,1)S(1)}, u32[]{:S(2)}, u32[]{:S(2)}) %collective-permute-start.37) | collective-permute-done | bytes 159776 | tf_op jit(solution)/shard_map/ppermute | solution.py:86
  106.2 2.0 %collective-permute-start.41 = (bf16[192,384]{1,0:T(8,128)(2,1)S(1)}, bf16[192,384]{1,0:T(8,128)(2,1)S(1)}, u32[]{:S(2)}, u32[]{:S(2)}) collective-permute-start(bf16[192,384]{1,0:T(8,128)(2,1)S(1)} %slice.208), channel_id=1, source_target_pairs={{0,4},{4,0},{8,12},{12,8},{16,20},{20,16},{24,28},{28,24},{1,5},{5... | collective-permute-start | bytes 442376 | tf_op jit(solution)/shard_map/ppermute | solution.py:86
  108.3 5.4 %collective-permute-done.38.refs_2_ = bf16[208,384]{1,0:T(8,128)(2,1)S(1)} collective-permute-done((bf16[208,384]{1,0:T(8,128)(2,1)S(1)}, bf16[208,384]{1,0:T(8,128)(2,1)S(1)}, u32[]{:S(2)}, u32[]{:S(2)}) %collective-permute-start.38) | collective-permute-done | bytes 159776 | tf_op jit(solution)/shard_map/ppermute | solution.py:86
  113.8 3.6 %collective-permute-start.43 = (bf16[192,384]{1,0:T(8,128)(2,1)S(1)}, bf16[192,384]{1,0:T(8,128)(2,1)S(1)}, u32[]{:S(2)}, u32[]{:S(2)}) collective-permute-start(bf16[192,384]{1,0:T(8,128)(2,1)S(1)} %slice.296), channel_id=1, source_target_pairs={{0,16},{4,20},{8,24},{12,28},{16,0},{20,4},{24,8},{28,12},{1,17},{... | collective-permute-start | bytes 442376 | tf_op jit(solution)/shard_map/ppermute | solution.py:86
  118.1 1.6 %collective-permute-start.45 = (bf16[384,384]{1,0:T(8,128)(2,1)S(1)}, bf16[384,384]{1,0:T(8,128)(2,1)S(1)}, u32[]{:S(2)}, u32[]{:S(2)}) collective-permute-start(bf16[384,384]{1,0:T(8,128)(2,1)S(1)} %pad_maximum_fusion.1), channel_id=1, source_target_pairs={{0,4},{4,0},{8,12},{12,8},{16,20},{20,16},{24,28},{28,24},{1,5},{5... | collective-permute-start | bytes 884744 | tf_op jit(solution)/shard_map/ppermute | solution.py:86
  119.7 2.4 %shard_map.170.refs_1_ = f32[768,768]{1,0:T(8,128)} custom-call(s32[5]{0:T(128)S(1)} %copy-done.11, bf16[192,384]{1,0:T(8,128)(2,1)S(1)} %add_convert_fusion.1.refs_1_, bf16[208,384]{1,0:T(8,128)(2,1)S(1)} %collective-permute-done.37.refs_2_, bf16[192,384]{1,0:T(8,128)(2,1)S(1)} %collective-permute-done.40.refs_3_, ...), custom_call_target="tpu_custom_call" | custom-call | flops 2000000000 | bytes 3000000 | tf_op jit(solution)/shard_map/pallas_call | solution.py:58
  122.2 0.7 collective-permute-done.43
  123.0 2.0 %collective-permute-done.45.refs_4_ = bf16[384,384]{1,0:T(8,128)(2,1)S(1)} collective-permute-done((bf16[384,384]{1,0:T(8,128)(2,1)S(1)}, bf16[384,384]{1,0:T(8,128)(2,1)S(1)}, u32[]{:S(2)}, u32[]{:S(2)}) %collective-permute-start.45) | collective-permute-done | bytes 294944 | tf_op jit(solution)/shard_map/ppermute | solution.py:86
  125.6 2.1 %shard_map.171 = f32[768,768]{1,0:T(8,128)} custom-call(s32[5]{0:T(128)S(1)} %copy-done.11, f32[768,768]{1,0:T(8,128)} %shard_map.170.refs_1_, bf16[208,384]{1,0:T(8,128)(2,1)S(1)} %collective-permute-done.38.refs_2_, bf16[208,384]{1,0:T(8,128)(2,1)S(1)} %collective-permute-done.39.refs_3_, ...), custom_call_target="tpu_custom_call", output_to_operand_aliasing={{}: (1, {})} | custom-call | flops 2000000000 | bytes 3000000 | tf_op jit(solution)/shard_map/pallas_call | solution.py:58
  127.7 2.6 %collective-permute-done.46 = bf16[208,384]{1,0:T(8,128)(2,1)S(1)} collective-permute-done((bf16[208,384]{1,0:T(8,128)(2,1)S(1)}, bf16[208,384]{1,0:T(8,128)(2,1)S(1)}, u32[]{:S(2)}, u32[]{:S(2)}) %collective-permute-start.46) | collective-permute-done | bytes 159776 | tf_op jit(solution)/shard_map/ppermute | solution.py:86
  130.7 1.6 %collective-permute-done.47 = bf16[400,384]{1,0:T(8,128)(2,1)S(1)} collective-permute-done((bf16[400,384]{1,0:T(8,128)(2,1)S(1)}, bf16[400,384]{1,0:T(8,128)(2,1)S(1)}, u32[]{:S(2)}, u32[]{:S(2)}) %collective-permute-start.47) | collective-permute-done | bytes 307232 | tf_op jit(solution)/shard_map/ppermute | solution.py:86
  132.3 0.6 slice_reduce_fusion
  132.9 1.1 fusion
  (173 shorter events, 9.8 us)
Async XLA Ops:
  0.6 13.3 %copy-start.19 = (s32[1,8,256]{2,1,0:T(8,128)S(1)}, s32[1,8,256]{2,1,0:T(8,128)}, u32[]{:S(2)}) copy-start(s32[1,8,256]{2,1,0:T(8,128)} %param.17) | copy-start | bytes 24580
  0.6 22.4 %copy-start.20 = (s32[1,4,256]{2,1,0:T(4,128)S(1)}, s32[1,4,256]{2,1,0:T(4,128)}, u32[]{:S(2)}) copy-start(s32[1,4,256]{2,1,0:T(4,128)} %param.12) | copy-start | bytes 12292
  0.7 22.5 %copy-start.8 = (bf16[768,768]{1,0:T(8,128)(2,1)S(1)}, bf16[768,768]{1,0:T(8,128)(2,1)}, u32[]{:S(2)}) copy-start(bf16[768,768]{1,0:T(8,128)(2,1)} %refs_8_.2) | copy-start | bytes 3538948
  5.2 17.9 %collective-permute-start.2 = (bf16[192,768]{1,0:T(8,128)(2,1)}, bf16[192,768]{1,0:T(8,128)(2,1)}, u32[]{:S(2)}, u32[]{:S(2)}) collective-permute-start(bf16[192,768]{1,0:T(8,128)(2,1)} %get-tuple-element.81), channel_id=1, source_target_pairs={{0,16},{4,20},{8,24},{12,28},{16,0},{20,4},{24,8},{28,12},{1,17},{... | collective-permute-start | bytes 884744 | tf_op jit(solution)/shard_map/ppermute | solution.py:86
  9.3 15.3 %collective-permute-start = (bf16[256,768]{1,0:T(8,128)(2,1)}, bf16[256,768]{1,0:T(8,128)(2,1)}, u32[]{:S(2)}, u32[]{:S(2)}) collective-permute-start(bf16[256,768]{1,0:T(8,128)(2,1)} %get-tuple-element.80.refs_3_), channel_id=1, source_target_pairs={{0,4},{4,0},{8,12},{12,8},{16,20},{20,16},{24,28},{28,24},{1,5},{5... | collective-permute-start | bytes 1179656 | tf_op jit(solution)/shard_map/ppermute | solution.py:86
  10.8 15.7 %collective-permute-start.1 = (bf16[256,768]{1,0:T(8,128)(2,1)}, bf16[256,768]{1,0:T(8,128)(2,1)S(1)}, u32[]{:S(2)}, u32[]{:S(2)}) collective-permute-start(bf16[256,768]{1,0:T(8,128)(2,1)} %get-tuple-element.80.refs_3_), channel_id=1, source_target_pairs={{0,8},{4,12},{8,0},{12,4},{16,24},{20,28},{24,16},{28,20},{1,9},{5... | collective-permute-start | bytes 1179656 | tf_op jit(solution)/shard_map/ppermute | solution.py:86
  12.4 14.1 %collective-permute-start.4 = (bf16[256,768]{1,0:T(8,128)(2,1)}, bf16[256,768]{1,0:T(8,128)(2,1)S(1)}, u32[]{:S(2)}, u32[]{:S(2)}) collective-permute-start(bf16[256,768]{1,0:T(8,128)(2,1)} %get-tuple-element.92.refs_4_), channel_id=1, source_target_pairs={{0,2},{1,3},{2,0},{3,1},{4,6},{5,7},{6,4},{7,5},{8,10},{9,11},{10,... | collective-permute-start | bytes 1179656 | tf_op jit(solution)/shard_map/ppermute | solution.py:86
  13.9 16.0 %collective-permute-start.7 = (bf16[256,768]{1,0:T(8,128)(2,1)}, bf16[256,768]{1,0:T(8,128)(2,1)}, u32[]{:S(2)}, u32[]{:S(2)}) collective-permute-start(bf16[256,768]{1,0:T(8,128)(2,1)} %get-tuple-element.92.refs_4_), channel_id=1, source_target_pairs={{0,1},{1,0},{2,3},{3,2},{4,5},{5,4},{6,7},{7,6},{8,9},{9,8},{10,11... | collective-permute-start | bytes 1179656 | tf_op jit(solution)/shard_map/ppermute | solution.py:86
  23.1 3.4 %collective-permute-start.3 = (bf16[192,768]{1,0:T(8,128)(2,1)}, bf16[192,768]{1,0:T(8,128)(2,1)S(1)}, u32[]{:S(2)}, u32[]{:S(2)}) collective-permute-start(bf16[192,768]{1,0:T(8,128)(2,1)} %collective-permute-done.2.refs_9_), channel_id=1, source_target_pairs={{0,1},{1,0},{2,3},{3,2},{4,5},{5,4},{6,7},{7,6},{8,9},{9,8},{10,11... | collective-permute-start | bytes 884744 | tf_op jit(solution)/shard_map/ppermute | solution.py:86
  23.2 5.6 %copy-start.15 = (bf16[256,768]{1,0:T(8,128)(2,1)S(1)}, bf16[256,768]{1,0:T(8,128)(2,1)}, u32[]{:S(2)}) copy-start(bf16[256,768]{1,0:T(8,128)(2,1)} %get-tuple-element.92.refs_4_) | copy-start | bytes 1179652
  23.2 6.7 %copy-start.7 = (bf16[1,1,256,768]{3,2,1,0:T(8,128)(2,1)S(1)}, bf16[1,1,256,768]{3,2,1,0:T(8,128)(2,1)}, u32[]{:S(2)}) copy-start(bf16[1,1,256,768]{3,2,1,0:T(8,128)(2,1)} %param.11) | copy-start | bytes 1179652
  23.2 6.7 %copy-start.9 = (bf16[768,768]{1,0:T(8,128)(2,1)S(1)}, bf16[768,768]{1,0:T(8,128)(2,1)}, u32[]{:S(2)}) copy-start(bf16[768,768]{1,0:T(8,128)(2,1)} %refs_9_.1) | copy-start | bytes 3538948
  23.2 6.7 %copy-start.10 = (s32[5]{0:T(128)S(1)}, s32[5]{0:T(128)}, u32[]{:S(2)}) copy-start(s32[5]{0:T(128)} %stack.23.refs_0_) | copy-start | bytes 64
  23.2 6.7 %copy-start.16 = (s32[4]{0:T(128)S(1)}, s32[4]{0:T(128)}, u32[]{:S(2)}) copy-start(s32[4]{0:T(128)} %refs_2_.1) | copy-start | bytes 52
  26.5 3.5 %collective-permute-start.8 = (bf16[256,768]{1,0:T(8,128)(2,1)S(1)}, bf16[256,768]{1,0:T(8,128)(2,1)S(1)}, u32[]{:S(2)}, u32[]{:S(2)}) collective-permute-start(bf16[256,768]{1,0:T(8,128)(2,1)S(1)} %collective-permute-done.4.refs_6_), channel_id=1, source_target_pairs={{0,1},{1,0},{2,3},{3,2},{4,5},{5,4},{6,7},{7,6},{8,9},{9,8},{10,11... | collective-permute-start | bytes 1179656 | tf_op jit(solution)/shard_map/ppermute | solution.py:86
  26.6 12.0 %collective-permute-start.5 = (bf16[256,768]{1,0:T(8,128)(2,1)}, bf16[256,768]{1,0:T(8,128)(2,1)S(1)}, u32[]{:S(2)}, u32[]{:S(2)}) collective-permute-start(bf16[256,768]{1,0:T(8,128)(2,1)} %collective-permute-done.refs_4_), channel_id=1, source_target_pairs={{0,8},{4,12},{8,0},{12,4},{16,24},{20,28},{24,16},{28,20},{1,9},{5... | collective-permute-start | bytes 1179656 | tf_op jit(solution)/shard_map/ppermute | solution.py:86
  27.2 11.4 %collective-permute-start.6 = (bf16[192,768]{1,0:T(8,128)(2,1)}, bf16[192,768]{1,0:T(8,128)(2,1)S(1)}, u32[]{:S(2)}, u32[]{:S(2)}) collective-permute-start(bf16[192,768]{1,0:T(8,128)(2,1)} %collective-permute-done.2.refs_9_), channel_id=1, source_target_pairs={{0,2},{1,3},{2,0},{3,1},{4,6},{5,7},{6,4},{7,5},{8,10},{9,11},{10,... | collective-permute-start | bytes 884744 | tf_op jit(solution)/shard_map/ppermute | solution.py:86
  28.8 10.7 %collective-permute-start.10 = (bf16[256,768]{1,0:T(8,128)(2,1)S(1)}, bf16[256,768]{1,0:T(8,128)(2,1)S(1)}, u32[]{:S(2)}, u32[]{:S(2)}) collective-permute-start(bf16[256,768]{1,0:T(8,128)(2,1)S(1)} %copy-done.15), channel_id=1, source_target_pairs={{0,4},{4,0},{8,12},{12,8},{16,20},{20,16},{24,28},{28,24},{1,5},{5... | collective-permute-start | bytes 1179656 | tf_op jit(solution)/shard_map/ppermute | solution.py:86
  34.6 3.9 %collective-permute-start.9 = (f32[4,1664]{1,0:T(4,128)S(1)}, f32[4,1664]{1,0:T(4,128)S(1)}, u32[]{:S(2)}, u32[]{:S(2)}) collective-permute-start(f32[4,1664]{1,0:T(4,128)S(1)} %get-tuple-element.89), channel_id=1, source_target_pairs={{0,2},{1,3},{2,0},{3,1},{4,6},{5,7},{6,4},{7,5},{8,10},{9,11},{10,... | collective-permute-start | bytes 79880 | tf_op jit(solution)/shard_map/ppermute | solution.py:86
  39.5 1.2 collective-permute-start.12
  39.5 1.7 %collective-permute-start.11 = (bf16[192,768]{1,0:T(8,128)(2,1)S(1)}, bf16[192,768]{1,0:T(8,128)(2,1)S(1)}, u32[]{:S(2)}, u32[]{:S(2)}) collective-permute-start(bf16[192,768]{1,0:T(8,128)(2,1)S(1)} %collective-permute-done.6.refs_10_), channel_id=1, source_target_pairs={{0,1},{1,0},{2,3},{3,2},{4,5},{5,4},{6,7},{7,6},{8,9},{9,8},{10,11... | collective-permute-start | bytes 884744 | tf_op jit(solution)/shard_map/ppermute | solution.py:86
  48.6 22.1 %copy-start.11 = (s32[5]{0:T(128)S(1)}, s32[5]{0:T(128)}, u32[]{:S(2)}) copy-start(s32[5]{0:T(128)} %stack.23.refs_0_) | copy-start | bytes 64
  48.6 4.0 %collective-permute-start.14 = (f32[4,768]{1,0:T(4,128)}, f32[4,768]{1,0:T(4,128)S(1)}, u32[]{:S(2)}, u32[]{:S(2)}) collective-permute-start(f32[4,768]{1,0:T(4,128)} %get-tuple-element.98), channel_id=1, source_target_pairs={{0,8},{4,12},{8,0},{12,4},{16,24},{20,28},{24,16},{28,20},{1,9},{5... | collective-permute-start | bytes 36872 | tf_op jit(solution)/shard_map/ppermute | solution.py:86
  50.3 4.8 %collective-permute-start.15 = (f32[4,768]{1,0:T(4,128)}, f32[4,768]{1,0:T(4,128)S(1)}, u32[]{:S(2)}, u32[]{:S(2)}) collective-permute-start(f32[4,768]{1,0:T(4,128)} %get-tuple-element.98), channel_id=1, source_target_pairs={{0,12},{4,8},{8,4},{12,0},{16,28},{20,24},{24,20},{28,16},{1,13},{... | collective-permute-start | bytes 36872 | tf_op jit(solution)/shard_map/ppermute | solution.py:86
  51.5 3.9 %collective-permute-start.13 = (f32[4,768]{1,0:T(4,128)}, f32[4,768]{1,0:T(4,128)S(1)}, u32[]{:S(2)}, u32[]{:S(2)}) collective-permute-start(f32[4,768]{1,0:T(4,128)} %get-tuple-element.98), channel_id=1, source_target_pairs={{0,4},{4,0},{8,12},{12,8},{16,20},{20,16},{24,28},{28,24},{1,5},{5... | collective-permute-start | bytes 36872 | tf_op jit(solution)/shard_map/ppermute | solution.py:86
  52.1 12.1 %collective-permute-start.19 = (bf16[256,768]{1,0:T(8,128)(2,1)S(1)}, bf16[256,768]{1,0:T(8,128)(2,1)S(1)}, u32[]{:S(2)}, u32[]{:S(2)}) collective-permute-start(bf16[256,768]{1,0:T(8,128)(2,1)S(1)} %collective-permute-done.10.refs_2_), channel_id=1, source_target_pairs={{0,2},{1,3},{2,0},{3,1},{4,6},{5,7},{6,4},{7,5},{8,10},{9,11},{10,... | collective-permute-start | bytes 1179656 | tf_op jit(solution)/shard_map/ppermute | solution.py:86
  52.6 11.7 %collective-permute-start.20 = (bf16[256,768]{1,0:T(8,128)(2,1)S(1)}, bf16[256,768]{1,0:T(8,128)(2,1)S(1)}, u32[]{:S(2)}, u32[]{:S(2)}) collective-permute-start(bf16[256,768]{1,0:T(8,128)(2,1)S(1)} %collective-permute-done.10.refs_2_), channel_id=1, source_target_pairs={{0,1},{1,0},{2,3},{3,2},{4,5},{5,4},{6,7},{7,6},{8,9},{9,8},{10,11... | collective-permute-start | bytes 1179656 | tf_op jit(solution)/shard_map/ppermute | solution.py:86
  52.6 3.9 %collective-permute-start.16 = (f32[4,1664]{1,0:T(4,128)S(1)}, f32[4,1664]{1,0:T(4,128)S(1)}, u32[]{:S(2)}, u32[]{:S(2)}) collective-permute-start(f32[4,1664]{1,0:T(4,128)S(1)} %add_select_fusion), channel_id=1, source_target_pairs={{0,4},{4,0},{8,12},{12,8},{16,20},{20,16},{24,28},{28,24},{1,5},{5... | collective-permute-start | bytes 79880 | tf_op jit(solution)/shard_map/ppermute | solution.py:86
  57.4 4.7 %collective-permute-start.17 = (f32[4,1152]{1,0:T(4,128)S(1)}, f32[4,1152]{1,0:T(4,128)S(1)}, u32[]{:S(2)}, u32[]{:S(2)}) collective-permute-start(f32[4,1152]{1,0:T(4,128)S(1)} %pad_maximum_fusion.5), channel_id=1, source_target_pairs={{0,16},{4,20},{8,24},{12,28},{16,0},{20,4},{24,8},{28,12},{1,17},{... | collective-permute-start | bytes 55304 | tf_op jit(solution)/shard_map/ppermute | solution.py:86
  60.1 4.1 %collective-permute-start.18 = (f32[8,1664]{1,0:T(8,128)S(1)}, f32[8,1664]{1,0:T(8,128)S(1)}, u32[]{:S(2)}, u32[]{:S(2)}) collective-permute-start(f32[8,1664]{1,0:T(8,128)S(1)} %maximum_select_fusion.6), channel_id=1, source_target_pairs={{0,8},{4,12},{8,0},{12,4},{16,24},{20,28},{24,16},{28,20},{1,9},{5... | collective-permute-start | bytes 159752 | tf_op jit(solution)/shard_map/ppermute | solution.py:86
  64.3 9.6 %collective-permute-start.21 = (f32[16,1664]{1,0:T(8,128)S(1)}, f32[16,1664]{1,0:T(8,128)S(1)}, u32[]{:S(2)}, u32[]{:S(2)}) collective-permute-start(f32[16,1664]{1,0:T(8,128)S(1)} %maximum_select_fusion.4), channel_id=1, source_target_pairs={{0,16},{4,20},{8,24},{12,28},{16,0},{20,4},{24,8},{28,12},{1,17},{... | collective-permute-start | bytes 319496 | tf_op jit(solution)/shard_map/ppermute | solution.py:86
  65.4 4.0 %collective-permute-start.22 = (f32[1,8,1152]{2,1,0:T(8,128)S(1)}, f32[1,8,1152]{2,1,0:T(8,128)S(1)}, u32[]{:S(2)}, u32[]{:S(2)}) collective-permute-start(f32[1,8,1152]{2,1,0:T(8,128)S(1)} %maximum_bitcast_fusion), channel_id=1, source_target_pairs={{0,2},{1,3},{2,0},{3,1},{4,6},{5,7},{6,4},{7,5},{8,10},{9,11},{10,... | collective-permute-start | bytes 110600 | tf_op jit(solution)/shard_map/ppermute | solution.py:86
  66.5 2.9 %collective-permute-start.23 = (bf16[64,768]{1,0:T(8,128)(2,1)S(1)}, bf16[64,768]{1,0:T(8,128)(2,1)S(1)}, u32[]{:S(2)}, u32[]{:S(2)}) collective-permute-start(bf16[64,768]{1,0:T(8,128)(2,1)S(1)} %get-tuple-element.170), channel_id=1, source_target_pairs={{0,1},{1,0},{2,3},{3,2},{4,5},{5,4},{6,7},{7,6},{8,9},{9,8},{10,11... | collective-permute-start | bytes 294920 | tf_op jit(solution)/shard_map/ppermute | solution.py:86
  66.5 2.8 %collective-permute-start.24 = (bf16[64,768]{1,0:T(8,128)(2,1)S(1)}, bf16[64,768]{1,0:T(8,128)(2,1)S(1)}, u32[]{:S(2)}, u32[]{:S(2)}) collective-permute-start(bf16[64,768]{1,0:T(8,128)(2,1)S(1)} %get-tuple-element.169), channel_id=1, source_target_pairs={{0,1},{1,0},{2,3},{3,2},{4,5},{5,4},{6,7},{7,6},{8,9},{9,8},{10,11... | collective-permute-start | bytes 294920 | tf_op jit(solution)/shard_map/ppermute | solution.py:86
  67.0 2.3 %collective-permute-start.25 = (bf16[64,768]{1,0:T(8,128)(2,1)S(1)}, bf16[64,768]{1,0:T(8,128)(2,1)S(1)}, u32[]{:S(2)}, u32[]{:S(2)}) collective-permute-start(bf16[64,768]{1,0:T(8,128)(2,1)S(1)} %get-tuple-element.168), channel_id=1, source_target_pairs={{0,1},{1,0},{2,3},{3,2},{4,5},{5,4},{6,7},{7,6},{8,9},{9,8},{10,11... | collective-permute-start | bytes 294920 | tf_op jit(solution)/shard_map/ppermute | solution.py:86
  69.3 1.3 collective-permute-start.26
  70.6 4.5 %copy-start.5 = (bf16[384,768]{1,0:T(8,128)(2,1)S(1)}, bf16[384,768]{1,0:T(8,128)(2,1)}, u32[]{:S(2)}) copy-start(bf16[384,768]{1,0:T(8,128)(2,1)} %get-tuple-element.113.refs_5_) | copy-start | bytes 1769476
  73.6 1.3 collective-permute-start.27
  73.9 3.8 %copy-start.4 = (f32[1024,384]{1,0:T(8,128)S(1)}, f32[1024,384]{1,0:T(8,128)}, u32[]{:S(2)}) copy-start(f32[1024,384]{1,0:T(8,128)} %copy-done.3) | copy-start | bytes 4718596
  77.7 7.0 %copy-start.6 = (bf16[768,384]{1,0:T(8,128)(2,1)S(1)}, bf16[768,384]{1,0:T(8,128)(2,1)}, u32[]{:S(2)}) copy-start(bf16[768,384]{1,0:T(8,128)(2,1)} %refs_4_.5) | copy-start | bytes 1769476
  77.7 7.0 %copy-start.13 = (f32[768]{0:T(1024)S(1)}, f32[768]{0:T(1024)}, u32[]{:S(2)}) copy-start(f32[768]{0:T(1024)} %refs_6_.3) | copy-start | bytes 9220
  77.7 7.0 %copy-start.14 = (s32[8]{0:T(128)S(1)}, s32[8]{0:T(128)}, u32[]{:S(2)}) copy-start(s32[8]{0:T(128)} %convert_reduce_fusion.refs_1_) | copy-start | bytes 100
  77.8 7.0 %copy-start.17 = (bf16[1024,768]{1,0:T(8,128)(2,1)S(1)}, bf16[1024,768]{1,0:T(8,128)(2,1)}, u32[]{:S(2)}) copy-start(bf16[1024,768]{1,0:T(8,128)(2,1)} %get-tuple-element.123.refs_2_) | copy-start | bytes 4718596
  77.8 7.0 %copy-start.18 = (bf16[768,384]{1,0:T(8,128)(2,1)S(1)}, bf16[768,384]{1,0:T(8,128)(2,1)}, u32[]{:S(2)}) copy-start(bf16[768,384]{1,0:T(8,128)(2,1)} %get-tuple-element.127.refs_5_) | copy-start | bytes 1769476
  80.3 16.2 %collective-permute-start.28 = (bf16[192,384]{1,0:T(8,128)(2,1)S(1)}, bf16[192,384]{1,0:T(8,128)(2,1)S(1)}, u32[]{:S(2)}, u32[]{:S(2)}) collective-permute-start(bf16[192,384]{1,0:T(8,128)(2,1)S(1)} %get-tuple-element.120), channel_id=1, source_target_pairs={{0,8},{4,12},{8,0},{12,4},{16,24},{20,28},{24,16},{28,20},{1,9},{5... | collective-permute-start | bytes 442376 | tf_op jit(solution)/shard_map/ppermute | solution.py:86
  81.2 15.3 %collective-permute-start.29 = (bf16[192,384]{1,0:T(8,128)(2,1)S(1)}, bf16[192,384]{1,0:T(8,128)(2,1)S(1)}, u32[]{:S(2)}, u32[]{:S(2)}) collective-permute-start(bf16[192,384]{1,0:T(8,128)(2,1)S(1)} %get-tuple-element.121), channel_id=1, source_target_pairs={{0,16},{4,20},{8,24},{12,28},{16,0},{20,4},{24,8},{28,12},{1,17},{... | collective-permute-start | bytes 442376 | tf_op jit(solution)/shard_map/ppermute | solution.py:86
  82.6 13.9 %collective-permute-start.30 = (bf16[192,384]{1,0:T(8,128)(2,1)S(1)}, bf16[192,384]{1,0:T(8,128)(2,1)S(1)}, u32[]{:S(2)}, u32[]{:S(2)}) collective-permute-start(bf16[192,384]{1,0:T(8,128)(2,1)S(1)} %get-tuple-element.122), channel_id=1, source_target_pairs={{0,24},{4,28},{8,16},{12,20},{16,8},{20,12},{24,0},{28,4},{1,25},{... | collective-permute-start | bytes 442376 | tf_op jit(solution)/shard_map/ppermute | solution.py:86
  89.6 3.9 %collective-permute-start.31 = (bf16[64,768]{1,0:T(8,128)(2,1)S(1)}, bf16[64,768]{1,0:T(8,128)(2,1)S(1)}, u32[]{:S(2)}, u32[]{:S(2)}) collective-permute-start(bf16[64,768]{1,0:T(8,128)(2,1)S(1)} %get-tuple-element.166), channel_id=1, source_target_pairs={{0,1},{1,0},{2,3},{3,2},{4,5},{5,4},{6,7},{7,6},{8,9},{9,8},{10,11... | collective-permute-start | bytes 294920 | tf_op jit(solution)/shard_map/ppermute | solution.py:86
  89.7 3.9 %collective-permute-start.32 = (bf16[64,768]{1,0:T(8,128)(2,1)S(1)}, bf16[64,768]{1,0:T(8,128)(2,1)S(1)}, u32[]{:S(2)}, u32[]{:S(2)}) collective-permute-start(bf16[64,768]{1,0:T(8,128)(2,1)S(1)} %get-tuple-element.165), channel_id=1, source_target_pairs={{0,1},{1,0},{2,3},{3,2},{4,5},{5,4},{6,7},{7,6},{8,9},{9,8},{10,11... | collective-permute-start | bytes 294920 | tf_op jit(solution)/shard_map/ppermute | solution.py:86
  93.5 1.3 collective-permute-start.33
  93.6 1.4 %collective-permute-start.34 = (bf16[64,768]{1,0:T(8,128)(2,1)S(1)}, bf16[64,768]{1,0:T(8,128)(2,1)S(1)}, u32[]{:S(2)}, u32[]{:S(2)}) collective-permute-start(bf16[64,768]{1,0:T(8,128)(2,1)S(1)} %get-tuple-element.163), channel_id=1, source_target_pairs={{0,1},{1,0},{2,3},{3,2},{4,5},{5,4},{6,7},{7,6},{8,9},{9,8},{10,11... | collective-permute-start | bytes 294920 | tf_op jit(solution)/shard_map/ppermute | solution.py:86
  94.8 1.3 collective-permute-start.35
  95.0 1.3 collective-permute-start.36
  96.6 11.7 %collective-permute-start.42 = (bf16[192,768]{1,0:T(8,128)(2,1)S(1)}, bf16[192,768]{1,0:T(8,128)(2,1)S(1)}, u32[]{:S(2)}, u32[]{:S(2)}) collective-permute-start(bf16[192,768]{1,0:T(8,128)(2,1)S(1)} %dynamic-slice_convert_fusion), channel_id=1, source_target_pairs={{0,2},{1,3},{2,0},{3,1},{4,6},{5,7},{6,4},{7,5},{8,10},{9,11},{10,... | collective-permute-start | bytes 884744 | tf_op jit(solution)/shard_map/ppermute | solution.py:86
  97.9 8.3 %collective-permute-start.37 = (bf16[208,384]{1,0:T(8,128)(2,1)S(1)}, bf16[208,384]{1,0:T(8,128)(2,1)S(1)}, u32[]{:S(2)}, u32[]{:S(2)}) collective-permute-start(bf16[208,384]{1,0:T(8,128)(2,1)S(1)} %pad_maximum_fusion.3), channel_id=1, source_target_pairs={{0,8},{4,12},{8,0},{12,4},{16,24},{20,28},{24,16},{28,20},{1,9},{5... | collective-permute-start | bytes 479240 | tf_op jit(solution)/shard_map/ppermute | solution.py:86
  99.7 14.0 %collective-permute-start.38 = (bf16[208,384]{1,0:T(8,128)(2,1)S(1)}, bf16[208,384]{1,0:T(8,128)(2,1)S(1)}, u32[]{:S(2)}, u32[]{:S(2)}) collective-permute-start(bf16[208,384]{1,0:T(8,128)(2,1)S(1)} %pad_maximum_fusion.3), channel_id=1, source_target_pairs={{0,16},{4,20},{8,24},{12,28},{16,0},{20,4},{24,8},{28,12},{1,17},{... | collective-permute-start | bytes 479240 | tf_op jit(solution)/shard_map/ppermute | solution.py:86
  100.8 13.0 %collective-permute-start.39 = (bf16[208,384]{1,0:T(8,128)(2,1)S(1)}, bf16[208,384]{1,0:T(8,128)(2,1)S(1)}, u32[]{:S(2)}, u32[]{:S(2)}) collective-permute-start(bf16[208,384]{1,0:T(8,128)(2,1)S(1)} %pad_maximum_fusion.3), channel_id=1, source_target_pairs={{0,24},{4,28},{8,16},{12,20},{16,8},{20,12},{24,0},{28,4},{1,25},{... | collective-permute-start | bytes 479240 | tf_op jit(solution)/shard_map/ppermute | solution.py:86
  102.3 6.0 %collective-permute-start.40 = (bf16[192,384]{1,0:T(8,128)(2,1)S(1)}, bf16[192,384]{1,0:T(8,128)(2,1)S(1)}, u32[]{:S(2)}, u32[]{:S(2)}) collective-permute-start(bf16[192,384]{1,0:T(8,128)(2,1)S(1)} %add_convert_fusion.1.refs_1_), channel_id=1, source_target_pairs={{0,4},{4,0},{8,12},{12,8},{16,20},{20,16},{24,28},{28,24},{1,5},{5... | collective-permute-start | bytes 442376 | tf_op jit(solution)/shard_map/ppermute | solution.py:86
  106.2 7.5 %collective-permute-start.41 = (bf16[192,384]{1,0:T(8,128)(2,1)S(1)}, bf16[192,384]{1,0:T(8,128)(2,1)S(1)}, u32[]{:S(2)}, u32[]{:S(2)}) collective-permute-start(bf16[192,384]{1,0:T(8,128)(2,1)S(1)} %slice.208), channel_id=1, source_target_pairs={{0,4},{4,0},{8,12},{12,8},{16,20},{20,16},{24,28},{28,24},{1,5},{5... | collective-permute-start | bytes 442376 | tf_op jit(solution)/shard_map/ppermute | solution.py:86
  113.8 9.1 %collective-permute-start.43 = (bf16[192,384]{1,0:T(8,128)(2,1)S(1)}, bf16[192,384]{1,0:T(8,128)(2,1)S(1)}, u32[]{:S(2)}, u32[]{:S(2)}) collective-permute-start(bf16[192,384]{1,0:T(8,128)(2,1)S(1)} %slice.296), channel_id=1, source_target_pairs={{0,16},{4,20},{8,24},{12,28},{16,0},{20,4},{24,8},{28,12},{1,17},{... | collective-permute-start | bytes 442376 | tf_op jit(solution)/shard_map/ppermute | solution.py:86
  117.5 4.6 %collective-permute-start.44 = (f32[2,768]{1,0:T(2,128)S(1)}, f32[2,768]{1,0:T(2,128)S(1)}, u32[]{:S(2)}, u32[]{:S(2)}) collective-permute-start(f32[2,768]{1,0:T(2,128)S(1)} %fusion.31), channel_id=1, source_target_pairs={{0,4},{4,0},{8,12},{12,8},{16,20},{20,16},{24,28},{28,24},{1,5},{5... | collective-permute-start | bytes 18440 | tf_op jit(solution)/shard_map/ppermute | solution.py:86
  118.1 6.8 %collective-permute-start.45 = (bf16[384,384]{1,0:T(8,128)(2,1)S(1)}, bf16[384,384]{1,0:T(8,128)(2,1)S(1)}, u32[]{:S(2)}, u32[]{:S(2)}) collective-permute-start(bf16[384,384]{1,0:T(8,128)(2,1)S(1)} %pad_maximum_fusion.1), channel_id=1, source_target_pairs={{0,4},{4,0},{8,12},{12,8},{16,20},{20,16},{24,28},{28,24},{1,5},{5... | collective-permute-start | bytes 884744 | tf_op jit(solution)/shard_map/ppermute | solution.py:86
  125.0 5.3 %collective-permute-start.46 = (bf16[208,384]{1,0:T(8,128)(2,1)S(1)}, bf16[208,384]{1,0:T(8,128)(2,1)S(1)}, u32[]{:S(2)}, u32[]{:S(2)}) collective-permute-start(bf16[208,384]{1,0:T(8,128)(2,1)S(1)} %pad_maximum_fusion.2), channel_id=1, source_target_pairs={{0,2},{1,3},{2,0},{3,1},{4,6},{5,7},{6,4},{7,5},{8,10},{9,11},{10,... | collective-permute-start | bytes 479240 | tf_op jit(solution)/shard_map/ppermute | solution.py:86
  130.6 1.7 %collective-permute-start.47 = (bf16[400,384]{1,0:T(8,128)(2,1)S(1)}, bf16[400,384]{1,0:T(8,128)(2,1)S(1)}, u32[]{:S(2)}, u32[]{:S(2)}) collective-permute-start(bf16[400,384]{1,0:T(8,128)(2,1)S(1)} %pad_maximum_fusion), channel_id=1, source_target_pairs={{0,1},{1,0},{2,3},{3,2},{4,5},{5,4},{6,7},{7,6},{8,9},{9,8},{10,11... | collective-permute-start | bytes 921608 | tf_op jit(solution)/shard_map/ppermute | solution.py:86
  (10 other events, 19.5 us)

commit v6 on v5

--- a/solution.py
+++ b/solution.py
@@ -35,7 +35,8 @@
             buffer = rest[n_own + j]
             copies[i] = pltpu.make_async_copy(ins[i], buffer, rest[-1].at[j])
             ins[i] = buffer
-        for wanted in (LOAD, LATE):
+
+        def start(wanted):
             for i in loads:
                 if in_specs[i] is wanted:
                     copies[i].start()
@@ -46,8 +47,9 @@
                     copies[i].wait()
 
         if staged:
-            body(arrive, *ins, *rest[:n_own])
+            body(start, arrive, *ins, *rest[:n_own])
         else:
+            start(LOAD)
             arrive(LOAD)
             body(*ins, *rest[:n_own])
 
@@ -150,6 +152,8 @@
 
 def prepare_kernel(
     fold,
+    start,
+    arrive,
     place,
     q_hbm,
     s_hbm,
@@ -189,8 +193,12 @@
             sems.at[2 + fold],
         )
     )
-    for copy in tokens + copies:
+    for copy in tokens:
         copy.start()
+    start(LOAD)
+    for copy in copies:
+        copy.start()
+    arrive(LOAD)
     tokens[0].wait()
     rms_rows(s_ref, s_gain, s_out)
     tokens[1].wait()
@@ -226,6 +234,7 @@
                 pltpu.SemaphoreType.DMA((fold + 3,)),
             ],
             limit=60,
+            staged=True,
         )(place, own_q, own_s, q_gain, s_gain, inner, outer)
     piece = lax.dynamic_slice_in_dim(inner, place[2] * (thin * fold), thin * fold, 0)
     piece = jnp.concatenate([piece[i * thin : (i + 1) * thin] for i in range(fold)], 1)
@@ -248,7 +257,7 @@
     return copies
 
 
-def forward_kernel(n, far, axis, arrive, place, lengths, positive, own, *refs):
+def forward_kernel(n, far, axis, start, arrive, place, lengths, positive, own, *refs):
     token_refs, refs = refs[:n], refs[n:]
     inners, outers = [refs[0]], [refs[1]]
     pieces = refs[2 : 2 + PARTS * far]
@@ -259,10 +268,12 @@
         refs = refs[2 + far :]
     else:
         part, outs, refs = refs[0], [refs[0]], refs[1:]
-    start = 0 if far else width
+    offset = 0 if far else width
     results, buffers, sems = refs[: 1 + 2 * far], refs[1 + 2 * far : -1], refs[-1]
     rows = buffers[0]
+    start(LOAD)
     gathered = gather_rows(token_refs, rows, sems)
+    start(LATE)
     leaving = [
         pltpu.make_async_copy(x, y, sems.at[i]) for i, (x, y) in enumerate(zip(buffers, results))
     ]
@@ -285,7 +296,7 @@
                 value = jnp.where(run_mask(span, 0, length), value, 0.0)
                 row = jnp.sum(value, axis=0, keepdims=True) / length.astype(F32)
                 tile = jnp.where(index == ((me ^ k) & (total - 1)), row, tile)
-            out[:, start + columns.start : start + columns.stop] = tile
+            out[:, offset + columns.start : offset + columns.stop] = tile
 
     pool(inners[0], outs[0])
     arrive(LATE)
@@ -321,7 +332,7 @@
     own_row = jnp.sum(x, axis=0, keepdims=True) / length.astype(F32)
     result = jnp.where(index == (me & (total - 1)), own_row, 0.0)
     for outer, out in zip(outers, outs):
-        units = out[:, start : start + outer.shape[0]]
+        units = out[:, offset : offset + outer.shape[0]]
         high = units.astype(BF16)
         rest = units - high.astype(F32)
         middle = rest.astype(BF16)
@@ -353,8 +364,10 @@
     body = functools.partial(forward_kernel, len(tokens), far, axis)
     if far:
         return call(
-            lambda arrive, place, lengths, *refs: body(arrive, place, lengths, None, *refs),
-            [SMEM] * 2 + [LOAD] + [HBM] * len(tokens) + [LOAD] * 2 + [LATE] * len(pieces),
+            lambda start, arrive, place, lengths, *refs: body(
+                start, arrive, place, lengths, None, *refs
+            ),
+            [SMEM] * 2 + [LATE] + [HBM] * len(tokens) + [LOAD, LATE] + [LATE] * len(pieces),
             [((count, width), F32)]
             + [((count, units), F32)] * (1 + far)
             + [(x, BF16) for x in large],
@@ -368,7 +381,7 @@
         )(place, lengths, own, *tokens, inner, outer, *pieces)
     return call(
         body,
-        [SMEM] * 3 + [LOAD] + [HBM] * len(tokens) + [LOAD] * 2,
+        [SMEM] * 3 + [LATE] + [HBM] * len(tokens) + [LOAD, LATE],
         [((count, columns), F32)] + [(x, BF16) for x in large],
         [pltpu.VMEM(x, BF16) for x in large] + [pltpu.SemaphoreType.DMA((len(tokens),))],
         flops=3 * 10**9,
@@ -415,7 +428,7 @@
     )(place, lengths, *tokens, *weights)
 
 
-def inner_gradient(row_refs, slope_refs, hidden, weights, gain, total, span):
+def inner_gradient(row_refs, slope_refs, hidden, weights, gain, total, span, arrive=None):
     base = 0
     gains = jnp.zeros((total.shape[0], 128), F32)
     for weight in weights:
@@ -443,14 +456,17 @@
             for c in range(0, shares.shape[1], 128):
                 gains = gains + shares[:, c : c + 128]
         base += weight.shape[1]
+    if arrive is not None:
+        arrive(LOAD)
     return jnp.sum(gains.T, axis=0, keepdims=True) / gain[...][None, :]
 
 
-def q_backward_kernel(pairs, span, place, *refs):
+def q_backward_kernel(pairs, span, start, arrive, place, *refs):
+    start(LOAD)
     rows, pair_rows, own_slope, pair_slope, hidden, weight, gain = refs[:7]
     sends, (keep, gains, total) = refs[7 : 6 + pairs], refs[6 + pairs :]
     gains[...] = inner_gradient(
-        [rows, pair_rows], [own_slope, pair_slope], hidden, [weight], gain, total, span
+        [rows, pair_rows], [own_slope, pair_slope], hidden, [weight], gain, total, span, arrive
     )
     mine = place[0] // 2
     size = keep.shape[0]
@@ -470,6 +486,7 @@
         [pltpu.VMEM((width, units), F32)],
         flops=4 * 10**9,
         bytes_accessed=3 * 10**6,
+        staged=True,
     )(place, rows, pair_rows, slope, pair_slope, hidden, weight, gain)
 
 
@@ -511,8 +528,9 @@
 
 
 def score_kernel(
-    n_sa, n_pb, width, place, q_ref, s_ref, q_outer, *refs
+    n_sa, n_pb, width, start, arrive, place, q_ref, s_ref, q_outer, *refs
 ):
+    start(LOAD)
     s_outers = refs[:-5]
     loss_ref, q_grad_ref, s_grad_ref, q_hidden, s_hidden = refs[-5:]
     p, a = place[0], place[1]
@@ -557,6 +575,7 @@
     pair = (index >= n_sa).astype(jnp.int32)
     hidden(q_grad, (p ^ pair) * n_sa + (a ^ (index - pair * n_sa)), [q_outer], q_hidden)
     index = lax.broadcasted_iota(jnp.int32, (8, 1), 0)
+    arrive(LOAD)
     hidden(s_grad, a * n_pb + (p ^ index), s_outers, s_hidden)
 
 
@@ -573,6 +592,7 @@
             ((2 * n_sa, q_outer.shape[0]), F32),
             ((8, units), F32),
         ],
+        staged=True,
     )(place, q_all, s_all, q_outer, *s_outers)
 
 
@@ -721,32 +741,25 @@
     )
     s_inners = [s_inner_weight] + far_weights[0::2]
     s_outers = [s_outer_weight] + far_weights[1::2]
-    s_part, q_all = together(s_part, q_all)
 
     s_others = [swap(s_part, "pb", k) for k in range(1, GROUP)]
-    pair_meta = swap(q_all, "pb", 1)
+    pair_meta, s_part = together(swap(q_all, "pb", 1), s_part)
     q_all = ordered(q_all, pair_meta, pair_bit)
     pair_lengths = pair_meta[:, width + units + 1].astype(jnp.int32)
+    q_all = ordered(q_all, swap(q_all, "pb", 2), bit_at(p, 2))
     s_part = (s_part + s_others[0]) + (s_others[1] + s_others[2])
-    s_part, q_all, pair_lengths = together(s_part, q_all, pair_lengths)
+    pair_tokens = [pair_token] + [None] * (n_sa - 1)
+    pair_tokens[top] = pair_far
+    for step in reversed(bits_of(n_sa)):
+        for k in range(0, n_sa, 2 * step):
+            if pair_tokens[k + step] is None:
+                pair_tokens[k + step] = swap(pair_tokens[k], "sa", step)
+    s_part, q_all, pair_lengths, pair_tokens = together(s_part, q_all, pair_lengths, pair_tokens)
 
     s_sent = [jnp.concatenate([s_part, s_pooled[0]], 1)]
     for i, k in enumerate(far, 1):
         s_sent.append(swap(jnp.concatenate([s_part, s_pooled[i]], 1), "pb", k))
-    q_all = ordered(q_all, swap(q_all, "pb", 2), bit_at(p, 2))
     s_all = canonical(s_sent, p // GROUP)[None]
-    pair_beside = swap(pair_token, "sa", 1)
-    s_all, q_all, pair_far, pair_beside = together(s_all, q_all, pair_far, pair_beside)
-    pair_tokens = [[pair_token], [pair_beside]] + [None] * (n_sa - 2)
-    pair_tokens[top] = [pair_far]
-    for step in reversed(bits_of(n_sa)):
-        for k in range(0, n_sa, 2 * step):
-            if pair_tokens[k + step] is None:
-                cuts = 4 if step == 1 else 1
-                pair_tokens[k + step] = [
-                    swap(x, "sa", step) for x in jnp.split(pair_tokens[k][0], cuts, axis=0)
-                ]
-    pair_tokens = [x for parts in pair_tokens for x in parts]
     for step in bits_of(n_pb)[2:]:
         q_all = ordered(q_all, swap(q_all, "pb", step), bit_at(p, step))
     pair_slope, pair_rows = slopes(place, pair_lengths, pair_tokens, [q_inner_half], 1, length)

time: 135 us -> 131 us (0.970)
    ppermute x48 -> x45, waiting for transfers between devices: 39 us -> 37.8 us  [swap(): return lax.ppermute(x, axis, [(i, i ^ step) for i in range(size)])]
    ppermute x48 -> x45, starting transfers between devices: 45.6 us -> 44.5 us  [swap(): return lax.ppermute(x, axis, [(i, i ^ step) for i in range(size)])]
  transfers between devices with their start and end apart: 48 -> 45, of which waited for: 24 -> 23; matrix products, arithmetic and copies ran while one was open for 6% -> 6% of each run, Pallas kernels for 14% -> 19%
where the time goes in v6:
time: 131 us; the launch traced here: 130 us
  starting transfers between devices  44.5 us (34%)
  waiting for transfers between devices  37.8 us (29%)
  Pallas kernels  33.8 us (26%)
  local copies, waits for them, and re-layouts  5.19 us (4%)
  other arithmetic  4.27 us (3%)
  matrix products  3.26 us (2%)
  between operations  1.51 us (1%)
    ppermute x45, starting transfers between devices, swap(): return lax.ppermute(x, axis, [(i, i ^ step) for i in range(size)])  44.5 us
    ppermute x45, waiting for transfers between devices, swap(): return lax.ppermute(x, axis, [(i, i ^ step) for i in range(size)])  37.8 us
    pallas_call x10, Pallas kernels, run(): pl.pallas_call(kernel, in_specs=[HBM if spec in (LOAD, LATE) else spec fo...  33.8 us
    dot_general x2, matrix products, outer_gradient(): lax.dot_general(left, right, CONTRACT_FIRST, preferred_element_type=F32)  3.26 us
  transfers between devices with their start and end apart: 45, of which 23 were waited for; matrix products, arithmetic and copies ran while one was open for 6% of the time, Pallas kernels for 19%

profile of v6, /device:TPU:0, one launch (start us, length us, event | category | flops | bytes accessed | tf_op | source)
XLA Modules:
  0.0 130.4 jit_solution(14174040042540772700)
XLA Ops:
  0.7 0.6 stack.23.refs_0_
  1.3 3.2 %shard_map.162 = (bf16[256,768]{1,0:T(8,128)(2,1)}, bf16[256,768]{1,0:T(8,128)(2,1)}, bf16[192,768]{1,0:T(8,128)(2,1)}) custom-call(s32[5]{0:T(128)} %stack.23.refs_0_, bf16[256,768]{1,0:T(8,128)(2,1)} %bitcast.18, bf16[256,768]{1,0:T(8,128)(2,1)} %bitcast.20, f32[768]{0:T(1024)} %refs_7_.3, f32[768]{0:T(1024)} %refs_6_.3, bf16[768,384]{1,0:T(8,128)(2,1)} %refs_4_.5, ...), custom_call_target="tpu_custom_call" | custom-call | tf_op jit(solution)/shard_map/pallas_call | solution.py:60
  4.5 4.1 %collective-permute-start.2 = (bf16[192,768]{1,0:T(8,128)(2,1)}, bf16[192,768]{1,0:T(8,128)(2,1)}, u32[]{:S(2)}, u32[]{:S(2)}) collective-permute-start(bf16[192,768]{1,0:T(8,128)(2,1)} %get-tuple-element.81), channel_id=1, source_target_pairs={{0,16},{4,20},{8,24},{12,28},{16,0},{20,4},{24,8},{28,12},{1,17},{... | collective-permute-start | bytes 884744 | tf_op jit(solution)/shard_map/ppermute | solution.py:88
  8.6 1.5 %collective-permute-start = (bf16[256,768]{1,0:T(8,128)(2,1)}, bf16[256,768]{1,0:T(8,128)(2,1)}, u32[]{:S(2)}, u32[]{:S(2)}) collective-permute-start(bf16[256,768]{1,0:T(8,128)(2,1)} %get-tuple-element.80.refs_3_), channel_id=1, source_target_pairs={{0,4},{4,0},{8,12},{12,8},{16,20},{20,16},{24,28},{28,24},{1,5},{5... | collective-permute-start | bytes 1179656 | tf_op jit(solution)/shard_map/ppermute | solution.py:88
  10.1 1.6 %collective-permute-start.1 = (bf16[256,768]{1,0:T(8,128)(2,1)}, bf16[256,768]{1,0:T(8,128)(2,1)S(1)}, u32[]{:S(2)}, u32[]{:S(2)}) collective-permute-start(bf16[256,768]{1,0:T(8,128)(2,1)} %get-tuple-element.80.refs_3_), channel_id=1, source_target_pairs={{0,8},{4,12},{8,0},{12,4},{16,24},{20,28},{24,16},{28,20},{1,9},{5... | collective-permute-start | bytes 1179656 | tf_op jit(solution)/shard_map/ppermute | solution.py:88
  11.6 1.5 %collective-permute-start.4 = (bf16[256,768]{1,0:T(8,128)(2,1)}, bf16[256,768]{1,0:T(8,128)(2,1)S(1)}, u32[]{:S(2)}, u32[]{:S(2)}) collective-permute-start(bf16[256,768]{1,0:T(8,128)(2,1)} %get-tuple-element.90.refs_4_), channel_id=1, source_target_pairs={{0,2},{1,3},{2,0},{3,1},{4,6},{5,7},{6,4},{7,5},{8,10},{9,11},{10,... | collective-permute-start | bytes 1179656 | tf_op jit(solution)/shard_map/ppermute | solution.py:88
  13.2 0.6 convert_reduce_fusion.refs_1_
  13.8 8.5 %collective-permute-done.2.refs_9_ = bf16[192,768]{1,0:T(8,128)(2,1)} collective-permute-done((bf16[192,768]{1,0:T(8,128)(2,1)}, bf16[192,768]{1,0:T(8,128)(2,1)}, u32[]{:S(2)}, u32[]{:S(2)}) %collective-permute-start.2) | collective-permute-done | bytes 294944 | tf_op jit(solution)/shard_map/ppermute | solution.py:88
  22.6 1.2 constant_dynamic-slice_fusion.refs_3_
  23.8 1.9 %collective-permute-done.1.refs_5_ = bf16[256,768]{1,0:T(8,128)(2,1)S(1)} collective-permute-done((bf16[256,768]{1,0:T(8,128)(2,1)}, bf16[256,768]{1,0:T(8,128)(2,1)S(1)}, u32[]{:S(2)}, u32[]{:S(2)}) %collective-permute-start.1) | collective-permute-done | bytes 393248 | tf_op jit(solution)/shard_map/ppermute | solution.py:88
  26.5 1.6 %collective-permute-start.6 = (bf16[192,768]{1,0:T(8,128)(2,1)}, bf16[192,768]{1,0:T(8,128)(2,1)S(1)}, u32[]{:S(2)}, u32[]{:S(2)}) collective-permute-start(bf16[192,768]{1,0:T(8,128)(2,1)} %collective-permute-done.2.refs_9_), channel_id=1, source_target_pairs={{0,2},{1,3},{2,0},{3,1},{4,6},{5,7},{6,4},{7,5},{8,10},{9,11},{10,... | collective-permute-start | bytes 884744 | tf_op jit(solution)/shard_map/ppermute | solution.py:88
  28.0 1.1 collective-permute-start.10
  29.2 4.3 %shard_map.163 = (f32[4,1664]{1,0:T(4,128)S(1)}, bf16[1024,768]{1,0:T(8,128)(2,1)S(1)}) custom-call(s32[5]{0:T(128)S(1)} %copy-done.10, s32[4]{0:T(128)S(1)} %convert_reduce_fusion.1.refs_1_, s32[4]{0:T(128)S(1)} %copy-done.16, bf16[256,768]{1,0:T(8,128)(2,1)S(1)} %bitcast.19, bf16[256,768]{1,0:T(8,128)(2,1)S(1)} %copy-done.15, ...), custom_call_target="tpu_custom_call" | custom-call | flops 3000000000 | bytes 3000000 | tf_op jit(solution)/shard_map/pallas_call | solution.py:60
  34.1 1.8 %shard_map.164.refs_3_ = f32[1024,384]{1,0:T(8,128)S(1)} custom-call(s32[5]{0:T(128)S(1)} %copy-done.10, s32[4]{0:T(128)S(1)} %convert_reduce_fusion.1.refs_1_, bf16[1024,768]{1,0:T(8,128)(2,1)S(1)} %get-tuple-element.88.refs_2_.refs_1_, bf16[768,384]{1,0:T(8,128)(2,1)S(1)} %constant_dynamic-slice_fusion.1.refs_3_.refs_6_), custom_call_target="tpu_custom_call" | custom-call | flops 905969664 | bytes 3000000 | tf_op jit(solution)/shard_map/pallas_call | solution.py:60
  36.0 1.2 copy-done.3
  37.6 1.1 collective-permute-done.10.refs_2_
  39.2 1.2 collective-permute-start.19
  40.4 0.9 collective-permute-start.12
  41.4 0.9 collective-permute-done.13.refs_12_
  42.3 6.5 %shard_map.165 = (f32[4,768]{1,0:T(4,128)}, f32[4,384]{1,0:T(4,128)}, f32[4,384]{1,0:T(4,128)}, bf16[1024,768]{1,0:T(8,128)(2,1)}, bf16[768,384]{1,0:T(8,128)(2,1)}, /*index=5*/bf16[384,768]{1,0:T(8,128)(2,1)}) custom-call(s32[5]{0:T(128)} %stack.23.refs_0_, s32[8]{0:T(128)} %convert_reduce_fusion.refs_1_, bf16[256,768]{1,0:T(8,128)(2,1)} %bitcast.21, ...), custom_call_target="tpu_custom_call" | custom-call | flops 3000000000 | bytes 3000000 | tf_op jit(solution)/shard_map/pallas_call | solution.py:60
  48.9 1.0 collective-permute-start.15
  49.9 1.2 collective-permute-start.16
  51.1 1.3 %collective-permute-start.14 = (f32[4,768]{1,0:T(4,128)}, f32[4,768]{1,0:T(4,128)S(1)}, u32[]{:S(2)}, u32[]{:S(2)}) collective-permute-start(f32[4,768]{1,0:T(4,128)} %get-tuple-element.98), channel_id=1, source_target_pairs={{0,4},{4,0},{8,12},{12,8},{16,20},{20,16},{24,28},{28,24},{1,5},{5... | collective-permute-start | bytes 36872 | tf_op jit(solution)/shard_map/ppermute | solution.py:88
  52.8 1.0 collective-permute-start.17
  53.9 0.8 collective-permute-done.16
  55.0 0.7 add_add_fusion
  55.7 1.2 collective-permute-done.17
  57.0 2.1 %collective-permute-start.21 = (f32[16,1664]{1,0:T(8,128)S(1)}, f32[16,1664]{1,0:T(8,128)S(1)}, u32[]{:S(2)}, u32[]{:S(2)}) collective-permute-start(f32[16,1664]{1,0:T(8,128)S(1)} %maximum_select_fusion.4), channel_id=1, source_target_pairs={{0,16},{4,20},{8,24},{12,28},{16,0},{20,4},{24,8},{28,12},{1,17},{... | collective-permute-start | bytes 319496 | tf_op jit(solution)/shard_map/ppermute | solution.py:88
  59.1 0.7 pad_maximum_fusion.5
  59.8 0.9 collective-permute-start.22
  60.7 0.7 constant_dynamic-update-slice_fusion
  61.4 3.2 %collective-permute-done.22 = f32[4,1152]{1,0:T(4,128)S(1)} collective-permute-done((f32[4,1152]{1,0:T(4,128)S(1)}, f32[4,1152]{1,0:T(4,128)S(1)}, u32[]{:S(2)}, u32[]{:S(2)}) %collective-permute-start.22) | collective-permute-done | bytes 18464 | tf_op jit(solution)/shard_map/ppermute | solution.py:88
  64.6 1.6 %collective-permute-start.23 = (f32[1,8,1152]{2,1,0:T(8,128)S(1)}, f32[1,8,1152]{2,1,0:T(8,128)S(1)}, u32[]{:S(2)}, u32[]{:S(2)}) collective-permute-start(f32[1,8,1152]{2,1,0:T(8,128)S(1)} %maximum_bitcast_fusion), channel_id=1, source_target_pairs={{0,2},{1,3},{2,0},{3,1},{4,6},{5,7},{6,4},{7,5},{8,10},{9,11},{10,... | collective-permute-start | bytes 110600 | tf_op jit(solution)/shard_map/ppermute | solution.py:88
  66.2 3.3 %shard_map.166 = (f32[1024,384]{1,0:T(8,128)S(1)}, bf16[1024,768]{1,0:T(8,128)(2,1)S(1)}) custom-call(s32[5]{0:T(128)S(1)} %copy-done.11, s32[4]{0:T(128)S(1)} %convert_reduce_fusion.2.refs_1_, bf16[256,768]{1,0:T(8,128)(2,1)S(1)} %collective-permute-done.10.refs_2_, bf16[256,768]{1,0:T(8,128)(2,1)S(1)} %collective-permute-done.18.refs_3_, ...), custom_call_target="tpu_custom_call" | custom-call | flops 905969664 | bytes 3000000 | tf_op jit(solution)/shard_map/pallas_call | solution.py:60
  69.7 1.2 collective-permute-done.24
  71.0 2.8 %shard_map.167 = (f32[1,1]{1,0:T(1,128)}, f32[32,768]{1,0:T(8,128)S(1)}, f32[32,768]{1,0:T(8,128)S(1)}, f32[8,384]{1,0:T(8,128)S(1)}, f32[8,768]{1,0:T(8,128)S(1)}) custom-call(s32[5]{0:T(128)S(1)} %copy-done.11, f32[32,1664]{1,0:T(8,128)S(1)} %maximum_select_fusion.2.refs_1_, f32[32,1152]{1,0:T(8,128)S(1)} %pad_maximum_fusion.4.refs_2_, ...), custom_call_target="tpu_custom_call" | custom-call | tf_op jit(solution)/shard_map/pallas_call | solution.py:60
  73.9 2.6 %shard_map.168 = (bf16[192,384]{1,0:T(8,128)(2,1)S(1)}, bf16[192,384]{1,0:T(8,128)(2,1)S(1)}, bf16[192,384]{1,0:T(8,128)(2,1)S(1)}, f32[192,384]{1,0:T(8,128)S(1)}, f32[1,768]{1,0:T(1,128)S(1)}) custom-call(s32[5]{0:T(128)S(1)} %copy-done.11, bf16[1024,768]{1,0:T(8,128)(2,1)S(1)} %copy-done.2, bf16[1024,768]{1,0:T(8,128)(2,1)S(1)} %get-tuple-element.115.refs_2_, ...), custom_call_target="tpu_custom_call" | custom-call | flops 4000000000 | bytes 3000000 | tf_op jit(solution)/shard_map/pallas_call | solution.py:60
  76.8 2.8 %collective-permute-start.26 = (bf16[192,384]{1,0:T(8,128)(2,1)S(1)}, bf16[192,384]{1,0:T(8,128)(2,1)S(1)}, u32[]{:S(2)}, u32[]{:S(2)}) collective-permute-start(bf16[192,384]{1,0:T(8,128)(2,1)S(1)} %get-tuple-element.121), channel_id=1, source_target_pairs={{0,16},{4,20},{8,24},{12,28},{16,0},{20,4},{24,8},{28,12},{1,17},{... | collective-permute-start | bytes 442376 | tf_op jit(solution)/shard_map/ppermute | solution.py:88
  79.6 1.3 %collective-permute-start.27 = (bf16[192,384]{1,0:T(8,128)(2,1)S(1)}, bf16[192,384]{1,0:T(8,128)(2,1)S(1)}, u32[]{:S(2)}, u32[]{:S(2)}) collective-permute-start(bf16[192,384]{1,0:T(8,128)(2,1)S(1)} %get-tuple-element.122), channel_id=1, source_target_pairs={{0,24},{4,28},{8,16},{12,20},{16,8},{20,12},{24,0},{28,4},{1,25},{... | collective-permute-start | bytes 442376 | tf_op jit(solution)/shard_map/ppermute | solution.py:88
  81.0 4.8 %shard_map.169 = (bf16[384,768]{1,0:T(8,128)(2,1)S(1)}, f32[384,768]{1,0:T(8,128)S(1)}, bf16[16,768]{1,0:T(8,128)(2,1)S(1)}) custom-call(s32[5]{0:T(128)S(1)} %copy-done.11, s32[8]{0:T(128)S(1)} %copy-done.14, bf16[1024,768]{1,0:T(8,128)(2,1)S(1)} %copy-done.17, f32[8,768]{1,0:T(8,128)S(1)} %get-tuple-element.126.refs_3_, bf16[768,384]{1,0:T(8,128)(2,1)S(1)} %copy-done.6, ...), custom_call_target="tpu_custom_call" | custom-call | flops 6000000000 | bytes 3000000 | tf_op jit(solution)/shard_map/pallas_call | solution.py:60
  86.4 1.9 %fusion.1 = f32[768,768]{1,0:T(8,128)} fusion(bf16[32,768]{1,0:T(8,128)(2,1)S(1)} %get-tuple-element.168, bf16[32,768]{1,0:T(8,128)(2,1)S(1)} %get-tuple-element.167, bf16[32,768]{1,0:T(8,128)(2,1)S(1)} %get-tuple-element.187, bf16[32,768]{1,0:T(8,128)(2,1)S(1)} %get-tuple-element.188), kind=kOutput, calls=%fused_computation.16 | convolution fusion | flops 114130944 | bytes 2555904 | tf_op jit(solution)/shard_map/dot_general | solution.py:802
  88.3 1.4 %fusion.12 = f32[384,768]{1,0:T(8,128)} fusion(bf16[32,768]{1,0:T(8,128)(2,1)S(1)} %get-tuple-element.176, bf16[32,768]{1,0:T(8,128)(2,1)S(1)} %get-tuple-element.175, bf16[32,384]{1,0:T(8,128)(2,1)S(1)} %get-tuple-element.170, bf16[32,384]{1,0:T(8,128)(2,1)S(1)} %get-tuple-element.169), kind=kOutput, calls=%fused_computation.27 | convolution fusion | flops 57286656 | bytes 1327104 | tf_op jit(solution)/shard_map/dot_general | solution.py:802
  90.3 0.7 collective-permute-done.30
  91.6 0.7 collective-permute-done.32
  92.8 0.7 collective-permute-start.39
  93.7 1.2 collective-permute-start.34
  94.8 1.9 %collective-permute-start.35 = (bf16[208,384]{1,0:T(8,128)(2,1)S(1)}, bf16[208,384]{1,0:T(8,128)(2,1)S(1)}, u32[]{:S(2)}, u32[]{:S(2)}) collective-permute-start(bf16[208,384]{1,0:T(8,128)(2,1)S(1)} %pad_maximum_fusion.3), channel_id=1, source_target_pairs={{0,16},{4,20},{8,24},{12,28},{16,0},{20,4},{24,8},{28,12},{1,17},{... | collective-permute-start | bytes 479240 | tf_op jit(solution)/shard_map/ppermute | solution.py:88
  96.8 1.3 %collective-permute-start.36 = (bf16[208,384]{1,0:T(8,128)(2,1)S(1)}, bf16[208,384]{1,0:T(8,128)(2,1)S(1)}, u32[]{:S(2)}, u32[]{:S(2)}) collective-permute-start(bf16[208,384]{1,0:T(8,128)(2,1)S(1)} %pad_maximum_fusion.3), channel_id=1, source_target_pairs={{0,24},{4,28},{8,16},{12,20},{16,8},{20,12},{24,0},{28,4},{1,25},{... | collective-permute-start | bytes 479240 | tf_op jit(solution)/shard_map/ppermute | solution.py:88
  98.1 0.8 collective-permute-start.37
  98.9 3.3 %collective-permute-done.34.refs_2_ = bf16[208,384]{1,0:T(8,128)(2,1)S(1)} collective-permute-done((bf16[208,384]{1,0:T(8,128)(2,1)S(1)}, bf16[208,384]{1,0:T(8,128)(2,1)S(1)}, u32[]{:S(2)}, u32[]{:S(2)}) %collective-permute-start.34) | collective-permute-done | bytes 159776 | tf_op jit(solution)/shard_map/ppermute | solution.py:88
  102.2 0.8 collective-permute-start.38
  103.3 6.2 %collective-permute-done.35.refs_2_ = bf16[208,384]{1,0:T(8,128)(2,1)S(1)} collective-permute-done((bf16[208,384]{1,0:T(8,128)(2,1)S(1)}, bf16[208,384]{1,0:T(8,128)(2,1)S(1)}, u32[]{:S(2)}, u32[]{:S(2)}) %collective-permute-start.35) | collective-permute-done | bytes 159776 | tf_op jit(solution)/shard_map/ppermute | solution.py:88
  109.5 3.7 %collective-permute-start.40 = (bf16[192,384]{1,0:T(8,128)(2,1)S(1)}, bf16[192,384]{1,0:T(8,128)(2,1)S(1)}, u32[]{:S(2)}, u32[]{:S(2)}) collective-permute-start(bf16[192,384]{1,0:T(8,128)(2,1)S(1)} %slice.293), channel_id=1, source_target_pairs={{0,16},{4,20},{8,24},{12,28},{16,0},{20,4},{24,8},{28,12},{1,17},{... | collective-permute-start | bytes 442376 | tf_op jit(solution)/shard_map/ppermute | solution.py:88
  113.3 1.0 collective-permute-start.41
  114.4 1.2 collective-permute-start.42
  115.5 2.4 %shard_map.170.refs_1_ = f32[768,768]{1,0:T(8,128)} custom-call(s32[5]{0:T(128)S(1)} %copy-done.11, bf16[192,384]{1,0:T(8,128)(2,1)S(1)} %add_convert_fusion.1.refs_1_, bf16[208,384]{1,0:T(8,128)(2,1)S(1)} %collective-permute-done.34.refs_2_, bf16[192,384]{1,0:T(8,128)(2,1)S(1)} %collective-permute-done.37.refs_3_, ...), custom_call_target="tpu_custom_call" | custom-call | flops 2000000000 | bytes 3000000 | tf_op jit(solution)/shard_map/pallas_call | solution.py:60
  118.0 0.8 collective-permute-done.40
  118.8 2.4 %collective-permute-done.42.refs_4_ = bf16[384,384]{1,0:T(8,128)(2,1)S(1)} collective-permute-done((bf16[384,384]{1,0:T(8,128)(2,1)S(1)}, bf16[384,384]{1,0:T(8,128)(2,1)S(1)}, u32[]{:S(2)}, u32[]{:S(2)}) %collective-permute-start.42) | collective-permute-done | bytes 294944 | tf_op jit(solution)/shard_map/ppermute | solution.py:88
  121.3 1.4 %collective-permute-start.43 = (bf16[208,384]{1,0:T(8,128)(2,1)S(1)}, bf16[208,384]{1,0:T(8,128)(2,1)S(1)}, u32[]{:S(2)}, u32[]{:S(2)}) collective-permute-start(bf16[208,384]{1,0:T(8,128)(2,1)S(1)} %pad_maximum_fusion.2), channel_id=1, source_target_pairs={{0,2},{1,3},{2,0},{3,1},{4,6},{5,7},{6,4},{7,5},{8,10},{9,11},{10,... | collective-permute-start | bytes 479240 | tf_op jit(solution)/shard_map/ppermute | solution.py:88
  122.7 2.1 %shard_map.171 = f32[768,768]{1,0:T(8,128)} custom-call(s32[5]{0:T(128)S(1)} %copy-done.11, f32[768,768]{1,0:T(8,128)} %shard_map.170.refs_1_, bf16[208,384]{1,0:T(8,128)(2,1)S(1)} %collective-permute-done.35.refs_2_, bf16[208,384]{1,0:T(8,128)(2,1)S(1)} %collective-permute-done.36.refs_3_, ...), custom_call_target="tpu_custom_call", output_to_operand_aliasing={{}: (1, {})} | custom-call | flops 2000000000 | bytes 3000000 | tf_op jit(solution)/shard_map/pallas_call | solution.py:60
  124.9 1.8 %collective-permute-done.43 = bf16[208,384]{1,0:T(8,128)(2,1)S(1)} collective-permute-done((bf16[208,384]{1,0:T(8,128)(2,1)S(1)}, bf16[208,384]{1,0:T(8,128)(2,1)S(1)}, u32[]{:S(2)}, u32[]{:S(2)}) %collective-permute-start.43) | collective-permute-done | bytes 159776 | tf_op jit(solution)/shard_map/ppermute | solution.py:88
  127.0 1.6 %collective-permute-done.44 = bf16[400,384]{1,0:T(8,128)(2,1)S(1)} collective-permute-done((bf16[400,384]{1,0:T(8,128)(2,1)S(1)}, bf16[400,384]{1,0:T(8,128)(2,1)S(1)}, u32[]{:S(2)}, u32[]{:S(2)}) %collective-permute-start.44) | collective-permute-done | bytes 307232 | tf_op jit(solution)/shard_map/ppermute | solution.py:88
  128.6 0.6 slice_reduce_fusion
  129.2 1.1 fusion
  (164 shorter events, 6.9 us)
Async XLA Ops:
  0.6 12.5 %copy-start.19 = (s32[1,8,256]{2,1,0:T(8,128)S(1)}, s32[1,8,256]{2,1,0:T(8,128)}, u32[]{:S(2)}) copy-start(s32[1,8,256]{2,1,0:T(8,128)} %param.17) | copy-start | bytes 24580
  0.6 21.7 %copy-start.20 = (s32[1,4,256]{2,1,0:T(4,128)S(1)}, s32[1,4,256]{2,1,0:T(4,128)}, u32[]{:S(2)}) copy-start(s32[1,4,256]{2,1,0:T(4,128)} %param.12) | copy-start | bytes 12292
  0.7 21.8 %copy-start.8 = (bf16[768,768]{1,0:T(8,128)(2,1)S(1)}, bf16[768,768]{1,0:T(8,128)(2,1)}, u32[]{:S(2)}) copy-start(bf16[768,768]{1,0:T(8,128)(2,1)} %refs_8_.2) | copy-start | bytes 3538948
  4.5 17.9 %collective-permute-start.2 = (bf16[192,768]{1,0:T(8,128)(2,1)}, bf16[192,768]{1,0:T(8,128)(2,1)}, u32[]{:S(2)}, u32[]{:S(2)}) collective-permute-start(bf16[192,768]{1,0:T(8,128)(2,1)} %get-tuple-element.81), channel_id=1, source_target_pairs={{0,16},{4,20},{8,24},{12,28},{16,0},{20,4},{24,8},{28,12},{1,17},{... | collective-permute-start | bytes 884744 | tf_op jit(solution)/shard_map/ppermute | solution.py:88
  8.6 15.3 %collective-permute-start = (bf16[256,768]{1,0:T(8,128)(2,1)}, bf16[256,768]{1,0:T(8,128)(2,1)}, u32[]{:S(2)}, u32[]{:S(2)}) collective-permute-start(bf16[256,768]{1,0:T(8,128)(2,1)} %get-tuple-element.80.refs_3_), channel_id=1, source_target_pairs={{0,4},{4,0},{8,12},{12,8},{16,20},{20,16},{24,28},{28,24},{1,5},{5... | collective-permute-start | bytes 1179656 | tf_op jit(solution)/shard_map/ppermute | solution.py:88
  10.1 15.7 %collective-permute-start.1 = (bf16[256,768]{1,0:T(8,128)(2,1)}, bf16[256,768]{1,0:T(8,128)(2,1)S(1)}, u32[]{:S(2)}, u32[]{:S(2)}) collective-permute-start(bf16[256,768]{1,0:T(8,128)(2,1)} %get-tuple-element.80.refs_3_), channel_id=1, source_target_pairs={{0,8},{4,12},{8,0},{12,4},{16,24},{20,28},{24,16},{28,20},{1,9},{5... | collective-permute-start | bytes 1179656 | tf_op jit(solution)/shard_map/ppermute | solution.py:88
  11.6 14.1 %collective-permute-start.4 = (bf16[256,768]{1,0:T(8,128)(2,1)}, bf16[256,768]{1,0:T(8,128)(2,1)S(1)}, u32[]{:S(2)}, u32[]{:S(2)}) collective-permute-start(bf16[256,768]{1,0:T(8,128)(2,1)} %get-tuple-element.90.refs_4_), channel_id=1, source_target_pairs={{0,2},{1,3},{2,0},{3,1},{4,6},{5,7},{6,4},{7,5},{8,10},{9,11},{10,... | collective-permute-start | bytes 1179656 | tf_op jit(solution)/shard_map/ppermute | solution.py:88
  13.1 16.0 %collective-permute-start.7 = (bf16[256,768]{1,0:T(8,128)(2,1)}, bf16[256,768]{1,0:T(8,128)(2,1)}, u32[]{:S(2)}, u32[]{:S(2)}) collective-permute-start(bf16[256,768]{1,0:T(8,128)(2,1)} %get-tuple-element.90.refs_4_), channel_id=1, source_target_pairs={{0,1},{1,0},{2,3},{3,2},{4,5},{5,4},{6,7},{7,6},{8,9},{9,8},{10,11... | collective-permute-start | bytes 1179656 | tf_op jit(solution)/shard_map/ppermute | solution.py:88
  22.3 3.4 %collective-permute-start.3 = (bf16[192,768]{1,0:T(8,128)(2,1)}, bf16[192,768]{1,0:T(8,128)(2,1)S(1)}, u32[]{:S(2)}, u32[]{:S(2)}) collective-permute-start(bf16[192,768]{1,0:T(8,128)(2,1)} %collective-permute-done.2.refs_9_), channel_id=1, source_target_pairs={{0,1},{1,0},{2,3},{3,2},{4,5},{5,4},{6,7},{7,6},{8,9},{9,8},{10,11... | collective-permute-start | bytes 884744 | tf_op jit(solution)/shard_map/ppermute | solution.py:88
  22.4 5.6 %copy-start.15 = (bf16[256,768]{1,0:T(8,128)(2,1)S(1)}, bf16[256,768]{1,0:T(8,128)(2,1)}, u32[]{:S(2)}) copy-start(bf16[256,768]{1,0:T(8,128)(2,1)} %get-tuple-element.90.refs_4_) | copy-start | bytes 1179652
  22.5 6.7 %copy-start.7 = (bf16[1,1,256,768]{3,2,1,0:T(8,128)(2,1)S(1)}, bf16[1,1,256,768]{3,2,1,0:T(8,128)(2,1)}, u32[]{:S(2)}) copy-start(bf16[1,1,256,768]{3,2,1,0:T(8,128)(2,1)} %param.11) | copy-start | bytes 1179652
  22.5 6.7 %copy-start.9 = (bf16[768,768]{1,0:T(8,128)(2,1)S(1)}, bf16[768,768]{1,0:T(8,128)(2,1)}, u32[]{:S(2)}) copy-start(bf16[768,768]{1,0:T(8,128)(2,1)} %refs_9_.1) | copy-start | bytes 3538948
  22.5 6.7 %copy-start.10 = (s32[5]{0:T(128)S(1)}, s32[5]{0:T(128)}, u32[]{:S(2)}) copy-start(s32[5]{0:T(128)} %stack.23.refs_0_) | copy-start | bytes 64
  22.5 6.7 %copy-start.16 = (s32[4]{0:T(128)S(1)}, s32[4]{0:T(128)}, u32[]{:S(2)}) copy-start(s32[4]{0:T(128)} %refs_2_.1) | copy-start | bytes 52
  25.7 3.5 %copy-start.23 = (bf16[192,768]{1,0:T(8,128)(2,1)}, bf16[192,768]{1,0:T(8,128)(2,1)S(1)}, u32[]{:S(2)}) copy-start(bf16[192,768]{1,0:T(8,128)(2,1)S(1)} %collective-permute-done.3.refs_11_) | copy-start | bytes 884740
  25.7 3.5 %collective-permute-start.8 = (bf16[256,768]{1,0:T(8,128)(2,1)S(1)}, bf16[256,768]{1,0:T(8,128)(2,1)S(1)}, u32[]{:S(2)}, u32[]{:S(2)}) collective-permute-start(bf16[256,768]{1,0:T(8,128)(2,1)S(1)} %collective-permute-done.4.refs_6_), channel_id=1, source_target_pairs={{0,1},{1,0},{2,3},{3,2},{4,5},{5,4},{6,7},{7,6},{8,9},{9,8},{10,11... | collective-permute-start | bytes 1179656 | tf_op jit(solution)/shard_map/ppermute | solution.py:88
  25.8 11.7 %collective-permute-start.5 = (bf16[256,768]{1,0:T(8,128)(2,1)}, bf16[256,768]{1,0:T(8,128)(2,1)S(1)}, u32[]{:S(2)}, u32[]{:S(2)}) collective-permute-start(bf16[256,768]{1,0:T(8,128)(2,1)} %collective-permute-done.refs_4_), channel_id=1, source_target_pairs={{0,8},{4,12},{8,0},{12,4},{16,24},{20,28},{24,16},{28,20},{1,9},{5... | collective-permute-start | bytes 1179656 | tf_op jit(solution)/shard_map/ppermute | solution.py:88
  26.5 11.0 %collective-permute-start.6 = (bf16[192,768]{1,0:T(8,128)(2,1)}, bf16[192,768]{1,0:T(8,128)(2,1)S(1)}, u32[]{:S(2)}, u32[]{:S(2)}) collective-permute-start(bf16[192,768]{1,0:T(8,128)(2,1)} %collective-permute-done.2.refs_9_), channel_id=1, source_target_pairs={{0,2},{1,3},{2,0},{3,1},{4,6},{5,7},{6,4},{7,5},{8,10},{9,11},{10,... | collective-permute-start | bytes 884744 | tf_op jit(solution)/shard_map/ppermute | solution.py:88
  28.0 10.7 %collective-permute-start.10 = (bf16[256,768]{1,0:T(8,128)(2,1)S(1)}, bf16[256,768]{1,0:T(8,128)(2,1)S(1)}, u32[]{:S(2)}, u32[]{:S(2)}) collective-permute-start(bf16[256,768]{1,0:T(8,128)(2,1)S(1)} %copy-done.15), channel_id=1, source_target_pairs={{0,4},{4,0},{8,12},{12,8},{16,20},{20,16},{24,28},{28,24},{1,5},{5... | collective-permute-start | bytes 1179656 | tf_op jit(solution)/shard_map/ppermute | solution.py:88
  33.5 3.9 %collective-permute-start.9 = (f32[4,1664]{1,0:T(4,128)S(1)}, f32[4,1664]{1,0:T(4,128)S(1)}, u32[]{:S(2)}, u32[]{:S(2)}) collective-permute-start(f32[4,1664]{1,0:T(4,128)S(1)} %get-tuple-element.87), channel_id=1, source_target_pairs={{0,2},{1,3},{2,0},{3,1},{4,6},{5,7},{6,4},{7,5},{8,10},{9,11},{10,... | collective-permute-start | bytes 79880 | tf_op jit(solution)/shard_map/ppermute | solution.py:88
  38.7 1.7 %collective-permute-start.11 = (f32[4,1664]{1,0:T(4,128)S(1)}, f32[4,1664]{1,0:T(4,128)S(1)}, u32[]{:S(2)}, u32[]{:S(2)}) collective-permute-start(f32[4,1664]{1,0:T(4,128)S(1)} %add_select_fusion.1), channel_id=1, source_target_pairs={{0,1},{1,0},{2,3},{3,2},{4,5},{5,4},{6,7},{7,6},{8,9},{9,8},{10,11... | collective-permute-start | bytes 79880 | tf_op jit(solution)/shard_map/ppermute | solution.py:88
  38.8 18.2 %collective-permute-start.18 = (bf16[256,768]{1,0:T(8,128)(2,1)S(1)}, bf16[256,768]{1,0:T(8,128)(2,1)S(1)}, u32[]{:S(2)}, u32[]{:S(2)}) collective-permute-start(bf16[256,768]{1,0:T(8,128)(2,1)S(1)} %collective-permute-done.10.refs_2_), channel_id=1, source_target_pairs={{0,1},{1,0},{2,3},{3,2},{4,5},{5,4},{6,7},{7,6},{8,9},{9,8},{10,11... | collective-permute-start | bytes 1179656 | tf_op jit(solution)/shard_map/ppermute | solution.py:88
  39.2 14.6 %collective-permute-start.19 = (bf16[256,768]{1,0:T(8,128)(2,1)S(1)}, bf16[256,768]{1,0:T(8,128)(2,1)}, u32[]{:S(2)}, u32[]{:S(2)}) collective-permute-start(bf16[256,768]{1,0:T(8,128)(2,1)S(1)} %collective-permute-done.10.refs_2_), channel_id=1, source_target_pairs={{0,2},{1,3},{2,0},{3,1},{4,6},{5,7},{6,4},{7,5},{8,10},{9,11},{10,... | collective-permute-start | bytes 1179656 | tf_op jit(solution)/shard_map/ppermute | solution.py:88
  40.4 1.9 %collective-permute-start.13 = (bf16[192,768]{1,0:T(8,128)(2,1)}, bf16[192,768]{1,0:T(8,128)(2,1)}, u32[]{:S(2)}, u32[]{:S(2)}) collective-permute-start(bf16[192,768]{1,0:T(8,128)(2,1)} %copy-done.24), channel_id=1, source_target_pairs={{0,1},{1,0},{2,3},{3,2},{4,5},{5,4},{6,7},{7,6},{8,9},{9,8},{10,11... | collective-permute-start | bytes 884744 | tf_op jit(solution)/shard_map/ppermute | solution.py:88
  40.4 25.8 %copy-start.11 = (s32[5]{0:T(128)S(1)}, s32[5]{0:T(128)}, u32[]{:S(2)}) copy-start(s32[5]{0:T(128)} %stack.23.refs_0_) | copy-start | bytes 64
  40.4 10.7 %collective-permute-start.12 = (f32[4,1664]{1,0:T(4,128)S(1)}, f32[4,1664]{1,0:T(4,128)S(1)}, u32[]{:S(2)}, u32[]{:S(2)}) collective-permute-start(f32[4,1664]{1,0:T(4,128)S(1)} %add_select_fusion), channel_id=1, source_target_pairs={{0,4},{4,0},{8,12},{12,8},{16,20},{20,16},{24,28},{28,24},{1,5},{5... | collective-permute-start | bytes 79880 | tf_op jit(solution)/shard_map/ppermute | solution.py:88
  48.9 4.0 %collective-permute-start.15 = (f32[4,768]{1,0:T(4,128)}, f32[4,768]{1,0:T(4,128)S(1)}, u32[]{:S(2)}, u32[]{:S(2)}) collective-permute-start(f32[4,768]{1,0:T(4,128)} %get-tuple-element.98), channel_id=1, source_target_pairs={{0,8},{4,12},{8,0},{12,4},{16,24},{20,28},{24,16},{28,20},{1,9},{5... | collective-permute-start | bytes 36872 | tf_op jit(solution)/shard_map/ppermute | solution.py:88
  49.9 4.8 %collective-permute-start.16 = (f32[4,768]{1,0:T(4,128)}, f32[4,768]{1,0:T(4,128)S(1)}, u32[]{:S(2)}, u32[]{:S(2)}) collective-permute-start(f32[4,768]{1,0:T(4,128)} %get-tuple-element.98), channel_id=1, source_target_pairs={{0,12},{4,8},{8,4},{12,0},{16,28},{20,24},{24,20},{28,16},{1,13},{... | collective-permute-start | bytes 36872 | tf_op jit(solution)/shard_map/ppermute | solution.py:88
  51.1 3.9 %collective-permute-start.14 = (f32[4,768]{1,0:T(4,128)}, f32[4,768]{1,0:T(4,128)S(1)}, u32[]{:S(2)}, u32[]{:S(2)}) collective-permute-start(f32[4,768]{1,0:T(4,128)} %get-tuple-element.98), channel_id=1, source_target_pairs={{0,4},{4,0},{8,12},{12,8},{16,20},{20,16},{24,28},{28,24},{1,5},{5... | collective-permute-start | bytes 36872 | tf_op jit(solution)/shard_map/ppermute | solution.py:88
  52.8 4.1 %collective-permute-start.17 = (f32[8,1664]{1,0:T(8,128)S(1)}, f32[8,1664]{1,0:T(8,128)S(1)}, u32[]{:S(2)}, u32[]{:S(2)}) collective-permute-start(f32[8,1664]{1,0:T(8,128)S(1)} %maximum_select_fusion.6), channel_id=1, source_target_pairs={{0,8},{4,12},{8,0},{12,4},{16,24},{20,28},{24,16},{28,20},{1,9},{5... | collective-permute-start | bytes 159752 | tf_op jit(solution)/shard_map/ppermute | solution.py:88
  53.8 3.1 %collective-permute-start.20 = (bf16[256,768]{1,0:T(8,128)(2,1)}, bf16[256,768]{1,0:T(8,128)(2,1)S(1)}, u32[]{:S(2)}, u32[]{:S(2)}) collective-permute-start(bf16[256,768]{1,0:T(8,128)(2,1)} %collective-permute-done.19.refs_4_), channel_id=1, source_target_pairs={{0,1},{1,0},{2,3},{3,2},{4,5},{5,4},{6,7},{7,6},{8,9},{9,8},{10,11... | collective-permute-start | bytes 1179656 | tf_op jit(solution)/shard_map/ppermute | solution.py:88
  57.0 12.6 %collective-permute-start.21 = (f32[16,1664]{1,0:T(8,128)S(1)}, f32[16,1664]{1,0:T(8,128)S(1)}, u32[]{:S(2)}, u32[]{:S(2)}) collective-permute-start(f32[16,1664]{1,0:T(8,128)S(1)} %maximum_select_fusion.4), channel_id=1, source_target_pairs={{0,16},{4,20},{8,24},{12,28},{16,0},{20,4},{24,8},{28,12},{1,17},{... | collective-permute-start | bytes 319496 | tf_op jit(solution)/shard_map/ppermute | solution.py:88
  59.8 4.8 %collective-permute-start.22 = (f32[4,1152]{1,0:T(4,128)S(1)}, f32[4,1152]{1,0:T(4,128)S(1)}, u32[]{:S(2)}, u32[]{:S(2)}) collective-permute-start(f32[4,1152]{1,0:T(4,128)S(1)} %pad_maximum_fusion.5), channel_id=1, source_target_pairs={{0,16},{4,20},{8,24},{12,28},{16,0},{20,4},{24,8},{28,12},{1,17},{... | collective-permute-start | bytes 55304 | tf_op jit(solution)/shard_map/ppermute | solution.py:88
  64.6 4.9 %collective-permute-start.23 = (f32[1,8,1152]{2,1,0:T(8,128)S(1)}, f32[1,8,1152]{2,1,0:T(8,128)S(1)}, u32[]{:S(2)}, u32[]{:S(2)}) collective-permute-start(f32[1,8,1152]{2,1,0:T(8,128)S(1)} %maximum_bitcast_fusion), channel_id=1, source_target_pairs={{0,2},{1,3},{2,0},{3,1},{4,6},{5,7},{6,4},{7,5},{8,10},{9,11},{10,... | collective-permute-start | bytes 110600 | tf_op jit(solution)/shard_map/ppermute | solution.py:88
  66.2 4.7 %copy-start.5 = (bf16[384,768]{1,0:T(8,128)(2,1)S(1)}, bf16[384,768]{1,0:T(8,128)(2,1)}, u32[]{:S(2)}) copy-start(bf16[384,768]{1,0:T(8,128)(2,1)} %get-tuple-element.113.refs_5_) | copy-start | bytes 1769476
  69.5 1.3 %collective-permute-start.24 = (f32[2,8,1152]{2,1,0:T(8,128)S(1)}, f32[2,8,1152]{2,1,0:T(8,128)S(1)}, u32[]{:S(2)}, u32[]{:S(2)}) collective-permute-start(f32[2,8,1152]{2,1,0:T(8,128)S(1)} %maximum_select_fusion.5), channel_id=1, source_target_pairs={{0,1},{1,0},{2,3},{3,2},{4,5},{5,4},{6,7},{7,6},{8,9},{9,8},{10,11... | collective-permute-start | bytes 221192 | tf_op jit(solution)/shard_map/ppermute | solution.py:88
  69.7 4.1 %copy-start.4 = (f32[1024,384]{1,0:T(8,128)S(1)}, f32[1024,384]{1,0:T(8,128)}, u32[]{:S(2)}) copy-start(f32[1024,384]{1,0:T(8,128)} %copy-done.3) | copy-start | bytes 4718596
  70.9 2.9 %copy-start.2 = (bf16[1024,768]{1,0:T(8,128)(2,1)S(1)}, bf16[1024,768]{1,0:T(8,128)(2,1)}, u32[]{:S(2)}) copy-start(bf16[1024,768]{1,0:T(8,128)(2,1)} %copy-done.1) | copy-start | bytes 4718596
  70.9 2.9 %copy-start.12 = (f32[768]{0:T(1024)S(1)}, f32[768]{0:T(1024)}, u32[]{:S(2)}) copy-start(f32[768]{0:T(1024)} %refs_7_.3) | copy-start | bytes 9220
  73.8 7.1 %copy-start.6 = (bf16[768,384]{1,0:T(8,128)(2,1)S(1)}, bf16[768,384]{1,0:T(8,128)(2,1)}, u32[]{:S(2)}) copy-start(bf16[768,384]{1,0:T(8,128)(2,1)} %refs_4_.5) | copy-start | bytes 1769476
  73.8 7.1 %copy-start.13 = (f32[768]{0:T(1024)S(1)}, f32[768]{0:T(1024)}, u32[]{:S(2)}) copy-start(f32[768]{0:T(1024)} %refs_6_.3) | copy-start | bytes 9220
  73.8 7.1 %copy-start.14 = (s32[8]{0:T(128)S(1)}, s32[8]{0:T(128)}, u32[]{:S(2)}) copy-start(s32[8]{0:T(128)} %convert_reduce_fusion.refs_1_) | copy-start | bytes 100
  73.9 7.1 %copy-start.17 = (bf16[1024,768]{1,0:T(8,128)(2,1)S(1)}, bf16[1024,768]{1,0:T(8,128)(2,1)}, u32[]{:S(2)}) copy-start(bf16[1024,768]{1,0:T(8,128)(2,1)} %get-tuple-element.123.refs_2_) | copy-start | bytes 4718596
  73.9 7.1 %copy-start.18 = (bf16[768,384]{1,0:T(8,128)(2,1)S(1)}, bf16[768,384]{1,0:T(8,128)(2,1)}, u32[]{:S(2)}) copy-start(bf16[768,384]{1,0:T(8,128)(2,1)} %get-tuple-element.127.refs_5_) | copy-start | bytes 1769476
  76.5 16.2 %collective-permute-start.25 = (bf16[192,384]{1,0:T(8,128)(2,1)S(1)}, bf16[192,384]{1,0:T(8,128)(2,1)S(1)}, u32[]{:S(2)}, u32[]{:S(2)}) collective-permute-start(bf16[192,384]{1,0:T(8,128)(2,1)S(1)} %get-tuple-element.120), channel_id=1, source_target_pairs={{0,8},{4,12},{8,0},{12,4},{16,24},{20,28},{24,16},{28,20},{1,9},{5... | collective-permute-start | bytes 442376 | tf_op jit(solution)/shard_map/ppermute | solution.py:88
  76.8 15.9 %collective-permute-start.26 = (bf16[192,384]{1,0:T(8,128)(2,1)S(1)}, bf16[192,384]{1,0:T(8,128)(2,1)S(1)}, u32[]{:S(2)}, u32[]{:S(2)}) collective-permute-start(bf16[192,384]{1,0:T(8,128)(2,1)S(1)} %get-tuple-element.121), channel_id=1, source_target_pairs={{0,16},{4,20},{8,24},{12,28},{16,0},{20,4},{24,8},{28,12},{1,17},{... | collective-permute-start | bytes 442376 | tf_op jit(solution)/shard_map/ppermute | solution.py:88
  79.6 13.1 %collective-permute-start.27 = (bf16[192,384]{1,0:T(8,128)(2,1)S(1)}, bf16[192,384]{1,0:T(8,128)(2,1)S(1)}, u32[]{:S(2)}, u32[]{:S(2)}) collective-permute-start(bf16[192,384]{1,0:T(8,128)(2,1)S(1)} %get-tuple-element.122), channel_id=1, source_target_pairs={{0,24},{4,28},{8,16},{12,20},{16,8},{20,12},{24,0},{28,4},{1,25},{... | collective-permute-start | bytes 442376 | tf_op jit(solution)/shard_map/ppermute | solution.py:88
  85.8 3.9 %collective-permute-start.28 = (bf16[64,768]{1,0:T(8,128)(2,1)S(1)}, bf16[64,768]{1,0:T(8,128)(2,1)S(1)}, u32[]{:S(2)}, u32[]{:S(2)}) collective-permute-start(bf16[64,768]{1,0:T(8,128)(2,1)S(1)} %get-tuple-element.166), channel_id=1, source_target_pairs={{0,1},{1,0},{2,3},{3,2},{4,5},{5,4},{6,7},{7,6},{8,9},{9,8},{10,11... | collective-permute-start | bytes 294920 | tf_op jit(solution)/shard_map/ppermute | solution.py:88
  85.9 3.9 %collective-permute-start.29 = (bf16[64,768]{1,0:T(8,128)(2,1)S(1)}, bf16[64,768]{1,0:T(8,128)(2,1)S(1)}, u32[]{:S(2)}, u32[]{:S(2)}) collective-permute-start(bf16[64,768]{1,0:T(8,128)(2,1)S(1)} %get-tuple-element.165), channel_id=1, source_target_pairs={{0,1},{1,0},{2,3},{3,2},{4,5},{5,4},{6,7},{7,6},{8,9},{9,8},{10,11... | collective-permute-start | bytes 294920 | tf_op jit(solution)/shard_map/ppermute | solution.py:88
  89.7 1.3 collective-permute-start.30
  89.8 1.4 %collective-permute-start.31 = (bf16[64,768]{1,0:T(8,128)(2,1)S(1)}, bf16[64,768]{1,0:T(8,128)(2,1)S(1)}, u32[]{:S(2)}, u32[]{:S(2)}) collective-permute-start(bf16[64,768]{1,0:T(8,128)(2,1)S(1)} %get-tuple-element.163), channel_id=1, source_target_pairs={{0,1},{1,0},{2,3},{3,2},{4,5},{5,4},{6,7},{7,6},{8,9},{9,8},{10,11... | collective-permute-start | bytes 294920 | tf_op jit(solution)/shard_map/ppermute | solution.py:88
  91.0 1.3 collective-permute-start.32
  91.2 1.3 collective-permute-start.33
  92.8 10.3 %collective-permute-start.39 = (bf16[192,768]{1,0:T(8,128)(2,1)S(1)}, bf16[192,768]{1,0:T(8,128)(2,1)S(1)}, u32[]{:S(2)}, u32[]{:S(2)}) collective-permute-start(bf16[192,768]{1,0:T(8,128)(2,1)S(1)} %dynamic-slice_convert_fusion), channel_id=1, source_target_pairs={{0,2},{1,3},{2,0},{3,1},{4,6},{5,7},{6,4},{7,5},{8,10},{9,11},{10,... | collective-permute-start | bytes 884744 | tf_op jit(solution)/shard_map/ppermute | solution.py:88
  93.7 8.5 %collective-permute-start.34 = (bf16[208,384]{1,0:T(8,128)(2,1)S(1)}, bf16[208,384]{1,0:T(8,128)(2,1)S(1)}, u32[]{:S(2)}, u32[]{:S(2)}) collective-permute-start(bf16[208,384]{1,0:T(8,128)(2,1)S(1)} %pad_maximum_fusion.3), channel_id=1, source_target_pairs={{0,8},{4,12},{8,0},{12,4},{16,24},{20,28},{24,16},{28,20},{1,9},{5... | collective-permute-start | bytes 479240 | tf_op jit(solution)/shard_map/ppermute | solution.py:88
  94.8 14.6 %collective-permute-start.35 = (bf16[208,384]{1,0:T(8,128)(2,1)S(1)}, bf16[208,384]{1,0:T(8,128)(2,1)S(1)}, u32[]{:S(2)}, u32[]{:S(2)}) collective-permute-start(bf16[208,384]{1,0:T(8,128)(2,1)S(1)} %pad_maximum_fusion.3), channel_id=1, source_target_pairs={{0,16},{4,20},{8,24},{12,28},{16,0},{20,4},{24,8},{28,12},{1,17},{... | collective-permute-start | bytes 479240 | tf_op jit(solution)/shard_map/ppermute | solution.py:88
  96.8 12.7 %collective-permute-start.36 = (bf16[208,384]{1,0:T(8,128)(2,1)S(1)}, bf16[208,384]{1,0:T(8,128)(2,1)S(1)}, u32[]{:S(2)}, u32[]{:S(2)}) collective-permute-start(bf16[208,384]{1,0:T(8,128)(2,1)S(1)} %pad_maximum_fusion.3), channel_id=1, source_target_pairs={{0,24},{4,28},{8,16},{12,20},{16,8},{20,12},{24,0},{28,4},{1,25},{... | collective-permute-start | bytes 479240 | tf_op jit(solution)/shard_map/ppermute | solution.py:88
  98.1 5.1 %collective-permute-start.37 = (bf16[192,384]{1,0:T(8,128)(2,1)S(1)}, bf16[192,384]{1,0:T(8,128)(2,1)S(1)}, u32[]{:S(2)}, u32[]{:S(2)}) collective-permute-start(bf16[192,384]{1,0:T(8,128)(2,1)S(1)} %add_convert_fusion.1.refs_1_), channel_id=1, source_target_pairs={{0,4},{4,0},{8,12},{12,8},{16,20},{20,16},{24,28},{28,24},{1,5},{5... | collective-permute-start | bytes 442376 | tf_op jit(solution)/shard_map/ppermute | solution.py:88
  102.2 7.2 %collective-permute-start.38 = (bf16[192,384]{1,0:T(8,128)(2,1)S(1)}, bf16[192,384]{1,0:T(8,128)(2,1)S(1)}, u32[]{:S(2)}, u32[]{:S(2)}) collective-permute-start(bf16[192,384]{1,0:T(8,128)(2,1)S(1)} %slice.207), channel_id=1, source_target_pairs={{0,4},{4,0},{8,12},{12,8},{16,20},{20,16},{24,28},{28,24},{1,5},{5... | collective-permute-start | bytes 442376 | tf_op jit(solution)/shard_map/ppermute | solution.py:88
  109.5 9.2 %collective-permute-start.40 = (bf16[192,384]{1,0:T(8,128)(2,1)S(1)}, bf16[192,384]{1,0:T(8,128)(2,1)S(1)}, u32[]{:S(2)}, u32[]{:S(2)}) collective-permute-start(bf16[192,384]{1,0:T(8,128)(2,1)S(1)} %slice.293), channel_id=1, source_target_pairs={{0,16},{4,20},{8,24},{12,28},{16,0},{20,4},{24,8},{28,12},{1,17},{... | collective-permute-start | bytes 442376 | tf_op jit(solution)/shard_map/ppermute | solution.py:88
  113.3 4.6 %collective-permute-start.41 = (f32[2,768]{1,0:T(2,128)S(1)}, f32[2,768]{1,0:T(2,128)S(1)}, u32[]{:S(2)}, u32[]{:S(2)}) collective-permute-start(f32[2,768]{1,0:T(2,128)S(1)} %fusion.31), channel_id=1, source_target_pairs={{0,4},{4,0},{8,12},{12,8},{16,20},{20,16},{24,28},{28,24},{1,5},{5... | collective-permute-start | bytes 18440 | tf_op jit(solution)/shard_map/ppermute | solution.py:88
  114.4 6.9 %collective-permute-start.42 = (bf16[384,384]{1,0:T(8,128)(2,1)S(1)}, bf16[384,384]{1,0:T(8,128)(2,1)S(1)}, u32[]{:S(2)}, u32[]{:S(2)}) collective-permute-start(bf16[384,384]{1,0:T(8,128)(2,1)S(1)} %pad_maximum_fusion.1), channel_id=1, source_target_pairs={{0,4},{4,0},{8,12},{12,8},{16,20},{20,16},{24,28},{28,24},{1,5},{5... | collective-permute-start | bytes 884744 | tf_op jit(solution)/shard_map/ppermute | solution.py:88
  121.3 5.3 %collective-permute-start.43 = (bf16[208,384]{1,0:T(8,128)(2,1)S(1)}, bf16[208,384]{1,0:T(8,128)(2,1)S(1)}, u32[]{:S(2)}, u32[]{:S(2)}) collective-permute-start(bf16[208,384]{1,0:T(8,128)(2,1)S(1)} %pad_maximum_fusion.2), channel_id=1, source_target_pairs={{0,2},{1,3},{2,0},{3,1},{4,6},{5,7},{6,4},{7,5},{8,10},{9,11},{10,... | collective-permute-start | bytes 479240 | tf_op jit(solution)/shard_map/ppermute | solution.py:88
  126.9 1.7 %collective-permute-start.44 = (bf16[400,384]{1,0:T(8,128)(2,1)S(1)}, bf16[400,384]{1,0:T(8,128)(2,1)S(1)}, u32[]{:S(2)}, u32[]{:S(2)}) collective-permute-start(bf16[400,384]{1,0:T(8,128)(2,1)S(1)} %pad_maximum_fusion), channel_id=1, source_target_pairs={{0,1},{1,0},{2,3},{3,2},{4,5},{5,4},{6,7},{7,6},{8,9},{9,8},{10,11... | collective-permute-start | bytes 921608 | tf_op jit(solution)/shard_map/ppermute | solution.py:88
  (6 other events, 8.2 us)

commit v7 on v6

--- a/solution.py
+++ b/solution.py
@@ -842,9 +842,10 @@
     sums = [gains] + [arrived_gains(x, rows)[1] for x in arrivals]
     while len(sums) > 1:
         sums = [sums[i] + sums[i + 1] for i in range(0, len(sums), 2)]
-    gains = sums[0] + swap(sums[0], "pb", 1)
     chunks = [q_total] + list(arrivals)
-    rest = swap(jnp.concatenate([x[:rows] for x in chunks[2:]], 0), "pb", 1)
+    sent, gains = with_gains(jnp.concatenate([x[:rows] for x in chunks[2:]], 0), sums[0])
+    rest = swap(sent, "pb", 1)
+    gains = gains + arrived_gains(rest, rows * (pairs - 2))[1]
     shape = (width, 2 * half)
     q_inner_grad = assemble(place, chunks[:2], [own_other, first], 0, rows, shape)
     s_sum = s_total[:, :block]

time: 131 us -> 130 us (level)
    ppermute x45 -> x44, starting transfers between devices: 44.5 us -> 43.3 us  [swap(): return lax.ppermute(x, axis, [(i, i ^ step) for i in range(size)])]
    ppermute x45 -> x44, waiting for transfers between devices: 37.8 us -> 38.4 us  [swap(): return lax.ppermute(x, axis, [(i, i ^ step) for i in range(size)])]
  transfers between devices with their start and end apart: 45 -> 44, of which waited for: 23 -> 23; matrix products, arithmetic and copies ran while one was open for 6% -> 6% of each run, Pallas kernels for 19% -> 19%
where the time goes in v7:
time: 130 us
  starting transfers between devices  43.3 us (33%)
  waiting for transfers between devices  38.4 us (30%)
  Pallas kernels  33.9 us (26%)
  local copies, waits for them, and re-layouts  5.21 us (4%)
  other arithmetic  4.32 us (3%)
  matrix products  3.26 us (3%)
  between operations  1.53 us (1%)
    ppermute x44, starting transfers between devices, swap(): return lax.ppermute(x, axis, [(i, i ^ step) for i in range(size)])  43.3 us
    ppermute x44, waiting for transfers between devices, swap(): return lax.ppermute(x, axis, [(i, i ^ step) for i in range(size)])  38.4 us
    pallas_call x10, Pallas kernels, run(): pl.pallas_call(kernel, in_specs=[HBM if spec in (LOAD, LATE) else spec fo...  33.9 us
    dot_general x2, matrix products, outer_gradient(): lax.dot_general(left, right, CONTRACT_FIRST, preferred_element_type=F32)  3.26 us
  transfers between devices with their start and end apart: 44, of which 23 were waited for; matrix products, arithmetic and copies ran while one was open for 6% of the time, Pallas kernels for 19%

profile of v7, /device:TPU:0, one launch (start us, length us, event | category | flops | bytes accessed | tf_op | source)
XLA Modules:
  0.0 129.9 jit_solution(7312632479553226042)
XLA Ops:
  0.7 0.6 stack.23.refs_0_
  1.3 3.2 %shard_map.162 = (bf16[256,768]{1,0:T(8,128)(2,1)}, bf16[256,768]{1,0:T(8,128)(2,1)}, bf16[192,768]{1,0:T(8,128)(2,1)}) custom-call(s32[5]{0:T(128)} %stack.23.refs_0_, bf16[256,768]{1,0:T(8,128)(2,1)} %bitcast.18, bf16[256,768]{1,0:T(8,128)(2,1)} %bitcast.20, f32[768]{0:T(1024)} %refs_7_.3, f32[768]{0:T(1024)} %refs_6_.3, bf16[768,384]{1,0:T(8,128)(2,1)} %refs_4_.5, ...), custom_call_target="tpu_custom_call" | custom-call | tf_op jit(solution)/shard_map/pallas_call | solution.py:60
  4.5 4.1 %collective-permute-start.2 = (bf16[192,768]{1,0:T(8,128)(2,1)}, bf16[192,768]{1,0:T(8,128)(2,1)}, u32[]{:S(2)}, u32[]{:S(2)}) collective-permute-start(bf16[192,768]{1,0:T(8,128)(2,1)} %get-tuple-element.81), channel_id=1, source_target_pairs={{0,16},{4,20},{8,24},{12,28},{16,0},{20,4},{24,8},{28,12},{1,17},{... | collective-permute-start | bytes 884744 | tf_op jit(solution)/shard_map/ppermute | solution.py:88
  8.6 1.5 %collective-permute-start = (bf16[256,768]{1,0:T(8,128)(2,1)}, bf16[256,768]{1,0:T(8,128)(2,1)}, u32[]{:S(2)}, u32[]{:S(2)}) collective-permute-start(bf16[256,768]{1,0:T(8,128)(2,1)} %get-tuple-element.80.refs_3_), channel_id=1, source_target_pairs={{0,4},{4,0},{8,12},{12,8},{16,20},{20,16},{24,28},{28,24},{1,5},{5... | collective-permute-start | bytes 1179656 | tf_op jit(solution)/shard_map/ppermute | solution.py:88
  10.1 1.6 %collective-permute-start.1 = (bf16[256,768]{1,0:T(8,128)(2,1)}, bf16[256,768]{1,0:T(8,128)(2,1)S(1)}, u32[]{:S(2)}, u32[]{:S(2)}) collective-permute-start(bf16[256,768]{1,0:T(8,128)(2,1)} %get-tuple-element.80.refs_3_), channel_id=1, source_target_pairs={{0,8},{4,12},{8,0},{12,4},{16,24},{20,28},{24,16},{28,20},{1,9},{5... | collective-permute-start | bytes 1179656 | tf_op jit(solution)/shard_map/ppermute | solution.py:88
  11.6 1.5 %collective-permute-start.4 = (bf16[256,768]{1,0:T(8,128)(2,1)}, bf16[256,768]{1,0:T(8,128)(2,1)S(1)}, u32[]{:S(2)}, u32[]{:S(2)}) collective-permute-start(bf16[256,768]{1,0:T(8,128)(2,1)} %get-tuple-element.90.refs_4_), channel_id=1, source_target_pairs={{0,2},{1,3},{2,0},{3,1},{4,6},{5,7},{6,4},{7,5},{8,10},{9,11},{10,... | collective-permute-start | bytes 1179656 | tf_op jit(solution)/shard_map/ppermute | solution.py:88
  13.2 0.6 convert_reduce_fusion.refs_1_
  13.8 8.5 %collective-permute-done.2.refs_9_ = bf16[192,768]{1,0:T(8,128)(2,1)} collective-permute-done((bf16[192,768]{1,0:T(8,128)(2,1)}, bf16[192,768]{1,0:T(8,128)(2,1)}, u32[]{:S(2)}, u32[]{:S(2)}) %collective-permute-start.2) | collective-permute-done | bytes 294944 | tf_op jit(solution)/shard_map/ppermute | solution.py:88
  22.6 1.2 constant_dynamic-slice_fusion.refs_3_
  23.8 1.9 %collective-permute-done.1.refs_5_ = bf16[256,768]{1,0:T(8,128)(2,1)S(1)} collective-permute-done((bf16[256,768]{1,0:T(8,128)(2,1)}, bf16[256,768]{1,0:T(8,128)(2,1)S(1)}, u32[]{:S(2)}, u32[]{:S(2)}) %collective-permute-start.1) | collective-permute-done | bytes 393248 | tf_op jit(solution)/shard_map/ppermute | solution.py:88
  26.5 1.6 %collective-permute-start.6 = (bf16[192,768]{1,0:T(8,128)(2,1)}, bf16[192,768]{1,0:T(8,128)(2,1)S(1)}, u32[]{:S(2)}, u32[]{:S(2)}) collective-permute-start(bf16[192,768]{1,0:T(8,128)(2,1)} %collective-permute-done.2.refs_9_), channel_id=1, source_target_pairs={{0,2},{1,3},{2,0},{3,1},{4,6},{5,7},{6,4},{7,5},{8,10},{9,11},{10,... | collective-permute-start | bytes 884744 | tf_op jit(solution)/shard_map/ppermute | solution.py:88
  28.0 1.2 collective-permute-start.10
  29.2 4.3 %shard_map.163 = (f32[4,1664]{1,0:T(4,128)S(1)}, bf16[1024,768]{1,0:T(8,128)(2,1)S(1)}) custom-call(s32[5]{0:T(128)S(1)} %copy-done.10, s32[4]{0:T(128)S(1)} %convert_reduce_fusion.1.refs_1_, s32[4]{0:T(128)S(1)} %copy-done.16, bf16[256,768]{1,0:T(8,128)(2,1)S(1)} %bitcast.19, bf16[256,768]{1,0:T(8,128)(2,1)S(1)} %copy-done.15, ...), custom_call_target="tpu_custom_call" | custom-call | flops 3000000000 | bytes 3000000 | tf_op jit(solution)/shard_map/pallas_call | solution.py:60
  33.5 0.6 collective-permute-start.9
  34.1 1.8 %shard_map.164.refs_3_ = f32[1024,384]{1,0:T(8,128)S(1)} custom-call(s32[5]{0:T(128)S(1)} %copy-done.10, s32[4]{0:T(128)S(1)} %convert_reduce_fusion.1.refs_1_, bf16[1024,768]{1,0:T(8,128)(2,1)S(1)} %get-tuple-element.88.refs_2_.refs_1_, bf16[768,384]{1,0:T(8,128)(2,1)S(1)} %constant_dynamic-slice_fusion.1.refs_3_.refs_6_), custom_call_target="tpu_custom_call" | custom-call | flops 905969664 | bytes 3000000 | tf_op jit(solution)/shard_map/pallas_call | solution.py:60
  36.0 1.2 copy-done.3
  37.6 1.1 collective-permute-done.10.refs_2_
  39.2 1.2 collective-permute-start.19
  40.5 0.9 collective-permute-start.12
  41.4 1.0 collective-permute-done.13.refs_12_
  42.4 6.5 %shard_map.165 = (f32[4,768]{1,0:T(4,128)}, f32[4,384]{1,0:T(4,128)}, f32[4,384]{1,0:T(4,128)}, bf16[1024,768]{1,0:T(8,128)(2,1)}, bf16[768,384]{1,0:T(8,128)(2,1)}, /*index=5*/bf16[384,768]{1,0:T(8,128)(2,1)}) custom-call(s32[5]{0:T(128)} %stack.23.refs_0_, s32[8]{0:T(128)} %convert_reduce_fusion.refs_1_, bf16[256,768]{1,0:T(8,128)(2,1)} %bitcast.21, ...), custom_call_target="tpu_custom_call" | custom-call | flops 3000000000 | bytes 3000000 | tf_op jit(solution)/shard_map/pallas_call | solution.py:60
  48.9 1.0 collective-permute-start.15
  49.9 1.2 collective-permute-start.16
  51.1 1.3 %collective-permute-start.14 = (f32[4,768]{1,0:T(4,128)}, f32[4,768]{1,0:T(4,128)S(1)}, u32[]{:S(2)}, u32[]{:S(2)}) collective-permute-start(f32[4,768]{1,0:T(4,128)} %get-tuple-element.98), channel_id=1, source_target_pairs={{0,4},{4,0},{8,12},{12,8},{16,20},{20,16},{24,28},{28,24},{1,5},{5... | collective-permute-start | bytes 36872 | tf_op jit(solution)/shard_map/ppermute | solution.py:88
  52.9 1.0 collective-permute-start.17
  53.9 0.9 collective-permute-done.16
  55.0 0.7 add_add_fusion
  55.7 1.3 collective-permute-done.17
  57.0 2.1 %collective-permute-start.21 = (f32[16,1664]{1,0:T(8,128)S(1)}, f32[16,1664]{1,0:T(8,128)S(1)}, u32[]{:S(2)}, u32[]{:S(2)}) collective-permute-start(f32[16,1664]{1,0:T(8,128)S(1)} %maximum_select_fusion.4), channel_id=1, source_target_pairs={{0,16},{4,20},{8,24},{12,28},{16,0},{20,4},{24,8},{28,12},{1,17},{... | collective-permute-start | bytes 319496 | tf_op jit(solution)/shard_map/ppermute | solution.py:88
  59.1 0.7 pad_maximum_fusion.5
  59.8 0.9 collective-permute-start.22
  60.7 0.7 constant_dynamic-update-slice_fusion
  61.4 3.2 %collective-permute-done.22 = f32[4,1152]{1,0:T(4,128)S(1)} collective-permute-done((f32[4,1152]{1,0:T(4,128)S(1)}, f32[4,1152]{1,0:T(4,128)S(1)}, u32[]{:S(2)}, u32[]{:S(2)}) %collective-permute-start.22) | collective-permute-done | bytes 18464 | tf_op jit(solution)/shard_map/ppermute | solution.py:88
  64.6 1.6 %collective-permute-start.23 = (f32[1,8,1152]{2,1,0:T(8,128)S(1)}, f32[1,8,1152]{2,1,0:T(8,128)S(1)}, u32[]{:S(2)}, u32[]{:S(2)}) collective-permute-start(f32[1,8,1152]{2,1,0:T(8,128)S(1)} %maximum_bitcast_fusion), channel_id=1, source_target_pairs={{0,2},{1,3},{2,0},{3,1},{4,6},{5,7},{6,4},{7,5},{8,10},{9,11},{10,... | collective-permute-start | bytes 110600 | tf_op jit(solution)/shard_map/ppermute | solution.py:88
  66.2 3.3 %shard_map.166 = (f32[1024,384]{1,0:T(8,128)S(1)}, bf16[1024,768]{1,0:T(8,128)(2,1)S(1)}) custom-call(s32[5]{0:T(128)S(1)} %copy-done.11, s32[4]{0:T(128)S(1)} %convert_reduce_fusion.2.refs_1_, bf16[256,768]{1,0:T(8,128)(2,1)S(1)} %collective-permute-done.10.refs_2_, bf16[256,768]{1,0:T(8,128)(2,1)S(1)} %collective-permute-done.18.refs_3_, ...), custom_call_target="tpu_custom_call" | custom-call | flops 905969664 | bytes 3000000 | tf_op jit(solution)/shard_map/pallas_call | solution.py:60
  69.7 1.2 collective-permute-done.24
  71.0 2.8 %shard_map.167 = (f32[1,1]{1,0:T(1,128)}, f32[32,768]{1,0:T(8,128)S(1)}, f32[32,768]{1,0:T(8,128)S(1)}, f32[8,384]{1,0:T(8,128)S(1)}, f32[8,768]{1,0:T(8,128)S(1)}) custom-call(s32[5]{0:T(128)S(1)} %copy-done.11, f32[32,1664]{1,0:T(8,128)S(1)} %maximum_select_fusion.2.refs_1_, f32[32,1152]{1,0:T(8,128)S(1)} %pad_maximum_fusion.4.refs_2_, ...), custom_call_target="tpu_custom_call" | custom-call | tf_op jit(solution)/shard_map/pallas_call | solution.py:60
  73.9 2.6 %shard_map.168 = (bf16[192,384]{1,0:T(8,128)(2,1)S(1)}, bf16[192,384]{1,0:T(8,128)(2,1)S(1)}, bf16[192,384]{1,0:T(8,128)(2,1)S(1)}, f32[192,384]{1,0:T(8,128)S(1)}, f32[1,768]{1,0:T(1,128)S(1)}) custom-call(s32[5]{0:T(128)S(1)} %copy-done.11, bf16[1024,768]{1,0:T(8,128)(2,1)S(1)} %copy-done.2, bf16[1024,768]{1,0:T(8,128)(2,1)S(1)} %get-tuple-element.115.refs_2_, ...), custom_call_target="tpu_custom_call" | custom-call | flops 4000000000 | bytes 3000000 | tf_op jit(solution)/shard_map/pallas_call | solution.py:60
  76.8 2.8 %collective-permute-start.26 = (bf16[192,384]{1,0:T(8,128)(2,1)S(1)}, bf16[192,384]{1,0:T(8,128)(2,1)S(1)}, u32[]{:S(2)}, u32[]{:S(2)}) collective-permute-start(bf16[192,384]{1,0:T(8,128)(2,1)S(1)} %get-tuple-element.121), channel_id=1, source_target_pairs={{0,16},{4,20},{8,24},{12,28},{16,0},{20,4},{24,8},{28,12},{1,17},{... | collective-permute-start | bytes 442376 | tf_op jit(solution)/shard_map/ppermute | solution.py:88
  79.6 1.3 %collective-permute-start.27 = (bf16[192,384]{1,0:T(8,128)(2,1)S(1)}, bf16[192,384]{1,0:T(8,128)(2,1)S(1)}, u32[]{:S(2)}, u32[]{:S(2)}) collective-permute-start(bf16[192,384]{1,0:T(8,128)(2,1)S(1)} %get-tuple-element.122), channel_id=1, source_target_pairs={{0,24},{4,28},{8,16},{12,20},{16,8},{20,12},{24,0},{28,4},{1,25},{... | collective-permute-start | bytes 442376 | tf_op jit(solution)/shard_map/ppermute | solution.py:88
  80.9 4.8 %shard_map.169 = (bf16[384,768]{1,0:T(8,128)(2,1)S(1)}, f32[384,768]{1,0:T(8,128)S(1)}, bf16[16,768]{1,0:T(8,128)(2,1)S(1)}) custom-call(s32[5]{0:T(128)S(1)} %copy-done.11, s32[8]{0:T(128)S(1)} %copy-done.14, bf16[1024,768]{1,0:T(8,128)(2,1)S(1)} %copy-done.17, f32[8,768]{1,0:T(8,128)S(1)} %get-tuple-element.126.refs_3_, bf16[768,384]{1,0:T(8,128)(2,1)S(1)} %copy-done.6, ...), custom_call_target="tpu_custom_call" | custom-call | flops 6000000000 | bytes 3000000 | tf_op jit(solution)/shard_map/pallas_call | solution.py:60
  86.4 1.9 %fusion.1 = f32[768,768]{1,0:T(8,128)} fusion(bf16[32,768]{1,0:T(8,128)(2,1)S(1)} %get-tuple-element.172, bf16[32,768]{1,0:T(8,128)(2,1)S(1)} %get-tuple-element.171, bf16[32,768]{1,0:T(8,128)(2,1)S(1)} %get-tuple-element.191, bf16[32,768]{1,0:T(8,128)(2,1)S(1)} %get-tuple-element.192), kind=kOutput, calls=%fused_computation.16 | convolution fusion | flops 114130944 | bytes 2555904 | tf_op jit(solution)/shard_map/dot_general | solution.py:802
  88.3 1.4 %fusion.12 = f32[384,768]{1,0:T(8,128)} fusion(bf16[32,768]{1,0:T(8,128)(2,1)S(1)} %get-tuple-element.180, bf16[32,768]{1,0:T(8,128)(2,1)S(1)} %get-tuple-element.179, bf16[32,384]{1,0:T(8,128)(2,1)S(1)} %get-tuple-element.174, bf16[32,384]{1,0:T(8,128)(2,1)S(1)} %get-tuple-element.173), kind=kOutput, calls=%fused_computation.27 | convolution fusion | flops 57286656 | bytes 1327104 | tf_op jit(solution)/shard_map/dot_general | solution.py:802
  90.3 0.7 collective-permute-done.30
  91.6 0.7 collective-permute-done.32
  92.8 0.7 collective-permute-start.39
  93.7 1.2 collective-permute-start.34
  94.9 1.9 %collective-permute-start.35 = (bf16[208,384]{1,0:T(8,128)(2,1)S(1)}, bf16[208,384]{1,0:T(8,128)(2,1)S(1)}, u32[]{:S(2)}, u32[]{:S(2)}) collective-permute-start(bf16[208,384]{1,0:T(8,128)(2,1)S(1)} %pad_maximum_fusion.3), channel_id=1, source_target_pairs={{0,16},{4,20},{8,24},{12,28},{16,0},{20,4},{24,8},{28,12},{1,17},{... | collective-permute-start | bytes 479240 | tf_op jit(solution)/shard_map/ppermute | solution.py:88
  96.8 1.3 %collective-permute-start.36 = (bf16[208,384]{1,0:T(8,128)(2,1)S(1)}, bf16[208,384]{1,0:T(8,128)(2,1)S(1)}, u32[]{:S(2)}, u32[]{:S(2)}) collective-permute-start(bf16[208,384]{1,0:T(8,128)(2,1)S(1)} %pad_maximum_fusion.3), channel_id=1, source_target_pairs={{0,24},{4,28},{8,16},{12,20},{16,8},{20,12},{24,0},{28,4},{1,25},{... | collective-permute-start | bytes 479240 | tf_op jit(solution)/shard_map/ppermute | solution.py:88
  98.1 0.8 collective-permute-start.37
  98.9 3.3 %collective-permute-done.34.refs_2_ = bf16[208,384]{1,0:T(8,128)(2,1)S(1)} collective-permute-done((bf16[208,384]{1,0:T(8,128)(2,1)S(1)}, bf16[208,384]{1,0:T(8,128)(2,1)S(1)}, u32[]{:S(2)}, u32[]{:S(2)}) %collective-permute-start.34) | collective-permute-done | bytes 159776 | tf_op jit(solution)/shard_map/ppermute | solution.py:88
  102.2 0.9 collective-permute-start.38
  103.3 6.2 %collective-permute-done.35.refs_2_ = bf16[208,384]{1,0:T(8,128)(2,1)S(1)} collective-permute-done((bf16[208,384]{1,0:T(8,128)(2,1)S(1)}, bf16[208,384]{1,0:T(8,128)(2,1)S(1)}, u32[]{:S(2)}, u32[]{:S(2)}) %collective-permute-start.35) | collective-permute-done | bytes 159776 | tf_op jit(solution)/shard_map/ppermute | solution.py:88
  109.6 3.7 %collective-permute-start.40 = (bf16[192,384]{1,0:T(8,128)(2,1)S(1)}, bf16[192,384]{1,0:T(8,128)(2,1)S(1)}, u32[]{:S(2)}, u32[]{:S(2)}) collective-permute-start(bf16[192,384]{1,0:T(8,128)(2,1)S(1)} %slice.329), channel_id=1, source_target_pairs={{0,16},{4,20},{8,24},{12,28},{16,0},{20,4},{24,8},{28,12},{1,17},{... | collective-permute-start | bytes 442376 | tf_op jit(solution)/shard_map/ppermute | solution.py:88
  113.5 1.0 collective-permute-start.41
  114.4 2.4 %shard_map.170.refs_1_ = f32[768,768]{1,0:T(8,128)} custom-call(s32[5]{0:T(128)S(1)} %copy-done.11, bf16[192,384]{1,0:T(8,128)(2,1)S(1)} %add_convert_fusion.1.refs_1_, bf16[208,384]{1,0:T(8,128)(2,1)S(1)} %collective-permute-done.34.refs_2_, bf16[192,384]{1,0:T(8,128)(2,1)S(1)} %collective-permute-done.37.refs_3_, ...), custom_call_target="tpu_custom_call" | custom-call | flops 2000000000 | bytes 3000000 | tf_op jit(solution)/shard_map/pallas_call | solution.py:60
  116.9 1.9 %collective-permute-done.40 = bf16[192,384]{1,0:T(8,128)(2,1)S(1)} collective-permute-done((bf16[192,384]{1,0:T(8,128)(2,1)S(1)}, bf16[192,384]{1,0:T(8,128)(2,1)S(1)}, u32[]{:S(2)}, u32[]{:S(2)}) %collective-permute-start.40) | collective-permute-done | bytes 147488 | tf_op jit(solution)/shard_map/ppermute | solution.py:88
  118.8 1.9 %collective-permute-done.41.refs_4_ = bf16[400,384]{1,0:T(8,128)(2,1)S(1)} collective-permute-done((bf16[400,384]{1,0:T(8,128)(2,1)S(1)}, bf16[400,384]{1,0:T(8,128)(2,1)S(1)}, u32[]{:S(2)}, u32[]{:S(2)}) %collective-permute-start.41) | collective-permute-done | bytes 307232 | tf_op jit(solution)/shard_map/ppermute | solution.py:88
  120.9 1.4 %collective-permute-start.42 = (bf16[208,384]{1,0:T(8,128)(2,1)S(1)}, bf16[208,384]{1,0:T(8,128)(2,1)S(1)}, u32[]{:S(2)}, u32[]{:S(2)}) collective-permute-start(bf16[208,384]{1,0:T(8,128)(2,1)S(1)} %pad_maximum_fusion.2), channel_id=1, source_target_pairs={{0,2},{1,3},{2,0},{3,1},{4,6},{5,7},{6,4},{7,5},{8,10},{9,11},{10,... | collective-permute-start | bytes 479240 | tf_op jit(solution)/shard_map/ppermute | solution.py:88
  122.3 2.2 %shard_map.171 = f32[768,768]{1,0:T(8,128)} custom-call(s32[5]{0:T(128)S(1)} %copy-done.11, f32[768,768]{1,0:T(8,128)} %shard_map.170.refs_1_, bf16[208,384]{1,0:T(8,128)(2,1)S(1)} %collective-permute-done.35.refs_2_, bf16[208,384]{1,0:T(8,128)(2,1)S(1)} %collective-permute-done.36.refs_3_, ...), custom_call_target="tpu_custom_call", output_to_operand_aliasing={{}: (1, {})} | custom-call | flops 2000000000 | bytes 3000000 | tf_op jit(solution)/shard_map/pallas_call | solution.py:60
  124.4 1.8 %collective-permute-done.42 = bf16[208,384]{1,0:T(8,128)(2,1)S(1)} collective-permute-done((bf16[208,384]{1,0:T(8,128)(2,1)S(1)}, bf16[208,384]{1,0:T(8,128)(2,1)S(1)}, u32[]{:S(2)}, u32[]{:S(2)}) %collective-permute-start.42) | collective-permute-done | bytes 159776 | tf_op jit(solution)/shard_map/ppermute | solution.py:88
  126.5 1.6 %collective-permute-done.43 = bf16[400,384]{1,0:T(8,128)(2,1)S(1)} collective-permute-done((bf16[400,384]{1,0:T(8,128)(2,1)S(1)}, bf16[400,384]{1,0:T(8,128)(2,1)S(1)}, u32[]{:S(2)}, u32[]{:S(2)}) %collective-permute-start.43) | collective-permute-done | bytes 307232 | tf_op jit(solution)/shard_map/ppermute | solution.py:88
  128.2 0.6 slice_reduce_fusion
  128.8 1.1 fusion
  (168 shorter events, 6.4 us)
Async XLA Ops:
  0.6 12.5 %copy-start.19 = (s32[1,8,256]{2,1,0:T(8,128)S(1)}, s32[1,8,256]{2,1,0:T(8,128)}, u32[]{:S(2)}) copy-start(s32[1,8,256]{2,1,0:T(8,128)} %param.17) | copy-start | bytes 24580
  0.6 21.7 %copy-start.20 = (s32[1,4,256]{2,1,0:T(4,128)S(1)}, s32[1,4,256]{2,1,0:T(4,128)}, u32[]{:S(2)}) copy-start(s32[1,4,256]{2,1,0:T(4,128)} %param.12) | copy-start | bytes 12292
  0.7 21.8 %copy-start.8 = (bf16[768,768]{1,0:T(8,128)(2,1)S(1)}, bf16[768,768]{1,0:T(8,128)(2,1)}, u32[]{:S(2)}) copy-start(bf16[768,768]{1,0:T(8,128)(2,1)} %refs_8_.2) | copy-start | bytes 3538948
  4.5 17.9 %collective-permute-start.2 = (bf16[192,768]{1,0:T(8,128)(2,1)}, bf16[192,768]{1,0:T(8,128)(2,1)}, u32[]{:S(2)}, u32[]{:S(2)}) collective-permute-start(bf16[192,768]{1,0:T(8,128)(2,1)} %get-tuple-element.81), channel_id=1, source_target_pairs={{0,16},{4,20},{8,24},{12,28},{16,0},{20,4},{24,8},{28,12},{1,17},{... | collective-permute-start | bytes 884744 | tf_op jit(solution)/shard_map/ppermute | solution.py:88
  8.6 15.3 %collective-permute-start = (bf16[256,768]{1,0:T(8,128)(2,1)}, bf16[256,768]{1,0:T(8,128)(2,1)}, u32[]{:S(2)}, u32[]{:S(2)}) collective-permute-start(bf16[256,768]{1,0:T(8,128)(2,1)} %get-tuple-element.80.refs_3_), channel_id=1, source_target_pairs={{0,4},{4,0},{8,12},{12,8},{16,20},{20,16},{24,28},{28,24},{1,5},{5... | collective-permute-start | bytes 1179656 | tf_op jit(solution)/shard_map/ppermute | solution.py:88
  10.1 15.7 %collective-permute-start.1 = (bf16[256,768]{1,0:T(8,128)(2,1)}, bf16[256,768]{1,0:T(8,128)(2,1)S(1)}, u32[]{:S(2)}, u32[]{:S(2)}) collective-permute-start(bf16[256,768]{1,0:T(8,128)(2,1)} %get-tuple-element.80.refs_3_), channel_id=1, source_target_pairs={{0,8},{4,12},{8,0},{12,4},{16,24},{20,28},{24,16},{28,20},{1,9},{5... | collective-permute-start | bytes 1179656 | tf_op jit(solution)/shard_map/ppermute | solution.py:88
  11.6 14.1 %collective-permute-start.4 = (bf16[256,768]{1,0:T(8,128)(2,1)}, bf16[256,768]{1,0:T(8,128)(2,1)S(1)}, u32[]{:S(2)}, u32[]{:S(2)}) collective-permute-start(bf16[256,768]{1,0:T(8,128)(2,1)} %get-tuple-element.90.refs_4_), channel_id=1, source_target_pairs={{0,2},{1,3},{2,0},{3,1},{4,6},{5,7},{6,4},{7,5},{8,10},{9,11},{10,... | collective-permute-start | bytes 1179656 | tf_op jit(solution)/shard_map/ppermute | solution.py:88
  13.2 16.0 %collective-permute-start.7 = (bf16[256,768]{1,0:T(8,128)(2,1)}, bf16[256,768]{1,0:T(8,128)(2,1)}, u32[]{:S(2)}, u32[]{:S(2)}) collective-permute-start(bf16[256,768]{1,0:T(8,128)(2,1)} %get-tuple-element.90.refs_4_), channel_id=1, source_target_pairs={{0,1},{1,0},{2,3},{3,2},{4,5},{5,4},{6,7},{7,6},{8,9},{9,8},{10,11... | collective-permute-start | bytes 1179656 | tf_op jit(solution)/shard_map/ppermute | solution.py:88
  22.3 3.4 %collective-permute-start.3 = (bf16[192,768]{1,0:T(8,128)(2,1)}, bf16[192,768]{1,0:T(8,128)(2,1)S(1)}, u32[]{:S(2)}, u32[]{:S(2)}) collective-permute-start(bf16[192,768]{1,0:T(8,128)(2,1)} %collective-permute-done.2.refs_9_), channel_id=1, source_target_pairs={{0,1},{1,0},{2,3},{3,2},{4,5},{5,4},{6,7},{7,6},{8,9},{9,8},{10,11... | collective-permute-start | bytes 884744 | tf_op jit(solution)/shard_map/ppermute | solution.py:88
  22.5 5.6 %copy-start.15 = (bf16[256,768]{1,0:T(8,128)(2,1)S(1)}, bf16[256,768]{1,0:T(8,128)(2,1)}, u32[]{:S(2)}) copy-start(bf16[256,768]{1,0:T(8,128)(2,1)} %get-tuple-element.90.refs_4_) | copy-start | bytes 1179652
  22.5 6.7 %copy-start.7 = (bf16[1,1,256,768]{3,2,1,0:T(8,128)(2,1)S(1)}, bf16[1,1,256,768]{3,2,1,0:T(8,128)(2,1)}, u32[]{:S(2)}) copy-start(bf16[1,1,256,768]{3,2,1,0:T(8,128)(2,1)} %param.11) | copy-start | bytes 1179652
  22.5 6.7 %copy-start.9 = (bf16[768,768]{1,0:T(8,128)(2,1)S(1)}, bf16[768,768]{1,0:T(8,128)(2,1)}, u32[]{:S(2)}) copy-start(bf16[768,768]{1,0:T(8,128)(2,1)} %refs_9_.1) | copy-start | bytes 3538948
  22.5 6.7 %copy-start.10 = (s32[5]{0:T(128)S(1)}, s32[5]{0:T(128)}, u32[]{:S(2)}) copy-start(s32[5]{0:T(128)} %stack.23.refs_0_) | copy-start | bytes 64
  22.5 6.7 %copy-start.16 = (s32[4]{0:T(128)S(1)}, s32[4]{0:T(128)}, u32[]{:S(2)}) copy-start(s32[4]{0:T(128)} %refs_2_.1) | copy-start | bytes 52
  25.7 3.5 %copy-start.23 = (bf16[192,768]{1,0:T(8,128)(2,1)}, bf16[192,768]{1,0:T(8,128)(2,1)S(1)}, u32[]{:S(2)}) copy-start(bf16[192,768]{1,0:T(8,128)(2,1)S(1)} %collective-permute-done.3.refs_11_) | copy-start | bytes 884740
  25.7 3.5 %collective-permute-start.8 = (bf16[256,768]{1,0:T(8,128)(2,1)S(1)}, bf16[256,768]{1,0:T(8,128)(2,1)S(1)}, u32[]{:S(2)}, u32[]{:S(2)}) collective-permute-start(bf16[256,768]{1,0:T(8,128)(2,1)S(1)} %collective-permute-done.4.refs_6_), channel_id=1, source_target_pairs={{0,1},{1,0},{2,3},{3,2},{4,5},{5,4},{6,7},{7,6},{8,9},{9,8},{10,11... | collective-permute-start | bytes 1179656 | tf_op jit(solution)/shard_map/ppermute | solution.py:88
  25.8 11.7 %collective-permute-start.5 = (bf16[256,768]{1,0:T(8,128)(2,1)}, bf16[256,768]{1,0:T(8,128)(2,1)S(1)}, u32[]{:S(2)}, u32[]{:S(2)}) collective-permute-start(bf16[256,768]{1,0:T(8,128)(2,1)} %collective-permute-done.refs_4_), channel_id=1, source_target_pairs={{0,8},{4,12},{8,0},{12,4},{16,24},{20,28},{24,16},{28,20},{1,9},{5... | collective-permute-start | bytes 1179656 | tf_op jit(solution)/shard_map/ppermute | solution.py:88
  26.5 11.0 %collective-permute-start.6 = (bf16[192,768]{1,0:T(8,128)(2,1)}, bf16[192,768]{1,0:T(8,128)(2,1)S(1)}, u32[]{:S(2)}, u32[]{:S(2)}) collective-permute-start(bf16[192,768]{1,0:T(8,128)(2,1)} %collective-permute-done.2.refs_9_), channel_id=1, source_target_pairs={{0,2},{1,3},{2,0},{3,1},{4,6},{5,7},{6,4},{7,5},{8,10},{9,11},{10,... | collective-permute-start | bytes 884744 | tf_op jit(solution)/shard_map/ppermute | solution.py:88
  28.0 10.7 %collective-permute-start.10 = (bf16[256,768]{1,0:T(8,128)(2,1)S(1)}, bf16[256,768]{1,0:T(8,128)(2,1)S(1)}, u32[]{:S(2)}, u32[]{:S(2)}) collective-permute-start(bf16[256,768]{1,0:T(8,128)(2,1)S(1)} %copy-done.15), channel_id=1, source_target_pairs={{0,4},{4,0},{8,12},{12,8},{16,20},{20,16},{24,28},{28,24},{1,5},{5... | collective-permute-start | bytes 1179656 | tf_op jit(solution)/shard_map/ppermute | solution.py:88
  33.5 2.4 %copy-start.1 = (bf16[1024,768]{1,0:T(8,128)(2,1)}, bf16[1024,768]{1,0:T(8,128)(2,1)S(1)}, u32[]{:S(2)}) copy-start(bf16[1024,768]{1,0:T(8,128)(2,1)S(1)} %get-tuple-element.88.refs_2_.refs_1_) | copy-start | bytes 4718596
  33.5 3.9 %collective-permute-start.9 = (f32[4,1664]{1,0:T(4,128)S(1)}, f32[4,1664]{1,0:T(4,128)S(1)}, u32[]{:S(2)}, u32[]{:S(2)}) collective-permute-start(f32[4,1664]{1,0:T(4,128)S(1)} %get-tuple-element.87), channel_id=1, source_target_pairs={{0,2},{1,3},{2,0},{3,1},{4,6},{5,7},{6,4},{7,5},{8,10},{9,11},{10,... | collective-permute-start | bytes 79880 | tf_op jit(solution)/shard_map/ppermute | solution.py:88
  38.7 1.7 %collective-permute-start.11 = (f32[4,1664]{1,0:T(4,128)S(1)}, f32[4,1664]{1,0:T(4,128)S(1)}, u32[]{:S(2)}, u32[]{:S(2)}) collective-permute-start(f32[4,1664]{1,0:T(4,128)S(1)} %add_select_fusion.1), channel_id=1, source_target_pairs={{0,1},{1,0},{2,3},{3,2},{4,5},{5,4},{6,7},{7,6},{8,9},{9,8},{10,11... | collective-permute-start | bytes 79880 | tf_op jit(solution)/shard_map/ppermute | solution.py:88
  38.8 18.2 %collective-permute-start.18 = (bf16[256,768]{1,0:T(8,128)(2,1)S(1)}, bf16[256,768]{1,0:T(8,128)(2,1)S(1)}, u32[]{:S(2)}, u32[]{:S(2)}) collective-permute-start(bf16[256,768]{1,0:T(8,128)(2,1)S(1)} %collective-permute-done.10.refs_2_), channel_id=1, source_target_pairs={{0,1},{1,0},{2,3},{3,2},{4,5},{5,4},{6,7},{7,6},{8,9},{9,8},{10,11... | collective-permute-start | bytes 1179656 | tf_op jit(solution)/shard_map/ppermute | solution.py:88
  39.2 14.6 %collective-permute-start.19 = (bf16[256,768]{1,0:T(8,128)(2,1)S(1)}, bf16[256,768]{1,0:T(8,128)(2,1)}, u32[]{:S(2)}, u32[]{:S(2)}) collective-permute-start(bf16[256,768]{1,0:T(8,128)(2,1)S(1)} %collective-permute-done.10.refs_2_), channel_id=1, source_target_pairs={{0,2},{1,3},{2,0},{3,1},{4,6},{5,7},{6,4},{7,5},{8,10},{9,11},{10,... | collective-permute-start | bytes 1179656 | tf_op jit(solution)/shard_map/ppermute | solution.py:88
  40.4 1.9 %collective-permute-start.13 = (bf16[192,768]{1,0:T(8,128)(2,1)}, bf16[192,768]{1,0:T(8,128)(2,1)}, u32[]{:S(2)}, u32[]{:S(2)}) collective-permute-start(bf16[192,768]{1,0:T(8,128)(2,1)} %copy-done.24), channel_id=1, source_target_pairs={{0,1},{1,0},{2,3},{3,2},{4,5},{5,4},{6,7},{7,6},{8,9},{9,8},{10,11... | collective-permute-start | bytes 884744 | tf_op jit(solution)/shard_map/ppermute | solution.py:88
  40.5 25.8 %copy-start.11 = (s32[5]{0:T(128)S(1)}, s32[5]{0:T(128)}, u32[]{:S(2)}) copy-start(s32[5]{0:T(128)} %stack.23.refs_0_) | copy-start | bytes 64
  40.5 10.6 %collective-permute-start.12 = (f32[4,1664]{1,0:T(4,128)S(1)}, f32[4,1664]{1,0:T(4,128)S(1)}, u32[]{:S(2)}, u32[]{:S(2)}) collective-permute-start(f32[4,1664]{1,0:T(4,128)S(1)} %add_select_fusion), channel_id=1, source_target_pairs={{0,4},{4,0},{8,12},{12,8},{16,20},{20,16},{24,28},{28,24},{1,5},{5... | collective-permute-start | bytes 79880 | tf_op jit(solution)/shard_map/ppermute | solution.py:88
  48.9 4.0 %collective-permute-start.15 = (f32[4,768]{1,0:T(4,128)}, f32[4,768]{1,0:T(4,128)S(1)}, u32[]{:S(2)}, u32[]{:S(2)}) collective-permute-start(f32[4,768]{1,0:T(4,128)} %get-tuple-element.98), channel_id=1, source_target_pairs={{0,8},{4,12},{8,0},{12,4},{16,24},{20,28},{24,16},{28,20},{1,9},{5... | collective-permute-start | bytes 36872 | tf_op jit(solution)/shard_map/ppermute | solution.py:88
  49.9 4.8 %collective-permute-start.16 = (f32[4,768]{1,0:T(4,128)}, f32[4,768]{1,0:T(4,128)S(1)}, u32[]{:S(2)}, u32[]{:S(2)}) collective-permute-start(f32[4,768]{1,0:T(4,128)} %get-tuple-element.98), channel_id=1, source_target_pairs={{0,12},{4,8},{8,4},{12,0},{16,28},{20,24},{24,20},{28,16},{1,13},{... | collective-permute-start | bytes 36872 | tf_op jit(solution)/shard_map/ppermute | solution.py:88
  51.1 3.9 %collective-permute-start.14 = (f32[4,768]{1,0:T(4,128)}, f32[4,768]{1,0:T(4,128)S(1)}, u32[]{:S(2)}, u32[]{:S(2)}) collective-permute-start(f32[4,768]{1,0:T(4,128)} %get-tuple-element.98), channel_id=1, source_target_pairs={{0,4},{4,0},{8,12},{12,8},{16,20},{20,16},{24,28},{28,24},{1,5},{5... | collective-permute-start | bytes 36872 | tf_op jit(solution)/shard_map/ppermute | solution.py:88
  52.9 4.1 %collective-permute-start.17 = (f32[8,1664]{1,0:T(8,128)S(1)}, f32[8,1664]{1,0:T(8,128)S(1)}, u32[]{:S(2)}, u32[]{:S(2)}) collective-permute-start(f32[8,1664]{1,0:T(8,128)S(1)} %maximum_select_fusion.6), channel_id=1, source_target_pairs={{0,8},{4,12},{8,0},{12,4},{16,24},{20,28},{24,16},{28,20},{1,9},{5... | collective-permute-start | bytes 159752 | tf_op jit(solution)/shard_map/ppermute | solution.py:88
  53.9 3.2 %collective-permute-start.20 = (bf16[256,768]{1,0:T(8,128)(2,1)}, bf16[256,768]{1,0:T(8,128)(2,1)S(1)}, u32[]{:S(2)}, u32[]{:S(2)}) collective-permute-start(bf16[256,768]{1,0:T(8,128)(2,1)} %collective-permute-done.19.refs_4_), channel_id=1, source_target_pairs={{0,1},{1,0},{2,3},{3,2},{4,5},{5,4},{6,7},{7,6},{8,9},{9,8},{10,11... | collective-permute-start | bytes 1179656 | tf_op jit(solution)/shard_map/ppermute | solution.py:88
  57.0 12.6 %collective-permute-start.21 = (f32[16,1664]{1,0:T(8,128)S(1)}, f32[16,1664]{1,0:T(8,128)S(1)}, u32[]{:S(2)}, u32[]{:S(2)}) collective-permute-start(f32[16,1664]{1,0:T(8,128)S(1)} %maximum_select_fusion.4), channel_id=1, source_target_pairs={{0,16},{4,20},{8,24},{12,28},{16,0},{20,4},{24,8},{28,12},{1,17},{... | collective-permute-start | bytes 319496 | tf_op jit(solution)/shard_map/ppermute | solution.py:88
  59.8 4.8 %collective-permute-start.22 = (f32[4,1152]{1,0:T(4,128)S(1)}, f32[4,1152]{1,0:T(4,128)S(1)}, u32[]{:S(2)}, u32[]{:S(2)}) collective-permute-start(f32[4,1152]{1,0:T(4,128)S(1)} %pad_maximum_fusion.5), channel_id=1, source_target_pairs={{0,16},{4,20},{8,24},{12,28},{16,0},{20,4},{24,8},{28,12},{1,17},{... | collective-permute-start | bytes 55304 | tf_op jit(solution)/shard_map/ppermute | solution.py:88
  64.6 4.9 %collective-permute-start.23 = (f32[1,8,1152]{2,1,0:T(8,128)S(1)}, f32[1,8,1152]{2,1,0:T(8,128)S(1)}, u32[]{:S(2)}, u32[]{:S(2)}) collective-permute-start(f32[1,8,1152]{2,1,0:T(8,128)S(1)} %maximum_bitcast_fusion), channel_id=1, source_target_pairs={{0,2},{1,3},{2,0},{3,1},{4,6},{5,7},{6,4},{7,5},{8,10},{9,11},{10,... | collective-permute-start | bytes 110600 | tf_op jit(solution)/shard_map/ppermute | solution.py:88
  66.2 4.7 %copy-start.5 = (bf16[384,768]{1,0:T(8,128)(2,1)S(1)}, bf16[384,768]{1,0:T(8,128)(2,1)}, u32[]{:S(2)}) copy-start(bf16[384,768]{1,0:T(8,128)(2,1)} %get-tuple-element.113.refs_5_) | copy-start | bytes 1769476
  69.5 1.3 %collective-permute-start.24 = (f32[2,8,1152]{2,1,0:T(8,128)S(1)}, f32[2,8,1152]{2,1,0:T(8,128)S(1)}, u32[]{:S(2)}, u32[]{:S(2)}) collective-permute-start(f32[2,8,1152]{2,1,0:T(8,128)S(1)} %maximum_select_fusion.5), channel_id=1, source_target_pairs={{0,1},{1,0},{2,3},{3,2},{4,5},{5,4},{6,7},{7,6},{8,9},{9,8},{10,11... | collective-permute-start | bytes 221192 | tf_op jit(solution)/shard_map/ppermute | solution.py:88
  69.6 4.1 %copy-start.4 = (f32[1024,384]{1,0:T(8,128)S(1)}, f32[1024,384]{1,0:T(8,128)}, u32[]{:S(2)}) copy-start(f32[1024,384]{1,0:T(8,128)} %copy-done.3) | copy-start | bytes 4718596
  70.9 2.9 %copy-start.2 = (bf16[1024,768]{1,0:T(8,128)(2,1)S(1)}, bf16[1024,768]{1,0:T(8,128)(2,1)}, u32[]{:S(2)}) copy-start(bf16[1024,768]{1,0:T(8,128)(2,1)} %copy-done.1) | copy-start | bytes 4718596
  70.9 2.9 %copy-start.12 = (f32[768]{0:T(1024)S(1)}, f32[768]{0:T(1024)}, u32[]{:S(2)}) copy-start(f32[768]{0:T(1024)} %refs_7_.3) | copy-start | bytes 9220
  73.8 7.1 %copy-start.6 = (bf16[768,384]{1,0:T(8,128)(2,1)S(1)}, bf16[768,384]{1,0:T(8,128)(2,1)}, u32[]{:S(2)}) copy-start(bf16[768,384]{1,0:T(8,128)(2,1)} %refs_4_.5) | copy-start | bytes 1769476
  73.8 7.1 %copy-start.13 = (f32[768]{0:T(1024)S(1)}, f32[768]{0:T(1024)}, u32[]{:S(2)}) copy-start(f32[768]{0:T(1024)} %refs_6_.3) | copy-start | bytes 9220
  73.8 7.1 %copy-start.14 = (s32[8]{0:T(128)S(1)}, s32[8]{0:T(128)}, u32[]{:S(2)}) copy-start(s32[8]{0:T(128)} %convert_reduce_fusion.refs_1_) | copy-start | bytes 100
  73.9 7.1 %copy-start.17 = (bf16[1024,768]{1,0:T(8,128)(2,1)S(1)}, bf16[1024,768]{1,0:T(8,128)(2,1)}, u32[]{:S(2)}) copy-start(bf16[1024,768]{1,0:T(8,128)(2,1)} %get-tuple-element.123.refs_2_) | copy-start | bytes 4718596
  73.9 7.1 %copy-start.18 = (bf16[768,384]{1,0:T(8,128)(2,1)S(1)}, bf16[768,384]{1,0:T(8,128)(2,1)}, u32[]{:S(2)}) copy-start(bf16[768,384]{1,0:T(8,128)(2,1)} %get-tuple-element.127.refs_5_) | copy-start | bytes 1769476
  76.5 16.2 %collective-permute-start.25 = (bf16[192,384]{1,0:T(8,128)(2,1)S(1)}, bf16[192,384]{1,0:T(8,128)(2,1)S(1)}, u32[]{:S(2)}, u32[]{:S(2)}) collective-permute-start(bf16[192,384]{1,0:T(8,128)(2,1)S(1)} %get-tuple-element.120), channel_id=1, source_target_pairs={{0,8},{4,12},{8,0},{12,4},{16,24},{20,28},{24,16},{28,20},{1,9},{5... | collective-permute-start | bytes 442376 | tf_op jit(solution)/shard_map/ppermute | solution.py:88
  76.8 15.9 %collective-permute-start.26 = (bf16[192,384]{1,0:T(8,128)(2,1)S(1)}, bf16[192,384]{1,0:T(8,128)(2,1)S(1)}, u32[]{:S(2)}, u32[]{:S(2)}) collective-permute-start(bf16[192,384]{1,0:T(8,128)(2,1)S(1)} %get-tuple-element.121), channel_id=1, source_target_pairs={{0,16},{4,20},{8,24},{12,28},{16,0},{20,4},{24,8},{28,12},{1,17},{... | collective-permute-start | bytes 442376 | tf_op jit(solution)/shard_map/ppermute | solution.py:88
  79.6 13.1 %collective-permute-start.27 = (bf16[192,384]{1,0:T(8,128)(2,1)S(1)}, bf16[192,384]{1,0:T(8,128)(2,1)S(1)}, u32[]{:S(2)}, u32[]{:S(2)}) collective-permute-start(bf16[192,384]{1,0:T(8,128)(2,1)S(1)} %get-tuple-element.122), channel_id=1, source_target_pairs={{0,24},{4,28},{8,16},{12,20},{16,8},{20,12},{24,0},{28,4},{1,25},{... | collective-permute-start | bytes 442376 | tf_op jit(solution)/shard_map/ppermute | solution.py:88
  85.8 3.9 %collective-permute-start.28 = (bf16[64,768]{1,0:T(8,128)(2,1)S(1)}, bf16[64,768]{1,0:T(8,128)(2,1)S(1)}, u32[]{:S(2)}, u32[]{:S(2)}) collective-permute-start(bf16[64,768]{1,0:T(8,128)(2,1)S(1)} %get-tuple-element.170), channel_id=1, source_target_pairs={{0,1},{1,0},{2,3},{3,2},{4,5},{5,4},{6,7},{7,6},{8,9},{9,8},{10,11... | collective-permute-start | bytes 294920 | tf_op jit(solution)/shard_map/ppermute | solution.py:88
  85.9 3.9 %collective-permute-start.29 = (bf16[64,768]{1,0:T(8,128)(2,1)S(1)}, bf16[64,768]{1,0:T(8,128)(2,1)S(1)}, u32[]{:S(2)}, u32[]{:S(2)}) collective-permute-start(bf16[64,768]{1,0:T(8,128)(2,1)S(1)} %get-tuple-element.169), channel_id=1, source_target_pairs={{0,1},{1,0},{2,3},{3,2},{4,5},{5,4},{6,7},{7,6},{8,9},{9,8},{10,11... | collective-permute-start | bytes 294920 | tf_op jit(solution)/shard_map/ppermute | solution.py:88
  89.7 1.3 %collective-permute-start.30 = (bf16[64,768]{1,0:T(8,128)(2,1)S(1)}, bf16[64,768]{1,0:T(8,128)(2,1)S(1)}, u32[]{:S(2)}, u32[]{:S(2)}) collective-permute-start(bf16[64,768]{1,0:T(8,128)(2,1)S(1)} %get-tuple-element.168), channel_id=1, source_target_pairs={{0,1},{1,0},{2,3},{3,2},{4,5},{5,4},{6,7},{7,6},{8,9},{9,8},{10,11... | collective-permute-start | bytes 294920 | tf_op jit(solution)/shard_map/ppermute | solution.py:88
  89.8 1.4 %collective-permute-start.31 = (bf16[64,768]{1,0:T(8,128)(2,1)S(1)}, bf16[64,768]{1,0:T(8,128)(2,1)S(1)}, u32[]{:S(2)}, u32[]{:S(2)}) collective-permute-start(bf16[64,768]{1,0:T(8,128)(2,1)S(1)} %get-tuple-element.167), channel_id=1, source_target_pairs={{0,1},{1,0},{2,3},{3,2},{4,5},{5,4},{6,7},{7,6},{8,9},{9,8},{10,11... | collective-permute-start | bytes 294920 | tf_op jit(solution)/shard_map/ppermute | solution.py:88
  91.0 1.3 %collective-permute-start.32 = (bf16[64,768]{1,0:T(8,128)(2,1)S(1)}, bf16[64,768]{1,0:T(8,128)(2,1)S(1)}, u32[]{:S(2)}, u32[]{:S(2)}) collective-permute-start(bf16[64,768]{1,0:T(8,128)(2,1)S(1)} %get-tuple-element.166), channel_id=1, source_target_pairs={{0,1},{1,0},{2,3},{3,2},{4,5},{5,4},{6,7},{7,6},{8,9},{9,8},{10,11... | collective-permute-start | bytes 294920 | tf_op jit(solution)/shard_map/ppermute | solution.py:88
  91.2 1.3 %collective-permute-start.33 = (bf16[64,768]{1,0:T(8,128)(2,1)S(1)}, bf16[64,768]{1,0:T(8,128)(2,1)S(1)}, u32[]{:S(2)}, u32[]{:S(2)}) collective-permute-start(bf16[64,768]{1,0:T(8,128)(2,1)S(1)} %get-tuple-element.165), channel_id=1, source_target_pairs={{0,1},{1,0},{2,3},{3,2},{4,5},{5,4},{6,7},{7,6},{8,9},{9,8},{10,11... | collective-permute-start | bytes 294920 | tf_op jit(solution)/shard_map/ppermute | solution.py:88
  92.8 10.3 %collective-permute-start.39 = (bf16[192,768]{1,0:T(8,128)(2,1)S(1)}, bf16[192,768]{1,0:T(8,128)(2,1)S(1)}, u32[]{:S(2)}, u32[]{:S(2)}) collective-permute-start(bf16[192,768]{1,0:T(8,128)(2,1)S(1)} %dynamic-slice_convert_fusion), channel_id=1, source_target_pairs={{0,2},{1,3},{2,0},{3,1},{4,6},{5,7},{6,4},{7,5},{8,10},{9,11},{10,... | collective-permute-start | bytes 884744 | tf_op jit(solution)/shard_map/ppermute | solution.py:88
  93.7 8.5 %collective-permute-start.34 = (bf16[208,384]{1,0:T(8,128)(2,1)S(1)}, bf16[208,384]{1,0:T(8,128)(2,1)S(1)}, u32[]{:S(2)}, u32[]{:S(2)}) collective-permute-start(bf16[208,384]{1,0:T(8,128)(2,1)S(1)} %pad_maximum_fusion.3), channel_id=1, source_target_pairs={{0,8},{4,12},{8,0},{12,4},{16,24},{20,28},{24,16},{28,20},{1,9},{5... | collective-permute-start | bytes 479240 | tf_op jit(solution)/shard_map/ppermute | solution.py:88
  94.9 14.6 %collective-permute-start.35 = (bf16[208,384]{1,0:T(8,128)(2,1)S(1)}, bf16[208,384]{1,0:T(8,128)(2,1)S(1)}, u32[]{:S(2)}, u32[]{:S(2)}) collective-permute-start(bf16[208,384]{1,0:T(8,128)(2,1)S(1)} %pad_maximum_fusion.3), channel_id=1, source_target_pairs={{0,16},{4,20},{8,24},{12,28},{16,0},{20,4},{24,8},{28,12},{1,17},{... | collective-permute-start | bytes 479240 | tf_op jit(solution)/shard_map/ppermute | solution.py:88
  96.8 12.7 %collective-permute-start.36 = (bf16[208,384]{1,0:T(8,128)(2,1)S(1)}, bf16[208,384]{1,0:T(8,128)(2,1)S(1)}, u32[]{:S(2)}, u32[]{:S(2)}) collective-permute-start(bf16[208,384]{1,0:T(8,128)(2,1)S(1)} %pad_maximum_fusion.3), channel_id=1, source_target_pairs={{0,24},{4,28},{8,16},{12,20},{16,8},{20,12},{24,0},{28,4},{1,25},{... | collective-permute-start | bytes 479240 | tf_op jit(solution)/shard_map/ppermute | solution.py:88
  98.1 5.1 %collective-permute-start.37 = (bf16[192,384]{1,0:T(8,128)(2,1)S(1)}, bf16[192,384]{1,0:T(8,128)(2,1)S(1)}, u32[]{:S(2)}, u32[]{:S(2)}) collective-permute-start(bf16[192,384]{1,0:T(8,128)(2,1)S(1)} %add_convert_fusion.1.refs_1_), channel_id=1, source_target_pairs={{0,4},{4,0},{8,12},{12,8},{16,20},{20,16},{24,28},{28,24},{1,5},{5... | collective-permute-start | bytes 442376 | tf_op jit(solution)/shard_map/ppermute | solution.py:88
  102.2 7.2 %collective-permute-start.38 = (bf16[192,384]{1,0:T(8,128)(2,1)S(1)}, bf16[192,384]{1,0:T(8,128)(2,1)S(1)}, u32[]{:S(2)}, u32[]{:S(2)}) collective-permute-start(bf16[192,384]{1,0:T(8,128)(2,1)S(1)} %slice.231), channel_id=1, source_target_pairs={{0,4},{4,0},{8,12},{12,8},{16,20},{20,16},{24,28},{28,24},{1,5},{5... | collective-permute-start | bytes 442376 | tf_op jit(solution)/shard_map/ppermute | solution.py:88
  109.6 9.2 %collective-permute-start.40 = (bf16[192,384]{1,0:T(8,128)(2,1)S(1)}, bf16[192,384]{1,0:T(8,128)(2,1)S(1)}, u32[]{:S(2)}, u32[]{:S(2)}) collective-permute-start(bf16[192,384]{1,0:T(8,128)(2,1)S(1)} %slice.329), channel_id=1, source_target_pairs={{0,16},{4,20},{8,24},{12,28},{16,0},{20,4},{24,8},{28,12},{1,17},{... | collective-permute-start | bytes 442376 | tf_op jit(solution)/shard_map/ppermute | solution.py:88
  113.5 7.3 %collective-permute-start.41 = (bf16[400,384]{1,0:T(8,128)(2,1)S(1)}, bf16[400,384]{1,0:T(8,128)(2,1)S(1)}, u32[]{:S(2)}, u32[]{:S(2)}) collective-permute-start(bf16[400,384]{1,0:T(8,128)(2,1)S(1)} %pad_maximum_fusion.1), channel_id=1, source_target_pairs={{0,4},{4,0},{8,12},{12,8},{16,20},{20,16},{24,28},{28,24},{1,5},{5... | collective-permute-start | bytes 921608 | tf_op jit(solution)/shard_map/ppermute | solution.py:88
  120.9 5.3 %collective-permute-start.42 = (bf16[208,384]{1,0:T(8,128)(2,1)S(1)}, bf16[208,384]{1,0:T(8,128)(2,1)S(1)}, u32[]{:S(2)}, u32[]{:S(2)}) collective-permute-start(bf16[208,384]{1,0:T(8,128)(2,1)S(1)} %pad_maximum_fusion.2), channel_id=1, source_target_pairs={{0,2},{1,3},{2,0},{3,1},{4,6},{5,7},{6,4},{7,5},{8,10},{9,11},{10,... | collective-permute-start | bytes 479240 | tf_op jit(solution)/shard_map/ppermute | solution.py:88
  126.5 1.7 %collective-permute-start.43 = (bf16[400,384]{1,0:T(8,128)(2,1)S(1)}, bf16[400,384]{1,0:T(8,128)(2,1)S(1)}, u32[]{:S(2)}, u32[]{:S(2)}) collective-permute-start(bf16[400,384]{1,0:T(8,128)(2,1)S(1)} %pad_maximum_fusion), channel_id=1, source_target_pairs={{0,1},{1,0},{2,3},{3,2},{4,5},{5,4},{6,7},{7,6},{8,9},{9,8},{10,11... | collective-permute-start | bytes 921608 | tf_op jit(solution)/shard_map/ppermute | solution.py:88
  (5 other events, 5.8 us)

commit v8 on v7

--- a/solution.py
+++ b/solution.py
@@ -463,10 +463,11 @@
 
 def q_backward_kernel(pairs, span, start, arrive, place, *refs):
     start(LOAD)
+    arrive(LOAD)
     rows, pair_rows, own_slope, pair_slope, hidden, weight, gain = refs[:7]
     sends, (keep, gains, total) = refs[7 : 6 + pairs], refs[6 + pairs :]
     gains[...] = inner_gradient(
-        [rows, pair_rows], [own_slope, pair_slope], hidden, [weight], gain, total, span, arrive
+        [rows, pair_rows], [own_slope, pair_slope], hidden, [weight], gain, total, span
     )
     mine = place[0] // 2
     size = keep.shape[0]
@@ -531,6 +532,7 @@
     n_sa, n_pb, width, start, arrive, place, q_ref, s_ref, q_outer, *refs
 ):
     start(LOAD)
+    arrive(LOAD)
     s_outers = refs[:-5]
     loss_ref, q_grad_ref, s_grad_ref, q_hidden, s_hidden = refs[-5:]
     p, a = place[0], place[1]
@@ -575,7 +577,6 @@
     pair = (index >= n_sa).astype(jnp.int32)
     hidden(q_grad, (p ^ pair) * n_sa + (a ^ (index - pair * n_sa)), [q_outer], q_hidden)
     index = lax.broadcasted_iota(jnp.int32, (8, 1), 0)
-    arrive(LOAD)
     hidden(s_grad, a * n_pb + (p ^ index), s_outers, s_hidden)
 
 

time: 130 us -> 130 us (level)
  transfers between devices with their start and end apart: 44 -> 44, of which waited for: 23 -> 23; matrix products, arithmetic and copies ran while one was open for 6% -> 6% of each run, Pallas kernels for 19% -> 20%
where the time goes in v8:
time: 130 us
  starting transfers between devices  43.3 us (33%)
  waiting for transfers between devices  38.4 us (30%)
  Pallas kernels  33.5 us (26%)
  local copies, waits for them, and re-layouts  5.21 us (4%)
  other arithmetic  4.32 us (3%)
  matrix products  3.26 us (3%)
  between operations  1.53 us (1%)
    ppermute x44, starting transfers between devices, swap(): return lax.ppermute(x, axis, [(i, i ^ step) for i in range(size)])  43.3 us
    ppermute x44, waiting for transfers between devices, swap(): return lax.ppermute(x, axis, [(i, i ^ step) for i in range(size)])  38.4 us
    pallas_call x10, Pallas kernels, run(): pl.pallas_call(kernel, in_specs=[HBM if spec in (LOAD, LATE) else spec fo...  33.5 us
    dot_general x2, matrix products, outer_gradient(): lax.dot_general(left, right, CONTRACT_FIRST, preferred_element_type=F32)  3.26 us
  transfers between devices with their start and end apart: 44, of which 23 were waited for; matrix products, arithmetic and copies ran while one was open for 6% of the time, Pallas kernels for 20%

profile of v8, /device:TPU:0, one launch (start us, length us, event | category | flops | bytes accessed | tf_op | source)
XLA Modules:
  0.0 129.6 jit_solution(5308389062293339769)
XLA Ops:
  0.7 0.6 stack.23.refs_0_
  1.3 3.2 %shard_map.162 = (bf16[256,768]{1,0:T(8,128)(2,1)}, bf16[256,768]{1,0:T(8,128)(2,1)}, bf16[192,768]{1,0:T(8,128)(2,1)}) custom-call(s32[5]{0:T(128)} %stack.23.refs_0_, bf16[256,768]{1,0:T(8,128)(2,1)} %bitcast.18, bf16[256,768]{1,0:T(8,128)(2,1)} %bitcast.20, f32[768]{0:T(1024)} %refs_7_.3, f32[768]{0:T(1024)} %refs_6_.3, bf16[768,384]{1,0:T(8,128)(2,1)} %refs_4_.5, ...), custom_call_target="tpu_custom_call" | custom-call | tf_op jit(solution)/shard_map/pallas_call | solution.py:60
  4.5 4.1 %collective-permute-start.2 = (bf16[192,768]{1,0:T(8,128)(2,1)}, bf16[192,768]{1,0:T(8,128)(2,1)}, u32[]{:S(2)}, u32[]{:S(2)}) collective-permute-start(bf16[192,768]{1,0:T(8,128)(2,1)} %get-tuple-element.81), channel_id=1, source_target_pairs={{0,16},{4,20},{8,24},{12,28},{16,0},{20,4},{24,8},{28,12},{1,17},{... | collective-permute-start | bytes 884744 | tf_op jit(solution)/shard_map/ppermute | solution.py:88
  8.6 1.5 %collective-permute-start = (bf16[256,768]{1,0:T(8,128)(2,1)}, bf16[256,768]{1,0:T(8,128)(2,1)}, u32[]{:S(2)}, u32[]{:S(2)}) collective-permute-start(bf16[256,768]{1,0:T(8,128)(2,1)} %get-tuple-element.80.refs_3_), channel_id=1, source_target_pairs={{0,4},{4,0},{8,12},{12,8},{16,20},{20,16},{24,28},{28,24},{1,5},{5... | collective-permute-start | bytes 1179656 | tf_op jit(solution)/shard_map/ppermute | solution.py:88
  10.1 1.6 %collective-permute-start.1 = (bf16[256,768]{1,0:T(8,128)(2,1)}, bf16[256,768]{1,0:T(8,128)(2,1)S(1)}, u32[]{:S(2)}, u32[]{:S(2)}) collective-permute-start(bf16[256,768]{1,0:T(8,128)(2,1)} %get-tuple-element.80.refs_3_), channel_id=1, source_target_pairs={{0,8},{4,12},{8,0},{12,4},{16,24},{20,28},{24,16},{28,20},{1,9},{5... | collective-permute-start | bytes 1179656 | tf_op jit(solution)/shard_map/ppermute | solution.py:88
  11.6 1.5 %collective-permute-start.4 = (bf16[256,768]{1,0:T(8,128)(2,1)}, bf16[256,768]{1,0:T(8,128)(2,1)S(1)}, u32[]{:S(2)}, u32[]{:S(2)}) collective-permute-start(bf16[256,768]{1,0:T(8,128)(2,1)} %get-tuple-element.90.refs_4_), channel_id=1, source_target_pairs={{0,2},{1,3},{2,0},{3,1},{4,6},{5,7},{6,4},{7,5},{8,10},{9,11},{10,... | collective-permute-start | bytes 1179656 | tf_op jit(solution)/shard_map/ppermute | solution.py:88
  13.2 0.6 convert_reduce_fusion.refs_1_
  13.8 8.5 %collective-permute-done.2.refs_9_ = bf16[192,768]{1,0:T(8,128)(2,1)} collective-permute-done((bf16[192,768]{1,0:T(8,128)(2,1)}, bf16[192,768]{1,0:T(8,128)(2,1)}, u32[]{:S(2)}, u32[]{:S(2)}) %collective-permute-start.2) | collective-permute-done | bytes 294944 | tf_op jit(solution)/shard_map/ppermute | solution.py:88
  22.6 1.2 constant_dynamic-slice_fusion.refs_3_
  23.8 1.9 %collective-permute-done.1.refs_5_ = bf16[256,768]{1,0:T(8,128)(2,1)S(1)} collective-permute-done((bf16[256,768]{1,0:T(8,128)(2,1)}, bf16[256,768]{1,0:T(8,128)(2,1)S(1)}, u32[]{:S(2)}, u32[]{:S(2)}) %collective-permute-start.1) | collective-permute-done | bytes 393248 | tf_op jit(solution)/shard_map/ppermute | solution.py:88
  26.5 1.6 %collective-permute-start.6 = (bf16[192,768]{1,0:T(8,128)(2,1)}, bf16[192,768]{1,0:T(8,128)(2,1)S(1)}, u32[]{:S(2)}, u32[]{:S(2)}) collective-permute-start(bf16[192,768]{1,0:T(8,128)(2,1)} %collective-permute-done.2.refs_9_), channel_id=1, source_target_pairs={{0,2},{1,3},{2,0},{3,1},{4,6},{5,7},{6,4},{7,5},{8,10},{9,11},{10,... | collective-permute-start | bytes 884744 | tf_op jit(solution)/shard_map/ppermute | solution.py:88
  28.0 1.2 collective-permute-start.10
  29.2 4.3 %shard_map.163 = (f32[4,1664]{1,0:T(4,128)S(1)}, bf16[1024,768]{1,0:T(8,128)(2,1)S(1)}) custom-call(s32[5]{0:T(128)S(1)} %copy-done.10, s32[4]{0:T(128)S(1)} %convert_reduce_fusion.1.refs_1_, s32[4]{0:T(128)S(1)} %copy-done.16, bf16[256,768]{1,0:T(8,128)(2,1)S(1)} %bitcast.19, bf16[256,768]{1,0:T(8,128)(2,1)S(1)} %copy-done.15, ...), custom_call_target="tpu_custom_call" | custom-call | flops 3000000000 | bytes 3000000 | tf_op jit(solution)/shard_map/pallas_call | solution.py:60
  33.5 0.6 collective-permute-start.9
  34.1 1.8 %shard_map.164.refs_3_ = f32[1024,384]{1,0:T(8,128)S(1)} custom-call(s32[5]{0:T(128)S(1)} %copy-done.10, s32[4]{0:T(128)S(1)} %convert_reduce_fusion.1.refs_1_, bf16[1024,768]{1,0:T(8,128)(2,1)S(1)} %get-tuple-element.88.refs_2_.refs_1_, bf16[768,384]{1,0:T(8,128)(2,1)S(1)} %constant_dynamic-slice_fusion.1.refs_3_.refs_6_), custom_call_target="tpu_custom_call" | custom-call | flops 905969664 | bytes 3000000 | tf_op jit(solution)/shard_map/pallas_call | solution.py:60
  36.0 1.2 copy-done.3
  37.6 1.1 collective-permute-done.10.refs_2_
  39.2 1.2 collective-permute-start.19
  40.5 0.9 collective-permute-start.12
  41.4 1.0 collective-permute-done.13.refs_12_
  42.4 6.5 %shard_map.165 = (f32[4,768]{1,0:T(4,128)}, f32[4,384]{1,0:T(4,128)}, f32[4,384]{1,0:T(4,128)}, bf16[1024,768]{1,0:T(8,128)(2,1)}, bf16[768,384]{1,0:T(8,128)(2,1)}, /*index=5*/bf16[384,768]{1,0:T(8,128)(2,1)}) custom-call(s32[5]{0:T(128)} %stack.23.refs_0_, s32[8]{0:T(128)} %convert_reduce_fusion.refs_1_, bf16[256,768]{1,0:T(8,128)(2,1)} %bitcast.21, ...), custom_call_target="tpu_custom_call" | custom-call | flops 3000000000 | bytes 3000000 | tf_op jit(solution)/shard_map/pallas_call | solution.py:60
  48.9 1.0 collective-permute-start.15
  49.9 1.2 collective-permute-start.16
  51.1 1.3 %collective-permute-start.14 = (f32[4,768]{1,0:T(4,128)}, f32[4,768]{1,0:T(4,128)S(1)}, u32[]{:S(2)}, u32[]{:S(2)}) collective-permute-start(f32[4,768]{1,0:T(4,128)} %get-tuple-element.98), channel_id=1, source_target_pairs={{0,4},{4,0},{8,12},{12,8},{16,20},{20,16},{24,28},{28,24},{1,5},{5... | collective-permute-start | bytes 36872 | tf_op jit(solution)/shard_map/ppermute | solution.py:88
  52.9 1.0 collective-permute-start.17
  53.9 0.9 collective-permute-done.16
  55.0 0.7 add_add_fusion
  55.7 1.3 collective-permute-done.17
  57.0 2.1 %collective-permute-start.21 = (f32[16,1664]{1,0:T(8,128)S(1)}, f32[16,1664]{1,0:T(8,128)S(1)}, u32[]{:S(2)}, u32[]{:S(2)}) collective-permute-start(f32[16,1664]{1,0:T(8,128)S(1)} %maximum_select_fusion.4), channel_id=1, source_target_pairs={{0,16},{4,20},{8,24},{12,28},{16,0},{20,4},{24,8},{28,12},{1,17},{... | collective-permute-start | bytes 319496 | tf_op jit(solution)/shard_map/ppermute | solution.py:88
  59.1 0.7 pad_maximum_fusion.5
  59.8 0.9 collective-permute-start.22
  60.7 0.7 constant_dynamic-update-slice_fusion
  61.4 3.2 %collective-permute-done.22 = f32[4,1152]{1,0:T(4,128)S(1)} collective-permute-done((f32[4,1152]{1,0:T(4,128)S(1)}, f32[4,1152]{1,0:T(4,128)S(1)}, u32[]{:S(2)}, u32[]{:S(2)}) %collective-permute-start.22) | collective-permute-done | bytes 18464 | tf_op jit(solution)/shard_map/ppermute | solution.py:88
  64.6 1.6 %collective-permute-start.23 = (f32[1,8,1152]{2,1,0:T(8,128)S(1)}, f32[1,8,1152]{2,1,0:T(8,128)S(1)}, u32[]{:S(2)}, u32[]{:S(2)}) collective-permute-start(f32[1,8,1152]{2,1,0:T(8,128)S(1)} %maximum_bitcast_fusion), channel_id=1, source_target_pairs={{0,2},{1,3},{2,0},{3,1},{4,6},{5,7},{6,4},{7,5},{8,10},{9,11},{10,... | collective-permute-start | bytes 110600 | tf_op jit(solution)/shard_map/ppermute | solution.py:88
  66.2 3.3 %shard_map.166 = (f32[1024,384]{1,0:T(8,128)S(1)}, bf16[1024,768]{1,0:T(8,128)(2,1)S(1)}) custom-call(s32[5]{0:T(128)S(1)} %copy-done.11, s32[4]{0:T(128)S(1)} %convert_reduce_fusion.2.refs_1_, bf16[256,768]{1,0:T(8,128)(2,1)S(1)} %collective-permute-done.10.refs_2_, bf16[256,768]{1,0:T(8,128)(2,1)S(1)} %collective-permute-done.18.refs_3_, ...), custom_call_target="tpu_custom_call" | custom-call | flops 905969664 | bytes 3000000 | tf_op jit(solution)/shard_map/pallas_call | solution.py:60
  69.7 1.2 collective-permute-done.24
  71.0 2.6 %shard_map.167 = (f32[1,1]{1,0:T(1,128)}, f32[32,768]{1,0:T(8,128)S(1)}, f32[32,768]{1,0:T(8,128)S(1)}, f32[8,384]{1,0:T(8,128)S(1)}, f32[8,768]{1,0:T(8,128)S(1)}) custom-call(s32[5]{0:T(128)S(1)} %copy-done.11, f32[32,1664]{1,0:T(8,128)S(1)} %maximum_select_fusion.2.refs_1_, f32[32,1152]{1,0:T(8,128)S(1)} %pad_maximum_fusion.4.refs_2_, ...), custom_call_target="tpu_custom_call" | custom-call | tf_op jit(solution)/shard_map/pallas_call | solution.py:60
  73.7 2.5 %shard_map.168 = (bf16[192,384]{1,0:T(8,128)(2,1)S(1)}, bf16[192,384]{1,0:T(8,128)(2,1)S(1)}, bf16[192,384]{1,0:T(8,128)(2,1)S(1)}, f32[192,384]{1,0:T(8,128)S(1)}, f32[1,768]{1,0:T(1,128)S(1)}) custom-call(s32[5]{0:T(128)S(1)} %copy-done.11, bf16[1024,768]{1,0:T(8,128)(2,1)S(1)} %copy-done.2, bf16[1024,768]{1,0:T(8,128)(2,1)S(1)} %get-tuple-element.115.refs_2_, ...), custom_call_target="tpu_custom_call" | custom-call | flops 4000000000 | bytes 3000000 | tf_op jit(solution)/shard_map/pallas_call | solution.py:60
  76.5 2.8 %collective-permute-start.26 = (bf16[192,384]{1,0:T(8,128)(2,1)S(1)}, bf16[192,384]{1,0:T(8,128)(2,1)S(1)}, u32[]{:S(2)}, u32[]{:S(2)}) collective-permute-start(bf16[192,384]{1,0:T(8,128)(2,1)S(1)} %get-tuple-element.121), channel_id=1, source_target_pairs={{0,16},{4,20},{8,24},{12,28},{16,0},{20,4},{24,8},{28,12},{1,17},{... | collective-permute-start | bytes 442376 | tf_op jit(solution)/shard_map/ppermute | solution.py:88
  79.3 1.3 %collective-permute-start.27 = (bf16[192,384]{1,0:T(8,128)(2,1)S(1)}, bf16[192,384]{1,0:T(8,128)(2,1)S(1)}, u32[]{:S(2)}, u32[]{:S(2)}) collective-permute-start(bf16[192,384]{1,0:T(8,128)(2,1)S(1)} %get-tuple-element.122), channel_id=1, source_target_pairs={{0,24},{4,28},{8,16},{12,20},{16,8},{20,12},{24,0},{28,4},{1,25},{... | collective-permute-start | bytes 442376 | tf_op jit(solution)/shard_map/ppermute | solution.py:88
  80.6 4.8 %shard_map.169 = (bf16[384,768]{1,0:T(8,128)(2,1)S(1)}, f32[384,768]{1,0:T(8,128)S(1)}, bf16[16,768]{1,0:T(8,128)(2,1)S(1)}) custom-call(s32[5]{0:T(128)S(1)} %copy-done.11, s32[8]{0:T(128)S(1)} %copy-done.14, bf16[1024,768]{1,0:T(8,128)(2,1)S(1)} %copy-done.17, f32[8,768]{1,0:T(8,128)S(1)} %get-tuple-element.126.refs_3_, bf16[768,384]{1,0:T(8,128)(2,1)S(1)} %copy-done.6, ...), custom_call_target="tpu_custom_call" | custom-call | flops 6000000000 | bytes 3000000 | tf_op jit(solution)/shard_map/pallas_call | solution.py:60
  86.1 1.9 %fusion.1 = f32[768,768]{1,0:T(8,128)} fusion(bf16[32,768]{1,0:T(8,128)(2,1)S(1)} %get-tuple-element.172, bf16[32,768]{1,0:T(8,128)(2,1)S(1)} %get-tuple-element.171, bf16[32,768]{1,0:T(8,128)(2,1)S(1)} %get-tuple-element.191, bf16[32,768]{1,0:T(8,128)(2,1)S(1)} %get-tuple-element.192), kind=kOutput, calls=%fused_computation.16 | convolution fusion | flops 114130944 | bytes 2555904 | tf_op jit(solution)/shard_map/dot_general | solution.py:803
  88.0 1.4 %fusion.12 = f32[384,768]{1,0:T(8,128)} fusion(bf16[32,768]{1,0:T(8,128)(2,1)S(1)} %get-tuple-element.180, bf16[32,768]{1,0:T(8,128)(2,1)S(1)} %get-tuple-element.179, bf16[32,384]{1,0:T(8,128)(2,1)S(1)} %get-tuple-element.174, bf16[32,384]{1,0:T(8,128)(2,1)S(1)} %get-tuple-element.173), kind=kOutput, calls=%fused_computation.27 | convolution fusion | flops 57286656 | bytes 1327104 | tf_op jit(solution)/shard_map/dot_general | solution.py:803
  90.0 0.7 collective-permute-done.30
  91.3 0.7 collective-permute-done.32
  92.5 0.7 collective-permute-start.39
  93.3 1.2 collective-permute-start.34
  94.6 1.9 %collective-permute-start.35 = (bf16[208,384]{1,0:T(8,128)(2,1)S(1)}, bf16[208,384]{1,0:T(8,128)(2,1)S(1)}, u32[]{:S(2)}, u32[]{:S(2)}) collective-permute-start(bf16[208,384]{1,0:T(8,128)(2,1)S(1)} %pad_maximum_fusion.3), channel_id=1, source_target_pairs={{0,16},{4,20},{8,24},{12,28},{16,0},{20,4},{24,8},{28,12},{1,17},{... | collective-permute-start | bytes 479240 | tf_op jit(solution)/shard_map/ppermute | solution.py:88
  96.5 1.3 %collective-permute-start.36 = (bf16[208,384]{1,0:T(8,128)(2,1)S(1)}, bf16[208,384]{1,0:T(8,128)(2,1)S(1)}, u32[]{:S(2)}, u32[]{:S(2)}) collective-permute-start(bf16[208,384]{1,0:T(8,128)(2,1)S(1)} %pad_maximum_fusion.3), channel_id=1, source_target_pairs={{0,24},{4,28},{8,16},{12,20},{16,8},{20,12},{24,0},{28,4},{1,25},{... | collective-permute-start | bytes 479240 | tf_op jit(solution)/shard_map/ppermute | solution.py:88
  97.8 0.8 collective-permute-start.37
  98.6 3.3 %collective-permute-done.34.refs_2_ = bf16[208,384]{1,0:T(8,128)(2,1)S(1)} collective-permute-done((bf16[208,384]{1,0:T(8,128)(2,1)S(1)}, bf16[208,384]{1,0:T(8,128)(2,1)S(1)}, u32[]{:S(2)}, u32[]{:S(2)}) %collective-permute-start.34) | collective-permute-done | bytes 159776 | tf_op jit(solution)/shard_map/ppermute | solution.py:88
  101.9 0.9 collective-permute-start.38
  102.9 6.2 %collective-permute-done.35.refs_2_ = bf16[208,384]{1,0:T(8,128)(2,1)S(1)} collective-permute-done((bf16[208,384]{1,0:T(8,128)(2,1)S(1)}, bf16[208,384]{1,0:T(8,128)(2,1)S(1)}, u32[]{:S(2)}, u32[]{:S(2)}) %collective-permute-start.35) | collective-permute-done | bytes 159776 | tf_op jit(solution)/shard_map/ppermute | solution.py:88
  109.2 3.7 %collective-permute-start.40 = (bf16[192,384]{1,0:T(8,128)(2,1)S(1)}, bf16[192,384]{1,0:T(8,128)(2,1)S(1)}, u32[]{:S(2)}, u32[]{:S(2)}) collective-permute-start(bf16[192,384]{1,0:T(8,128)(2,1)S(1)} %slice.329), channel_id=1, source_target_pairs={{0,16},{4,20},{8,24},{12,28},{16,0},{20,4},{24,8},{28,12},{1,17},{... | collective-permute-start | bytes 442376 | tf_op jit(solution)/shard_map/ppermute | solution.py:88
  113.1 1.0 collective-permute-start.41
  114.1 2.4 %shard_map.170.refs_1_ = f32[768,768]{1,0:T(8,128)} custom-call(s32[5]{0:T(128)S(1)} %copy-done.11, bf16[192,384]{1,0:T(8,128)(2,1)S(1)} %add_convert_fusion.1.refs_1_, bf16[208,384]{1,0:T(8,128)(2,1)S(1)} %collective-permute-done.34.refs_2_, bf16[192,384]{1,0:T(8,128)(2,1)S(1)} %collective-permute-done.37.refs_3_, ...), custom_call_target="tpu_custom_call" | custom-call | flops 2000000000 | bytes 3000000 | tf_op jit(solution)/shard_map/pallas_call | solution.py:60
  116.6 1.9 %collective-permute-done.40 = bf16[192,384]{1,0:T(8,128)(2,1)S(1)} collective-permute-done((bf16[192,384]{1,0:T(8,128)(2,1)S(1)}, bf16[192,384]{1,0:T(8,128)(2,1)S(1)}, u32[]{:S(2)}, u32[]{:S(2)}) %collective-permute-start.40) | collective-permute-done | bytes 147488 | tf_op jit(solution)/shard_map/ppermute | solution.py:88
  118.5 1.9 %collective-permute-done.41.refs_4_ = bf16[400,384]{1,0:T(8,128)(2,1)S(1)} collective-permute-done((bf16[400,384]{1,0:T(8,128)(2,1)S(1)}, bf16[400,384]{1,0:T(8,128)(2,1)S(1)}, u32[]{:S(2)}, u32[]{:S(2)}) %collective-permute-start.41) | collective-permute-done | bytes 307232 | tf_op jit(solution)/shard_map/ppermute | solution.py:88
  120.6 1.4 %collective-permute-start.42 = (bf16[208,384]{1,0:T(8,128)(2,1)S(1)}, bf16[208,384]{1,0:T(8,128)(2,1)S(1)}, u32[]{:S(2)}, u32[]{:S(2)}) collective-permute-start(bf16[208,384]{1,0:T(8,128)(2,1)S(1)} %pad_maximum_fusion.2), channel_id=1, source_target_pairs={{0,2},{1,3},{2,0},{3,1},{4,6},{5,7},{6,4},{7,5},{8,10},{9,11},{10,... | collective-permute-start | bytes 479240 | tf_op jit(solution)/shard_map/ppermute | solution.py:88
  122.0 2.2 %shard_map.171 = f32[768,768]{1,0:T(8,128)} custom-call(s32[5]{0:T(128)S(1)} %copy-done.11, f32[768,768]{1,0:T(8,128)} %shard_map.170.refs_1_, bf16[208,384]{1,0:T(8,128)(2,1)S(1)} %collective-permute-done.35.refs_2_, bf16[208,384]{1,0:T(8,128)(2,1)S(1)} %collective-permute-done.36.refs_3_, ...), custom_call_target="tpu_custom_call", output_to_operand_aliasing={{}: (1, {})} | custom-call | flops 2000000000 | bytes 3000000 | tf_op jit(solution)/shard_map/pallas_call | solution.py:60
  124.1 1.8 %collective-permute-done.42 = bf16[208,384]{1,0:T(8,128)(2,1)S(1)} collective-permute-done((bf16[208,384]{1,0:T(8,128)(2,1)S(1)}, bf16[208,384]{1,0:T(8,128)(2,1)S(1)}, u32[]{:S(2)}, u32[]{:S(2)}) %collective-permute-start.42) | collective-permute-done | bytes 159776 | tf_op jit(solution)/shard_map/ppermute | solution.py:88
  126.2 1.6 %collective-permute-done.43 = bf16[400,384]{1,0:T(8,128)(2,1)S(1)} collective-permute-done((bf16[400,384]{1,0:T(8,128)(2,1)S(1)}, bf16[400,384]{1,0:T(8,128)(2,1)S(1)}, u32[]{:S(2)}, u32[]{:S(2)}) %collective-permute-start.43) | collective-permute-done | bytes 307232 | tf_op jit(solution)/shard_map/ppermute | solution.py:88
  127.8 0.6 slice_reduce_fusion
  128.5 1.1 fusion
  (168 shorter events, 6.4 us)
Async XLA Ops:
  0.6 12.5 %copy-start.19 = (s32[1,8,256]{2,1,0:T(8,128)S(1)}, s32[1,8,256]{2,1,0:T(8,128)}, u32[]{:S(2)}) copy-start(s32[1,8,256]{2,1,0:T(8,128)} %param.17) | copy-start | bytes 24580
  0.6 21.7 %copy-start.20 = (s32[1,4,256]{2,1,0:T(4,128)S(1)}, s32[1,4,256]{2,1,0:T(4,128)}, u32[]{:S(2)}) copy-start(s32[1,4,256]{2,1,0:T(4,128)} %param.12) | copy-start | bytes 12292
  0.7 21.8 %copy-start.8 = (bf16[768,768]{1,0:T(8,128)(2,1)S(1)}, bf16[768,768]{1,0:T(8,128)(2,1)}, u32[]{:S(2)}) copy-start(bf16[768,768]{1,0:T(8,128)(2,1)} %refs_8_.2) | copy-start | bytes 3538948
  4.5 17.9 %collective-permute-start.2 = (bf16[192,768]{1,0:T(8,128)(2,1)}, bf16[192,768]{1,0:T(8,128)(2,1)}, u32[]{:S(2)}, u32[]{:S(2)}) collective-permute-start(bf16[192,768]{1,0:T(8,128)(2,1)} %get-tuple-element.81), channel_id=1, source_target_pairs={{0,16},{4,20},{8,24},{12,28},{16,0},{20,4},{24,8},{28,12},{1,17},{... | collective-permute-start | bytes 884744 | tf_op jit(solution)/shard_map/ppermute | solution.py:88
  8.6 15.3 %collective-permute-start = (bf16[256,768]{1,0:T(8,128)(2,1)}, bf16[256,768]{1,0:T(8,128)(2,1)}, u32[]{:S(2)}, u32[]{:S(2)}) collective-permute-start(bf16[256,768]{1,0:T(8,128)(2,1)} %get-tuple-element.80.refs_3_), channel_id=1, source_target_pairs={{0,4},{4,0},{8,12},{12,8},{16,20},{20,16},{24,28},{28,24},{1,5},{5... | collective-permute-start | bytes 1179656 | tf_op jit(solution)/shard_map/ppermute | solution.py:88
  10.1 15.7 %collective-permute-start.1 = (bf16[256,768]{1,0:T(8,128)(2,1)}, bf16[256,768]{1,0:T(8,128)(2,1)S(1)}, u32[]{:S(2)}, u32[]{:S(2)}) collective-permute-start(bf16[256,768]{1,0:T(8,128)(2,1)} %get-tuple-element.80.refs_3_), channel_id=1, source_target_pairs={{0,8},{4,12},{8,0},{12,4},{16,24},{20,28},{24,16},{28,20},{1,9},{5... | collective-permute-start | bytes 1179656 | tf_op jit(solution)/shard_map/ppermute | solution.py:88
  11.6 14.1 %collective-permute-start.4 = (bf16[256,768]{1,0:T(8,128)(2,1)}, bf16[256,768]{1,0:T(8,128)(2,1)S(1)}, u32[]{:S(2)}, u32[]{:S(2)}) collective-permute-start(bf16[256,768]{1,0:T(8,128)(2,1)} %get-tuple-element.90.refs_4_), channel_id=1, source_target_pairs={{0,2},{1,3},{2,0},{3,1},{4,6},{5,7},{6,4},{7,5},{8,10},{9,11},{10,... | collective-permute-start | bytes 1179656 | tf_op jit(solution)/shard_map/ppermute | solution.py:88
  13.2 16.0 %collective-permute-start.7 = (bf16[256,768]{1,0:T(8,128)(2,1)}, bf16[256,768]{1,0:T(8,128)(2,1)}, u32[]{:S(2)}, u32[]{:S(2)}) collective-permute-start(bf16[256,768]{1,0:T(8,128)(2,1)} %get-tuple-element.90.refs_4_), channel_id=1, source_target_pairs={{0,1},{1,0},{2,3},{3,2},{4,5},{5,4},{6,7},{7,6},{8,9},{9,8},{10,11... | collective-permute-start | bytes 1179656 | tf_op jit(solution)/shard_map/ppermute | solution.py:88
  22.3 3.4 %collective-permute-start.3 = (bf16[192,768]{1,0:T(8,128)(2,1)}, bf16[192,768]{1,0:T(8,128)(2,1)S(1)}, u32[]{:S(2)}, u32[]{:S(2)}) collective-permute-start(bf16[192,768]{1,0:T(8,128)(2,1)} %collective-permute-done.2.refs_9_), channel_id=1, source_target_pairs={{0,1},{1,0},{2,3},{3,2},{4,5},{5,4},{6,7},{7,6},{8,9},{9,8},{10,11... | collective-permute-start | bytes 884744 | tf_op jit(solution)/shard_map/ppermute | solution.py:88
  22.5 5.6 %copy-start.15 = (bf16[256,768]{1,0:T(8,128)(2,1)S(1)}, bf16[256,768]{1,0:T(8,128)(2,1)}, u32[]{:S(2)}) copy-start(bf16[256,768]{1,0:T(8,128)(2,1)} %get-tuple-element.90.refs_4_) | copy-start | bytes 1179652
  22.5 6.7 %copy-start.7 = (bf16[1,1,256,768]{3,2,1,0:T(8,128)(2,1)S(1)}, bf16[1,1,256,768]{3,2,1,0:T(8,128)(2,1)}, u32[]{:S(2)}) copy-start(bf16[1,1,256,768]{3,2,1,0:T(8,128)(2,1)} %param.11) | copy-start | bytes 1179652
  22.5 6.7 %copy-start.9 = (bf16[768,768]{1,0:T(8,128)(2,1)S(1)}, bf16[768,768]{1,0:T(8,128)(2,1)}, u32[]{:S(2)}) copy-start(bf16[768,768]{1,0:T(8,128)(2,1)} %refs_9_.1) | copy-start | bytes 3538948
  22.5 6.7 %copy-start.10 = (s32[5]{0:T(128)S(1)}, s32[5]{0:T(128)}, u32[]{:S(2)}) copy-start(s32[5]{0:T(128)} %stack.23.refs_0_) | copy-start | bytes 64
  22.5 6.7 %copy-start.16 = (s32[4]{0:T(128)S(1)}, s32[4]{0:T(128)}, u32[]{:S(2)}) copy-start(s32[4]{0:T(128)} %refs_2_.1) | copy-start | bytes 52
  25.7 3.5 %copy-start.23 = (bf16[192,768]{1,0:T(8,128)(2,1)}, bf16[192,768]{1,0:T(8,128)(2,1)S(1)}, u32[]{:S(2)}) copy-start(bf16[192,768]{1,0:T(8,128)(2,1)S(1)} %collective-permute-done.3.refs_11_) | copy-start | bytes 884740
  25.7 3.5 %collective-permute-start.8 = (bf16[256,768]{1,0:T(8,128)(2,1)S(1)}, bf16[256,768]{1,0:T(8,128)(2,1)S(1)}, u32[]{:S(2)}, u32[]{:S(2)}) collective-permute-start(bf16[256,768]{1,0:T(8,128)(2,1)S(1)} %collective-permute-done.4.refs_6_), channel_id=1, source_target_pairs={{0,1},{1,0},{2,3},{3,2},{4,5},{5,4},{6,7},{7,6},{8,9},{9,8},{10,11... | collective-permute-start | bytes 1179656 | tf_op jit(solution)/shard_map/ppermute | solution.py:88
  25.8 11.7 %collective-permute-start.5 = (bf16[256,768]{1,0:T(8,128)(2,1)}, bf16[256,768]{1,0:T(8,128)(2,1)S(1)}, u32[]{:S(2)}, u32[]{:S(2)}) collective-permute-start(bf16[256,768]{1,0:T(8,128)(2,1)} %collective-permute-done.refs_4_), channel_id=1, source_target_pairs={{0,8},{4,12},{8,0},{12,4},{16,24},{20,28},{24,16},{28,20},{1,9},{5... | collective-permute-start | bytes 1179656 | tf_op jit(solution)/shard_map/ppermute | solution.py:88
  26.5 11.0 %collective-permute-start.6 = (bf16[192,768]{1,0:T(8,128)(2,1)}, bf16[192,768]{1,0:T(8,128)(2,1)S(1)}, u32[]{:S(2)}, u32[]{:S(2)}) collective-permute-start(bf16[192,768]{1,0:T(8,128)(2,1)} %collective-permute-done.2.refs_9_), channel_id=1, source_target_pairs={{0,2},{1,3},{2,0},{3,1},{4,6},{5,7},{6,4},{7,5},{8,10},{9,11},{10,... | collective-permute-start | bytes 884744 | tf_op jit(solution)/shard_map/ppermute | solution.py:88
  28.0 10.7 %collective-permute-start.10 = (bf16[256,768]{1,0:T(8,128)(2,1)S(1)}, bf16[256,768]{1,0:T(8,128)(2,1)S(1)}, u32[]{:S(2)}, u32[]{:S(2)}) collective-permute-start(bf16[256,768]{1,0:T(8,128)(2,1)S(1)} %copy-done.15), channel_id=1, source_target_pairs={{0,4},{4,0},{8,12},{12,8},{16,20},{20,16},{24,28},{28,24},{1,5},{5... | collective-permute-start | bytes 1179656 | tf_op jit(solution)/shard_map/ppermute | solution.py:88
  33.5 2.4 %copy-start.1 = (bf16[1024,768]{1,0:T(8,128)(2,1)}, bf16[1024,768]{1,0:T(8,128)(2,1)S(1)}, u32[]{:S(2)}) copy-start(bf16[1024,768]{1,0:T(8,128)(2,1)S(1)} %get-tuple-element.88.refs_2_.refs_1_) | copy-start | bytes 4718596
  33.5 3.9 %collective-permute-start.9 = (f32[4,1664]{1,0:T(4,128)S(1)}, f32[4,1664]{1,0:T(4,128)S(1)}, u32[]{:S(2)}, u32[]{:S(2)}) collective-permute-start(f32[4,1664]{1,0:T(4,128)S(1)} %get-tuple-element.87), channel_id=1, source_target_pairs={{0,2},{1,3},{2,0},{3,1},{4,6},{5,7},{6,4},{7,5},{8,10},{9,11},{10,... | collective-permute-start | bytes 79880 | tf_op jit(solution)/shard_map/ppermute | solution.py:88
  38.7 1.7 %collective-permute-start.11 = (f32[4,1664]{1,0:T(4,128)S(1)}, f32[4,1664]{1,0:T(4,128)S(1)}, u32[]{:S(2)}, u32[]{:S(2)}) collective-permute-start(f32[4,1664]{1,0:T(4,128)S(1)} %add_select_fusion.1), channel_id=1, source_target_pairs={{0,1},{1,0},{2,3},{3,2},{4,5},{5,4},{6,7},{7,6},{8,9},{9,8},{10,11... | collective-permute-start | bytes 79880 | tf_op jit(solution)/shard_map/ppermute | solution.py:88
  38.8 18.2 %collective-permute-start.18 = (bf16[256,768]{1,0:T(8,128)(2,1)S(1)}, bf16[256,768]{1,0:T(8,128)(2,1)S(1)}, u32[]{:S(2)}, u32[]{:S(2)}) collective-permute-start(bf16[256,768]{1,0:T(8,128)(2,1)S(1)} %collective-permute-done.10.refs_2_), channel_id=1, source_target_pairs={{0,1},{1,0},{2,3},{3,2},{4,5},{5,4},{6,7},{7,6},{8,9},{9,8},{10,11... | collective-permute-start | bytes 1179656 | tf_op jit(solution)/shard_map/ppermute | solution.py:88
  39.2 14.6 %collective-permute-start.19 = (bf16[256,768]{1,0:T(8,128)(2,1)S(1)}, bf16[256,768]{1,0:T(8,128)(2,1)}, u32[]{:S(2)}, u32[]{:S(2)}) collective-permute-start(bf16[256,768]{1,0:T(8,128)(2,1)S(1)} %collective-permute-done.10.refs_2_), channel_id=1, source_target_pairs={{0,2},{1,3},{2,0},{3,1},{4,6},{5,7},{6,4},{7,5},{8,10},{9,11},{10,... | collective-permute-start | bytes 1179656 | tf_op jit(solution)/shard_map/ppermute | solution.py:88
  40.4 1.9 %collective-permute-start.13 = (bf16[192,768]{1,0:T(8,128)(2,1)}, bf16[192,768]{1,0:T(8,128)(2,1)}, u32[]{:S(2)}, u32[]{:S(2)}) collective-permute-start(bf16[192,768]{1,0:T(8,128)(2,1)} %copy-done.24), channel_id=1, source_target_pairs={{0,1},{1,0},{2,3},{3,2},{4,5},{5,4},{6,7},{7,6},{8,9},{9,8},{10,11... | collective-permute-start | bytes 884744 | tf_op jit(solution)/shard_map/ppermute | solution.py:88
  40.5 25.8 %copy-start.11 = (s32[5]{0:T(128)S(1)}, s32[5]{0:T(128)}, u32[]{:S(2)}) copy-start(s32[5]{0:T(128)} %stack.23.refs_0_) | copy-start | bytes 64
  40.5 10.6 %collective-permute-start.12 = (f32[4,1664]{1,0:T(4,128)S(1)}, f32[4,1664]{1,0:T(4,128)S(1)}, u32[]{:S(2)}, u32[]{:S(2)}) collective-permute-start(f32[4,1664]{1,0:T(4,128)S(1)} %add_select_fusion), channel_id=1, source_target_pairs={{0,4},{4,0},{8,12},{12,8},{16,20},{20,16},{24,28},{28,24},{1,5},{5... | collective-permute-start | bytes 79880 | tf_op jit(solution)/shard_map/ppermute | solution.py:88
  48.9 4.0 %collective-permute-start.15 = (f32[4,768]{1,0:T(4,128)}, f32[4,768]{1,0:T(4,128)S(1)}, u32[]{:S(2)}, u32[]{:S(2)}) collective-permute-start(f32[4,768]{1,0:T(4,128)} %get-tuple-element.98), channel_id=1, source_target_pairs={{0,8},{4,12},{8,0},{12,4},{16,24},{20,28},{24,16},{28,20},{1,9},{5... | collective-permute-start | bytes 36872 | tf_op jit(solution)/shard_map/ppermute | solution.py:88
  49.9 4.8 %collective-permute-start.16 = (f32[4,768]{1,0:T(4,128)}, f32[4,768]{1,0:T(4,128)S(1)}, u32[]{:S(2)}, u32[]{:S(2)}) collective-permute-start(f32[4,768]{1,0:T(4,128)} %get-tuple-element.98), channel_id=1, source_target_pairs={{0,12},{4,8},{8,4},{12,0},{16,28},{20,24},{24,20},{28,16},{1,13},{... | collective-permute-start | bytes 36872 | tf_op jit(solution)/shard_map/ppermute | solution.py:88
  51.1 3.9 %collective-permute-start.14 = (f32[4,768]{1,0:T(4,128)}, f32[4,768]{1,0:T(4,128)S(1)}, u32[]{:S(2)}, u32[]{:S(2)}) collective-permute-start(f32[4,768]{1,0:T(4,128)} %get-tuple-element.98), channel_id=1, source_target_pairs={{0,4},{4,0},{8,12},{12,8},{16,20},{20,16},{24,28},{28,24},{1,5},{5... | collective-permute-start | bytes 36872 | tf_op jit(solution)/shard_map/ppermute | solution.py:88
  52.9 4.1 %collective-permute-start.17 = (f32[8,1664]{1,0:T(8,128)S(1)}, f32[8,1664]{1,0:T(8,128)S(1)}, u32[]{:S(2)}, u32[]{:S(2)}) collective-permute-start(f32[8,1664]{1,0:T(8,128)S(1)} %maximum_select_fusion.6), channel_id=1, source_target_pairs={{0,8},{4,12},{8,0},{12,4},{16,24},{20,28},{24,16},{28,20},{1,9},{5... | collective-permute-start | bytes 159752 | tf_op jit(solution)/shard_map/ppermute | solution.py:88
  53.9 3.2 %collective-permute-start.20 = (bf16[256,768]{1,0:T(8,128)(2,1)}, bf16[256,768]{1,0:T(8,128)(2,1)S(1)}, u32[]{:S(2)}, u32[]{:S(2)}) collective-permute-start(bf16[256,768]{1,0:T(8,128)(2,1)} %collective-permute-done.19.refs_4_), channel_id=1, source_target_pairs={{0,1},{1,0},{2,3},{3,2},{4,5},{5,4},{6,7},{7,6},{8,9},{9,8},{10,11... | collective-permute-start | bytes 1179656 | tf_op jit(solution)/shard_map/ppermute | solution.py:88
  57.0 12.6 %collective-permute-start.21 = (f32[16,1664]{1,0:T(8,128)S(1)}, f32[16,1664]{1,0:T(8,128)S(1)}, u32[]{:S(2)}, u32[]{:S(2)}) collective-permute-start(f32[16,1664]{1,0:T(8,128)S(1)} %maximum_select_fusion.4), channel_id=1, source_target_pairs={{0,16},{4,20},{8,24},{12,28},{16,0},{20,4},{24,8},{28,12},{1,17},{... | collective-permute-start | bytes 319496 | tf_op jit(solution)/shard_map/ppermute | solution.py:88
  59.8 4.8 %collective-permute-start.22 = (f32[4,1152]{1,0:T(4,128)S(1)}, f32[4,1152]{1,0:T(4,128)S(1)}, u32[]{:S(2)}, u32[]{:S(2)}) collective-permute-start(f32[4,1152]{1,0:T(4,128)S(1)} %pad_maximum_fusion.5), channel_id=1, source_target_pairs={{0,16},{4,20},{8,24},{12,28},{16,0},{20,4},{24,8},{28,12},{1,17},{... | collective-permute-start | bytes 55304 | tf_op jit(solution)/shard_map/ppermute | solution.py:88
  64.6 4.9 %collective-permute-start.23 = (f32[1,8,1152]{2,1,0:T(8,128)S(1)}, f32[1,8,1152]{2,1,0:T(8,128)S(1)}, u32[]{:S(2)}, u32[]{:S(2)}) collective-permute-start(f32[1,8,1152]{2,1,0:T(8,128)S(1)} %maximum_bitcast_fusion), channel_id=1, source_target_pairs={{0,2},{1,3},{2,0},{3,1},{4,6},{5,7},{6,4},{7,5},{8,10},{9,11},{10,... | collective-permute-start | bytes 110600 | tf_op jit(solution)/shard_map/ppermute | solution.py:88
  66.2 4.7 %copy-start.5 = (bf16[384,768]{1,0:T(8,128)(2,1)S(1)}, bf16[384,768]{1,0:T(8,128)(2,1)}, u32[]{:S(2)}) copy-start(bf16[384,768]{1,0:T(8,128)(2,1)} %get-tuple-element.113.refs_5_) | copy-start | bytes 1769476
  69.5 1.3 %collective-permute-start.24 = (f32[2,8,1152]{2,1,0:T(8,128)S(1)}, f32[2,8,1152]{2,1,0:T(8,128)S(1)}, u32[]{:S(2)}, u32[]{:S(2)}) collective-permute-start(f32[2,8,1152]{2,1,0:T(8,128)S(1)} %maximum_select_fusion.5), channel_id=1, source_target_pairs={{0,1},{1,0},{2,3},{3,2},{4,5},{5,4},{6,7},{7,6},{8,9},{9,8},{10,11... | collective-permute-start | bytes 221192 | tf_op jit(solution)/shard_map/ppermute | solution.py:88
  69.6 3.9 %copy-start.4 = (f32[1024,384]{1,0:T(8,128)S(1)}, f32[1024,384]{1,0:T(8,128)}, u32[]{:S(2)}) copy-start(f32[1024,384]{1,0:T(8,128)} %copy-done.3) | copy-start | bytes 4718596
  70.9 2.7 %copy-start.2 = (bf16[1024,768]{1,0:T(8,128)(2,1)S(1)}, bf16[1024,768]{1,0:T(8,128)(2,1)}, u32[]{:S(2)}) copy-start(bf16[1024,768]{1,0:T(8,128)(2,1)} %copy-done.1) | copy-start | bytes 4718596
  70.9 2.7 %copy-start.12 = (f32[768]{0:T(1024)S(1)}, f32[768]{0:T(1024)}, u32[]{:S(2)}) copy-start(f32[768]{0:T(1024)} %refs_7_.3) | copy-start | bytes 9220
  73.6 7.0 %copy-start.6 = (bf16[768,384]{1,0:T(8,128)(2,1)S(1)}, bf16[768,384]{1,0:T(8,128)(2,1)}, u32[]{:S(2)}) copy-start(bf16[768,384]{1,0:T(8,128)(2,1)} %refs_4_.5) | copy-start | bytes 1769476
  73.6 7.0 %copy-start.13 = (f32[768]{0:T(1024)S(1)}, f32[768]{0:T(1024)}, u32[]{:S(2)}) copy-start(f32[768]{0:T(1024)} %refs_6_.3) | copy-start | bytes 9220
  73.6 7.0 %copy-start.14 = (s32[8]{0:T(128)S(1)}, s32[8]{0:T(128)}, u32[]{:S(2)}) copy-start(s32[8]{0:T(128)} %convert_reduce_fusion.refs_1_) | copy-start | bytes 100
  73.6 7.0 %copy-start.17 = (bf16[1024,768]{1,0:T(8,128)(2,1)S(1)}, bf16[1024,768]{1,0:T(8,128)(2,1)}, u32[]{:S(2)}) copy-start(bf16[1024,768]{1,0:T(8,128)(2,1)} %get-tuple-element.123.refs_2_) | copy-start | bytes 4718596
  73.7 7.0 %copy-start.18 = (bf16[768,384]{1,0:T(8,128)(2,1)S(1)}, bf16[768,384]{1,0:T(8,128)(2,1)}, u32[]{:S(2)}) copy-start(bf16[768,384]{1,0:T(8,128)(2,1)} %get-tuple-element.127.refs_5_) | copy-start | bytes 1769476
  76.2 16.2 %collective-permute-start.25 = (bf16[192,384]{1,0:T(8,128)(2,1)S(1)}, bf16[192,384]{1,0:T(8,128)(2,1)S(1)}, u32[]{:S(2)}, u32[]{:S(2)}) collective-permute-start(bf16[192,384]{1,0:T(8,128)(2,1)S(1)} %get-tuple-element.120), channel_id=1, source_target_pairs={{0,8},{4,12},{8,0},{12,4},{16,24},{20,28},{24,16},{28,20},{1,9},{5... | collective-permute-start | bytes 442376 | tf_op jit(solution)/shard_map/ppermute | solution.py:88
  76.5 15.9 %collective-permute-start.26 = (bf16[192,384]{1,0:T(8,128)(2,1)S(1)}, bf16[192,384]{1,0:T(8,128)(2,1)S(1)}, u32[]{:S(2)}, u32[]{:S(2)}) collective-permute-start(bf16[192,384]{1,0:T(8,128)(2,1)S(1)} %get-tuple-element.121), channel_id=1, source_target_pairs={{0,16},{4,20},{8,24},{12,28},{16,0},{20,4},{24,8},{28,12},{1,17},{... | collective-permute-start | bytes 442376 | tf_op jit(solution)/shard_map/ppermute | solution.py:88
  79.3 13.1 %collective-permute-start.27 = (bf16[192,384]{1,0:T(8,128)(2,1)S(1)}, bf16[192,384]{1,0:T(8,128)(2,1)S(1)}, u32[]{:S(2)}, u32[]{:S(2)}) collective-permute-start(bf16[192,384]{1,0:T(8,128)(2,1)S(1)} %get-tuple-element.122), channel_id=1, source_target_pairs={{0,24},{4,28},{8,16},{12,20},{16,8},{20,12},{24,0},{28,4},{1,25},{... | collective-permute-start | bytes 442376 | tf_op jit(solution)/shard_map/ppermute | solution.py:88
  85.5 3.9 %collective-permute-start.28 = (bf16[64,768]{1,0:T(8,128)(2,1)S(1)}, bf16[64,768]{1,0:T(8,128)(2,1)S(1)}, u32[]{:S(2)}, u32[]{:S(2)}) collective-permute-start(bf16[64,768]{1,0:T(8,128)(2,1)S(1)} %get-tuple-element.170), channel_id=1, source_target_pairs={{0,1},{1,0},{2,3},{3,2},{4,5},{5,4},{6,7},{7,6},{8,9},{9,8},{10,11... | collective-permute-start | bytes 294920 | tf_op jit(solution)/shard_map/ppermute | solution.py:88
  85.6 3.9 %collective-permute-start.29 = (bf16[64,768]{1,0:T(8,128)(2,1)S(1)}, bf16[64,768]{1,0:T(8,128)(2,1)S(1)}, u32[]{:S(2)}, u32[]{:S(2)}) collective-permute-start(bf16[64,768]{1,0:T(8,128)(2,1)S(1)} %get-tuple-element.169), channel_id=1, source_target_pairs={{0,1},{1,0},{2,3},{3,2},{4,5},{5,4},{6,7},{7,6},{8,9},{9,8},{10,11... | collective-permute-start | bytes 294920 | tf_op jit(solution)/shard_map/ppermute | solution.py:88
  89.4 1.3 %collective-permute-start.30 = (bf16[64,768]{1,0:T(8,128)(2,1)S(1)}, bf16[64,768]{1,0:T(8,128)(2,1)S(1)}, u32[]{:S(2)}, u32[]{:S(2)}) collective-permute-start(bf16[64,768]{1,0:T(8,128)(2,1)S(1)} %get-tuple-element.168), channel_id=1, source_target_pairs={{0,1},{1,0},{2,3},{3,2},{4,5},{5,4},{6,7},{7,6},{8,9},{9,8},{10,11... | collective-permute-start | bytes 294920 | tf_op jit(solution)/shard_map/ppermute | solution.py:88
  89.5 1.4 %collective-permute-start.31 = (bf16[64,768]{1,0:T(8,128)(2,1)S(1)}, bf16[64,768]{1,0:T(8,128)(2,1)S(1)}, u32[]{:S(2)}, u32[]{:S(2)}) collective-permute-start(bf16[64,768]{1,0:T(8,128)(2,1)S(1)} %get-tuple-element.167), channel_id=1, source_target_pairs={{0,1},{1,0},{2,3},{3,2},{4,5},{5,4},{6,7},{7,6},{8,9},{9,8},{10,11... | collective-permute-start | bytes 294920 | tf_op jit(solution)/shard_map/ppermute | solution.py:88
  90.7 1.3 %collective-permute-start.32 = (bf16[64,768]{1,0:T(8,128)(2,1)S(1)}, bf16[64,768]{1,0:T(8,128)(2,1)S(1)}, u32[]{:S(2)}, u32[]{:S(2)}) collective-permute-start(bf16[64,768]{1,0:T(8,128)(2,1)S(1)} %get-tuple-element.166), channel_id=1, source_target_pairs={{0,1},{1,0},{2,3},{3,2},{4,5},{5,4},{6,7},{7,6},{8,9},{9,8},{10,11... | collective-permute-start | bytes 294920 | tf_op jit(solution)/shard_map/ppermute | solution.py:88
  90.9 1.3 %collective-permute-start.33 = (bf16[64,768]{1,0:T(8,128)(2,1)S(1)}, bf16[64,768]{1,0:T(8,128)(2,1)S(1)}, u32[]{:S(2)}, u32[]{:S(2)}) collective-permute-start(bf16[64,768]{1,0:T(8,128)(2,1)S(1)} %get-tuple-element.165), channel_id=1, source_target_pairs={{0,1},{1,0},{2,3},{3,2},{4,5},{5,4},{6,7},{7,6},{8,9},{9,8},{10,11... | collective-permute-start | bytes 294920 | tf_op jit(solution)/shard_map/ppermute | solution.py:88
  92.5 10.3 %collective-permute-start.39 = (bf16[192,768]{1,0:T(8,128)(2,1)S(1)}, bf16[192,768]{1,0:T(8,128)(2,1)S(1)}, u32[]{:S(2)}, u32[]{:S(2)}) collective-permute-start(bf16[192,768]{1,0:T(8,128)(2,1)S(1)} %dynamic-slice_convert_fusion), channel_id=1, source_target_pairs={{0,2},{1,3},{2,0},{3,1},{4,6},{5,7},{6,4},{7,5},{8,10},{9,11},{10,... | collective-permute-start | bytes 884744 | tf_op jit(solution)/shard_map/ppermute | solution.py:88
  93.3 8.5 %collective-permute-start.34 = (bf16[208,384]{1,0:T(8,128)(2,1)S(1)}, bf16[208,384]{1,0:T(8,128)(2,1)S(1)}, u32[]{:S(2)}, u32[]{:S(2)}) collective-permute-start(bf16[208,384]{1,0:T(8,128)(2,1)S(1)} %pad_maximum_fusion.3), channel_id=1, source_target_pairs={{0,8},{4,12},{8,0},{12,4},{16,24},{20,28},{24,16},{28,20},{1,9},{5... | collective-permute-start | bytes 479240 | tf_op jit(solution)/shard_map/ppermute | solution.py:88
  94.6 14.6 %collective-permute-start.35 = (bf16[208,384]{1,0:T(8,128)(2,1)S(1)}, bf16[208,384]{1,0:T(8,128)(2,1)S(1)}, u32[]{:S(2)}, u32[]{:S(2)}) collective-permute-start(bf16[208,384]{1,0:T(8,128)(2,1)S(1)} %pad_maximum_fusion.3), channel_id=1, source_target_pairs={{0,16},{4,20},{8,24},{12,28},{16,0},{20,4},{24,8},{28,12},{1,17},{... | collective-permute-start | bytes 479240 | tf_op jit(solution)/shard_map/ppermute | solution.py:88
  96.5 12.7 %collective-permute-start.36 = (bf16[208,384]{1,0:T(8,128)(2,1)S(1)}, bf16[208,384]{1,0:T(8,128)(2,1)S(1)}, u32[]{:S(2)}, u32[]{:S(2)}) collective-permute-start(bf16[208,384]{1,0:T(8,128)(2,1)S(1)} %pad_maximum_fusion.3), channel_id=1, source_target_pairs={{0,24},{4,28},{8,16},{12,20},{16,8},{20,12},{24,0},{28,4},{1,25},{... | collective-permute-start | bytes 479240 | tf_op jit(solution)/shard_map/ppermute | solution.py:88
  97.8 5.1 %collective-permute-start.37 = (bf16[192,384]{1,0:T(8,128)(2,1)S(1)}, bf16[192,384]{1,0:T(8,128)(2,1)S(1)}, u32[]{:S(2)}, u32[]{:S(2)}) collective-permute-start(bf16[192,384]{1,0:T(8,128)(2,1)S(1)} %add_convert_fusion.1.refs_1_), channel_id=1, source_target_pairs={{0,4},{4,0},{8,12},{12,8},{16,20},{20,16},{24,28},{28,24},{1,5},{5... | collective-permute-start | bytes 442376 | tf_op jit(solution)/shard_map/ppermute | solution.py:88
  101.9 7.2 %collective-permute-start.38 = (bf16[192,384]{1,0:T(8,128)(2,1)S(1)}, bf16[192,384]{1,0:T(8,128)(2,1)S(1)}, u32[]{:S(2)}, u32[]{:S(2)}) collective-permute-start(bf16[192,384]{1,0:T(8,128)(2,1)S(1)} %slice.231), channel_id=1, source_target_pairs={{0,4},{4,0},{8,12},{12,8},{16,20},{20,16},{24,28},{28,24},{1,5},{5... | collective-permute-start | bytes 442376 | tf_op jit(solution)/shard_map/ppermute | solution.py:88
  109.2 9.2 %collective-permute-start.40 = (bf16[192,384]{1,0:T(8,128)(2,1)S(1)}, bf16[192,384]{1,0:T(8,128)(2,1)S(1)}, u32[]{:S(2)}, u32[]{:S(2)}) collective-permute-start(bf16[192,384]{1,0:T(8,128)(2,1)S(1)} %slice.329), channel_id=1, source_target_pairs={{0,16},{4,20},{8,24},{12,28},{16,0},{20,4},{24,8},{28,12},{1,17},{... | collective-permute-start | bytes 442376 | tf_op jit(solution)/shard_map/ppermute | solution.py:88
  113.1 7.3 %collective-permute-start.41 = (bf16[400,384]{1,0:T(8,128)(2,1)S(1)}, bf16[400,384]{1,0:T(8,128)(2,1)S(1)}, u32[]{:S(2)}, u32[]{:S(2)}) collective-permute-start(bf16[400,384]{1,0:T(8,128)(2,1)S(1)} %pad_maximum_fusion.1), channel_id=1, source_target_pairs={{0,4},{4,0},{8,12},{12,8},{16,20},{20,16},{24,28},{28,24},{1,5},{5... | collective-permute-start | bytes 921608 | tf_op jit(solution)/shard_map/ppermute | solution.py:88
  120.6 5.3 %collective-permute-start.42 = (bf16[208,384]{1,0:T(8,128)(2,1)S(1)}, bf16[208,384]{1,0:T(8,128)(2,1)S(1)}, u32[]{:S(2)}, u32[]{:S(2)}) collective-permute-start(bf16[208,384]{1,0:T(8,128)(2,1)S(1)} %pad_maximum_fusion.2), channel_id=1, source_target_pairs={{0,2},{1,3},{2,0},{3,1},{4,6},{5,7},{6,4},{7,5},{8,10},{9,11},{10,... | collective-permute-start | bytes 479240 | tf_op jit(solution)/shard_map/ppermute | solution.py:88
  126.1 1.7 %collective-permute-start.43 = (bf16[400,384]{1,0:T(8,128)(2,1)S(1)}, bf16[400,384]{1,0:T(8,128)(2,1)S(1)}, u32[]{:S(2)}, u32[]{:S(2)}) collective-permute-start(bf16[400,384]{1,0:T(8,128)(2,1)S(1)} %pad_maximum_fusion), channel_id=1, source_target_pairs={{0,1},{1,0},{2,3},{3,2},{4,5},{5,4},{6,7},{7,6},{8,9},{9,8},{10,11... | collective-permute-start | bytes 921608 | tf_op jit(solution)/shard_map/ppermute | solution.py:88
  (5 other events, 5.8 us)
